TPU v7x, 32 devices: a whole 2x2x4 slice. The times are simulated.
32 devices in a mesh: ctx: 8 (over z, core), mp: 4 (over y, x).
Axes of the slice: x: 2, y: 2, z: 4, core: 2. Of those that a mesh axis runs over, the one named last changes fastest.
Arguments:
- grad_out: bfloat16 [4096, 4096], P('ctx', 'mp'), may hold values from -6 to 6
- proj_out: bfloat16 [4096, 4096], P('mp', 'ctx'), may hold values from -0.09375 to 0.09375
- query: bfloat16 [4096, 4096], P('ctx', 'mp'), may hold values from -6 to 6
- key_in: bfloat16 [4096, 4096], P('ctx', 'mp'), may hold values from -6 to 6
- value_in: bfloat16 [4096, 4096], P('ctx', 'mp'), may hold values from -6 to 6
- filters: float32 [4096, 4096], P(('mp', 'ctx')), may hold values from -0.09375 to 0.09375
Outputs:
- grad_query: bfloat16 [4096, 4096], P('ctx', 'mp')
- grad_key: bfloat16 [4096, 4096], P('ctx', 'mp')
- grad_value: bfloat16 [4096, 4096], P('ctx', 'mp')
- filter_grad: float32 [4096, 4096], P(('mp', 'ctx'))
All inputs are finite; a program needn't handle non-finite values.
Results may differ from a plain program's by a relative error of at most 0.013.
Values may be sent and summed in bfloat16 or wider, within the bound.
No kernel may reach another device: no remote copies, remote signals or barrier semaphores. Data moves between devices by JAX's collectives and lax.ppermute only.
A program may use at most 128 MiB of HBM per device.

v0:
```python
import math

import jax
import jax.numpy as jnp
from jax import lax
from jax.sharding import PartitionSpec as P


def phase_table(rows_n, cols_n, modulus):
    prod_idx = (
        jnp.arange(rows_n, dtype=jnp.int32)[:, None]
        * jnp.arange(cols_n, dtype=jnp.int32)[None, :]
        % modulus
    )
    angles = prod_idx.astype(jnp.float32) * (2.0 * math.pi / modulus)
    return (jnp.cos(angles), jnp.sin(angles))


def make_tables(length_all):
    size_second = min(128, length_all)
    size_first = length_all // size_second
    cos_first, sin_first = phase_table(size_first, size_first, size_first)
    twist_cos, twist_sin = phase_table(size_first, size_second, length_all)
    cos_second, sin_second = phase_table(size_second, size_second, size_second)
    return (cos_first, sin_first, twist_cos, twist_sin, cos_second, sin_second)


def contract(form, left, right):
    return jnp.einsum(form, left, right, precision=lax.Precision.HIGHEST)


def forward_real(signal, tables):
    cos_first, sin_first, twist_cos, twist_sin, cos_second, sin_second = tables
    part_re = contract("kn,cnm->ckm", cos_first, signal)
    part_im = -contract("kn,cnm->ckm", sin_first, signal)
    turned_re = part_re * twist_cos + part_im * twist_sin
    turned_im = part_im * twist_cos - part_re * twist_sin
    spec_re = contract("ckm,mj->ckj", turned_re, cos_second) + contract(
        "ckm,mj->ckj", turned_im, sin_second
    )
    spec_im = contract("ckm,mj->ckj", turned_im, cos_second) - contract(
        "ckm,mj->ckj", turned_re, sin_second
    )
    return (spec_re, spec_im)


def inverse_real(spec_re, spec_im, tables):
    cos_first, sin_first, twist_cos, twist_sin, cos_second, sin_second = tables
    back_re = contract("ckj,jm->ckm", spec_re, cos_second) - contract(
        "ckj,jm->ckm", spec_im, sin_second
    )
    back_im = contract("ckj,jm->ckm", spec_re, sin_second) + contract(
        "ckj,jm->ckm", spec_im, cos_second
    )
    twist_re = back_re * twist_cos - back_im * twist_sin
    twist_im = back_re * twist_sin + back_im * twist_cos
    return contract("nk,ckm->cnm", cos_first, twist_re) - contract(
        "nk,ckm->cnm", sin_first, twist_im
    )


def long_filter_grads(gated, scaled, kernel):
    channels, seq_len = kernel.shape
    length_all = 2 * seq_len
    tables = make_tables(length_all)
    spec_shape = (channels, tables[0].shape[0], tables[4].shape[0])

    def padded(values):
        wide = jnp.concatenate(
            [values.astype(jnp.float32), jnp.zeros((channels, seq_len), jnp.float32)], axis=1
        )
        return wide.reshape(spec_shape)

    def restore(spec_re, spec_im):
        return (
            inverse_real(spec_re, spec_im, tables).reshape(channels, length_all)[:, :seq_len]
            / length_all
        )

    gated_re, gated_im = forward_real(padded(gated), tables)
    scaled_re, scaled_im = forward_real(padded(scaled), tables)
    kernel_re, kernel_im = forward_real(padded(kernel), tables)
    conv_out = restore(
        kernel_re * gated_re - kernel_im * gated_im, kernel_re * gated_im + kernel_im * gated_re
    )
    grad_gated = restore(
        scaled_re * kernel_re + scaled_im * kernel_im, scaled_im * kernel_re - scaled_re * kernel_im
    )
    grad_kernel = restore(
        scaled_re * gated_re + scaled_im * gated_im, scaled_im * gated_re - scaled_re * gated_im
    )
    filter_grad = grad_kernel / math.sqrt(seq_len)
    return (conv_out.astype(jnp.bfloat16), grad_gated.astype(jnp.bfloat16), filter_grad)


def product(left, right):
    return (left.astype(jnp.float32) * right.astype(jnp.float32)).astype(jnp.bfloat16)


def body(grad_out, proj_out, query, key_in, value_in, filters):
    weight_rows = lax.all_gather(proj_out, "ctx", axis=1, tiled=True)
    grad_mix = lax.dot_general(
        lax.all_gather(grad_out, "mp", axis=1, tiled=True),
        weight_rows,
        (((1,), (1,)), ((), ())),
        preferred_element_type=jnp.float32,
    ).astype(jnp.bfloat16)
    gated = product(key_in, value_in)
    scaled = product(grad_mix, query)
    chan_gated, chan_scaled = (
        lax.all_to_all(gated.T, "ctx", split_axis=0, concat_axis=1, tiled=True),
        lax.all_to_all(scaled.T, "ctx", split_axis=0, concat_axis=1, tiled=True),
    )
    conv_out, grad_gated, filter_grad = long_filter_grads(chan_gated, chan_scaled, filters)
    back_grad, back_conv = (
        lax.all_to_all(grad_gated, "ctx", split_axis=1, concat_axis=0, tiled=True),
        lax.all_to_all(conv_out, "ctx", split_axis=1, concat_axis=0, tiled=True),
    )
    grad_query = product(grad_mix, back_conv.T)
    grad_key = product(back_grad.T, value_in)
    grad_value = product(back_grad.T, key_in)
    return (grad_query, grad_key, grad_value, filter_grad)


def solution(mesh):
    return jax.shard_map(
        body,
        mesh=mesh,
        in_specs=(
            P("ctx", "mp"),
            P("mp", "ctx"),
            P("ctx", "mp"),
            P("ctx", "mp"),
            P("ctx", "mp"),
            P(("mp", "ctx"), None),
        ),
        out_specs=(P("ctx", "mp"), P("ctx", "mp"), P("ctx", "mp"), P(("mp", "ctx"), None)),
        check_vma=False,
    )
```

profile of v0, /device:TPU:1, one launch (start us, length us, event | category | flops | bytes accessed | tf_op | source)
XLA Modules:
  0.0 502.6 jit_solution(5378611335699397729)
XLA Ops:
  8.7 1.5 copy.100
  11.0 1.3 copy.102
  12.4 6.4 %all-to-all-start = ((bf16[8,128,512]{1,2,0:T(8,128)(2,1)}), bf16[8,128,512]{1,2,0:T(8,128)(2,1)S(1)}, u32[]{:S(2)}, u32[]{:S(2)}) async-start(bf16[8,128,512]{1,2,0:T(8,128)(2,1)} %copy.102), calls=%async_computation | async-start | bytes 2097152 | tf_op jit(solution)/shard_map/all_to_all | solution.py:111
  18.7 4.2 pad_bitcast_fusion
  22.9 41.7 %all-gather.3.cloned.1.call-done = bf16[512,4096]{1,0:T(8,128)(2,1)} async-done(((bf16[512,1024]{1,0:T(8,128)(2,1)}), bf16[512,4096]{1,0:T(8,128)(2,1)}) %all-gather.3.cloned.1.call-update) | async-done | bytes 4194320 | tf_op jit(solution)/shard_map/all_gather | solution.py:103
  64.7 84.1 %all-gather.5.cloned.1.call-done = bf16[1024,4096]{1,0:T(8,128)(2,1)} async-done(((bf16[1024,512]{1,0:T(8,128)(2,1)}), bf16[1024,4096]{1,0:T(8,128)(2,1)}) %all-gather.5.cloned.1.call-update) | async-done | bytes 8388624 | tf_op jit(solution)/shard_map/all_gather | solution.py:101
  148.8 9.2 %convolution_convert_fusion = bf16[512,1024]{1,0:T(8,128)(2,1)S(1)} fusion(bf16[512,4096]{1,0:T(8,128)(2,1)} %all-gather.3.cloned.1.call-done, bf16[1024,4096]{1,0:T(8,128)(2,1)} %all-gather.5.cloned.1.call-done), kind=kOutput, calls=%fused_computation.143 | convolution fusion | flops 4295491584 | bytes 13631488 | tf_op jit(solution)/shard_map/dot_general | solution.py:102
  158.9 1.3 copy_bitcast_fusion.1
  160.2 4.2 all-to-all-start.2
  164.6 2.9 copy.157
  167.5 5.5 %fusion.184 = f32[128,128,64]{1,2,0:T(8,128)} fusion(f32[128,64,128]{2,1,0:T(8,128)S(1)} %bitcast.184), kind=kOutput, calls=%fused_computation.198 | convolution fusion | flops 805363712 | bytes 8388608 | tf_op jit(solution)/shard_map/kn,cnm->ckm/dot_general | solution.py:29
  173.0 5.4 %fusion.193 = f32[128,128,64]{1,2,0:T(8,128)} fusion(f32[128,64,128]{2,1,0:T(8,128)S(1)} %bitcast.185), kind=kOutput, calls=%fused_computation.207 | convolution fusion | flops 805363712 | bytes 8388608 | tf_op jit(solution)/shard_map/kn,cnm->ckm/dot_general | solution.py:29
  179.9 4.0 fusion.191
  183.8 3.9 fusion.182
  187.7 2.4 all-to-all-done.2
  190.1 1.5 concatenate.11
  191.7 3.5 copy.153
  195.1 3.9 fusion.179
  199.1 14.2 %fusion = (f32[128,64,128]{2,1,0:T(8,128)}, f32[128,64,128]{2,1,0:T(8,128)}, f32[128,64,128]{2,1,0:T(8,128)}, f32[128,64,128]{2,1,0:T(8,128)}, f32[128,64,128]{2,1,0:T(8,128)}, /*index=5*/f32[128,64,128]{2,1,0:T(8,128)}) fusion(f32[128,128,64]{1,2,0:T(8,128)} %fusion.179, f32[64,128]{1,0:T(8,128)S(1)} %get-tuple-element.30, ...), kind=kOutput, calls=%fused_computation.3 | convolution fusion | flops 827383808 | bytes 48300032 | tf_op jit(solution)/shard_map/kn,cnm->ckm/dot_general | solution.py:29
  213.3 10.4 %fusion.54 = f32[128,64,128]{2,0,1:T(8,128)} fusion(f32[128,64,128]{2,1,0:T(8,128)} %get-tuple-element.15), kind=kOutput, calls=%fused_computation.76 | convolution fusion | flops 1610842112 | bytes 8388608 | tf_op jit(solution)/shard_map/ckm,mj->ckj/dot_general | solution.py:29
  223.7 7.1 %fusion.56 = f32[128,64,128]{2,0,1:T(8,128)S(1)} fusion(f32[128,64,128]{2,1,0:T(8,128)S(1)} %copy-done.6), kind=kOutput, calls=%fused_computation.78 | convolution fusion | flops 1610842112 | bytes 8388608 | tf_op jit(solution)/shard_map/ckm,mj->ckj/dot_general | solution.py:29
  230.8 7.4 %fusion.62 = f32[128,64,128]{2,0,1:T(8,128)S(1)} fusion(f32[128,64,128]{2,1,0:T(8,128)S(1)} %copy-done.5), kind=kOutput, calls=%fused_computation.84 | convolution fusion | flops 1610842112 | bytes 8388608 | tf_op jit(solution)/shard_map/ckm,mj->ckj/dot_general | solution.py:29
  238.2 7.1 %fusion.64 = f32[128,64,128]{2,0,1:T(8,128)S(1)} fusion(f32[128,64,128]{2,1,0:T(8,128)S(1)} %copy-done.5), kind=kOutput, calls=%fused_computation.86 | convolution fusion | flops 1610842112 | bytes 8388608 | tf_op jit(solution)/shard_map/ckm,mj->ckj/dot_general | solution.py:29
  245.3 7.2 %fusion.70 = f32[128,64,128]{2,0,1:T(8,128)S(1)} fusion(f32[128,64,128]{2,1,0:T(8,128)S(1)} %copy-done.4), kind=kOutput, calls=%fused_computation.92 | convolution fusion | flops 1610842112 | bytes 8388608 | tf_op jit(solution)/shard_map/ckm,mj->ckj/dot_general | solution.py:29
  252.5 7.1 %fusion.72 = f32[128,64,128]{2,0,1:T(8,128)S(1)} fusion(f32[128,64,128]{2,1,0:T(8,128)S(1)} %copy-done.4), kind=kOutput, calls=%fused_computation.94 | convolution fusion | flops 1610842112 | bytes 8388608 | tf_op jit(solution)/shard_map/ckm,mj->ckj/dot_general | solution.py:29
  259.6 8.5 %fusion.84 = f32[128,64,128]{2,0,1:T(8,128)} fusion(f32[128,64,128]{2,0,1:T(8,128)S(1)} %fusion.64, f32[128,64,128]{2,1,0:T(8,128)S(1)} %copy-done.1), kind=kOutput, calls=%fused_computation.107 | convolution fusion | flops 1611890688 | bytes 12582912 | tf_op jit(solution)/shard_map/ckm,mj->ckj/dot_general | solution.py:29
  268.1 8.2 %fusion.87 = f32[128,64,128]{2,0,1:T(8,128)} fusion(f32[128,64,128]{2,0,1:T(8,128)S(1)} %fusion.62, f32[128,64,128]{2,1,0:T(8,128)S(1)} %copy-done.1), kind=kOutput, calls=%fused_computation.108 | convolution fusion | flops 1611890688 | bytes 12582912 | tf_op jit(solution)/shard_map/ckm,mj->ckj/dot_general | solution.py:29
  276.3 8.3 %fusion.78 = f32[128,64,128]{2,0,1:T(8,128)} fusion(f32[128,64,128]{2,0,1:T(8,128)S(1)} %fusion.72, f32[128,64,128]{2,1,0:T(8,128)S(1)} %copy-done), kind=kOutput, calls=%fused_computation.105 | convolution fusion | flops 1611890688 | bytes 12582912 | tf_op jit(solution)/shard_map/ckm,mj->ckj/dot_general | solution.py:29
  284.6 8.8 %fusion.81 = f32[128,64,128]{2,0,1:T(8,128)} fusion(f32[128,64,128]{2,0,1:T(8,128)S(1)} %fusion.70, f32[128,64,128]{2,1,0:T(8,128)S(1)} %copy-done), kind=kOutput, calls=%fused_computation.106 | convolution fusion | flops 1611890688 | bytes 12582912 | tf_op jit(solution)/shard_map/ckm,mj->ckj/dot_general | solution.py:29
  293.4 8.3 %fusion.90 = f32[128,64,128]{2,0,1:T(8,128)} fusion(f32[128,64,128]{2,0,1:T(8,128)S(1)} %fusion.56, f32[128,64,128]{2,1,0:T(8,128)S(1)} %copy-done.8), kind=kOutput, calls=%fused_computation.109 | convolution fusion | flops 1611890688 | bytes 12582912 | tf_op jit(solution)/shard_map/ckm,mj->ckj/dot_general | solution.py:29
  301.6 19.0 %multiply_add_fusion = (f32[128,64,128]{2,0,1:T(8,128)}, f32[128,64,128]{2,0,1:T(8,128)}, f32[128,64,128]{2,0,1:T(8,128)}, f32[128,64,128]{2,0,1:T(8,128)}, f32[128,64,128]{2,0,1:T(8,128)}, /*index=5*/f32[128,64,128]{2,0,1:T(8,128)}) fusion(f32[128,64,128]{2,0,1:T(8,128)} %fusion.87, f32[128,64,128]{2,0,1:T(8,128)} %fusion.90, f32[128,64,128]{2,0,1:T(8,128)} %fusion.84, ...), kind=kOutput, calls=%fused_computation.28 | convolution fusion | flops 1630765056 | bytes 54525952 | tf_op jit(solution)/shard_map/ckm,mj->ckj/dot_general | solution.py:29
  320.7 9.9 %fusion.30 = f32[128,64,128]{2,1,0:T(8,128)} fusion(f32[128,64,128]{2,0,1:T(8,128)} %get-tuple-element.9), kind=kOutput, calls=%fused_computation.52 | convolution fusion | flops 1610842112 | bytes 8388608 | tf_op jit(solution)/shard_map/ckj,jm->ckm/dot_general | solution.py:29
  330.6 7.1 %fusion.32 = f32[128,64,128]{2,1,0:T(8,128)} fusion(f32[128,64,128]{2,0,1:T(8,128)S(1)} %copy-done.13), kind=kOutput, calls=%fused_computation.54 | convolution fusion | flops 1610842112 | bytes 8388608 | tf_op jit(solution)/shard_map/ckj,jm->ckm/dot_general | solution.py:29
  337.7 6.8 %fusion.46 = f32[128,64,128]{2,1,0:T(8,128)S(1)} fusion(f32[128,64,128]{2,0,1:T(8,128)S(1)} %copy-done.12), kind=kOutput, calls=%fused_computation.68 | convolution fusion | flops 1610842112 | bytes 8388608 | tf_op jit(solution)/shard_map/ckj,jm->ckm/dot_general | solution.py:29
  344.4 7.2 %fusion.48 = f32[128,64,128]{2,1,0:T(8,128)S(1)} fusion(f32[128,64,128]{2,0,1:T(8,128)S(1)} %copy-done.12), kind=kOutput, calls=%fused_computation.70 | convolution fusion | flops 1610842112 | bytes 8388608 | tf_op jit(solution)/shard_map/ckj,jm->ckm/dot_general | solution.py:29
  351.7 7.3 %fusion.38 = f32[128,64,128]{2,1,0:T(8,128)} fusion(f32[128,64,128]{2,0,1:T(8,128)S(1)} %copy-done.11), kind=kOutput, calls=%fused_computation.60 | convolution fusion | flops 1610842112 | bytes 8388608 | tf_op jit(solution)/shard_map/ckj,jm->ckm/dot_general | solution.py:29
  359.0 7.2 %fusion.40 = f32[128,64,128]{2,1,0:T(8,128)} fusion(f32[128,64,128]{2,0,1:T(8,128)S(1)} %copy-done.11), kind=kOutput, calls=%fused_computation.62 | convolution fusion | flops 1610842112 | bytes 8388608 | tf_op jit(solution)/shard_map/ckj,jm->ckm/dot_general | solution.py:29
  366.2 6.8 %fusion.99 = f32[128,64,128]{2,1,0:T(8,128)S(1)} fusion(f32[128,64,128]{2,1,0:T(8,128)S(1)} %fusion.46, f32[128,64,128]{2,0,1:T(8,128)S(1)} %copy-done.10), kind=kOutput, calls=%fused_computation.112 | convolution fusion | flops 1611890688 | bytes 12582912 | tf_op jit(solution)/shard_map/ckj,jm->ckm/dot_general | solution.py:29
  373.0 7.0 %fusion.96 = f32[128,64,128]{2,1,0:T(8,128)S(1)} fusion(f32[128,64,128]{2,1,0:T(8,128)S(1)} %fusion.48, f32[128,64,128]{2,0,1:T(8,128)S(1)} %copy-done.10), kind=kOutput, calls=%fused_computation.111 | convolution fusion | flops 1611890688 | bytes 12582912 | tf_op jit(solution)/shard_map/ckj,jm->ckm/dot_general | solution.py:29
  380.0 4.8 fusion.22
  384.8 6.4 %subtract_bitcast_fusion.1 = f32[128,64,128]{2,1,0:T(8,128)} fusion(f32[128,128,64]{1,2,0:T(8,128)S(1)} %fusion.22, f32[128,64,128]{2,1,0:T(8,128)S(1)} %fusion.99, f32[128,64,128]{2,1,0:T(8,128)S(1)} %fusion.96, f32[64,128]{1,0:T(8,128)S(1)} %get-tuple-element.30, f32[64,128]{1,0:T(8,128)S(1)} %get-tuple-element.31), kind=kOutput, calls=%fused_computation.40 | convolution fusion | flops 809558016 | bytes 16842752 | tf_op jit(solution)/shard_map/nk,ckm->cnm/dot_general | solution.py:29
  391.2 5.4 %copy.152 = f32[128,64,128]{0,2,1:T(8,128)} copy(f32[128,64,128]{2,1,0:T(8,128)} %subtract_bitcast_fusion.1) | data formatting | bytes 8388608 | tf_op jit(solution)/shard_map/reshape | solution.py:76
  396.6 10.9 %fusion.105 = f32[128,64,128]{2,1,0:T(8,128)S(1)} fusion(f32[128,64,128]{2,1,0:T(8,128)} %fusion.38, f32[128,64,128]{2,0,1:T(8,128)} %get-tuple-element.23), kind=kOutput, calls=%fused_computation.114 | convolution fusion | flops 1611890688 | bytes 12582912 | tf_op jit(solution)/shard_map/ckj,jm->ckm/dot_general | solution.py:29
  407.5 6.8 %fusion.102 = f32[128,64,128]{2,1,0:T(8,128)S(1)} fusion(f32[128,64,128]{2,1,0:T(8,128)S(1)} %copy-done.15, f32[128,64,128]{2,0,1:T(8,128)S(1)} %copy-done.9), kind=kOutput, calls=%fused_computation.113 | convolution fusion | flops 1611890688 | bytes 12582912 | tf_op jit(solution)/shard_map/ckj,jm->ckm/dot_general | solution.py:29
  414.3 4.8 fusion.14
  419.1 6.5 %subtract_bitcast_fusion = f32[128,64,128]{2,1,0:T(8,128)} fusion(f32[128,128,64]{1,2,0:T(8,128)S(1)} %fusion.14, f32[128,64,128]{2,1,0:T(8,128)S(1)} %fusion.105, f32[128,64,128]{2,1,0:T(8,128)S(1)} %fusion.102, f32[64,128]{1,0:T(8,128)S(1)} %get-tuple-element.30, f32[64,128]{1,0:T(8,128)S(1)} %get-tuple-element.31), kind=kOutput, calls=%fused_computation.29 | convolution fusion | flops 809558016 | bytes 16842752 | tf_op jit(solution)/shard_map/nk,ckm->cnm/dot_general | solution.py:29
  425.5 5.5 %copy.154 = f32[128,64,128]{0,2,1:T(8,128)} copy(f32[128,64,128]{2,1,0:T(8,128)} %subtract_bitcast_fusion) | data formatting | bytes 8388608 | tf_op jit(solution)/shard_map/reshape | solution.py:76
  431.0 1.7 fusion.119
  432.8 1.3 copy.127
  434.1 4.3 all-to-all-start.3
  438.4 9.9 %fusion.111 = f32[128,64,128]{2,1,0:T(8,128)S(1)} fusion(f32[128,64,128]{2,1,0:T(8,128)} %fusion.30, f32[128,64,128]{2,0,1:T(8,128)} %get-tuple-element.8), kind=kOutput, calls=%fused_computation.116 | convolution fusion | flops 1611890688 | bytes 12582912 | tf_op jit(solution)/shard_map/ckj,jm->ckm/dot_general | solution.py:29
  448.4 6.6 %fusion.108 = f32[128,64,128]{2,1,0:T(8,128)S(1)} fusion(f32[128,64,128]{2,1,0:T(8,128)S(1)} %copy-done.14, f32[128,64,128]{2,0,1:T(8,128)S(1)} %copy-done.7), kind=kOutput, calls=%fused_computation.115 | convolution fusion | flops 1611890688 | bytes 12582912 | tf_op jit(solution)/shard_map/ckj,jm->ckm/dot_general | solution.py:29
  454.9 6.3 %fusion.6 = f32[128,128,64]{1,2,0:T(8,128)} fusion(f32[128,64,128]{2,1,0:T(8,128)S(1)} %fusion.111, f32[128,64,128]{2,1,0:T(8,128)S(1)} %fusion.108, f32[64,128]{1,0:T(8,128)S(1)} %get-tuple-element.30, f32[64,128]{1,0:T(8,128)S(1)} %get-tuple-element.31), kind=kOutput, calls=%fused_computation.19 | convolution fusion | flops 808509440 | bytes 12648448 | tf_op jit(solution)/shard_map/nk,ckm->cnm/dot_general | solution.py:29
  461.3 1.1 fusion.120
  462.4 1.8 all-to-all-done.3
  464.1 4.3 all-to-all-start.1
  468.5 9.6 %fusion.131 = f32[128,128,64]{1,2,0:T(8,128)S(1)} fusion(f32[128,128,64]{1,2,0:T(8,128)} %fusion.6, f32[128,64,128]{2,1,0:T(8,128)} %copy-done.2, f32[128,64,128]{2,1,0:T(8,128)} %copy-done.3, f32[64,128]{1,0:T(8,128)S(1)} %get-tuple-element.30, f32[64,128]{1,0:T(8,128)S(1)} %get-tuple-element.31), kind=kOutput, calls=%fused_computation.136 | convolution fusion | flops 809558016 | bytes 16842752 | tf_op jit(solution)/shard_map/nk,ckm->cnm/dot_general | solution.py:29
  478.0 3.3 copy.237
  481.3 1.5 slice_multiply_fusion
  483.6 1.9 fusion.116
  485.5 2.3 copy.133
  487.8 2.3 copy.132
  490.0 4.2 all-to-all-done.1
  494.2 1.3 fusion.114
  (61 shorter events, 5.7 us)
Async XLA Ops:
  7.2 3.0 copy-start.24
  7.2 57.5 %all-gather.3.cloned.1.call-start = ((), (), s32[]{:S(2)}) async-start(), calls=%async_computation.4 | async-start | bytes 5242880 | tf_op jit(solution)/shard_map/all_gather | solution.py:103
  7.9 140.9 %all-gather.5.cloned.1.call-start = ((), (), s32[]{:S(2)}) async-start(), calls=%async_computation.5 | async-start | bytes 9437184 | tf_op jit(solution)/shard_map/all_gather | solution.py:101
  10.2 2.2 copy-start.16
  10.7 12.2 %copy-start.18 = (bf16[512,1024]{0,1:T(8,128)(2,1)}, bf16[512,1024]{0,1:T(8,128)(2,1)S(1)}, u32[]{:S(2)}) copy-start(bf16[512,1024]{0,1:T(8,128)(2,1)S(1)} %copy.101) | copy-start | bytes 3145732
  12.4 147.8 %all-to-all-start = ((bf16[8,128,512]{1,2,0:T(8,128)(2,1)}), bf16[8,128,512]{1,2,0:T(8,128)(2,1)S(1)}, u32[]{:S(2)}, u32[]{:S(2)}) async-start(bf16[8,128,512]{1,2,0:T(8,128)(2,1)} %copy.102), calls=%async_computation | async-start | bytes 2097152 | tf_op jit(solution)/shard_map/all_to_all | solution.py:111
  22.9 136.0 %copy-start.23 = (bf16[512,1024]{1,0:T(8,128)(2,1)S(1)}, bf16[512,1024]{1,0:T(8,128)(2,1)}, u32[]{:S(2)}) copy-start(bf16[512,1024]{1,0:T(8,128)(2,1)} %param.8) | copy-start | bytes 3145732
  158.0 1.0 copy-start.21
  160.2 29.9 %all-to-all-start.2 = ((bf16[8,128,512]{1,2,0:T(8,128)(2,1)}), bf16[8,128,512]{1,2,0:T(8,128)(2,1)S(1)}, u32[]{:S(2)}, u32[]{:S(2)}) async-start(bf16[8,128,512]{1,2,0:T(8,128)(2,1)} %copy_bitcast_fusion.1), calls=%async_computation.2 | async-start | bytes 2097152 | tf_op jit(solution)/shard_map/all_to_all | solution.py:112
  213.3 10.4 %copy-start.6 = (f32[128,64,128]{2,1,0:T(8,128)S(1)}, f32[128,64,128]{2,1,0:T(8,128)}, u32[]{:S(2)}) copy-start(f32[128,64,128]{2,1,0:T(8,128)} %get-tuple-element.15) | copy-start | bytes 12582916
  223.7 7.1 %copy-start.5 = (f32[128,64,128]{2,1,0:T(8,128)S(1)}, f32[128,64,128]{2,1,0:T(8,128)}, u32[]{:S(2)}) copy-start(f32[128,64,128]{2,1,0:T(8,128)} %get-tuple-element.26) | copy-start | bytes 12582916
  238.2 7.1 %copy-start.4 = (f32[128,64,128]{2,1,0:T(8,128)S(1)}, f32[128,64,128]{2,1,0:T(8,128)}, u32[]{:S(2)}) copy-start(f32[128,64,128]{2,1,0:T(8,128)} %get-tuple-element.28) | copy-start | bytes 12582916
  252.5 7.1 %copy-start.1 = (f32[128,64,128]{2,1,0:T(8,128)S(1)}, f32[128,64,128]{2,1,0:T(8,128)}, u32[]{:S(2)}) copy-start(f32[128,64,128]{2,1,0:T(8,128)} %get-tuple-element.27) | copy-start | bytes 12582916
  268.1 8.2 %copy-start = (f32[128,64,128]{2,1,0:T(8,128)S(1)}, f32[128,64,128]{2,1,0:T(8,128)}, u32[]{:S(2)}) copy-start(f32[128,64,128]{2,1,0:T(8,128)} %get-tuple-element.29) | copy-start | bytes 12582916
  284.6 8.8 %copy-start.8 = (f32[128,64,128]{2,1,0:T(8,128)S(1)}, f32[128,64,128]{2,1,0:T(8,128)}, u32[]{:S(2)}) copy-start(f32[128,64,128]{2,1,0:T(8,128)} %get-tuple-element.14) | copy-start | bytes 12582916
  320.7 9.9 %copy-start.13 = (f32[128,64,128]{2,0,1:T(8,128)S(1)}, f32[128,64,128]{2,0,1:T(8,128)}, u32[]{:S(2)}) copy-start(f32[128,64,128]{2,0,1:T(8,128)} %get-tuple-element.9) | copy-start | bytes 12582916
  330.6 7.1 %copy-start.12 = (f32[128,64,128]{2,0,1:T(8,128)S(1)}, f32[128,64,128]{2,0,1:T(8,128)}, u32[]{:S(2)}) copy-start(f32[128,64,128]{2,0,1:T(8,128)} %get-tuple-element.20) | copy-start | bytes 12582916
  344.4 7.2 %copy-start.11 = (f32[128,64,128]{2,0,1:T(8,128)S(1)}, f32[128,64,128]{2,0,1:T(8,128)}, u32[]{:S(2)}) copy-start(f32[128,64,128]{2,0,1:T(8,128)} %get-tuple-element.22) | copy-start | bytes 12582916
  359.0 7.2 %copy-start.10 = (f32[128,64,128]{2,0,1:T(8,128)S(1)}, f32[128,64,128]{2,0,1:T(8,128)}, u32[]{:S(2)}) copy-start(f32[128,64,128]{2,0,1:T(8,128)} %get-tuple-element.21) | copy-start | bytes 12582916
  396.6 10.9 %copy-start.9 = (f32[128,64,128]{2,0,1:T(8,128)S(1)}, f32[128,64,128]{2,0,1:T(8,128)}, u32[]{:S(2)}) copy-start(f32[128,64,128]{2,0,1:T(8,128)} %get-tuple-element.23) | copy-start | bytes 12582916
  396.6 10.9 %copy-start.15 = (f32[128,64,128]{2,1,0:T(8,128)S(1)}, f32[128,64,128]{2,1,0:T(8,128)}, u32[]{:S(2)}) copy-start(f32[128,64,128]{2,1,0:T(8,128)} %fusion.40) | copy-start | bytes 12582916
  434.1 30.1 %all-to-all-start.3 = ((bf16[128,8,512]{2,0,1:T(8,128)(2,1)}), bf16[128,8,512]{2,0,1:T(8,128)(2,1)S(1)}, u32[]{:S(2)}, u32[]{:S(2)}) async-start(bf16[128,8,512]{2,0,1:T(8,128)(2,1)} %copy.127), calls=%async_computation.3 | async-start | bytes 2097152 | tf_op jit(solution)/shard_map/all_to_all | solution.py:116
  438.4 9.9 %copy-start.7 = (f32[128,64,128]{2,0,1:T(8,128)S(1)}, f32[128,64,128]{2,0,1:T(8,128)}, u32[]{:S(2)}) copy-start(f32[128,64,128]{2,0,1:T(8,128)} %get-tuple-element.8) | copy-start | bytes 12582916
  438.4 9.9 %copy-start.14 = (f32[128,64,128]{2,1,0:T(8,128)S(1)}, f32[128,64,128]{2,1,0:T(8,128)}, u32[]{:S(2)}) copy-start(f32[128,64,128]{2,1,0:T(8,128)} %fusion.32) | copy-start | bytes 12582916
  448.3 6.6 %copy-start.2 = (f32[128,64,128]{2,1,0:T(8,128)}, f32[128,64,128]{2,1,0:T(8,128)S(1)}, u32[]{:S(2)}) copy-start(f32[128,64,128]{2,1,0:T(8,128)S(1)} %fusion.111) | copy-start | bytes 12582916
  454.9 6.3 %copy-start.3 = (f32[128,64,128]{2,1,0:T(8,128)}, f32[128,64,128]{2,1,0:T(8,128)S(1)}, u32[]{:S(2)}) copy-start(f32[128,64,128]{2,1,0:T(8,128)S(1)} %fusion.108) | copy-start | bytes 12582916
  454.9 6.3 %copy-start.20 = (f32[128,64,128]{0,2,1:T(8,128)S(1)}, f32[128,64,128]{0,2,1:T(8,128)}, u32[]{:S(2)}) copy-start(f32[128,64,128]{0,2,1:T(8,128)} %copy.152) | copy-start | bytes 12582916
  464.1 30.1 %all-to-all-start.1 = ((bf16[128,8,512]{0,2,1:T(8,128)(2,1)}), bf16[128,8,512]{0,2,1:T(8,128)(2,1)S(1)}, u32[]{:S(2)}, u32[]{:S(2)}) async-start(bf16[128,8,512]{0,2,1:T(8,128)(2,1)} %bitcast.14), calls=%async_computation.1 | async-start | bytes 2097152 | tf_op jit(solution)/shard_map/all_to_all | solution.py:117
  481.3 1.5 copy-start.17
  481.3 2.3 copy-start.19
  483.6 10.6 %copy-start.22 = (bf16[512,1024]{1,0:T(8,128)(2,1)S(1)}, bf16[512,1024]{1,0:T(8,128)(2,1)}, u32[]{:S(2)}) copy-start(bf16[512,1024]{1,0:T(8,128)(2,1)} %copy-done.21) | copy-start | bytes 3145732
Sparse Core Ops, SparseCore 0:
  9.9 54.7 all-gather.2
  66.3 82.4 all-gather.4
where the time goes:
time: 509 us; the launch traced here: 503 us
  matrix products  285 us (56%)
  waiting for transfers between devices  136 us (27%)
  local copies, waits for them, and re-layouts  38.8 us (8%)
  starting transfers between devices  19.3 us (4%)
  between operations  14.7 us (3%)
  other arithmetic  9.1 us (2%)
    dot_general x36, matrix products, contract(): return jnp.einsum(form, left, right, precision=lax.Precision.HIGHEST)  276 us
    all_gather x1, waiting for transfers between devices, body(): weight_rows = lax.all_gather(proj_out, 'ctx', axis=1, tiled=True)  84.1 us
    all_gather x1, waiting for transfers between devices, body(): lax.all_gather(grad_out, 'mp', axis=1, tiled=True)  41.7 us
    unnamed x59, local copies, waits for them, and re-layouts  19.7 us
    reshape x2, local copies, waits for them, and re-layouts, restore(): inverse_real(spec_re, spec_im, tables).reshape(channels, length_all)  10.9 us
  transfers between devices with their start and end apart: 6, of which 5 were waited for; matrix products, arithmetic and copies ran while one was open for 17% of the time, Pallas kernels for 0%

commit v1 on v0

--- a/solution.py
+++ b/solution.py
@@ -1,10 +1,14 @@
+import functools
 import math
 
 import jax
 import jax.numpy as jnp
+import ml_dtypes
+import numpy as np
 from jax import lax
+from jax.experimental import pallas as pl
+from jax.experimental.pallas import tpu as pltpu
 from jax.sharding import PartitionSpec as P
-
 
 def phase_table(rows_n, cols_n, modulus):
     prod_idx = (
@@ -97,7 +101,7 @@
     return (left.astype(jnp.float32) * right.astype(jnp.float32)).astype(jnp.bfloat16)
 
 
-def body(grad_out, proj_out, query, key_in, value_in, filters):
+def general_body(grad_out, proj_out, query, key_in, value_in, filters):
     weight_rows = lax.all_gather(proj_out, "ctx", axis=1, tiled=True)
     grad_mix = lax.dot_general(
         lax.all_gather(grad_out, "mp", axis=1, tiled=True),
@@ -120,6 +124,309 @@
     grad_key = product(back_grad.T, value_in)
     grad_value = product(back_grad.T, key_in)
     return (grad_query, grad_key, grad_value, filter_grad)
+
+
+FAST = 32
+LANES = 128
+F32, BF16 = jnp.float32, jnp.bfloat16
+
+def tables(seq):
+    size = 2 * seq
+    slow = size // FAST
+    half = slow // 2
+    b = np.arange(half)
+    s = np.arange(half)
+    ang = 2 * np.pi * ((s[:, None] * b[None, :]) % slow) / slow
+    first = np.concatenate([np.cos(ang), -np.sin(ang)], 0)
+    first[half] = 1.0 - 2.0 * (b % 2)
+    weight = np.full((half,), 2.0); weight[0] = 1.0
+    last = np.concatenate([np.cos(ang) * weight[:, None], -np.sin(ang) * weight[:, None]], 0)
+    last[half] = 1.0 - 2.0 * (b % 2)
+    last = last.T / size
+    a = np.arange(FAST)
+    kb = np.arange(half + 1)
+    k = kb[:, None] + slow * a[None, :]
+    th = 2 * np.pi * ((k[:, :, None] * a[None, None, :]) % size) / size
+    c, sn = np.cos(th), np.sin(th)
+    fwd = np.concatenate([np.concatenate([c, sn], 2), np.concatenate([-sn, c], 2)], 1)
+    fwd[0, :, FAST:] = 0.0
+    fwd[half, :, FAST:] = np.concatenate([c[half], -sn[half]], 0)
+    fwd[half, :, :FAST] = 0.0
+    ct, st = c.transpose(0, 2, 1), sn.transpose(0, 2, 1)
+    inv = np.concatenate([np.concatenate([ct, -st], 2), np.concatenate([st, ct], 2)], 1)
+    inv[0, FAST:] = 0.0
+    inv[half, FAST:] = np.concatenate([ct[half], -st[half]], 1)
+    inv[half, :FAST] = 0.0
+    return [jnp.asarray(t.astype(ml_dtypes.bfloat16)) for t in (first, fwd, inv, last)]
+
+def dot(l, r):
+    return jnp.dot(l, r, preferred_element_type=F32)
+
+U1, U2 = 4, 8
+
+def loop(lo, n, unroll, fn):
+    def step(i, carry):
+        for u in range(unroll):
+            fn(lo + i * unroll + u)
+        return carry
+    lax.fori_loop(0, n // unroll, step, 0)
+
+def spread(signal, first_ref, mid_ref):
+    half = first_ref.shape[1]
+    def one(a):
+        out = dot(first_ref[...], signal(a))
+        mid_ref[pl.ds(a, half, stride=2 * FAST), :] = out[:half]
+        mid_ref[pl.ds(FAST + a, half, stride=2 * FAST), :] = out[half:]
+    loop(0, FAST, U1, one)
+
+def spectrum_row(kb, half, fwd_ref, mid_ref):
+    slot = lax.rem(kb, half) if not isinstance(kb, int) else kb % half
+    rows = mid_ref[pl.ds(pl.multiple_of(slot * 2 * FAST, 2 * FAST), 2 * FAST), :].astype(BF16)
+    return dot(fwd_ref[kb], rows)
+
+def gather(last_ref, mid_ref, emit):
+    half = last_ref.shape[0]
+    def one(a):
+        re = mid_ref[pl.ds(a, half, stride=2 * FAST), :]
+        im = mid_ref[pl.ds(FAST + a, half, stride=2 * FAST), :]
+        emit(a, dot(last_ref[...], jnp.concatenate([re, im], 0).astype(BF16)))
+    loop(0, FAST, U1, one)
+
+def put(mid_ref, slot, value):
+    mid_ref[pl.ds(pl.multiple_of(slot * 2 * FAST, 2 * FAST), 2 * FAST), :] = value
+
+def cmul(x, y):
+    xr, xi, yr, yi = x[:FAST], x[FAST:], y[:FAST], y[FAST:]
+    return jnp.concatenate([xr * yr - xi * yi, xr * yi + xi * yr], 0)
+
+def cmulc(x, y):
+    xr, xi, yr, yi = x[:FAST], x[FAST:], y[:FAST], y[FAST:]
+    return jnp.concatenate([xr * yr + xi * yi, xi * yr - xr * yi], 0)
+
+def filter_kernel(h_ref, first_ref, fwd_ref, spec_ref, time_ref, mid_ref):
+    half = first_ref.shape[1]
+    seq = h_ref.shape[1]
+    def turn(i):
+        cols = pl.ds(pl.multiple_of(i * LANES, LANES), LANES)
+        time_ref[cols, :] = h_ref[:, cols].T
+    loop(0, seq // LANES, 4, turn)
+    spread(lambda a: time_ref[pl.ds(a, half, stride=FAST), :].astype(BF16), first_ref, mid_ref)
+    def one(kb):
+        spec_ref[kb] = spectrum_row(kb, half, fwd_ref, mid_ref)
+    loop(0, half, U2, one)
+    one(half)
+
+def pair_kernel(conj, x_ref, h_ref, first_ref, fwd_ref, inv_ref, last_ref, out_ref, spec_ref, mid_ref, back_ref):
+    half = first_ref.shape[1]
+    n, _, per, _ = x_ref.shape
+    mul = cmulc if conj else cmul
+    spread(lambda a: x_ref[:, a].reshape(half, LANES), first_ref, mid_ref)
+    def row(kb):
+        x = spectrum_row(kb, half, fwd_ref, mid_ref)
+        spec_ref[kb] = x
+        return dot(inv_ref[kb], mul(x, h_ref[kb]).astype(BF16))
+    put(back_ref, 0, row(0) + row(half))
+    def one(kb):
+        put(back_ref, kb, row(kb))
+    loop(1, half - 8, U2, one)
+    for kb in range(half - 7, half):
+        one(kb)
+    def emit(a, rows):
+        out_ref[:, a] = rows.reshape(n, per, LANES).astype(out_ref.dtype)
+    gather(last_ref, back_ref, emit)
+
+def grad_kernel(scale, s_ref, g_ref, inv_ref, last_ref, out_ref, time_ref, back_ref):
+    half = last_ref.shape[0]
+    seq = out_ref.shape[1]
+    def row(kb):
+        return dot(inv_ref[kb], cmulc(s_ref[kb], g_ref[kb]).astype(BF16))
+    put(back_ref, 0, row(0) + row(half))
+    def one(kb):
+        put(back_ref, kb, row(kb))
+    loop(1, half - 8, U2, one)
+    for kb in range(half - 7, half):
+        one(kb)
+    def emit(a, rows):
+        time_ref[pl.ds(a, half, stride=FAST), :] = rows * scale
+    gather(last_ref, back_ref, emit)
+    def turn(i):
+        cols = pl.ds(pl.multiple_of(i * LANES, LANES), LANES)
+        out_ref[:, cols] = time_ref[cols, :].T
+    loop(0, seq // LANES, 4, turn)
+
+PARAMS = pltpu.CompilerParams(vmem_limit_bytes=56 * 2**20)
+VM = pl.BlockSpec(memory_space=pltpu.VMEM)
+
+def sds(shape, dt): return jax.ShapeDtypeStruct(shape, dt)
+
+def filter_spectrum(h, tabs):
+    first, fwd, inv, last = tabs
+    seq = h.shape[1]; half = seq // FAST
+    return pl.pallas_call(filter_kernel, out_shape=sds((half + 1, 2 * FAST, LANES), F32),
+        in_specs=[VM] * 3, out_specs=VM, name="filter_spectrum",
+        scratch_shapes=[pltpu.VMEM((seq, LANES), F32), pltpu.VMEM((2 * seq, LANES), F32)],
+        compiler_params=PARAMS)(h, first, fwd)
+
+def convolve(x, spec, tabs, conj):
+    first, fwd, inv, last = tabs
+    half = first.shape[1]; seq = half * FAST
+    return pl.pallas_call(functools.partial(pair_kernel, conj),
+        out_shape=(sds(x.shape, BF16), sds(spec.shape, F32)),
+        in_specs=[VM] * 6, out_specs=(VM, VM), name="convolve",
+        scratch_shapes=[pltpu.VMEM((2 * seq, LANES), F32), pltpu.VMEM((2 * seq, LANES), F32)],
+        compiler_params=PARAMS)(x, spec, first, fwd, inv, last)
+
+def filter_gradient(s, g, tabs, scale):
+    first, fwd, inv, last = tabs
+    half = first.shape[1]; seq = half * FAST
+    return pl.pallas_call(functools.partial(grad_kernel, scale),
+        out_shape=sds((LANES, seq), F32),
+        in_specs=[VM] * 4, out_specs=VM, name="filter_gradient",
+        scratch_shapes=[pltpu.VMEM((seq, LANES), F32), pltpu.VMEM((2 * seq, LANES), F32)],
+        compiler_params=PARAMS)(s, g, inv, last)
+
+
+def permuted(value, hold_ref, emit):
+    hold_ref[...] = value
+    per = value.shape[0] // FAST
+    for a in range(FAST):
+        emit(a, hold_ref[pl.ds(a, per, stride=FAST), :].astype(BF16))
+
+
+def gate_kernel(key_ref, value_ref, out_ref, hold_ref):
+    def emit(a, rows):
+        out_ref[0, a] = rows
+
+    permuted(key_ref[...].astype(F32) * value_ref[...].astype(F32), hold_ref, emit)
+
+
+def gate(key_in, value_in, groups):
+    rows = key_in.shape[0]
+    block = pl.BlockSpec((rows, LANES), lambda j: (0, j))
+    return pl.pallas_call(
+        gate_kernel,
+        grid=(groups,),
+        out_shape=sds((groups, FAST, rows // FAST, LANES), BF16),
+        in_specs=[block, block],
+        out_specs=pl.BlockSpec((1, FAST, rows // FAST, LANES), lambda j: (j, 0, 0, 0)),
+        scratch_shapes=[pltpu.VMEM((rows, LANES), F32)],
+        compiler_params=PARAMS,
+        name="gate",
+    )(key_in, value_in)
+
+
+WIDE = 256
+
+
+def mix_kernel(x_ref, w_ref, query_ref, mix_ref, out_ref, hold_ref):
+    parts, depth = w_ref.shape[0], w_ref.shape[2]
+    piece = x_ref.shape[2]
+    total = None
+    for i in range(parts):
+        col = i * depth
+        left = x_ref[col // piece, :, col % piece : col % piece + depth]
+        part = lax.dot_general(left, w_ref[i], (((1,), (1,)), ((), ())), preferred_element_type=F32)
+        total = part if total is None else total + part
+    mix = total.astype(BF16)
+    mix_ref[...] = mix
+    scaled = mix.astype(F32) * query_ref[...].astype(F32)
+    for g in range(WIDE // LANES):
+        def emit(a, rows):
+            out_ref[g, a] = rows
+
+        permuted(scaled[:, g * LANES : (g + 1) * LANES], hold_ref, emit)
+
+
+def mix(x, w, query, groups):
+    rows, cols = query.shape
+    return pl.pallas_call(
+        mix_kernel,
+        grid=(cols // WIDE,),
+        out_shape=(sds((rows, cols), BF16), sds((groups, FAST, rows // FAST, LANES), BF16)),
+        in_specs=[
+            pl.BlockSpec(x.shape, lambda j: (0, 0, 0)),
+            pl.BlockSpec((w.shape[0], WIDE, w.shape[2]), lambda j: (0, j, 0)),
+            pl.BlockSpec((rows, WIDE), lambda j: (0, j)),
+        ],
+        out_specs=(
+            pl.BlockSpec((rows, WIDE), lambda j: (0, j)),
+            pl.BlockSpec((WIDE // LANES, FAST, rows // FAST, LANES), lambda j: (j, 0, 0, 0)),
+        ),
+        scratch_shapes=[pltpu.VMEM((rows, LANES), F32)],
+        compiler_params=PARAMS,
+        name="mix",
+    )(x, w, query)
+
+
+def unpermuted(part_ref, hold_ref):
+    per = part_ref.shape[2]
+    for a in range(FAST):
+        hold_ref[pl.ds(a, per, stride=FAST), :] = part_ref[0, a].astype(F32)
+    return hold_ref[...]
+
+
+def finish_kernel(conv_ref, back_ref, mix_ref, key_ref, value_ref, gq_ref, gk_ref, gv_ref, hold_ref):
+    conv = unpermuted(conv_ref, hold_ref)
+    gq_ref[...] = (mix_ref[...].astype(F32) * conv).astype(BF16)
+    back = unpermuted(back_ref, hold_ref)
+    gk_ref[...] = (back * value_ref[...].astype(F32)).astype(BF16)
+    gv_ref[...] = (back * key_ref[...].astype(F32)).astype(BF16)
+
+
+def finish(conv, back, grad_mix, key_in, value_in):
+    groups, _, per, _ = conv.shape
+    rows, cols = key_in.shape
+    block = pl.BlockSpec((rows, LANES), lambda j: (0, j))
+    part = pl.BlockSpec((1, FAST, per, LANES), lambda j: (j, 0, 0, 0))
+    return pl.pallas_call(
+        finish_kernel,
+        grid=(groups,),
+        out_shape=(sds((rows, cols), BF16),) * 3,
+        in_specs=[part, part, block, block, block],
+        out_specs=(block,) * 3,
+        scratch_shapes=[pltpu.VMEM((rows, LANES), F32)],
+        compiler_params=PARAMS,
+        name="finish",
+    )(conv, back, grad_mix, key_in, value_in)
+
+
+def exchange(parts):
+    return lax.all_to_all(parts, "ctx", split_axis=0, concat_axis=0, tiled=True)
+
+
+def lane_body(grad_out, proj_out, query, key_in, value_in, filters):
+    seq = filters.shape[1]
+    groups = seq // key_in.shape[0]
+    tabs = tables(seq)
+    gated = exchange(gate(key_in, value_in, groups))
+    spec = filter_spectrum(filters, tabs)
+    conv_out, gated_spec = convolve(gated, spec, tabs, False)
+    conv_back = exchange(conv_out)
+    x = lax.all_gather(grad_out, "mp", axis=0)
+    w = lax.all_gather(proj_out, "ctx", axis=0)
+    grad_mix, scaled = mix(x, w, query, groups)
+    scaled = exchange(scaled)
+    grad_gated, scaled_spec = convolve(scaled, spec, tabs, True)
+    grad_back = exchange(grad_gated)
+    filter_grad = filter_gradient(scaled_spec, gated_spec, tabs, 1.0 / math.sqrt(seq))
+    grad_query, grad_key, grad_value = finish(conv_back, grad_back, grad_mix, key_in, value_in)
+    return (grad_query, grad_key, grad_value, filter_grad)
+
+
+def body(grad_out, proj_out, query, key_in, value_in, filters):
+    rows, cols = key_in.shape
+    lanes, seq = filters.shape
+    fits = (
+        lanes == LANES
+        and rows % (16 * FAST) == 0
+        and cols % WIDE == 0
+        and seq % (LANES * FAST) == 0
+        and seq // FAST <= 2 * LANES
+        and proj_out.shape[1] % LANES == 0
+        and grad_out.shape[1] % proj_out.shape[1] == 0
+    )
+    args = (grad_out, proj_out, query, key_in, value_in, filters)
+    return lane_body(*args) if fits else general_body(*args)
 
 
 def solution(mesh):

time: 509 us -> 273 us (0.54)
  matrix products: 285 us -> 0 us
  Pallas kernels: 0 us -> 88.7 us
  local copies, waits for them, and re-layouts: 38.8 us -> 1 us
  waiting for transfers between devices: 136 us -> 148 us
  other arithmetic: 9.1 us -> 0 us
    dot_general x37 -> x0, matrix products: 285 us -> none  [the longest x36 276 us: contract(): return jnp.einsum(form, left, right, precision=lax.Precision.HIGHEST)]
    pallas_call x0 -> x7, Pallas kernels: none -> 88.7 us  [the longest x2 37.7 us: convolve(): pl.pallas_call(functools.partial(pair_kernel, conj), out_shape=(sds(x.sha...]
    unnamed x59 -> x8, local copies, waits for them, and re-layouts: 19.7 us -> 1 us
    reshape x3 -> x0, local copies, waits for them, and re-layouts: 14.4 us -> none  [the longest x2 10.9 us: restore(): inverse_real(spec_re, spec_im, tables).reshape(channels, length_all)]
    all_to_all x4, waiting for transfers between devices: 8.38 us -> 19.2 us  [exchange(): return lax.all_to_all(parts, 'ctx', split_axis=0, concat_axis=0, tiled=True)]
    convert_element_type x5 -> x0, other arithmetic: 6.22 us -> none  [the longest x3 3.42 us: product(): (left.astype(jnp.float32) * right.astype(jnp.float32)).astype(jnp.bfloat16)]
  transfers between devices with their start and end apart: 6 -> 6, of which waited for: 5 -> 4; matrix products, arithmetic and copies ran while one was open for 17% -> 0% of each run, Pallas kernels for 0% -> 30%
where the time goes in v1:
time: 273 us; the launch traced here: 272 us
  waiting for transfers between devices  148 us (54%)
  Pallas kernels  88.7 us (32%)
  starting transfers between devices  19.7 us (7%)
  between operations  14.1 us (5%)
    all_gather x1, waiting for transfers between devices, lane_body(): w = lax.all_gather(proj_out, 'ctx', axis=0)  84.1 us
    all_gather x1, waiting for transfers between devices, lane_body(): x = lax.all_gather(grad_out, 'mp', axis=0)  43.5 us
    pallas_call x2, Pallas kernels, convolve(): pl.pallas_call(functools.partial(pair_kernel, conj), out_shape=(sds(x.sha...  37.7 us
    all_to_all x4, starting transfers between devices, exchange(): return lax.all_to_all(parts, 'ctx', split_axis=0, concat_axis=0, tiled=True)  19.6 us
    all_to_all x4, waiting for transfers between devices, exchange(): return lax.all_to_all(parts, 'ctx', split_axis=0, concat_axis=0, tiled=True)  19.2 us
    pallas_call x1, Pallas kernels, filter_gradient(): pl.pallas_call(functools.partial(grad_kernel, scale), out_shape=sds((LANE...  13.4 us
    pallas_call x1, Pallas kernels, filter_spectrum(): pl.pallas_call(filter_kernel, out_shape=sds((half + 1, 2 * FAST, LANES),...  12.8 us
    pallas_call x1, Pallas kernels, mix(): pl.pallas_call(mix_kernel, grid=(cols // WIDE,), out_shape=(sds((rows, co...  10.4 us
  transfers between devices with their start and end apart: 6, of which 4 were waited for; matrix products, arithmetic and copies ran while one was open for 0% of the time, Pallas kernels for 30%

profile of v1, /device:TPU:1, one launch (start us, length us, event | category | flops | bytes accessed | tf_op | source)
XLA Modules:
  0.0 271.6 jit_solution(16926523358811285273)
XLA Ops:
  7.2 0.0 all-gather.5.cloned.1.call-start
  7.2 0.7 all-gather.5.cloned.1.call-update
  7.9 0.0 all-gather.7.cloned.1.call-start
  7.9 0.7 all-gather.7.cloned.1.call-update
  8.6 6.1 %gate.1 = bf16[8,32,16,128]{3,2,1,0:T(8,128)(2,1)} custom-call(bf16[512,1024]{1,0:T(8,128)(2,1)} %key_ref.3, bf16[512,1024]{1,0:T(8,128)(2,1)} %value_ref.3), custom_call_target="tpu_custom_call" | custom-call | tf_op jit(solution)/shard_map/gate/pallas_call | solution.py:306
  14.8 6.4 %all-to-all-start = ((bf16[8,32,16,128]{3,2,1,0:T(8,128)(2,1)}), bf16[8,32,16,128]{3,2,1,0:T(8,128)(2,1)S(1)}, u32[]{:S(2)}, u32[]{:S(2)}) async-start(bf16[8,32,16,128]{3,2,1,0:T(8,128)(2,1)} %gate.1), calls=%async_computation | async-start | bytes 2097152 | tf_op jit(solution)/shard_map/all_to_all | solution.py:394
  21.2 43.5 %all-gather.5.cloned.1.call-done = bf16[2048,1024]{1,0:T(8,128)(2,1)} async-done(((bf16[512,1024]{1,0:T(8,128)(2,1)}), bf16[2048,1024]{1,0:T(8,128)(2,1)}) %all-gather.5.cloned.1.call-update) | async-done | bytes 4194320 | tf_op jit(solution)/shard_map/all_gather | solution.py:405
  64.7 84.1 %all-gather.7.cloned.1.call-done = bf16[8192,512]{1,0:T(8,128)(2,1)} async-done(((bf16[1024,512]{1,0:T(8,128)(2,1)}), bf16[8192,512]{1,0:T(8,128)(2,1)}) %all-gather.7.cloned.1.call-update) | async-done | bytes 8388624 | tf_op jit(solution)/shard_map/all_gather | solution.py:406
  148.8 10.4 %mix.1 = (bf16[512,1024]{1,0:T(8,128)(2,1)}, bf16[8,32,16,128]{3,2,1,0:T(8,128)(2,1)}) custom-call(bf16[4,512,1024]{2,1,0:T(8,128)(2,1)} %bitcast.3, bf16[8,1024,512]{2,1,0:T(8,128)(2,1)} %bitcast.2, bf16[512,1024]{1,0:T(8,128)(2,1)} %query_ref.1), custom_call_target="tpu_custom_call" | custom-call | tf_op jit(solution)/shard_map/mix/pallas_call | solution.py:342
  159.1 0.0 all-to-all-done.x_ref
  159.1 0.0 copy-start.1
  159.1 3.7 %all-to-all-start.2 = ((bf16[8,32,16,128]{3,2,1,0:T(8,128)(2,1)}), bf16[8,32,16,128]{3,2,1,0:T(8,128)(2,1)S(1)}, u32[]{:S(2)}, u32[]{:S(2)}) async-start(bf16[8,32,16,128]{3,2,1,0:T(8,128)(2,1)} %get-tuple-element.14), calls=%async_computation.2 | async-start | bytes 2097152 | tf_op jit(solution)/shard_map/all_to_all | solution.py:394
  162.9 12.8 %filter_spectrum.1.h_ref = f32[129,64,128]{2,1,0:T(8,128)} custom-call(f32[128,4096]{1,0:T(8,128)} %h_ref.1, bf16[256,128]{1,0:T(8,128)(2,1)} %constant.8.clone.first_ref, bf16[129,64,64]{2,1,0:T(8,128)(2,1)} %constant.9.clone.fwd_ref), custom_call_target="tpu_custom_call" | custom-call | tf_op jit(solution)/shard_map/filter_spectrum/pallas_call | solution.py:265
  175.7 0.0 copy-done.1
  175.7 18.9 %convolve.2 = (bf16[8,32,16,128]{3,2,1,0:T(8,128)(2,1)}, f32[129,64,128]{2,1,0:T(8,128)}) custom-call(bf16[8,32,16,128]{3,2,1,0:T(8,128)(2,1)} %copy-done.1, f32[129,64,128]{2,1,0:T(8,128)} %filter_spectrum.1.h_ref, bf16[256,128]{1,0:T(8,128)(2,1)} %constant.8.clone.first_ref, bf16[129,64,64]{2,1,0:T(8,128)(2,1)} %constant.9.clone.fwd_ref, ...), custom_call_target="tpu_custom_call" | custom-call | tf_op jit(solution)/shard_map/convolve/pallas_call | solution.py:273
  194.6 0.0 all-to-all-done.2.x_ref
  194.6 0.0 copy-start.2
  194.6 5.1 %all-to-all-start.1 = ((bf16[8,32,16,128]{3,2,1,0:T(8,128)(2,1)}), bf16[8,32,16,128]{3,2,1,0:T(8,128)(2,1)S(1)}, u32[]{:S(2)}, u32[]{:S(2)}) async-start(bf16[8,32,16,128]{3,2,1,0:T(8,128)(2,1)} %get-tuple-element.13), calls=%async_computation.1 | async-start | bytes 2097152 | tf_op jit(solution)/shard_map/all_to_all | solution.py:394
  199.7 0.0 copy-done.2
  199.7 18.9 %convolve.3 = (bf16[8,32,16,128]{3,2,1,0:T(8,128)(2,1)}, f32[129,64,128]{2,1,0:T(8,128)}) custom-call(bf16[8,32,16,128]{3,2,1,0:T(8,128)(2,1)} %copy-done.2, f32[129,64,128]{2,1,0:T(8,128)} %filter_spectrum.1.h_ref, bf16[256,128]{1,0:T(8,128)(2,1)} %constant.8.clone.first_ref, bf16[129,64,64]{2,1,0:T(8,128)(2,1)} %constant.9.clone.fwd_ref, ...), custom_call_target="tpu_custom_call" | custom-call | tf_op jit(solution)/shard_map/convolve/pallas_call | solution.py:273
  218.6 6.9 %all-to-all-done.1.conv_ref = bf16[8,32,16,128]{3,2,1,0:T(8,128)(2,1)S(1)} async-done(((bf16[8,32,16,128]{3,2,1,0:T(8,128)(2,1)}), bf16[8,32,16,128]{3,2,1,0:T(8,128)(2,1)S(1)}, u32[]{:S(2)}, u32[]{:S(2)}) %all-to-all-start.1) | async-done | bytes 1048608 | tf_op jit(solution)/shard_map/all_to_all | solution.py:394
  225.4 0.0 copy-start
  225.4 4.3 %all-to-all-start.3 = ((bf16[8,32,16,128]{3,2,1,0:T(8,128)(2,1)}), bf16[8,32,16,128]{3,2,1,0:T(8,128)(2,1)S(1)}, u32[]{:S(2)}, u32[]{:S(2)}) async-start(bf16[8,32,16,128]{3,2,1,0:T(8,128)(2,1)} %get-tuple-element.15), calls=%async_computation.3 | async-start | bytes 2097152 | tf_op jit(solution)/shard_map/all_to_all | solution.py:394
  229.8 13.4 %filter_gradient.1 = f32[128,4096]{1,0:T(8,128)} custom-call(f32[129,64,128]{2,1,0:T(8,128)} %get-tuple-element.20.s_ref, f32[129,64,128]{2,1,0:T(8,128)} %get-tuple-element.21.g_ref, bf16[129,64,64]{2,1,0:T(8,128)(2,1)} %constant.10.clone.inv_ref, bf16[128,256]{1,0:T(8,128)(2,1)} %constant.11.clone.last_ref), custom_call_target="tpu_custom_call" | custom-call | tf_op jit(solution)/shard_map/filter_gradient/pallas_call | solution.py:282
  243.2 0.0 copy-done
  243.2 12.4 %all-to-all-done.3.back_ref = bf16[8,32,16,128]{3,2,1,0:T(8,128)(2,1)S(1)} async-done(((bf16[8,32,16,128]{3,2,1,0:T(8,128)(2,1)}), bf16[8,32,16,128]{3,2,1,0:T(8,128)(2,1)S(1)}, u32[]{:S(2)}, u32[]{:S(2)}) %all-to-all-start.3) | async-done | bytes 1048608 | tf_op jit(solution)/shard_map/all_to_all | solution.py:394
  255.5 0.0 copy-start.3
  255.5 1.0 copy-done.3
  256.5 8.3 %finish.1 = (bf16[512,1024]{1,0:T(8,128)(2,1)}, bf16[512,1024]{1,0:T(8,128)(2,1)}, bf16[512,1024]{1,0:T(8,128)(2,1)}) custom-call(bf16[8,32,16,128]{3,2,1,0:T(8,128)(2,1)} %copy-done, bf16[8,32,16,128]{3,2,1,0:T(8,128)(2,1)} %copy-done.3, bf16[512,1024]{1,0:T(8,128)(2,1)} %get-tuple-element.16.mix_ref, bf16[512,1024]{1,0:T(8,128)(2,1)} %key_ref.3, ...), custom_call_target="tpu_custom_call" | custom-call | tf_op jit(solution)/shard_map/finish/pallas_call | solution.py:381
Async XLA Ops:
  7.2 57.5 %all-gather.5.cloned.1.call-start = ((), (), s32[]{:S(2)}) async-start(), calls=%async_computation.4 | async-start | bytes 5242880 | tf_op jit(solution)/shard_map/all_gather | solution.py:405
  7.9 140.9 %all-gather.7.cloned.1.call-start = ((), (), s32[]{:S(2)}) async-start(), calls=%async_computation.5 | async-start | bytes 9437184 | tf_op jit(solution)/shard_map/all_gather | solution.py:406
  14.8 144.3 %all-to-all-start = ((bf16[8,32,16,128]{3,2,1,0:T(8,128)(2,1)}), bf16[8,32,16,128]{3,2,1,0:T(8,128)(2,1)S(1)}, u32[]{:S(2)}, u32[]{:S(2)}) async-start(bf16[8,32,16,128]{3,2,1,0:T(8,128)(2,1)} %gate.1), calls=%async_computation | async-start | bytes 2097152 | tf_op jit(solution)/shard_map/all_to_all | solution.py:394
  159.1 16.6 %copy-start.1 = (bf16[8,32,16,128]{3,2,1,0:T(8,128)(2,1)}, bf16[8,32,16,128]{3,2,1,0:T(8,128)(2,1)S(1)}, u32[]{:S(2)}) copy-start(bf16[8,32,16,128]{3,2,1,0:T(8,128)(2,1)S(1)} %all-to-all-done.x_ref) | copy-start | bytes 3145732
  159.1 35.4 %all-to-all-start.2 = ((bf16[8,32,16,128]{3,2,1,0:T(8,128)(2,1)}), bf16[8,32,16,128]{3,2,1,0:T(8,128)(2,1)S(1)}, u32[]{:S(2)}, u32[]{:S(2)}) async-start(bf16[8,32,16,128]{3,2,1,0:T(8,128)(2,1)} %get-tuple-element.14), calls=%async_computation.2 | async-start | bytes 2097152 | tf_op jit(solution)/shard_map/all_to_all | solution.py:394
  194.6 5.1 %copy-start.2 = (bf16[8,32,16,128]{3,2,1,0:T(8,128)(2,1)}, bf16[8,32,16,128]{3,2,1,0:T(8,128)(2,1)S(1)}, u32[]{:S(2)}) copy-start(bf16[8,32,16,128]{3,2,1,0:T(8,128)(2,1)S(1)} %all-to-all-done.2.x_ref) | copy-start | bytes 3145732
  194.6 30.9 %all-to-all-start.1 = ((bf16[8,32,16,128]{3,2,1,0:T(8,128)(2,1)}), bf16[8,32,16,128]{3,2,1,0:T(8,128)(2,1)S(1)}, u32[]{:S(2)}, u32[]{:S(2)}) async-start(bf16[8,32,16,128]{3,2,1,0:T(8,128)(2,1)} %get-tuple-element.13), calls=%async_computation.1 | async-start | bytes 2097152 | tf_op jit(solution)/shard_map/all_to_all | solution.py:394
  225.4 17.7 %copy-start = (bf16[8,32,16,128]{3,2,1,0:T(8,128)(2,1)}, bf16[8,32,16,128]{3,2,1,0:T(8,128)(2,1)S(1)}, u32[]{:S(2)}) copy-start(bf16[8,32,16,128]{3,2,1,0:T(8,128)(2,1)S(1)} %all-to-all-done.1.conv_ref) | copy-start | bytes 3145732
  225.4 30.1 %all-to-all-start.3 = ((bf16[8,32,16,128]{3,2,1,0:T(8,128)(2,1)}), bf16[8,32,16,128]{3,2,1,0:T(8,128)(2,1)S(1)}, u32[]{:S(2)}, u32[]{:S(2)}) async-start(bf16[8,32,16,128]{3,2,1,0:T(8,128)(2,1)} %get-tuple-element.15), calls=%async_computation.3 | async-start | bytes 2097152 | tf_op jit(solution)/shard_map/all_to_all | solution.py:394
  255.5 1.0 copy-start.3
Sparse Core Ops, SparseCore 0:
  9.8 54.7 all-gather.4
  66.3 82.4 all-gather.6

commit v2 on v0

--- a/solution.py
+++ b/solution.py
@@ -1,8 +1,13 @@
+import functools
 import math
 
 import jax
 import jax.numpy as jnp
+import ml_dtypes
+import numpy as np
 from jax import lax
+from jax.experimental import pallas as pl
+from jax.experimental.pallas import tpu as pltpu
 from jax.sharding import PartitionSpec as P
 
 
@@ -97,7 +102,7 @@
     return (left.astype(jnp.float32) * right.astype(jnp.float32)).astype(jnp.bfloat16)
 
 
-def body(grad_out, proj_out, query, key_in, value_in, filters):
+def general_body(grad_out, proj_out, query, key_in, value_in, filters):
     weight_rows = lax.all_gather(proj_out, "ctx", axis=1, tiled=True)
     grad_mix = lax.dot_general(
         lax.all_gather(grad_out, "mp", axis=1, tiled=True),
@@ -120,6 +125,507 @@
     grad_key = product(back_grad.T, value_in)
     grad_value = product(back_grad.T, key_in)
     return (grad_query, grad_key, grad_value, filter_grad)
+
+
+FAST = 32
+SLOT = 2 * FAST
+PAIR = 2 * SLOT
+LANES = 128
+F32, BF16 = jnp.float32, jnp.bfloat16
+PARAMS = pltpu.CompilerParams(vmem_limit_bytes=60 * 2**20)
+VM = pl.BlockSpec(memory_space=pltpu.VMEM)
+ANY = pl.BlockSpec(memory_space=pl.ANY)
+U1, U2 = 16, 16
+
+
+def sds(shape, dtype):
+    return jax.ShapeDtypeStruct(shape, dtype)
+
+
+def cost(flops, moved):
+    return pl.CostEstimate(flops=flops // 10**6, bytes_accessed=moved // 10**3, transcendentals=0)
+
+
+def tables(seq):
+    size = 2 * seq
+    slow = size // FAST
+    half = slow // 2
+    s = np.arange(half)
+    angle = 2 * np.pi * ((s[:, None] * s[None, :]) % slow) / slow
+    first = np.concatenate([np.cos(angle), -np.sin(angle)], 0)
+    first[half] = 1.0 - 2.0 * (s % 2)
+    weight = np.full((2 * half, 1), 2.0)
+    weight[0] = weight[half] = 1.0
+    last = (first * weight).T / size
+    a = np.arange(FAST)
+    k = np.arange(half + 1)[:, None] + slow * a[None, :]
+    turn = 2 * np.pi * ((k[:, :, None] * a[None, None, :]) % size) / size
+    c, d = np.cos(turn), np.sin(turn)
+    fwd = np.concatenate([np.concatenate([c, d], 2), np.concatenate([-d, c], 2)], 1)
+    inv = fwd.transpose(0, 2, 1).copy()
+    fwd[0, :, FAST:] = 0.0
+    inv[0, FAST:] = 0.0
+
+    def paired(blocks):
+        out = np.zeros((half // 2 + 1, PAIR, PAIR))
+        out[:-1, :SLOT, :SLOT] = blocks[0:half:2]
+        out[:-1, SLOT:, SLOT:] = blocks[1:half:2]
+        return out
+
+    fwd, inv, edge_fwd, edge_inv = paired(fwd), paired(inv), fwd[half], inv[half]
+    fwd[-1, :SLOT, FAST:SLOT] = edge_fwd[:, :FAST]
+    inv[-1, FAST:SLOT, :SLOT] = edge_inv[:FAST]
+    return [jnp.asarray(t.astype(ml_dtypes.bfloat16)) for t in (first, fwd, inv, last)]
+
+
+def dot(left, right):
+    return jnp.dot(left, right, preferred_element_type=F32)
+
+
+def loop(count, unroll, step):
+    def some(i, carry):
+        for u in range(unroll):
+            step(i * unroll + u)
+        return carry
+
+    lax.fori_loop(0, count // unroll, some, 0)
+
+
+def span(start, size):
+    return pl.ds(pl.multiple_of(start * size, size), size)
+
+
+def spread(signal, first_ref, mid_ref):
+    half = first_ref.shape[1]
+
+    def step(a):
+        out = dot(first_ref[...], signal(a))
+        mid_ref[pl.ds(a, half, stride=SLOT), :] = out[:half]
+        mid_ref[pl.ds(FAST + a, half, stride=SLOT), :] = out[half:]
+
+    loop(FAST, U1, step)
+
+
+def collect(last_ref, back_ref, emit):
+    half = last_ref.shape[0]
+
+    def step(a):
+        re = back_ref[pl.ds(a, half, stride=SLOT), :]
+        im = back_ref[pl.ds(FAST + a, half, stride=SLOT), :]
+        emit(a, dot(last_ref[...], jnp.concatenate([re, im], 0).astype(BF16)))
+
+    loop(FAST, U1, step)
+
+
+def times(x, y, conjugate):
+    parts = []
+    for i in range(0, x.shape[0], SLOT):
+        xr, xi, yr, yi = (v[i + j : i + j + FAST] for v in (x, y) for j in (0, FAST))
+        if conjugate:
+            parts += [xr * yr + xi * yi, xi * yr - xr * yi]
+        else:
+            parts += [xr * yr - xi * yi, xr * yi + xi * yr]
+    return jnp.concatenate(parts, 0).astype(BF16)
+
+
+def filter_kernel(h_ref, first_ref, fwd_ref, spec_ref, time_ref, mid_ref):
+    half = first_ref.shape[1]
+    seq = h_ref.shape[1]
+
+    def turn(i):
+        time_ref[span(i, LANES), :] = h_ref[:, span(i, LANES)].T
+
+    loop(seq // LANES, 8, turn)
+    spread(lambda a: time_ref[pl.ds(a, half, stride=FAST), :].astype(BF16), first_ref, mid_ref)
+
+    def step(p):
+        spec_ref[span(p, PAIR), :] = dot(fwd_ref[p], mid_ref[span(p, PAIR), :].astype(BF16))
+
+    loop(half // 2, U2, step)
+    spec_ref[span(half // 2, PAIR), :] = dot(fwd_ref[half // 2], mid_ref[:PAIR, :].astype(BF16))
+
+
+def convolve_kernel(conjugate, x_ref, h_any, first_ref, fwd_any, inv_any, last_ref,
+                    out_ref, spec_any, h_ref, fwd_ref, inv_ref, spec_ref, mid_ref, back_ref, sem):
+    half = first_ref.shape[1]
+    groups, _, per, _ = x_ref.shape
+    loads = [
+        pltpu.make_async_copy(source, target, sem.at[i])
+        for i, (source, target) in enumerate(((fwd_any, fwd_ref), (h_any, h_ref), (inv_any, inv_ref)))
+    ]
+    for load in loads:
+        load.start()
+    spread(lambda a: x_ref[:, a].reshape(half, LANES), first_ref, mid_ref)
+    for load in loads:
+        load.wait()
+
+    def step(p):
+        x = dot(fwd_ref[p], mid_ref[span(p, PAIR), :].astype(BF16))
+        spec_ref[span(p, PAIR), :] = x
+        back_ref[span(p, PAIR), :] = dot(inv_ref[p], times(x, h_ref[span(p, PAIR), :], conjugate))
+
+    loop(half // 2, U2, step)
+    tail = span(half // 2, PAIR)
+    x = dot(fwd_ref[half // 2], mid_ref[:PAIR, :].astype(BF16))
+    spec_ref[tail, :] = x
+    store = pltpu.make_async_copy(spec_ref, spec_any, sem.at[3])
+    store.start()
+    back_ref[:PAIR, :] += dot(inv_ref[half // 2], times(x, h_ref[tail, :], conjugate))
+
+    def emit(a, rows):
+        out_ref[:, a] = rows.reshape(groups, per, LANES).astype(BF16)
+
+    collect(last_ref, back_ref, emit)
+    store.wait()
+
+
+def gradient_kernel(scale, s_ref, g_ref, inv_ref, last_ref, out_ref, time_ref, back_ref):
+    half = last_ref.shape[0]
+    seq = out_ref.shape[1]
+
+    def step(p):
+        rows = span(p, PAIR)
+        back_ref[rows, :] = dot(inv_ref[p], times(s_ref[rows, :], g_ref[rows, :], True))
+
+    loop(half // 2, U2, step)
+    tail = span(half // 2, PAIR)
+    back_ref[:PAIR, :] += dot(inv_ref[half // 2], times(s_ref[tail, :], g_ref[tail, :], True))
+
+    def emit(a, rows):
+        time_ref[pl.ds(a, half, stride=FAST), :] = rows * scale
+
+    collect(last_ref, back_ref, emit)
+
+    def turn(i):
+        out_ref[:, span(i, LANES)] = time_ref[span(i, LANES), :].T
+
+    loop(seq // LANES, 8, turn)
+
+
+def filter_spectrum(h, tabs):
+    first, fwd = tabs[:2]
+    seq = h.shape[1]
+    return pl.pallas_call(
+        filter_kernel,
+        out_shape=sds((2 * seq + PAIR, LANES), F32),
+        in_specs=[VM] * 3,
+        out_specs=VM,
+        scratch_shapes=[pltpu.VMEM((seq, LANES), F32), pltpu.VMEM((2 * seq, LANES), F32)],
+        compiler_params=PARAMS,
+        cost_estimate=cost(10**9, 8 * 2**20),
+        name="filter_spectrum",
+    )(h, first, fwd)
+
+
+def convolve(x, spec, tabs, conjugate):
+    fwd = tabs[1]
+    rows = spec.shape[0]
+    big = pltpu.VMEM((rows - PAIR, LANES), F32)
+    return pl.pallas_call(
+        functools.partial(convolve_kernel, conjugate),
+        out_shape=(sds(x.shape, BF16), sds(spec.shape, F32)),
+        in_specs=[VM, ANY, VM, ANY, ANY, VM],
+        out_specs=(VM, ANY),
+        scratch_shapes=[
+            pltpu.VMEM(spec.shape, F32),
+            pltpu.VMEM(fwd.shape, BF16),
+            pltpu.VMEM(fwd.shape, BF16),
+            pltpu.VMEM(spec.shape, F32),
+            big,
+            big,
+            pltpu.SemaphoreType.DMA((4,)),
+        ],
+        compiler_params=PARAMS,
+        cost_estimate=cost(2 * 10**9, 14 * 2**20),
+        name="convolve",
+    )(x, spec, *tabs)
+
+
+def filter_gradient(scaled_spec, gated_spec, tabs, scale):
+    inv, last = tabs[2:]
+    seq = (scaled_spec.shape[0] - PAIR) // 2
+    return pl.pallas_call(
+        functools.partial(gradient_kernel, scale),
+        out_shape=sds((LANES, seq), F32),
+        in_specs=[VM] * 4,
+        out_specs=VM,
+        scratch_shapes=[pltpu.VMEM((seq, LANES), F32), pltpu.VMEM((2 * seq, LANES), F32)],
+        compiler_params=PARAMS,
+        cost_estimate=cost(10**9, 12 * 2**20),
+        name="filter_gradient",
+    )(scaled_spec, gated_spec, inv, last)
+
+
+def permuted(value, hold_ref, emit):
+    hold_ref[...] = value
+    per = value.shape[0] // FAST
+    for a in range(FAST):
+        emit(a, hold_ref[pl.ds(a, per, stride=FAST), :].astype(BF16))
+
+
+def gate_kernel(key_ref, value_ref, out_ref, hold_ref):
+    product = key_ref[...].astype(F32) * value_ref[...].astype(F32)
+    for g in range(WIDE // LANES):
+
+        def emit(a, rows):
+            out_ref[g, a] = rows
+
+        permuted(product[:, g * LANES : (g + 1) * LANES], hold_ref, emit)
+
+
+def gate(key_in, value_in, groups):
+    rows, cols = key_in.shape
+    block = pl.BlockSpec((rows, WIDE), lambda j: (0, j))
+    return pl.pallas_call(
+        gate_kernel,
+        grid=(cols // WIDE,),
+        out_shape=sds((groups, FAST, rows // FAST, LANES), BF16),
+        in_specs=[block, block],
+        out_specs=pl.BlockSpec((WIDE // LANES, FAST, rows // FAST, LANES), lambda j: (j, 0, 0, 0)),
+        scratch_shapes=[pltpu.VMEM((rows, LANES), F32)],
+        compiler_params=PARAMS,
+        cost_estimate=cost(10**6, 3 * 2**20),
+        name="gate",
+    )(key_in, value_in)
+
+
+WIDE = 256
+CHIPS = 4
+
+
+def pieces_of(x_ref, piece, lane, depth):
+    return x_ref[piece, :, pl.ds(pl.multiple_of(lane * depth, depth), depth)]
+
+
+def against(left, w_ref):
+    return lax.dot_general(left, w_ref[...], (((1,), (1,)), ((), ())), preferred_element_type=F32)
+
+
+def terms_kernel(dists, place_ref, *refs):
+    count = 2 * sum(1 if d == 0 else 2 for d in dists)
+    x_ref, ws, before, sum_ref = refs[0], refs[1 : 1 + count], refs[1 + count : -1], refs[-1]
+    here, core = place_ref[0], place_ref[1]
+    depth = ws[0].shape[1]
+
+    def part(piece, near_ref, swap_ref):
+        one = against(pieces_of(x_ref, piece, core, depth), near_ref)
+        return one + against(pieces_of(x_ref, piece, 1 - core, depth), swap_ref)
+
+    if before:
+        sum_ref[...] = before[0][...]
+    for d in dists:
+        if d == 0:
+            sum_ref[...] = part(here, ws[0], ws[1])
+            ws = ws[2:]
+            continue
+        up, up_swap, down, down_swap = ws[:4]
+        ws = ws[4:]
+
+        @pl.when(here >= d)
+        def _():
+            sum_ref[...] += part(here - d, up, up_swap)
+
+        @pl.when(here + d < CHIPS)
+        def _():
+            sum_ref[...] += part(here + d, down, down_swap)
+
+
+def above(d):
+    return lambda j, place: (jnp.where(place[0] >= d, j, 0), 0)
+
+
+def below(d):
+    return lambda j, place: (jnp.where(place[0] + d < CHIPS, j, 0), 0)
+
+
+def terms(dists, place, x, ws, *before):
+    _, rows, _ = x.shape
+    cols, depth = ws[0].shape
+    maps = []
+    for d in dists:
+        maps += [above(d), above(d)] + ([below(d), below(d)] if d else [])
+    wide = pl.BlockSpec((rows, WIDE), lambda j, place: (0, j))
+    return pl.pallas_call(
+        functools.partial(terms_kernel, dists),
+        out_shape=sds((rows, cols), F32),
+        grid_spec=pltpu.PrefetchScalarGridSpec(
+            num_scalar_prefetch=1,
+            grid=(cols // WIDE,),
+            in_specs=[pl.BlockSpec(x.shape, lambda j, place: (0, 0, 0))]
+            + [pl.BlockSpec((WIDE, depth), m) for m in maps]
+            + [wide] * len(before),
+            out_specs=wide,
+        ),
+        compiler_params=PARAMS,
+        cost_estimate=cost(2 * 10**9, 14 * 2**20),
+        name="terms",
+    )(place, x, *ws, *before)
+
+
+def late_kernel(place_ref, *refs):
+    x_ref, ws = refs[0], refs[1:5]
+    sum_ref, query_ref, mix_ref, out_ref, total_ref, hold_ref = refs[5:]
+    here, core = place_ref[0], place_ref[1]
+    depth = ws[0].shape[1]
+
+    def part(near_ref, swap_ref):
+        one = against(pieces_of(x_ref, 0, core, depth), near_ref)
+        return one + against(pieces_of(x_ref, 0, 1 - core, depth), swap_ref)
+
+    total_ref[...] = sum_ref[...]
+
+    @pl.when(here == CHIPS - 1)
+    def _():
+        total_ref[...] += part(ws[0], ws[1])
+
+    @pl.when(here == 0)
+    def _():
+        total_ref[...] += part(ws[2], ws[3])
+
+    mix = total_ref[...].astype(BF16)
+    mix_ref[...] = mix
+    scaled = mix.astype(F32) * query_ref[...].astype(F32)
+    for g in range(WIDE // LANES):
+
+        def emit(a, rows):
+            out_ref[g, a] = rows
+
+        permuted(scaled[:, g * LANES : (g + 1) * LANES], hold_ref, emit)
+
+
+def mix_late(place, x, ws, total, query, groups):
+    rows, cols = query.shape
+    depth = ws[0].shape[1]
+    maps = [above(CHIPS - 1)] * 2 + [below(CHIPS - 1)] * 2
+    wide = pl.BlockSpec((rows, WIDE), lambda j, place: (0, j))
+    parts = pl.BlockSpec((WIDE // LANES, FAST, rows // FAST, LANES), lambda j, place: (j, 0, 0, 0))
+    return pl.pallas_call(
+        late_kernel,
+        out_shape=(sds((rows, cols), BF16), sds((groups, FAST, rows // FAST, LANES), BF16)),
+        grid_spec=pltpu.PrefetchScalarGridSpec(
+            num_scalar_prefetch=1,
+            grid=(cols // WIDE,),
+            in_specs=[pl.BlockSpec((1,) + x.shape[1:], lambda j, place: (jnp.where(place[0] == 0, CHIPS - 1, 0), 0, 0))]
+            + [pl.BlockSpec((WIDE, depth), m) for m in maps]
+            + [wide, wide],
+            out_specs=(wide, parts),
+            scratch_shapes=[
+                pltpu.VMEM((rows, WIDE), F32),
+                pltpu.VMEM((rows, LANES), F32),
+            ],
+        ),
+        compiler_params=PARAMS,
+        cost_estimate=cost(10**9, 8 * 2**20),
+        name="mix_late",
+    )(place, x, *ws, total, query)
+
+
+def unpermuted(part_ref, g, hold_ref):
+    per = part_ref.shape[2]
+    for a in range(FAST):
+        hold_ref[pl.ds(a, per, stride=FAST), :] = part_ref[g, a].astype(F32)
+    return hold_ref[...]
+
+
+def finish_kernel(count, *refs):
+    part_ref, factors, outs, hold_ref = refs[0], refs[1 : 1 + count], refs[1 + count : 1 + 2 * count], refs[-1]
+    for g in range(WIDE // LANES):
+        value = unpermuted(part_ref, g, hold_ref)
+        lanes = pl.ds(g * LANES, LANES)
+        for factor_ref, out_ref in zip(factors, outs):
+            out_ref[:, lanes] = (value * factor_ref[:, lanes].astype(F32)).astype(BF16)
+
+
+def finish(parts, *factors):
+    _, _, per, _ = parts.shape
+    rows, cols = factors[0].shape
+    count = len(factors)
+    wide = pl.BlockSpec((rows, WIDE), lambda j: (0, j))
+    part = pl.BlockSpec((WIDE // LANES, FAST, per, LANES), lambda j: (j, 0, 0, 0))
+    return pl.pallas_call(
+        functools.partial(finish_kernel, count),
+        grid=(cols // WIDE,),
+        out_shape=(sds((rows, cols), BF16),) * count,
+        in_specs=[part] + [wide] * count,
+        out_specs=(wide,) * count,
+        scratch_shapes=[pltpu.VMEM((rows, LANES), F32)],
+        compiler_params=PARAMS,
+        cost_estimate=cost(10**6, (1 + 2 * count) * 2**20),
+        name="finish",
+    )(parts, *factors)
+
+
+def exchange(parts):
+    return lax.all_to_all(parts, "ctx", split_axis=0, concat_axis=0, tiled=True)
+
+
+SWAP = [(i, i ^ 1) for i in range(2 * CHIPS)]
+
+
+def hop(low, high, d):
+    up = [(i, i + 2) for i in range(2 * (d - 1), 2 * CHIPS - 2)]
+    down = [(i, i - 2) for i in range(2, 2 * (CHIPS - d + 1))]
+    return lax.ppermute(low, "ctx", up), lax.ppermute(high, "ctx", down)
+
+
+def with_swaps(low, high, d):
+    low_swap = lax.ppermute(low, "ctx", [p for p in SWAP if p[0] >= 2 * d])
+    high_swap = lax.ppermute(high, "ctx", [p for p in SWAP if p[0] < 2 * (CHIPS - d)])
+    return [low, low_swap, high, high_swap]
+
+
+def lane_body(grad_out, proj_out, query, key_in, value_in, filters):
+    seq = filters.shape[1]
+    groups = seq // key_in.shape[0]
+    tabs = tables(seq)
+    tie = lax.optimization_barrier
+    ctx = lax.axis_index("ctx")
+    place = jnp.stack([ctx // 2, ctx % 2]).astype(jnp.int32)
+
+    low1, high1 = hop(proj_out, proj_out, 1)
+    x = lax.all_gather(grad_out, "mp", axis=0)
+    gated = exchange(gate(key_in, value_in, groups))
+    spec = filter_spectrum(filters, tabs)
+    low1, high1, spec, own = tie((low1, high1, spec, proj_out))
+
+    low2, high2 = hop(low1, high1, 2)
+    ws = [own, lax.ppermute(own, "ctx", SWAP)] + with_swaps(low1, high1, 1)
+    conv_out, gated_spec = convolve(gated, spec, tabs, False)
+    low2, high2, conv_out, *ws = tie((low2, high2, conv_out, *ws))
+
+    low3, high3 = hop(low2, high2, 3)
+    ws += with_swaps(low2, high2, 2)
+    conv_back = exchange(conv_out)
+    total = terms((0, 1, 2), place, x, ws)
+    low3, high3, total = tie((low3, high3, total))
+
+    ws = with_swaps(low3, high3, 3)
+    grad_mix, scaled = mix_late(place, x, ws, total, query, groups)
+    scaled, conv_back = tie((scaled, conv_back))
+    scaled = exchange(scaled)
+    grad_gated, scaled_spec = convolve(scaled, spec, tabs, True)
+    grad_back = exchange(grad_gated)
+    filter_grad = filter_gradient(scaled_spec, gated_spec, tabs, 1.0 / math.sqrt(seq))
+    (grad_query,) = finish(conv_back, grad_mix)
+    grad_key, grad_value = finish(grad_back, value_in, key_in)
+    return (grad_query, grad_key, grad_value, filter_grad)
+
+
+def body(grad_out, proj_out, query, key_in, value_in, filters):
+    rows, cols = key_in.shape
+    lanes, seq = filters.shape
+    fits = (
+        lax.axis_size("ctx") == 2 * CHIPS
+        and lax.axis_size("mp") == 4
+        and lanes == LANES
+        and rows % (16 * FAST) == 0
+        and cols == 2 * CHIPS * LANES
+        and seq == 2 * CHIPS * rows
+        and seq == FAST * LANES
+        and grad_out.shape[1] == 2 * proj_out.shape[1]
+    )
+    args = (grad_out, proj_out, query, key_in, value_in, filters)
+    return lane_body(*args) if fits else general_body(*args)
 
 
 def solution(mesh):

time: 509 us -> 226 us (0.44)
  matrix products: 285 us -> 0 us
  waiting for transfers between devices: 136 us -> 55.9 us
  Pallas kernels: 0 us -> 76.1 us
  local copies, waits for them, and re-layouts: 38.8 us -> 1.97 us
  blocking collectives: 0 us -> 30.2 us
  starting transfers between devices: 19.3 us -> 45.5 us
  other arithmetic: 9.1 us -> 0.67 us
    dot_general x37 -> x0, matrix products: 285 us -> none  [the longest x36 276 us: contract(): return jnp.einsum(form, left, right, precision=lax.Precision.HIGHEST)]
    all_gather x2 -> x1, waiting for transfers between devices: 126 us -> 0.01 us  [lane_body(): x = lax.all_gather(grad_out, 'mp', axis=0)]
    pallas_call x0 -> x9, Pallas kernels: none -> 76.1 us  [the longest x2 21.9 us: convolve(): pl.pallas_call(functools.partial(convolve_kernel, conjugate), out_shape=(...]
    ppermute x0 -> x13, waiting for transfers between devices: none -> 33 us  [the longest x6 30.4 us: hop(): return (lax.ppermute(low, 'ctx', up), lax.ppermute(high, 'ctx', down))]
    all_to_all x0 -> x1, blocking collectives: none -> 30.2 us  [exchange(): return lax.all_to_all(parts, 'ctx', split_axis=0, concat_axis=0, tiled=True)]
    ppermute x0 -> x13, starting transfers between devices: none -> 25.7 us  [the longest x3 11.3 us: with_swaps(): lax.ppermute(high, 'ctx', [p for p in SWAP if p[0] < 2 * (CHIPS - d)])]
    unnamed x59 -> x14, local copies, waits for them, and re-layouts: 19.7 us -> 1.97 us
    reshape x3 -> x0, local copies, waits for them, and re-layouts: 14.4 us -> none  [the longest x2 10.9 us: restore(): inverse_real(spec_re, spec_im, tables).reshape(channels, length_all)]
  transfers between devices with their start and end apart: 6 -> 17, of which waited for: 5 -> 6; matrix products, arithmetic and copies ran while one was open for 17% -> 0% of each run, Pallas kernels for 0% -> 27%
where the time goes in v2:
time: 226 us; the launch traced here: 224 us
  Pallas kernels  76.1 us (34%)
  waiting for transfers between devices  55.9 us (25%)
  starting transfers between devices  45.5 us (20%)
  blocking collectives  30.2 us (13%)
  between operations  14.2 us (6%)
    ppermute x6, waiting for transfers between devices, hop(): return (lax.ppermute(low, 'ctx', up), lax.ppermute(high, 'ctx', down))  30.4 us
    all_to_all x1, blocking collectives, exchange(): return lax.all_to_all(parts, 'ctx', split_axis=0, concat_axis=0, tiled=True)  30.2 us
    all_to_all x3, waiting for transfers between devices, exchange(): return lax.all_to_all(parts, 'ctx', split_axis=0, concat_axis=0, tiled=True)  22.1 us
    pallas_call x2, Pallas kernels, convolve(): pl.pallas_call(functools.partial(convolve_kernel, conjugate), out_shape=(...  21.9 us
    all_to_all x3, starting transfers between devices, exchange(): return lax.all_to_all(parts, 'ctx', split_axis=0, concat_axis=0, tiled=True)  19.8 us
    pallas_call x1, Pallas kernels, filter_gradient(): pl.pallas_call(functools.partial(gradient_kernel, scale), out_shape=sds((...  11.5 us
    ppermute x3, starting transfers between devices, with_swaps(): lax.ppermute(high, 'ctx', [p for p in SWAP if p[0] < 2 * (CHIPS - d)])  11.3 us
    pallas_call x1, Pallas kernels, terms(): pl.pallas_call(functools.partial(terms_kernel, dists), out_shape=sds((row...  10.9 us
  transfers between devices with their start and end apart: 17, of which 6 were waited for; matrix products, arithmetic and copies ran while one was open for 0% of the time, Pallas kernels for 27%

profile of v2, /device:TPU:1, one launch (start us, length us, event | category | flops | bytes accessed | tf_op | source)
XLA Modules:
  0.0 224.5 jit_solution(45182954761495214)
XLA Ops:
  7.2 0.0 all-gather.3.cloned.1.call-start
  7.2 0.7 all-gather.3.cloned.1.call-update
  7.9 4.1 %collective-permute-start = (bf16[1024,512]{1,0:T(8,128)(2,1)}, bf16[1024,512]{1,0:T(8,128)(2,1)S(1)}, u32[]{:S(2)}, u32[]{:S(2)}) collective-permute-start(bf16[1024,512]{1,0:T(8,128)(2,1)} %refs_1_.1), channel_id=1, source_target_pairs={{0,8},{4,12},{8,16},{12,20},{16,24},{20,28},{1,9},{5,13},{9,17},{1... | collective-permute-start | bytes 3145736 | tf_op jit(solution)/shard_map/ppermute | solution.py:568
  12.0 1.3 collective-permute-start.1
  13.3 4.3 %gate.1 = bf16[8,32,16,128]{3,2,1,0:T(8,128)(2,1)} custom-call(bf16[512,1024]{1,0:T(8,128)(2,1)} %refs_2_.1, bf16[512,1024]{1,0:T(8,128)(2,1)} %refs_1_.2), custom_call_target="tpu_custom_call" | custom-call | flops 1 | bytes 3145 | tf_op jit(solution)/shard_map/gate/pallas_call | solution.py:379
  17.6 7.9 %all-to-all-start = ((bf16[8,32,16,128]{3,2,1,0:T(8,128)(2,1)}), bf16[8,32,16,128]{3,2,1,0:T(8,128)(2,1)S(1)}, u32[]{:S(2)}, u32[]{:S(2)}) async-start(bf16[8,32,16,128]{3,2,1,0:T(8,128)(2,1)} %gate.1), calls=%async_computation | async-start | bytes 2097152 | tf_op jit(solution)/shard_map/all_to_all | solution.py:559
  25.5 0.0 copy-start.3
  25.5 10.5 %filter_spectrum.1.h_any = f32[8320,128]{1,0:T(8,128)} custom-call(f32[128,4096]{1,0:T(8,128)} %h_ref.1, bf16[256,128]{1,0:T(8,128)(2,1)} %constant.38.clone.first_ref, bf16[65,128,128]{2,1,0:T(8,128)(2,1)} %constant.39.clone.fwd_ref.fwd_any), custom_call_target="tpu_custom_call" | custom-call | flops 1000 | bytes 8388 | tf_op jit(solution)/shard_map/filter_spectrum/pallas_call | solution.py:308
  36.0 0.0 collective-permute-done.refs_3_
  36.0 0.0 copy-start.4
  36.0 1.9 collective-permute-done.1.refs_5_
  37.9 1.6 collective-permute-start.2
  39.6 1.6 collective-permute-start.5
  41.2 1.3 collective-permute-start.3
  42.5 6.2 %collective-permute-start.6 = (bf16[1024,512]{1,0:T(8,128)(2,1)}, bf16[1024,512]{1,0:T(8,128)(2,1)}, u32[]{:S(2)}, u32[]{:S(2)}) collective-permute-start(bf16[1024,512]{1,0:T(8,128)(2,1)} %collective-permute-done.1.refs_5_), channel_id=1, source_target_pairs={{0,4},{4,0},{8,12},{12,8},{16,20},{20,16},{1,5},{5,1},{9,13},{13,9... | collective-permute-start | bytes 3145736 | tf_op jit(solution)/shard_map/ppermute | solution.py:573
  48.7 0.0 copy-done.3
  48.7 0.1 collective-permute-start.4
  48.8 12.4 %all-to-all-done.x_ref = bf16[8,32,16,128]{3,2,1,0:T(8,128)(2,1)S(1)} async-done(((bf16[8,32,16,128]{3,2,1,0:T(8,128)(2,1)}), bf16[8,32,16,128]{3,2,1,0:T(8,128)(2,1)S(1)}, u32[]{:S(2)}, u32[]{:S(2)}) %all-to-all-start) | async-done | bytes 1048608 | tf_op jit(solution)/shard_map/all_to_all | solution.py:559
  61.2 0.0 copy-start.1
  61.2 1.0 copy-done.1
  62.1 10.9 %convolve.2 = (bf16[8,32,16,128]{3,2,1,0:T(8,128)(2,1)}, f32[8320,128]{1,0:T(8,128)}) custom-call(bf16[8,32,16,128]{3,2,1,0:T(8,128)(2,1)} %copy-done.1, f32[8320,128]{1,0:T(8,128)} %filter_spectrum.1.h_any, bf16[256,128]{1,0:T(8,128)(2,1)} %constant.38.clone.first_ref, bf16[65,128,128]{2,1,0:T(8,128)(2,1)} %constant.39.clone.fwd_ref.fwd_any, ...), custom_call_target="tpu_custom_call" | custom-call | flops 2000 | bytes 14680 | tf_op jit(solution)/shard_map/convolve/pallas_call | solution.py:324
  73.1 0.0 collective-permute-done.2.refs_7_
  73.1 7.7 %collective-permute-done.3.refs_9_ = bf16[1024,512]{1,0:T(8,128)(2,1)} collective-permute-done((bf16[1024,512]{1,0:T(8,128)(2,1)}, bf16[1024,512]{1,0:T(8,128)(2,1)}, u32[]{:S(2)}, u32[]{:S(2)}) %collective-permute-start.3) | collective-permute-done | bytes 1048608 | tf_op jit(solution)/shard_map/ppermute | solution.py:568
  80.8 0.0 collective-permute-done.5.refs_4_
  80.8 0.0 collective-permute-done.6.refs_6_
  80.8 0.0 collective-permute-done.4.refs_2_
  80.8 2.3 %collective-permute-start.10 = (bf16[1024,512]{1,0:T(8,128)(2,1)}, bf16[1024,512]{1,0:T(8,128)(2,1)}, u32[]{:S(2)}, u32[]{:S(2)}) collective-permute-start(bf16[1024,512]{1,0:T(8,128)(2,1)} %collective-permute-done.3.refs_9_), channel_id=1, source_target_pairs={{0,4},{4,0},{8,12},{12,8},{1,5},{5,1},{9,13},{13,9},{2,6},{6,2},{1... | collective-permute-start | bytes 3145736 | tf_op jit(solution)/shard_map/ppermute | solution.py:573
  83.2 1.7 collective-permute-start.9
  84.8 0.7 collective-permute-start.7
  85.6 1.3 collective-permute-start.8
  86.9 7.4 %all-to-all-start.1 = ((bf16[8,32,16,128]{3,2,1,0:T(8,128)(2,1)}), bf16[8,32,16,128]{3,2,1,0:T(8,128)(2,1)S(1)}, u32[]{:S(2)}, u32[]{:S(2)}) async-start(bf16[8,32,16,128]{3,2,1,0:T(8,128)(2,1)} %get-tuple-element.47), calls=%async_computation.1 | async-start | bytes 2097152 | tf_op jit(solution)/shard_map/all_to_all | solution.py:559
  94.3 0.7 pad_add_fusion.place_ref
  95.0 0.0 collective-permute-done.10.refs_10_
  95.0 0.0 collective-permute-done.9.refs_8_
  95.0 0.0 all-gather.3.cloned.1.call-done
  95.0 0.0 copy-done.4
  95.0 10.9 %terms.1.refs_5_ = f32[512,1024]{1,0:T(8,128)} custom-call(s32[2]{0:T(128)} %pad_add_fusion.place_ref, bf16[4,512,1024]{2,1,0:T(8,128)(2,1)} %bitcast.3, bf16[1024,512]{1,0:T(8,128)(2,1)} %refs_1_.1, bf16[1024,512]{1,0:T(8,128)(2,1)} %collective-permute-done.4.refs_2_, bf16[1024,512]{1,0:T(8,128)(2,1)} %copy-done.4, ...), custom_call_target="tpu_custom_call" | custom-call | flops 2000 | bytes 14680 | tf_op jit(solution)/shard_map/terms/pallas_call | solution.py:448
  105.9 0.0 collective-permute-done.7.refs_1_
  105.9 0.0 copy-start.5
  105.9 20.8 %collective-permute-done.8.refs_3_ = bf16[1024,512]{1,0:T(8,128)(2,1)} collective-permute-done((bf16[1024,512]{1,0:T(8,128)(2,1)}, bf16[1024,512]{1,0:T(8,128)(2,1)}, u32[]{:S(2)}, u32[]{:S(2)}) %collective-permute-start.8) | collective-permute-done | bytes 1048608 | tf_op jit(solution)/shard_map/ppermute | solution.py:568
  126.7 0.7 collective-permute-start.11
  127.4 2.7 %collective-permute-start.12 = (bf16[1024,512]{1,0:T(8,128)(2,1)}, bf16[1024,512]{1,0:T(8,128)(2,1)}, u32[]{:S(2)}, u32[]{:S(2)}) collective-permute-start(bf16[1024,512]{1,0:T(8,128)(2,1)} %collective-permute-done.8.refs_3_), channel_id=1, source_target_pairs={{0,4},{4,0},{1,5},{5,1},{2,6},{6,2},{3,7},{7,3}} | collective-permute-start | bytes 3145736 | tf_op jit(solution)/shard_map/ppermute | solution.py:573
  130.1 0.0 collective-permute-done.11.refs_2_
  130.1 0.0 copy-start.6
  130.1 2.6 %collective-permute-done.12.refs_4_ = bf16[1024,512]{1,0:T(8,128)(2,1)} collective-permute-done((bf16[1024,512]{1,0:T(8,128)(2,1)}, bf16[1024,512]{1,0:T(8,128)(2,1)}, u32[]{:S(2)}, u32[]{:S(2)}) %collective-permute-start.12) | collective-permute-done | bytes 1048608 | tf_op jit(solution)/shard_map/ppermute | solution.py:573
  132.7 0.0 copy-done.5
  132.7 0.0 copy-done.6
  132.7 7.6 %mix_late.1 = (bf16[512,1024]{1,0:T(8,128)(2,1)}, bf16[8,32,16,128]{3,2,1,0:T(8,128)(2,1)}) custom-call(s32[2]{0:T(128)} %pad_add_fusion.place_ref, bf16[4,512,1024]{2,1,0:T(8,128)(2,1)} %bitcast.4, bf16[1024,512]{1,0:T(8,128)(2,1)} %copy-done.5, bf16[1024,512]{1,0:T(8,128)(2,1)} %copy-done.6, bf16[1024,512]{1,0:T(8,128)(2,1)} %collective-permute-done.8.refs_3_, ...), custom_call_target="tpu_custom_call" | custom-call | flops 1000 | bytes 8388 | tf_op jit(solution)/shard_map/mix_late/pallas_call | solution.py:502
  140.3 0.0 all-to-all-done.1.refs_0_
  140.3 0.0 copy-start
  140.3 30.2 %all_to_all.20.x_ref = bf16[8,32,16,128]{3,2,1,0:T(8,128)(2,1)} all-to-all(bf16[8,32,16,128]{3,2,1,0:T(8,128)(2,1)} %get-tuple-element.50), channel_id=1, replica_groups=mesh['ctx'=8,'mp'=4] {'ctx'}, dimensions={0} | all-to-all | bytes 2097152 | tf_op jit(solution)/shard_map/all_to_all | solution.py:559
  170.5 10.9 %convolve.3 = (bf16[8,32,16,128]{3,2,1,0:T(8,128)(2,1)}, f32[8320,128]{1,0:T(8,128)}) custom-call(bf16[8,32,16,128]{3,2,1,0:T(8,128)(2,1)} %all_to_all.20.x_ref, f32[8320,128]{1,0:T(8,128)} %filter_spectrum.1.h_any, bf16[256,128]{1,0:T(8,128)(2,1)} %constant.38.clone.first_ref, bf16[65,128,128]{2,1,0:T(8,128)(2,1)} %constant.39.clone.fwd_ref.fwd_any, ...), custom_call_target="tpu_custom_call" | custom-call | flops 2000 | bytes 14680 | tf_op jit(solution)/shard_map/convolve/pallas_call | solution.py:324
  181.4 0.0 copy-done
  181.4 4.5 %all-to-all-start.3 = ((bf16[8,32,16,128]{3,2,1,0:T(8,128)(2,1)}), bf16[8,32,16,128]{3,2,1,0:T(8,128)(2,1)S(1)}, u32[]{:S(2)}, u32[]{:S(2)}) async-start(bf16[8,32,16,128]{3,2,1,0:T(8,128)(2,1)} %get-tuple-element.51), calls=%async_computation.3 | async-start | bytes 2097152 | tf_op jit(solution)/shard_map/all_to_all | solution.py:559
  185.9 4.5 %finish.2 = bf16[512,1024]{1,0:T(8,128)(2,1)} custom-call(bf16[8,32,16,128]{3,2,1,0:T(8,128)(2,1)} %copy-done, bf16[512,1024]{1,0:T(8,128)(2,1)} %get-tuple-element.49.refs_1_), custom_call_target="tpu_custom_call" | custom-call | flops 1 | bytes 3145 | tf_op jit(solution)/shard_map/finish/pallas_call | solution.py:545
  190.4 11.5 %filter_gradient.1 = f32[128,4096]{1,0:T(8,128)} custom-call(f32[8320,128]{1,0:T(8,128)} %get-tuple-element.54.s_ref, f32[8320,128]{1,0:T(8,128)} %get-tuple-element.55.g_ref, bf16[65,128,128]{2,1,0:T(8,128)(2,1)} %constant.40.clone.inv_any.inv_ref, bf16[128,256]{1,0:T(8,128)(2,1)} %constant.41.clone.last_ref), custom_call_target="tpu_custom_call" | custom-call | flops 1000 | bytes 12582 | tf_op jit(solution)/shard_map/filter_gradient/pallas_call | solution.py:347
  201.9 9.8 %all-to-all-done.3.refs_0_ = bf16[8,32,16,128]{3,2,1,0:T(8,128)(2,1)S(1)} async-done(((bf16[8,32,16,128]{3,2,1,0:T(8,128)(2,1)}), bf16[8,32,16,128]{3,2,1,0:T(8,128)(2,1)S(1)}, u32[]{:S(2)}, u32[]{:S(2)}) %all-to-all-start.3) | async-done | bytes 1048608 | tf_op jit(solution)/shard_map/all_to_all | solution.py:559
  211.7 0.0 copy-start.2
  211.7 1.0 copy-done.2
  212.7 5.0 %finish.3 = (bf16[512,1024]{1,0:T(8,128)(2,1)}, bf16[512,1024]{1,0:T(8,128)(2,1)}) custom-call(bf16[8,32,16,128]{3,2,1,0:T(8,128)(2,1)} %copy-done.2, bf16[512,1024]{1,0:T(8,128)(2,1)} %refs_1_.2, bf16[512,1024]{1,0:T(8,128)(2,1)} %refs_2_.1), custom_call_target="tpu_custom_call" | custom-call | flops 1 | bytes 5242 | tf_op jit(solution)/shard_map/finish/pallas_call | solution.py:545
Async XLA Ops:
  7.2 87.8 %all-gather.3.cloned.1.call-start = ((), (), s32[]{:S(2)}) async-start(), calls=%async_computation.4 | async-start | bytes 5242880 | tf_op jit(solution)/shard_map/all_gather | solution.py:586
  7.9 28.1 %collective-permute-start = (bf16[1024,512]{1,0:T(8,128)(2,1)}, bf16[1024,512]{1,0:T(8,128)(2,1)S(1)}, u32[]{:S(2)}, u32[]{:S(2)}) collective-permute-start(bf16[1024,512]{1,0:T(8,128)(2,1)} %refs_1_.1), channel_id=1, source_target_pairs={{0,8},{4,12},{8,16},{12,20},{16,24},{20,28},{1,9},{5,13},{9,17},{1... | collective-permute-start | bytes 3145736 | tf_op jit(solution)/shard_map/ppermute | solution.py:568
  12.0 25.9 %collective-permute-start.1 = (bf16[1024,512]{1,0:T(8,128)(2,1)}, bf16[1024,512]{1,0:T(8,128)(2,1)}, u32[]{:S(2)}, u32[]{:S(2)}) collective-permute-start(bf16[1024,512]{1,0:T(8,128)(2,1)} %refs_1_.1), channel_id=1, source_target_pairs={{8,0},{12,4},{16,8},{20,12},{24,16},{28,20},{9,1},{13,5},{17,9},{2... | collective-permute-start | bytes 3145736 | tf_op jit(solution)/shard_map/ppermute | solution.py:568
  17.6 43.6 %all-to-all-start = ((bf16[8,32,16,128]{3,2,1,0:T(8,128)(2,1)}), bf16[8,32,16,128]{3,2,1,0:T(8,128)(2,1)S(1)}, u32[]{:S(2)}, u32[]{:S(2)}) async-start(bf16[8,32,16,128]{3,2,1,0:T(8,128)(2,1)} %gate.1), calls=%async_computation | async-start | bytes 2097152 | tf_op jit(solution)/shard_map/all_to_all | solution.py:559
  25.5 23.3 %copy-start.3 = (bf16[1024,512]{1,0:T(8,128)(2,1)S(1)}, bf16[1024,512]{1,0:T(8,128)(2,1)}, u32[]{:S(2)}) copy-start(bf16[1024,512]{1,0:T(8,128)(2,1)} %refs_1_.1) | copy-start | bytes 3145732
  36.0 59.0 %copy-start.4 = (bf16[1024,512]{1,0:T(8,128)(2,1)}, bf16[1024,512]{1,0:T(8,128)(2,1)S(1)}, u32[]{:S(2)}) copy-start(bf16[1024,512]{1,0:T(8,128)(2,1)S(1)} %collective-permute-done.refs_3_) | copy-start | bytes 3145732
  37.9 35.2 %collective-permute-start.2 = (bf16[1024,512]{1,0:T(8,128)(2,1)S(1)}, bf16[1024,512]{1,0:T(8,128)(2,1)}, u32[]{:S(2)}, u32[]{:S(2)}) collective-permute-start(bf16[1024,512]{1,0:T(8,128)(2,1)S(1)} %collective-permute-done.refs_3_), channel_id=1, source_target_pairs={{8,16},{12,20},{16,24},{20,28},{9,17},{13,21},{17,25},{21,29},{10,... | collective-permute-start | bytes 3145736 | tf_op jit(solution)/shard_map/ppermute | solution.py:568
  39.6 41.3 %collective-permute-start.5 = (bf16[1024,512]{1,0:T(8,128)(2,1)S(1)}, bf16[1024,512]{1,0:T(8,128)(2,1)}, u32[]{:S(2)}, u32[]{:S(2)}) collective-permute-start(bf16[1024,512]{1,0:T(8,128)(2,1)S(1)} %collective-permute-done.refs_3_), channel_id=1, source_target_pairs={{8,12},{12,8},{16,20},{20,16},{24,28},{28,24},{9,13},{13,9},{17,21... | collective-permute-start | bytes 3145736 | tf_op jit(solution)/shard_map/ppermute | solution.py:572
  41.2 39.6 %collective-permute-start.3 = (bf16[1024,512]{1,0:T(8,128)(2,1)}, bf16[1024,512]{1,0:T(8,128)(2,1)}, u32[]{:S(2)}, u32[]{:S(2)}) collective-permute-start(bf16[1024,512]{1,0:T(8,128)(2,1)} %collective-permute-done.1.refs_5_), channel_id=1, source_target_pairs={{8,0},{12,4},{16,8},{20,12},{9,1},{13,5},{17,9},{21,13},{10,2},{14... | collective-permute-start | bytes 3145736 | tf_op jit(solution)/shard_map/ppermute | solution.py:568
  42.5 38.3 %collective-permute-start.6 = (bf16[1024,512]{1,0:T(8,128)(2,1)}, bf16[1024,512]{1,0:T(8,128)(2,1)}, u32[]{:S(2)}, u32[]{:S(2)}) collective-permute-start(bf16[1024,512]{1,0:T(8,128)(2,1)} %collective-permute-done.1.refs_5_), channel_id=1, source_target_pairs={{0,4},{4,0},{8,12},{12,8},{16,20},{20,16},{1,5},{5,1},{9,13},{13,9... | collective-permute-start | bytes 3145736 | tf_op jit(solution)/shard_map/ppermute | solution.py:573
  48.7 32.1 %collective-permute-start.4 = (bf16[1024,512]{1,0:T(8,128)(2,1)S(1)}, bf16[1024,512]{1,0:T(8,128)(2,1)}, u32[]{:S(2)}, u32[]{:S(2)}) collective-permute-start(bf16[1024,512]{1,0:T(8,128)(2,1)S(1)} %copy-done.3), channel_id=1, source_target_pairs={{0,4},{4,0},{8,12},{12,8},{16,20},{20,16},{24,28},{28,24},{1,5},{5... | collective-permute-start | bytes 3145736 | tf_op jit(solution)/shard_map/ppermute | solution.py:592
  61.2 1.0 copy-start.1
  80.8 14.1 %collective-permute-start.10 = (bf16[1024,512]{1,0:T(8,128)(2,1)}, bf16[1024,512]{1,0:T(8,128)(2,1)}, u32[]{:S(2)}, u32[]{:S(2)}) collective-permute-start(bf16[1024,512]{1,0:T(8,128)(2,1)} %collective-permute-done.3.refs_9_), channel_id=1, source_target_pairs={{0,4},{4,0},{8,12},{12,8},{1,5},{5,1},{9,13},{13,9},{2,6},{6,2},{1... | collective-permute-start | bytes 3145736 | tf_op jit(solution)/shard_map/ppermute | solution.py:573
  83.2 11.8 %collective-permute-start.9 = (bf16[1024,512]{1,0:T(8,128)(2,1)}, bf16[1024,512]{1,0:T(8,128)(2,1)}, u32[]{:S(2)}, u32[]{:S(2)}) collective-permute-start(bf16[1024,512]{1,0:T(8,128)(2,1)} %collective-permute-done.2.refs_7_), channel_id=1, source_target_pairs={{16,20},{20,16},{24,28},{28,24},{17,21},{21,17},{25,29},{29,25},{1... | collective-permute-start | bytes 3145736 | tf_op jit(solution)/shard_map/ppermute | solution.py:572
  84.8 21.0 %collective-permute-start.7 = (bf16[1024,512]{1,0:T(8,128)(2,1)}, bf16[1024,512]{1,0:T(8,128)(2,1)S(1)}, u32[]{:S(2)}, u32[]{:S(2)}) collective-permute-start(bf16[1024,512]{1,0:T(8,128)(2,1)} %collective-permute-done.2.refs_7_), channel_id=1, source_target_pairs={{16,24},{20,28},{17,25},{21,29},{18,26},{22,30},{19,27},{23,31}} | collective-permute-start | bytes 3145736 | tf_op jit(solution)/shard_map/ppermute | solution.py:568
  85.6 41.1 %collective-permute-start.8 = (bf16[1024,512]{1,0:T(8,128)(2,1)}, bf16[1024,512]{1,0:T(8,128)(2,1)}, u32[]{:S(2)}, u32[]{:S(2)}) collective-permute-start(bf16[1024,512]{1,0:T(8,128)(2,1)} %collective-permute-done.3.refs_9_), channel_id=1, source_target_pairs={{8,0},{12,4},{9,1},{13,5},{10,2},{14,6},{11,3},{15,7}} | collective-permute-start | bytes 3145736 | tf_op jit(solution)/shard_map/ppermute | solution.py:568
  86.9 53.4 %all-to-all-start.1 = ((bf16[8,32,16,128]{3,2,1,0:T(8,128)(2,1)}), bf16[8,32,16,128]{3,2,1,0:T(8,128)(2,1)S(1)}, u32[]{:S(2)}, u32[]{:S(2)}) async-start(bf16[8,32,16,128]{3,2,1,0:T(8,128)(2,1)} %get-tuple-element.47), calls=%async_computation.1 | async-start | bytes 2097152 | tf_op jit(solution)/shard_map/all_to_all | solution.py:559
  105.9 26.8 %copy-start.5 = (bf16[1024,512]{1,0:T(8,128)(2,1)}, bf16[1024,512]{1,0:T(8,128)(2,1)S(1)}, u32[]{:S(2)}) copy-start(bf16[1024,512]{1,0:T(8,128)(2,1)S(1)} %collective-permute-done.7.refs_1_) | copy-start | bytes 3145732
  126.7 3.4 %collective-permute-start.11 = (bf16[1024,512]{1,0:T(8,128)(2,1)S(1)}, bf16[1024,512]{1,0:T(8,128)(2,1)S(1)}, u32[]{:S(2)}, u32[]{:S(2)}) collective-permute-start(bf16[1024,512]{1,0:T(8,128)(2,1)S(1)} %collective-permute-done.7.refs_1_), channel_id=1, source_target_pairs={{24,28},{28,24},{25,29},{29,25},{26,30},{30,26},{27,31},{31,27}} | collective-permute-start | bytes 3145736 | tf_op jit(solution)/shard_map/ppermute | solution.py:572
  127.4 5.3 %collective-permute-start.12 = (bf16[1024,512]{1,0:T(8,128)(2,1)}, bf16[1024,512]{1,0:T(8,128)(2,1)}, u32[]{:S(2)}, u32[]{:S(2)}) collective-permute-start(bf16[1024,512]{1,0:T(8,128)(2,1)} %collective-permute-done.8.refs_3_), channel_id=1, source_target_pairs={{0,4},{4,0},{1,5},{5,1},{2,6},{6,2},{3,7},{7,3}} | collective-permute-start | bytes 3145736 | tf_op jit(solution)/shard_map/ppermute | solution.py:573
  130.1 2.6 %copy-start.6 = (bf16[1024,512]{1,0:T(8,128)(2,1)}, bf16[1024,512]{1,0:T(8,128)(2,1)S(1)}, u32[]{:S(2)}) copy-start(bf16[1024,512]{1,0:T(8,128)(2,1)S(1)} %collective-permute-done.11.refs_2_) | copy-start | bytes 3145732
  140.3 41.1 %copy-start = (bf16[8,32,16,128]{3,2,1,0:T(8,128)(2,1)}, bf16[8,32,16,128]{3,2,1,0:T(8,128)(2,1)S(1)}, u32[]{:S(2)}) copy-start(bf16[8,32,16,128]{3,2,1,0:T(8,128)(2,1)S(1)} %all-to-all-done.1.refs_0_) | copy-start | bytes 3145732
  181.4 30.3 %all-to-all-start.3 = ((bf16[8,32,16,128]{3,2,1,0:T(8,128)(2,1)}), bf16[8,32,16,128]{3,2,1,0:T(8,128)(2,1)S(1)}, u32[]{:S(2)}, u32[]{:S(2)}) async-start(bf16[8,32,16,128]{3,2,1,0:T(8,128)(2,1)} %get-tuple-element.51), calls=%async_computation.3 | async-start | bytes 2097152 | tf_op jit(solution)/shard_map/all_to_all | solution.py:559
  211.7 1.0 copy-start.2
Sparse Core Ops, SparseCore 0:
  9.8 54.7 all-gather.2

commit v3 on v2

--- a/solution.py
+++ b/solution.py
@@ -131,6 +131,7 @@
 SLOT = 2 * FAST
 PAIR = 2 * SLOT
 LANES = 128
+CHIPS = 4
 F32, BF16 = jnp.float32, jnp.bfloat16
 PARAMS = pltpu.CompilerParams(vmem_limit_bytes=60 * 2**20)
 VM = pl.BlockSpec(memory_space=pltpu.VMEM)
@@ -175,7 +176,10 @@
     fwd, inv, edge_fwd, edge_inv = paired(fwd), paired(inv), fwd[half], inv[half]
     fwd[-1, :SLOT, FAST:SLOT] = edge_fwd[:, :FAST]
     inv[-1, FAST:SLOT, :SLOT] = edge_inv[:FAST]
-    return [jnp.asarray(t.astype(ml_dtypes.bfloat16)) for t in (first, fwd, inv, last)]
+    blocks = np.arange(half).reshape(2 * CHIPS, -1)
+    order = [np.concatenate([blocks[c ^ d] for d in range(2 * CHIPS)]) for c in range(2 * CHIPS)]
+    firsts, lasts = np.stack([first[:, o] for o in order]), np.stack([last[o] for o in order])
+    return [jnp.asarray(t.astype(ml_dtypes.bfloat16)) for t in (firsts, fwd, inv, lasts)]
 
 
 def dot(left, right):
@@ -245,17 +249,21 @@
     spec_ref[span(half // 2, PAIR), :] = dot(fwd_ref[half // 2], mid_ref[:PAIR, :].astype(BF16))
 
 
-def convolve_kernel(conjugate, x_ref, h_any, first_ref, fwd_any, inv_any, last_ref,
-                    out_ref, spec_any, h_ref, fwd_ref, inv_ref, spec_ref, mid_ref, back_ref, sem):
+def convolve_kernel(conjugate, count, place_ref, *refs):
+    x_refs, (h_any, first_ref, fwd_any, inv_any, last_ref) = refs[:count], refs[count : count + 5]
+    outs, (spec_any, h_ref, fwd_ref, inv_ref, spec_ref, mid_ref, back_ref, sem) = refs[count + 5 : -8], refs[-8:]
+    first_ref, last_ref = first_ref.at[0], last_ref.at[0]
     half = first_ref.shape[1]
-    groups, _, per, _ = x_ref.shape
     loads = [
         pltpu.make_async_copy(source, target, sem.at[i])
         for i, (source, target) in enumerate(((fwd_any, fwd_ref), (h_any, h_ref), (inv_any, inv_ref)))
     ]
     for load in loads:
         load.start()
-    spread(lambda a: x_ref[:, a].reshape(half, LANES), first_ref, mid_ref)
+    if count == 1:
+        spread(lambda a: x_refs[0][:, a].reshape(half, LANES), first_ref, mid_ref)
+    else:
+        spread(lambda a: jnp.concatenate([x_ref[a] for x_ref in x_refs], 0), first_ref, mid_ref)
     for load in loads:
         load.wait()
 
@@ -271,11 +279,20 @@
     store = pltpu.make_async_copy(spec_ref, spec_any, sem.at[3])
     store.start()
     back_ref[:PAIR, :] += dot(inv_ref[half // 2], times(x, h_ref[tail, :], conjugate))
-
-    def emit(a, rows):
-        out_ref[:, a] = rows.reshape(groups, per, LANES).astype(BF16)
-
-    collect(last_ref, back_ref, emit)
+    if len(outs) == 1:
+
+        def emit(a, rows):
+            outs[0][:, a] = rows.reshape(outs[0].shape[0], -1, LANES).astype(BF16)
+
+        collect(last_ref, back_ref, emit)
+    else:
+        per = half // len(outs)
+
+        def emit(a, rows):
+            for i, out_ref in enumerate(outs):
+                out_ref[a] = rows[i * per : (i + 1) * per].astype(BF16)
+
+        collect(last_ref, back_ref, emit)
     store.wait()
 
 
@@ -317,28 +334,42 @@
     )(h, first, fwd)
 
 
-def convolve(x, spec, tabs, conjugate):
-    fwd = tabs[1]
-    rows = spec.shape[0]
-    big = pltpu.VMEM((rows - PAIR, LANES), F32)
-    return pl.pallas_call(
-        functools.partial(convolve_kernel, conjugate),
-        out_shape=(sds(x.shape, BF16), sds(spec.shape, F32)),
-        in_specs=[VM, ANY, VM, ANY, ANY, VM],
-        out_specs=(VM, ANY),
-        scratch_shapes=[
-            pltpu.VMEM(spec.shape, F32),
-            pltpu.VMEM(fwd.shape, BF16),
-            pltpu.VMEM(fwd.shape, BF16),
-            pltpu.VMEM(spec.shape, F32),
-            big,
-            big,
-            pltpu.SemaphoreType.DMA((4,)),
-        ],
+def convolve(index, parts, spec, tabs, conjugate, whole):
+    first, fwd, inv, last = tabs
+    count = len(parts)
+    groups = 2 * CHIPS
+    half = last.shape[1]
+
+    def own(table):
+        return pl.BlockSpec((1,) + table.shape[1:], lambda i, index: (index[0], 0, 0))
+
+    outs = (sds((FAST, half // groups, LANES), BF16),) * groups
+    if whole:
+        outs = (sds((groups, FAST, half // groups, LANES), BF16),)
+    big = pltpu.VMEM((spec.shape[0] - PAIR, LANES), F32)
+    *out, spec = pl.pallas_call(
+        functools.partial(convolve_kernel, conjugate, count),
+        out_shape=outs + (sds(spec.shape, F32),),
+        grid_spec=pltpu.PrefetchScalarGridSpec(
+            num_scalar_prefetch=1,
+            grid=(1,),
+            in_specs=[VM] * count + [ANY, own(first), ANY, ANY, own(last)],
+            out_specs=(VM,) * len(outs) + (ANY,),
+            scratch_shapes=[
+                pltpu.VMEM(spec.shape, F32),
+                pltpu.VMEM(fwd.shape, BF16),
+                pltpu.VMEM(fwd.shape, BF16),
+                pltpu.VMEM(spec.shape, F32),
+                big,
+                big,
+                pltpu.SemaphoreType.DMA((4,)),
+            ],
+        ),
         compiler_params=PARAMS,
         cost_estimate=cost(2 * 10**9, 14 * 2**20),
         name="convolve",
-    )(x, spec, *tabs)
+    )(index, *parts, spec, *tabs)
+    return out, spec
 
 
 def filter_gradient(scaled_spec, gated_spec, tabs, scale):
@@ -390,7 +421,6 @@
 
 
 WIDE = 256
-CHIPS = 4
 
 
 def pieces_of(x_ref, piece, lane, depth):
@@ -403,7 +433,17 @@
 
 def terms_kernel(dists, place_ref, *refs):
     count = 2 * sum(1 if d == 0 else 2 for d in dists)
-    x_ref, ws, before, sum_ref = refs[0], refs[1 : 1 + count], refs[1 + count : -1], refs[-1]
+    xs, ws, sum_ref, x_ref, sem = refs[:4], refs[4 : 4 + count], refs[4 + count], refs[-2], refs[-1]
+    mine = place_ref[2]
+
+    @pl.when(pl.program_id(0) == 0)
+    def _():
+        copies = [pltpu.make_async_copy(xs[i], x_ref.at[mine ^ i], sem.at[i]) for i in range(4)]
+        for copy in copies:
+            copy.start()
+        for copy in copies:
+            copy.wait()
+
     here, core = place_ref[0], place_ref[1]
     depth = ws[0].shape[1]
 
@@ -411,8 +451,6 @@
         one = against(pieces_of(x_ref, piece, core, depth), near_ref)
         return one + against(pieces_of(x_ref, piece, 1 - core, depth), swap_ref)
 
-    if before:
-        sum_ref[...] = before[0][...]
     for d in dists:
         if d == 0:
             sum_ref[...] = part(here, ws[0], ws[1])
@@ -438,8 +476,8 @@
     return lambda j, place: (jnp.where(place[0] + d < CHIPS, j, 0), 0)
 
 
-def terms(dists, place, x, ws, *before):
-    _, rows, _ = x.shape
+def terms(dists, place, xs, ws):
+    rows, piece = xs[0].shape
     cols, depth = ws[0].shape
     maps = []
     for d in dists:
@@ -451,112 +489,179 @@
         grid_spec=pltpu.PrefetchScalarGridSpec(
             num_scalar_prefetch=1,
             grid=(cols // WIDE,),
-            in_specs=[pl.BlockSpec(x.shape, lambda j, place: (0, 0, 0))]
-            + [pl.BlockSpec((WIDE, depth), m) for m in maps]
-            + [wide] * len(before),
+            in_specs=[ANY] * 4 + [pl.BlockSpec((WIDE, depth), m) for m in maps],
             out_specs=wide,
+            scratch_shapes=[pltpu.VMEM((4, rows, piece), BF16), pltpu.SemaphoreType.DMA((4,))],
         ),
         compiler_params=PARAMS,
         cost_estimate=cost(2 * 10**9, 14 * 2**20),
         name="terms",
-    )(place, x, *ws, *before)
+    )(place, *xs, *ws)
 
 
 def late_kernel(place_ref, *refs):
-    x_ref, ws = refs[0], refs[1:5]
-    sum_ref, query_ref, mix_ref, out_ref, total_ref, hold_ref = refs[5:]
-    here, core = place_ref[0], place_ref[1]
+    xs, ws, sum_ref, query_ref, mix_ref = refs[:4], refs[4:10], refs[10], refs[11], refs[12]
+    outs, (hold_ref, x_ref, sem) = refs[13:-3], refs[-3:]
+    here, core, mine = place_ref[0], place_ref[1], place_ref[2]
+    two_ref, three_ref = x_ref.at[pl.ds(0, 1)], x_ref.at[pl.ds(1, 1)]
+
+    @pl.when(pl.program_id(0) == 0)
+    def _():
+        for start in (True, False):
+            for slot, piece in enumerate((here ^ 2, CHIPS - 1 - here)):
+                for i in range(4):
+
+                    @pl.when(mine ^ piece == i)
+                    def _():
+                        copy = pltpu.make_async_copy(xs[i], x_ref.at[slot], sem.at[slot])
+                        copy.start() if start else copy.wait()
+
+    rows = sum_ref.shape[0]
     depth = ws[0].shape[1]
-
-    def part(near_ref, swap_ref):
-        one = against(pieces_of(x_ref, 0, core, depth), near_ref)
-        return one + against(pieces_of(x_ref, 0, 1 - core, depth), swap_ref)
-
-    total_ref[...] = sum_ref[...]
-
-    @pl.when(here == CHIPS - 1)
-    def _():
-        total_ref[...] += part(ws[0], ws[1])
-
-    @pl.when(here == 0)
-    def _():
-        total_ref[...] += part(ws[2], ws[3])
-
-    mix = total_ref[...].astype(BF16)
-    mix_ref[...] = mix
-    scaled = mix.astype(F32) * query_ref[...].astype(F32)
-    for g in range(WIDE // LANES):
-
-        def emit(a, rows):
-            out_ref[g, a] = rows
-
-        permuted(scaled[:, g * LANES : (g + 1) * LANES], hold_ref, emit)
-
-
-def mix_late(place, x, ws, total, query, groups):
+    per = rows // FAST
+
+    def part(piece_ref, near_ref, swap_ref):
+        one = against(pieces_of(piece_ref, 0, core, depth), near_ref)
+        return one + against(pieces_of(piece_ref, 0, 1 - core, depth), swap_ref)
+
+    def give(total):
+        mix = total.astype(BF16)
+        mix_ref[...] = mix
+        scaled = mix.astype(F32) * query_ref[...].astype(F32)
+        for g in range(2):
+            hold_ref[g] = scaled[:, g * LANES : (g + 1) * LANES]
+
+    for place, two, last in ((0, 2, True), (1, 2, False), (2, 0, False), (3, 0, True)):
+
+        @pl.when(here == place)
+        def _():
+            total = sum_ref[...] + part(two_ref, ws[two], ws[two + 1])
+            give(total + part(three_ref, ws[4], ws[5]) if last else total)
+
+    for k in range(CHIPS):
+
+        @pl.when(pl.program_id(0) == k)
+        def _():
+            for e in range(2):
+                for a in range(FAST):
+                    outs[2 * k + e][a] = hold_ref[e ^ core, pl.ds(a, per, stride=FAST), :].astype(BF16)
+
+
+def mix_late(place, xs, ws, total, query):
     rows, cols = query.shape
     depth = ws[0].shape[1]
-    maps = [above(CHIPS - 1)] * 2 + [below(CHIPS - 1)] * 2
-    wide = pl.BlockSpec((rows, WIDE), lambda j, place: (0, j))
-    parts = pl.BlockSpec((WIDE // LANES, FAST, rows // FAST, LANES), lambda j, place: (j, 0, 0, 0))
-    return pl.pallas_call(
+
+    def block(j, place):
+        return j ^ place[0]
+
+    def above(j, place):
+        return (jnp.where(place[0] >= 2, block(j, place), 0), 0)
+
+    def below(j, place):
+        return (jnp.where(place[0] < 2, block(j, place), 0), 0)
+
+    def last(j, place):
+        return (jnp.where((place[0] == 0) | (place[0] == CHIPS - 1), block(j, place), 0), 0)
+
+    wide = pl.BlockSpec((rows, WIDE), lambda j, place: (0, block(j, place)))
+    part = pl.BlockSpec((FAST, rows // FAST, LANES), lambda j, place: (0, 0, 0))
+    grad_mix, *scaled = pl.pallas_call(
         late_kernel,
-        out_shape=(sds((rows, cols), BF16), sds((groups, FAST, rows // FAST, LANES), BF16)),
+        out_shape=(sds((rows, cols), BF16),) + (sds((FAST, rows // FAST, LANES), BF16),) * (2 * CHIPS),
         grid_spec=pltpu.PrefetchScalarGridSpec(
             num_scalar_prefetch=1,
-            grid=(cols // WIDE,),
-            in_specs=[pl.BlockSpec((1,) + x.shape[1:], lambda j, place: (jnp.where(place[0] == 0, CHIPS - 1, 0), 0, 0))]
-            + [pl.BlockSpec((WIDE, depth), m) for m in maps]
+            grid=(CHIPS,),
+            in_specs=[ANY] * 4
+            + [pl.BlockSpec((WIDE, depth), m) for m in (above, above, below, below, last, last)]
             + [wide, wide],
-            out_specs=(wide, parts),
+            out_specs=(wide,) + (part,) * (2 * CHIPS),
             scratch_shapes=[
-                pltpu.VMEM((rows, WIDE), F32),
-                pltpu.VMEM((rows, LANES), F32),
+                pltpu.VMEM((2, rows, LANES), F32),
+                pltpu.VMEM((2,) + xs[0].shape, BF16),
+                pltpu.SemaphoreType.DMA((2,)),
             ],
         ),
         compiler_params=PARAMS,
         cost_estimate=cost(10**9, 8 * 2**20),
         name="mix_late",
-    )(place, x, *ws, total, query)
-
-
-def unpermuted(part_ref, g, hold_ref):
-    per = part_ref.shape[2]
-    for a in range(FAST):
-        hold_ref[pl.ds(a, per, stride=FAST), :] = part_ref[g, a].astype(F32)
-    return hold_ref[...]
-
-
-def finish_kernel(count, *refs):
-    part_ref, factors, outs, hold_ref = refs[0], refs[1 : 1 + count], refs[1 + count : 1 + 2 * count], refs[-1]
-    for g in range(WIDE // LANES):
-        value = unpermuted(part_ref, g, hold_ref)
+    )(place, *xs, *ws, total, query)
+    return grad_mix, scaled
+
+
+def finish_kernel(count, place_ref, *refs):
+    parts, factors, outs = refs[: 2 * CHIPS], refs[2 * CHIPS : 2 * CHIPS + count], refs[2 * CHIPS + count : -1]
+    hold_ref = refs[-1]
+    core = place_ref[1]
+    per = parts[0].shape[1]
+    for k in range(CHIPS):
+
+        @pl.when(pl.program_id(0) == k)
+        def _():
+            for e in range(2):
+                for a in range(FAST):
+                    hold_ref[e ^ core, pl.ds(a, per, stride=FAST), :] = parts[2 * k + e][a].astype(F32)
+
+    for g in range(2):
         lanes = pl.ds(g * LANES, LANES)
+        value = hold_ref[g]
         for factor_ref, out_ref in zip(factors, outs):
             out_ref[:, lanes] = (value * factor_ref[:, lanes].astype(F32)).astype(BF16)
 
 
-def finish(parts, *factors):
-    _, _, per, _ = parts.shape
+def finish(place, parts, *factors):
     rows, cols = factors[0].shape
     count = len(factors)
-    wide = pl.BlockSpec((rows, WIDE), lambda j: (0, j))
-    part = pl.BlockSpec((WIDE // LANES, FAST, per, LANES), lambda j: (j, 0, 0, 0))
+    wide = pl.BlockSpec((rows, WIDE), lambda j, place: (0, j ^ place[0]))
+    part = pl.BlockSpec(parts[0].shape, lambda j, place: (0, 0, 0))
     return pl.pallas_call(
         functools.partial(finish_kernel, count),
-        grid=(cols // WIDE,),
         out_shape=(sds((rows, cols), BF16),) * count,
-        in_specs=[part] + [wide] * count,
-        out_specs=(wide,) * count,
-        scratch_shapes=[pltpu.VMEM((rows, LANES), F32)],
+        grid_spec=pltpu.PrefetchScalarGridSpec(
+            num_scalar_prefetch=1,
+            grid=(CHIPS,),
+            in_specs=[part] * (2 * CHIPS) + [wide] * count,
+            out_specs=(wide,) * count,
+            scratch_shapes=[pltpu.VMEM((2, rows, LANES), F32)],
+        ),
         compiler_params=PARAMS,
         cost_estimate=cost(10**6, (1 + 2 * count) * 2**20),
         name="finish",
-    )(parts, *factors)
+    )(place, *parts, *factors)
+
+
+def finish_whole_kernel(part_ref, factor_ref, out_ref, hold_ref):
+    per = part_ref.shape[2]
+    for g in range(2):
+        for a in range(FAST):
+            hold_ref[pl.ds(a, per, stride=FAST), :] = part_ref[g, a].astype(F32)
+        lanes = pl.ds(g * LANES, LANES)
+        out_ref[:, lanes] = (hold_ref[...] * factor_ref[:, lanes].astype(F32)).astype(BF16)
+
+
+def finish_whole(parts, factor):
+    rows, cols = factor.shape
+    wide = pl.BlockSpec((rows, WIDE), lambda j: (0, j))
+    part = pl.BlockSpec((2,) + parts.shape[1:], lambda j: (j, 0, 0, 0))
+    return pl.pallas_call(
+        finish_whole_kernel,
+        out_shape=sds((rows, cols), BF16),
+        grid=(CHIPS,),
+        in_specs=[part, wide],
+        out_specs=wide,
+        scratch_shapes=[pltpu.VMEM((rows, LANES), F32)],
+        compiler_params=PARAMS,
+        cost_estimate=cost(10**6, 3 * 2**20),
+        name="finish_whole",
+    )(parts, factor)
 
 
 def exchange(parts):
     return lax.all_to_all(parts, "ctx", split_axis=0, concat_axis=0, tiled=True)
+
+
+def scatter(parts, first=0):
+    ids = range(2 * CHIPS)
+    return [lax.ppermute(p, "ctx", [(i, i ^ (first + d)) for i in ids]) if first + d else p for d, p in enumerate(parts)]
 
 
 SWAP = [(i, i ^ 1) for i in range(2 * CHIPS)]
@@ -577,37 +682,46 @@
 def lane_body(grad_out, proj_out, query, key_in, value_in, filters):
     seq = filters.shape[1]
     groups = seq // key_in.shape[0]
-    tabs = tables(seq)
+    firsts, fwd, inv, lasts = tables(seq)
     tie = lax.optimization_barrier
     ctx = lax.axis_index("ctx")
-    place = jnp.stack([ctx // 2, ctx % 2]).astype(jnp.int32)
+    place = jnp.stack([ctx // 2, ctx % 2, lax.axis_index("mp")]).astype(jnp.int32)
+    index = ctx.astype(jnp.int32)[None]
+
+    def across(x, d):
+        return lax.ppermute(x, "mp", [(i, i ^ d) for i in range(4)])
 
     low1, high1 = hop(proj_out, proj_out, 1)
-    x = lax.all_gather(grad_out, "mp", axis=0)
+    x1, x2 = across(grad_out, 1), across(grad_out, 2)
     gated = exchange(gate(key_in, value_in, groups))
-    spec = filter_spectrum(filters, tabs)
+    spec = filter_spectrum(filters, (firsts[0], fwd))
     low1, high1, spec, own = tie((low1, high1, spec, proj_out))
 
     low2, high2 = hop(low1, high1, 2)
+    x3, _, _ = tie((grad_out, x1, x2))
+    xs = [grad_out, x1, x2, across(x3, 3)]
+    (conv,), gated_spec = convolve(index * 0, [gated], spec, (firsts, fwd, inv, lasts), False, True)
+    own, low1, high1, _ = tie((own, low1, high1, conv))
     ws = [own, lax.ppermute(own, "ctx", SWAP)] + with_swaps(low1, high1, 1)
-    conv_out, gated_spec = convolve(gated, spec, tabs, False)
-    low2, high2, conv_out, *ws = tie((low2, high2, conv_out, *ws))
-
-    low3, high3 = hop(low2, high2, 3)
-    ws += with_swaps(low2, high2, 2)
-    conv_back = exchange(conv_out)
-    total = terms((0, 1, 2), place, x, ws)
-    low3, high3, total = tie((low3, high3, total))
-
-    ws = with_swaps(low3, high3, 3)
-    grad_mix, scaled = mix_late(place, x, ws, total, query, groups)
-    scaled, conv_back = tie((scaled, conv_back))
-    scaled = exchange(scaled)
-    grad_gated, scaled_spec = convolve(scaled, spec, tabs, True)
-    grad_back = exchange(grad_gated)
-    filter_grad = filter_gradient(scaled_spec, gated_spec, tabs, 1.0 / math.sqrt(seq))
-    (grad_query,) = finish(conv_back, grad_mix)
-    grad_key, grad_value = finish(grad_back, value_in, key_in)
+    low2, high2, _ = tie((low2, high2, conv))
+
+    end = [(i, i + 2) for i in (4, 5)] + [(i, i - 2) for i in (2, 3)]
+    end_swap = [p for p in SWAP if p[0] in (0, 1, 6, 7)]
+    last = lax.ppermute(jnp.where(ctx >= CHIPS, low2, high2), "ctx", end)
+    total = terms((0, 1), place, xs, ws)
+    conv, _ = tie((conv, total))
+    conv = exchange(conv)
+    ws = with_swaps(low2, high2, 2)
+    last, _ = tie((last, total))
+    ws += [last, lax.ppermute(last, "ctx", end_swap)]
+    grad_mix, scaled = mix_late(place, xs, ws, total, query)
+    scaled = scatter(scaled)
+    *scaled, conv = tie((*scaled, conv))
+    back, scaled_spec = convolve(index, scaled, spec, (firsts, fwd, inv, lasts), True, False)
+    back = scatter(back)
+    filter_grad = filter_gradient(scaled_spec, gated_spec, (None, fwd, inv, lasts[0]), 1.0 / math.sqrt(seq))
+    grad_query = finish_whole(conv, grad_mix)
+    grad_key, grad_value = finish(place, back, value_in, key_in)
     return (grad_query, grad_key, grad_value, filter_grad)
 
 

time: 226 us -> 202 us (0.89)
  starting transfers between devices: 45.5 us -> 81.8 us
  blocking collectives: 30.2 us -> 0 us
  waiting for transfers between devices: 55.9 us -> 34.8 us
  between operations: 14.2 us -> 1.03 us
  other arithmetic: 0.67 us -> 2.93 us
    ppermute x0 -> x19, starting transfers between devices: none -> 45.3 us  [the longest x14 30 us: scatter(): lax.ppermute(p, 'ctx', [(i, i ^ first + d) for i in ids])]
    all_to_all x1 -> x0, blocking collectives: 30.2 us -> none  [exchange(): return lax.all_to_all(parts, 'ctx', split_axis=0, concat_axis=0, tiled=True)]
    ppermute x6 -> x4, waiting for transfers between devices: 30.4 us -> 0.47 us  [hop(): return (lax.ppermute(low, 'ctx', up), lax.ppermute(high, 'ctx', down))]
    ppermute x0 -> x19, waiting for transfers between devices: none -> 25.3 us  [the longest x14 11.1 us: scatter(): lax.ppermute(p, 'ctx', [(i, i ^ first + d) for i in ids])]
    all_to_all x3 -> x2, waiting for transfers between devices: 22.1 us -> 9.07 us  [exchange(): return lax.all_to_all(parts, 'ctx', split_axis=0, concat_axis=0, tiled=True)]
    ppermute x3 -> x2, starting transfers between devices: 11.3 us -> 3.86 us  [with_swaps(): lax.ppermute(high, 'ctx', [p for p in SWAP if p[0] < 2 * (CHIPS - d)])]
    pallas_call x5, Pallas kernels: 38.9 us -> 42.3 us  [the longest x2 21.9 us: convolve(): pl.pallas_call(functools.partial(convolve_kernel, conjugate, count), out_...]
    ppermute x1, starting transfers between devices: 0.08 us -> 3.27 us  [lane_body(): ws = [own, lax.ppermute(own, 'ctx', SWAP)] + with_swaps(low1, high1, 1)]
  transfers between devices with their start and end apart: 17 -> 30, of which waited for: 6 -> 8; matrix products, arithmetic and copies ran while one was open for 0% -> 1% of each run, Pallas kernels for 27% -> 30%
where the time goes in v3:
time: 202 us; the launch traced here: 201 us
  starting transfers between devices  81.8 us (40%)
  Pallas kernels  78.1 us (39%)
  waiting for transfers between devices  34.8 us (17%)
  other arithmetic  2.93 us (1%)
  local copies, waits for them, and re-layouts  2.79 us (1%)
    ppermute x14, starting transfers between devices, scatter(): lax.ppermute(p, 'ctx', [(i, i ^ first + d) for i in ids])  30 us
    pallas_call x2, Pallas kernels, convolve(): pl.pallas_call(functools.partial(convolve_kernel, conjugate, count), out_...  21.9 us
    all_to_all x2, starting transfers between devices, exchange(): return lax.all_to_all(parts, 'ctx', split_axis=0, concat_axis=0, tiled=True)  18.6 us
    pallas_call x1, Pallas kernels, filter_gradient(): pl.pallas_call(functools.partial(gradient_kernel, scale), out_shape=sds((...  11.5 us
    ppermute x14, waiting for transfers between devices, scatter(): lax.ppermute(p, 'ctx', [(i, i ^ first + d) for i in ids])  11.1 us
    pallas_call x1, Pallas kernels, filter_spectrum(): pl.pallas_call(filter_kernel, out_shape=sds((2 * seq + PAIR, LANES), F32)...  10.5 us
    ppermute x1, starting transfers between devices, lane_body(): ws += [last, lax.ppermute(last, 'ctx', end_swap)]  10.2 us
    pallas_call x1, Pallas kernels, mix_late(): pl.pallas_call(late_kernel, out_shape=(sds((rows, cols), BF16),) + (sds((...  10.1 us
  transfers between devices with their start and end apart: 30, of which 8 were waited for; matrix products, arithmetic and copies ran while one was open for 1% of the time, Pallas kernels for 30%

profile of v3, /device:TPU:1, one launch (start us, length us, event | category | flops | bytes accessed | tf_op | source)
XLA Modules:
  0.0 201.5 jit_solution(9564832216731618611)
XLA Ops:
  0.6 0.0 copy-start.1
  0.6 5.1 %collective-permute-start.3 = (bf16[1024,512]{1,0:T(8,128)(2,1)}, bf16[1024,512]{1,0:T(8,128)(2,1)}, u32[]{:S(2)}, u32[]{:S(2)}) collective-permute-start(bf16[1024,512]{1,0:T(8,128)(2,1)} %refs_4_.1), channel_id=1, source_target_pairs={{0,8},{4,12},{8,16},{12,20},{16,24},{20,28},{1,9},{5,13},{9,17},{1... | collective-permute-start | bytes 3145736 | tf_op jit(solution)/shard_map/ppermute | solution.py:673
  5.8 1.3 collective-permute-start.4
  7.1 4.3 %gate.1 = bf16[8,32,16,128]{3,2,1,0:T(8,128)(2,1)} custom-call(bf16[512,1024]{1,0:T(8,128)(2,1)} %refs_9_.2, bf16[512,1024]{1,0:T(8,128)(2,1)} %refs_8_.1), custom_call_target="tpu_custom_call" | custom-call | flops 1 | bytes 3145 | tf_op jit(solution)/shard_map/gate/pallas_call | solution.py:410
  11.4 6.9 %all-to-all-start = ((bf16[8,32,16,128]{3,2,1,0:T(8,128)(2,1)}), bf16[8,32,16,128]{3,2,1,0:T(8,128)(2,1)}, u32[]{:S(2)}, u32[]{:S(2)}) async-start(bf16[8,32,16,128]{3,2,1,0:T(8,128)(2,1)} %gate.1), calls=%async_computation | async-start | bytes 2097152 | tf_op jit(solution)/shard_map/all_to_all | solution.py:659
  18.3 1.2 collective-permute-start
  19.5 1.2 collective-permute-start.1
  20.7 10.5 %filter_spectrum.1.refs_1_.refs_8_ = f32[8320,128]{1,0:T(8,128)} custom-call(f32[128,4096]{1,0:T(8,128)} %h_ref.1, bf16[256,128]{1,0:T(8,128)(2,1)} %constant.50.first_ref, bf16[65,128,128]{2,1,0:T(8,128)(2,1)} %constant.46.clone.fwd_ref.refs_3_.refs_10_), custom_call_target="tpu_custom_call" | custom-call | flops 1000 | bytes 8388 | tf_op jit(solution)/shard_map/filter_spectrum/pallas_call | solution.py:325
  31.2 0.5 collective-permute-done.4.refs_8_
  31.7 1.6 collective-permute-start.5
  33.3 1.3 collective-permute-start.6
  34.6 8.5 %collective-permute-done.refs_1_ = bf16[512,1024]{1,0:T(8,128)(2,1)S(1)} collective-permute-done((bf16[512,1024]{1,0:T(8,128)(2,1)S(1)}, bf16[512,1024]{1,0:T(8,128)(2,1)S(1)}, u32[]{:S(2)}, u32[]{:S(2)}) %collective-permute-start) | collective-permute-done | bytes 1048608 | tf_op jit(solution)/shard_map/ppermute | solution.py:692
  43.1 0.9 collective-permute-done.1.refs_2_
  44.0 1.3 collective-permute-start.2
  45.3 9.1 %all-to-all-done.refs_0_ = bf16[8,32,16,128]{3,2,1,0:T(8,128)(2,1)} async-done(((bf16[8,32,16,128]{3,2,1,0:T(8,128)(2,1)}), bf16[8,32,16,128]{3,2,1,0:T(8,128)(2,1)}, u32[]{:S(2)}, u32[]{:S(2)}) %all-to-all-start) | async-done | bytes 1048608 | tf_op jit(solution)/shard_map/all_to_all | solution.py:659
  54.4 10.9 %convolve.2 = (bf16[8,32,16,128]{3,2,1,0:T(8,128)(2,1)}, f32[8320,128]{1,0:T(8,128)}) custom-call(s32[1]{0:T(128)} %constant.43.clone.1.place_ref, bf16[8,32,16,128]{3,2,1,0:T(8,128)(2,1)} %all-to-all-done.refs_0_, f32[8320,128]{1,0:T(8,128)} %filter_spectrum.1.refs_1_.refs_8_, bf16[8,256,128]{2,1,0:T(8,128)(2,1)} %constant.45.clone.refs_2_.refs_9_, ...), custom_call_target="tpu_custom_call" | custom-call | flops 2000 | bytes 14680 | tf_op jit(solution)/shard_map/convolve/pallas_call | solution.py:350
  65.4 3.3 %collective-permute-start.10 = (bf16[1024,512]{1,0:T(8,128)(2,1)}, bf16[1024,512]{1,0:T(8,128)(2,1)S(1)}, u32[]{:S(2)}, u32[]{:S(2)}) collective-permute-start(bf16[1024,512]{1,0:T(8,128)(2,1)} %refs_4_.1), channel_id=1, source_target_pairs={{0,4},{4,0},{8,12},{12,8},{16,20},{20,16},{24,28},{28,24},{1,5},{5... | collective-permute-start | bytes 3145736 | tf_op jit(solution)/shard_map/ppermute | solution.py:705
  68.6 0.7 collective-permute-start.11
  69.4 1.9 collective-permute-start.12
  71.3 0.0 collective-permute-done.6.refs_6_
  71.3 2.3 %broadcast_select_fusion = bf16[1024,512]{1,0:T(8,128)(2,1)} fusion(bf16[1024,512]{1,0:T(8,128)(2,1)} %collective-permute-done.5.refs_4_, bf16[1024,512]{1,0:T(8,128)(2,1)} %collective-permute-done.6.refs_6_, pred[]{:T(512)S(6)} %ge.3), kind=kLoop, calls=%fused_computation | loop fusion | flops 524288 | bytes 3145729 | tf_op jit(solution)/shard_map/jit(_where)/select_n | solution.py:710
  73.7 1.3 collective-permute-start.9
  75.0 0.6 pad_add_fusion.place_ref
  75.6 0.0 collective-permute-done.10.refs_5_
  75.6 0.0 collective-permute-done.11.refs_7_
  75.6 0.0 collective-permute-done.12.refs_9_
  75.6 1.0 copy-done.4
  76.6 0.3 copy-done.5
  76.9 9.6 %terms.1.refs_10_ = f32[512,1024]{1,0:T(8,128)} custom-call(s32[3]{0:T(128)} %pad_add_fusion.place_ref, bf16[512,1024]{1,0:T(8,128)(2,1)} %refs_0_.3, bf16[512,1024]{1,0:T(8,128)(2,1)} %copy-done.2, bf16[512,1024]{1,0:T(8,128)(2,1)} %copy-done.3, bf16[512,1024]{1,0:T(8,128)(2,1)} %collective-permute-done.2.refs_3_, bf16[1024,512]{1,0:T(8,128)(2,1)} %refs_4_.1, ...), custom_call_target="tpu_custom_call" | custom-call | flops 2000 | bytes 14680 | tf_op jit(solution)/shard_map/terms/pallas_call | solution.py:486
  86.5 11.7 %all-to-all-start.1 = ((bf16[8,32,16,128]{3,2,1,0:T(8,128)(2,1)}), bf16[8,32,16,128]{3,2,1,0:T(8,128)(2,1)S(1)}, u32[]{:S(2)}, u32[]{:S(2)}) async-start(bf16[8,32,16,128]{3,2,1,0:T(8,128)(2,1)} %get-tuple-element.67), calls=%async_computation.1 | async-start | bytes 2097152 | tf_op jit(solution)/shard_map/all_to_all | solution.py:659
  98.2 0.7 collective-permute-start.7
  98.9 1.9 collective-permute-start.8
  100.9 2.4 %collective-permute-done.9.refs_8_ = bf16[1024,512]{1,0:T(8,128)(2,1)} collective-permute-done((bf16[1024,512]{1,0:T(8,128)(2,1)}, bf16[1024,512]{1,0:T(8,128)(2,1)}, u32[]{:S(2)}, u32[]{:S(2)}) %collective-permute-start.9) | collective-permute-done | bytes 1048608 | tf_op jit(solution)/shard_map/ppermute | solution.py:710
  103.3 10.2 %collective-permute-start.13 = (bf16[1024,512]{1,0:T(8,128)(2,1)}, bf16[1024,512]{1,0:T(8,128)(2,1)}, u32[]{:S(2)}, u32[]{:S(2)}) collective-permute-start(bf16[1024,512]{1,0:T(8,128)(2,1)} %collective-permute-done.9.refs_8_), channel_id=1, source_target_pairs={{0,4},{4,0},{24,28},{28,24},{1,5},{5,1},{25,29},{29,25},{2,6},{6,2... | collective-permute-start | bytes 3145736 | tf_op jit(solution)/shard_map/ppermute | solution.py:716
  113.5 0.0 collective-permute-done.7.refs_5_
  113.5 2.4 %collective-permute-done.13.refs_9_ = bf16[1024,512]{1,0:T(8,128)(2,1)} collective-permute-done((bf16[1024,512]{1,0:T(8,128)(2,1)}, bf16[1024,512]{1,0:T(8,128)(2,1)}, u32[]{:S(2)}, u32[]{:S(2)}) %collective-permute-start.13) | collective-permute-done | bytes 1048608 | tf_op jit(solution)/shard_map/ppermute | solution.py:716
  115.9 10.1 %mix_late.1 = (bf16[512,1024]{1,0:T(8,128)(2,1)}, bf16[32,16,128]{2,1,0:T(8,128)(2,1)}, bf16[32,16,128]{2,1,0:T(8,128)(2,1)}, bf16[32,16,128]{2,1,0:T(8,128)(2,1...) custom-call(s32[3]{0:T(128)} %pad_add_fusion.place_ref, ...), custom_call_target="tpu_custom_call" | custom-call | flops 1000 | bytes 8388 | tf_op jit(solution)/shard_map/mix_late/pallas_call | solution.py:568
  126.0 0.4 collective-permute-start.14
  126.5 1.8 collective-permute-start.16
  128.3 2.2 %collective-permute-start.17 = (bf16[32,16,128]{2,1,0:T(8,128)(2,1)}, bf16[32,16,128]{2,1,0:T(8,128)(2,1)S(1)}, u32[]{:S(2)}, u32[]{:S(2)}) collective-permute-start(bf16[32,16,128]{2,1,0:T(8,128)(2,1)} %get-tuple-element.63), channel_id=1, source_target_pairs={{0,16},{4,20},{8,24},{12,28},{16,0},{20,4},{24,8},{28,12},{1,17},{... | collective-permute-start | bytes 393224 | tf_op jit(solution)/shard_map/ppermute | solution.py:664
  130.5 0.4 collective-permute-start.18
  130.8 3.7 %collective-permute-start.19 = (bf16[32,16,128]{2,1,0:T(8,128)(2,1)}, bf16[32,16,128]{2,1,0:T(8,128)(2,1)S(1)}, u32[]{:S(2)}, u32[]{:S(2)}) collective-permute-start(bf16[32,16,128]{2,1,0:T(8,128)(2,1)} %get-tuple-element.65), channel_id=1, source_target_pairs={{0,24},{4,28},{8,16},{12,20},{16,8},{20,12},{24,0},{28,4},{1,25},{... | collective-permute-start | bytes 393224 | tf_op jit(solution)/shard_map/ppermute | solution.py:664
  134.5 3.3 %collective-permute-start.20 = (bf16[32,16,128]{2,1,0:T(8,128)(2,1)}, bf16[32,16,128]{2,1,0:T(8,128)(2,1)S(1)}, u32[]{:S(2)}, u32[]{:S(2)}) collective-permute-start(bf16[32,16,128]{2,1,0:T(8,128)(2,1)} %get-tuple-element.66), channel_id=1, source_target_pairs={{0,28},{4,24},{8,20},{12,16},{16,12},{20,8},{24,4},{28,0},{1,29},{... | collective-permute-start | bytes 393224 | tf_op jit(solution)/shard_map/ppermute | solution.py:664
  137.8 2.3 %collective-permute-done.16.refs_3_ = bf16[32,16,128]{2,1,0:T(8,128)(2,1)S(1)} collective-permute-done((bf16[32,16,128]{2,1,0:T(8,128)(2,1)}, bf16[32,16,128]{2,1,0:T(8,128)(2,1)S(1)}, u32[]{:S(2)}, u32[]{:S(2)}) %collective-permute-start.16) | collective-permute-done | bytes 131104 | tf_op jit(solution)/shard_map/ppermute | solution.py:664
  140.2 8.8 %collective-permute-done.18.refs_5_ = bf16[32,16,128]{2,1,0:T(8,128)(2,1)S(1)} collective-permute-done((bf16[32,16,128]{2,1,0:T(8,128)(2,1)}, bf16[32,16,128]{2,1,0:T(8,128)(2,1)S(1)}, u32[]{:S(2)}, u32[]{:S(2)}) %collective-permute-start.18) | collective-permute-done | bytes 131104 | tf_op jit(solution)/shard_map/ppermute | solution.py:664
  149.0 0.0 copy-start
  149.0 0.6 copy-done.12
  149.6 0.0 copy-done.13
  149.6 0.0 copy-done.14
  149.7 11.0 %convolve.3 = (bf16[32,16,128]{2,1,0:T(8,128)(2,1)}, bf16[32,16,128]{2,1,0:T(8,128)(2,1)}, bf16[32,16,128]{2,1,0:T(8,128)(2,1)}, bf16[32,16,128]{2,1,0:T(8,128)(...) custom-call(s32[1]{0:T(128)} %bitcast.3.place_ref, ...), custom_call_target="tpu_custom_call" | custom-call | flops 2000 | bytes 14680 | tf_op jit(solution)/shard_map/convolve/pallas_call | solution.py:350
  160.7 0.5 collective-permute-start.21
  161.1 6.5 %collective-permute-start.22 = (bf16[32,16,128]{2,1,0:T(8,128)(2,1)}, bf16[32,16,128]{2,1,0:T(8,128)(2,1)S(1)}, u32[]{:S(2)}, u32[]{:S(2)}) collective-permute-start(bf16[32,16,128]{2,1,0:T(8,128)(2,1)} %get-tuple-element.80), channel_id=1, source_target_pairs={{0,8},{4,12},{8,0},{12,4},{16,24},{20,28},{24,16},{28,20},{1,9},{5... | collective-permute-start | bytes 393224 | tf_op jit(solution)/shard_map/ppermute | solution.py:664
  167.6 0.0 collective-permute-start.23
  167.6 3.2 %collective-permute-start.24 = (bf16[32,16,128]{2,1,0:T(8,128)(2,1)}, bf16[32,16,128]{2,1,0:T(8,128)(2,1)S(1)}, u32[]{:S(2)}, u32[]{:S(2)}) collective-permute-start(bf16[32,16,128]{2,1,0:T(8,128)(2,1)} %get-tuple-element.82), channel_id=1, source_target_pairs={{0,16},{4,20},{8,24},{12,28},{16,0},{20,4},{24,8},{28,12},{1,17},{... | collective-permute-start | bytes 393224 | tf_op jit(solution)/shard_map/ppermute | solution.py:664
  170.9 2.4 %collective-permute-start.26 = (bf16[32,16,128]{2,1,0:T(8,128)(2,1)}, bf16[32,16,128]{2,1,0:T(8,128)(2,1)S(1)}, u32[]{:S(2)}, u32[]{:S(2)}) collective-permute-start(bf16[32,16,128]{2,1,0:T(8,128)(2,1)} %get-tuple-element.84), channel_id=1, source_target_pairs={{0,24},{4,28},{8,16},{12,20},{16,8},{20,12},{24,0},{28,4},{1,25},{... | collective-permute-start | bytes 393224 | tf_op jit(solution)/shard_map/ppermute | solution.py:664
  173.2 5.7 %collective-permute-start.27 = (bf16[32,16,128]{2,1,0:T(8,128)(2,1)}, bf16[32,16,128]{2,1,0:T(8,128)(2,1)S(1)}, u32[]{:S(2)}, u32[]{:S(2)}) collective-permute-start(bf16[32,16,128]{2,1,0:T(8,128)(2,1)} %get-tuple-element.85), channel_id=1, source_target_pairs={{0,28},{4,24},{8,20},{12,16},{16,12},{20,8},{24,4},{28,0},{1,29},{... | collective-permute-start | bytes 393224 | tf_op jit(solution)/shard_map/ppermute | solution.py:664
  178.9 4.5 %finish_whole.1 = bf16[512,1024]{1,0:T(8,128)(2,1)} custom-call(bf16[8,32,16,128]{3,2,1,0:T(8,128)(2,1)} %copy-done, bf16[512,1024]{1,0:T(8,128)(2,1)} %get-tuple-element.69.factor_ref), custom_call_target="tpu_custom_call" | custom-call | flops 1 | bytes 3145 | tf_op jit(solution)/shard_map/finish_whole/pallas_call | solution.py:645
  183.4 11.5 %filter_gradient.1 = f32[128,4096]{1,0:T(8,128)} custom-call(f32[8320,128]{1,0:T(8,128)} %get-tuple-element.88.s_ref, f32[8320,128]{1,0:T(8,128)} %get-tuple-element.89.g_ref, bf16[65,128,128]{2,1,0:T(8,128)(2,1)} %constant.47.clone.refs_4_.refs_11_.inv_ref, bf16[128,256]{1,0:T(8,128)(2,1)} %constant.52.last_ref), custom_call_target="tpu_custom_call" | custom-call | flops 1000 | bytes 12582 | tf_op jit(solution)/shard_map/filter_gradient/pallas_call | solution.py:378
  195.0 0.6 copy-done.17
  195.5 0.0 copy-done.18
  195.6 0.1 copy-done.19
  195.6 0.0 copy-done.20
  195.7 0.1 copy-done.21
  195.7 5.7 %finish.1 = (bf16[512,1024]{1,0:T(8,128)(2,1)}, bf16[512,1024]{1,0:T(8,128)(2,1)}) custom-call(s32[3]{0:T(128)} %pad_add_fusion.place_ref, bf16[32,16,128]{2,1,0:T(8,128)(2,1)} %get-tuple-element.78.refs_0_, bf16[32,16,128]{2,1,0:T(8,128)(2,1)} %copy-done.15, bf16[32,16,128]{2,1,0:T(8,128)(2,1)} %copy-done.16, bf16[32,16,128]{2,1,0:T(8,128)(2,1)} %copy-done.17, ...), custom_call_target="tpu_custom_call" | custom-call | flops 1 | bytes 5242 | tf_op jit(solution)/shard_map/finish/pallas_call | solution.py:616
  (51 shorter events, 0.1 us)
Async XLA Ops:
  0.6 17.7 %copy-start.1 = (bf16[512,1024]{1,0:T(8,128)(2,1)S(1)}, bf16[512,1024]{1,0:T(8,128)(2,1)}, u32[]{:S(2)}) copy-start(bf16[512,1024]{1,0:T(8,128)(2,1)} %refs_0_.3) | copy-start | bytes 3145732
  0.6 30.6 %collective-permute-start.3 = (bf16[1024,512]{1,0:T(8,128)(2,1)}, bf16[1024,512]{1,0:T(8,128)(2,1)}, u32[]{:S(2)}, u32[]{:S(2)}) collective-permute-start(bf16[1024,512]{1,0:T(8,128)(2,1)} %refs_4_.1), channel_id=1, source_target_pairs={{0,8},{4,12},{8,16},{12,20},{16,24},{20,28},{1,9},{5,13},{9,17},{1... | collective-permute-start | bytes 3145736 | tf_op jit(solution)/shard_map/ppermute | solution.py:673
  5.8 25.9 %collective-permute-start.4 = (bf16[1024,512]{1,0:T(8,128)(2,1)}, bf16[1024,512]{1,0:T(8,128)(2,1)}, u32[]{:S(2)}, u32[]{:S(2)}) collective-permute-start(bf16[1024,512]{1,0:T(8,128)(2,1)} %refs_4_.1), channel_id=1, source_target_pairs={{8,0},{12,4},{16,8},{20,12},{24,16},{28,20},{9,1},{13,5},{17,9},{2... | collective-permute-start | bytes 3145736 | tf_op jit(solution)/shard_map/ppermute | solution.py:673
  11.4 43.0 %all-to-all-start = ((bf16[8,32,16,128]{3,2,1,0:T(8,128)(2,1)}), bf16[8,32,16,128]{3,2,1,0:T(8,128)(2,1)}, u32[]{:S(2)}, u32[]{:S(2)}) async-start(bf16[8,32,16,128]{3,2,1,0:T(8,128)(2,1)} %gate.1), calls=%async_computation | async-start | bytes 2097152 | tf_op jit(solution)/shard_map/all_to_all | solution.py:659
  18.3 24.8 %collective-permute-start = (bf16[512,1024]{1,0:T(8,128)(2,1)S(1)}, bf16[512,1024]{1,0:T(8,128)(2,1)S(1)}, u32[]{:S(2)}, u32[]{:S(2)}) collective-permute-start(bf16[512,1024]{1,0:T(8,128)(2,1)S(1)} %copy-done.1), channel_id=1, source_target_pairs={{0,1},{1,0},{2,3},{3,2},{4,5},{5,4},{6,7},{7,6},{8,9},{9,8},{10,11... | collective-permute-start | bytes 3145736 | tf_op jit(solution)/shard_map/ppermute | solution.py:692
  19.5 24.5 %collective-permute-start.1 = (bf16[512,1024]{1,0:T(8,128)(2,1)S(1)}, bf16[512,1024]{1,0:T(8,128)(2,1)S(1)}, u32[]{:S(2)}, u32[]{:S(2)}) collective-permute-start(bf16[512,1024]{1,0:T(8,128)(2,1)S(1)} %copy-done.1), channel_id=1, source_target_pairs={{0,2},{1,3},{2,0},{3,1},{4,6},{5,7},{6,4},{7,5},{8,10},{9,11},{10,... | collective-permute-start | bytes 3145736 | tf_op jit(solution)/shard_map/ppermute | solution.py:692
  31.7 37.7 %collective-permute-start.5 = (bf16[1024,512]{1,0:T(8,128)(2,1)}, bf16[1024,512]{1,0:T(8,128)(2,1)}, u32[]{:S(2)}, u32[]{:S(2)}) collective-permute-start(bf16[1024,512]{1,0:T(8,128)(2,1)} %collective-permute-done.3.refs_6_), channel_id=1, source_target_pairs={{8,16},{12,20},{16,24},{20,28},{9,17},{13,21},{17,25},{21,29},{10,... | collective-permute-start | bytes 3145736 | tf_op jit(solution)/shard_map/ppermute | solution.py:673
  33.3 38.0 %collective-permute-start.6 = (bf16[1024,512]{1,0:T(8,128)(2,1)}, bf16[1024,512]{1,0:T(8,128)(2,1)}, u32[]{:S(2)}, u32[]{:S(2)}) collective-permute-start(bf16[1024,512]{1,0:T(8,128)(2,1)} %collective-permute-done.4.refs_8_), channel_id=1, source_target_pairs={{8,0},{12,4},{16,8},{20,12},{9,1},{13,5},{17,9},{21,13},{10,2},{14... | collective-permute-start | bytes 3145736 | tf_op jit(solution)/shard_map/ppermute | solution.py:673
  43.1 22.2 %copy-start.2 = (bf16[512,1024]{1,0:T(8,128)(2,1)}, bf16[512,1024]{1,0:T(8,128)(2,1)S(1)}, u32[]{:S(2)}) copy-start(bf16[512,1024]{1,0:T(8,128)(2,1)S(1)} %collective-permute-done.refs_1_) | copy-start | bytes 3145732
  44.0 21.4 %copy-start.3 = (bf16[512,1024]{1,0:T(8,128)(2,1)}, bf16[512,1024]{1,0:T(8,128)(2,1)S(1)}, u32[]{:S(2)}) copy-start(bf16[512,1024]{1,0:T(8,128)(2,1)S(1)} %collective-permute-done.1.refs_2_) | copy-start | bytes 3145732
  44.0 31.6 %collective-permute-start.2 = (bf16[512,1024]{1,0:T(8,128)(2,1)S(1)}, bf16[512,1024]{1,0:T(8,128)(2,1)}, u32[]{:S(2)}, u32[]{:S(2)}) collective-permute-start(bf16[512,1024]{1,0:T(8,128)(2,1)S(1)} %copy-done.1), channel_id=1, source_target_pairs={{0,3},{1,2},{2,1},{3,0},{4,7},{5,6},{6,5},{7,4},{8,11},{9,10},{10,... | collective-permute-start | bytes 3145736 | tf_op jit(solution)/shard_map/ppermute | solution.py:692
  65.4 10.2 %collective-permute-start.10 = (bf16[1024,512]{1,0:T(8,128)(2,1)}, bf16[1024,512]{1,0:T(8,128)(2,1)S(1)}, u32[]{:S(2)}, u32[]{:S(2)}) collective-permute-start(bf16[1024,512]{1,0:T(8,128)(2,1)} %refs_4_.1), channel_id=1, source_target_pairs={{0,4},{4,0},{8,12},{12,8},{16,20},{20,16},{24,28},{28,24},{1,5},{5... | collective-permute-start | bytes 3145736 | tf_op jit(solution)/shard_map/ppermute | solution.py:705
  68.6 6.9 %collective-permute-start.11 = (bf16[1024,512]{1,0:T(8,128)(2,1)}, bf16[1024,512]{1,0:T(8,128)(2,1)S(1)}, u32[]{:S(2)}, u32[]{:S(2)}) collective-permute-start(bf16[1024,512]{1,0:T(8,128)(2,1)} %collective-permute-done.3.refs_6_), channel_id=1, source_target_pairs={{8,12},{12,8},{16,20},{20,16},{24,28},{28,24},{9,13},{13,9},{17,21... | collective-permute-start | bytes 3145736 | tf_op jit(solution)/shard_map/ppermute | solution.py:677
  69.4 6.2 %collective-permute-start.12 = (bf16[1024,512]{1,0:T(8,128)(2,1)}, bf16[1024,512]{1,0:T(8,128)(2,1)}, u32[]{:S(2)}, u32[]{:S(2)}) collective-permute-start(bf16[1024,512]{1,0:T(8,128)(2,1)} %collective-permute-done.4.refs_8_), channel_id=1, source_target_pairs={{0,4},{4,0},{8,12},{12,8},{16,20},{20,16},{1,5},{5,1},{9,13},{13,9... | collective-permute-start | bytes 3145736 | tf_op jit(solution)/shard_map/ppermute | solution.py:678
  73.7 29.6 %collective-permute-start.9 = (bf16[1024,512]{1,0:T(8,128)(2,1)}, bf16[1024,512]{1,0:T(8,128)(2,1)}, u32[]{:S(2)}, u32[]{:S(2)}) collective-permute-start(bf16[1024,512]{1,0:T(8,128)(2,1)} %broadcast_select_fusion), channel_id=1, source_target_pairs={{16,24},{20,28},{8,0},{12,4},{17,25},{21,29},{9,1},{13,5},{18,26},... | collective-permute-start | bytes 3145736 | tf_op jit(solution)/shard_map/ppermute | solution.py:710
  75.6 1.0 copy-start.4
  75.6 1.3 copy-start.5
  86.5 62.5 %all-to-all-start.1 = ((bf16[8,32,16,128]{3,2,1,0:T(8,128)(2,1)}), bf16[8,32,16,128]{3,2,1,0:T(8,128)(2,1)S(1)}, u32[]{:S(2)}, u32[]{:S(2)}) async-start(bf16[8,32,16,128]{3,2,1,0:T(8,128)(2,1)} %get-tuple-element.67), calls=%async_computation.1 | async-start | bytes 2097152 | tf_op jit(solution)/shard_map/all_to_all | solution.py:659
  98.2 15.2 %collective-permute-start.7 = (bf16[1024,512]{1,0:T(8,128)(2,1)}, bf16[1024,512]{1,0:T(8,128)(2,1)S(1)}, u32[]{:S(2)}, u32[]{:S(2)}) collective-permute-start(bf16[1024,512]{1,0:T(8,128)(2,1)} %collective-permute-done.5.refs_4_), channel_id=1, source_target_pairs={{16,20},{20,16},{24,28},{28,24},{17,21},{21,17},{25,29},{29,25},{1... | collective-permute-start | bytes 3145736 | tf_op jit(solution)/shard_map/ppermute | solution.py:677
  98.9 14.5 %collective-permute-start.8 = (bf16[1024,512]{1,0:T(8,128)(2,1)}, bf16[1024,512]{1,0:T(8,128)(2,1)S(1)}, u32[]{:S(2)}, u32[]{:S(2)}) collective-permute-start(bf16[1024,512]{1,0:T(8,128)(2,1)} %collective-permute-done.6.refs_6_), channel_id=1, source_target_pairs={{0,4},{4,0},{8,12},{12,8},{1,5},{5,1},{9,13},{13,9},{2,6},{6,2},{1... | collective-permute-start | bytes 3145736 | tf_op jit(solution)/shard_map/ppermute | solution.py:678
  103.3 12.6 %collective-permute-start.13 = (bf16[1024,512]{1,0:T(8,128)(2,1)}, bf16[1024,512]{1,0:T(8,128)(2,1)}, u32[]{:S(2)}, u32[]{:S(2)}) collective-permute-start(bf16[1024,512]{1,0:T(8,128)(2,1)} %collective-permute-done.9.refs_8_), channel_id=1, source_target_pairs={{0,4},{4,0},{24,28},{28,24},{1,5},{5,1},{25,29},{29,25},{2,6},{6,2... | collective-permute-start | bytes 3145736 | tf_op jit(solution)/shard_map/ppermute | solution.py:716
  113.5 2.4 %copy-start.6 = (bf16[1024,512]{1,0:T(8,128)(2,1)}, bf16[1024,512]{1,0:T(8,128)(2,1)S(1)}, u32[]{:S(2)}) copy-start(bf16[1024,512]{1,0:T(8,128)(2,1)S(1)} %collective-permute-done.7.refs_5_) | copy-start | bytes 3145732
  113.5 2.4 %copy-start.7 = (bf16[1024,512]{1,0:T(8,128)(2,1)}, bf16[1024,512]{1,0:T(8,128)(2,1)S(1)}, u32[]{:S(2)}) copy-start(bf16[1024,512]{1,0:T(8,128)(2,1)S(1)} %collective-permute-done.8.refs_7_) | copy-start | bytes 3145732
  126.0 4.8 %collective-permute-start.14 = (bf16[32,16,128]{2,1,0:T(8,128)(2,1)}, bf16[32,16,128]{2,1,0:T(8,128)(2,1)S(1)}, u32[]{:S(2)}, u32[]{:S(2)}) collective-permute-start(bf16[32,16,128]{2,1,0:T(8,128)(2,1)} %get-tuple-element.60), channel_id=1, source_target_pairs={{0,4},{4,0},{8,12},{12,8},{16,20},{20,16},{24,28},{28,24},{1,5},{5... | collective-permute-start | bytes 393224 | tf_op jit(solution)/shard_map/ppermute | solution.py:664
  126.5 8.1 %collective-permute-start.15 = (bf16[32,16,128]{2,1,0:T(8,128)(2,1)}, bf16[32,16,128]{2,1,0:T(8,128)(2,1)S(1)}, u32[]{:S(2)}, u32[]{:S(2)}) collective-permute-start(bf16[32,16,128]{2,1,0:T(8,128)(2,1)} %get-tuple-element.61), channel_id=1, source_target_pairs={{0,8},{4,12},{8,0},{12,4},{16,24},{20,28},{24,16},{28,20},{1,9},{5... | collective-permute-start | bytes 393224 | tf_op jit(solution)/shard_map/ppermute | solution.py:664
  126.5 13.7 %collective-permute-start.16 = (bf16[32,16,128]{2,1,0:T(8,128)(2,1)}, bf16[32,16,128]{2,1,0:T(8,128)(2,1)S(1)}, u32[]{:S(2)}, u32[]{:S(2)}) collective-permute-start(bf16[32,16,128]{2,1,0:T(8,128)(2,1)} %get-tuple-element.62), channel_id=1, source_target_pairs={{0,12},{4,8},{8,4},{12,0},{16,28},{20,24},{24,20},{28,16},{1,13},{... | collective-permute-start | bytes 393224 | tf_op jit(solution)/shard_map/ppermute | solution.py:664
  128.3 11.9 %collective-permute-start.17 = (bf16[32,16,128]{2,1,0:T(8,128)(2,1)}, bf16[32,16,128]{2,1,0:T(8,128)(2,1)S(1)}, u32[]{:S(2)}, u32[]{:S(2)}) collective-permute-start(bf16[32,16,128]{2,1,0:T(8,128)(2,1)} %get-tuple-element.63), channel_id=1, source_target_pairs={{0,16},{4,20},{8,24},{12,28},{16,0},{20,4},{24,8},{28,12},{1,17},{... | collective-permute-start | bytes 393224 | tf_op jit(solution)/shard_map/ppermute | solution.py:664
  130.5 18.5 %collective-permute-start.18 = (bf16[32,16,128]{2,1,0:T(8,128)(2,1)}, bf16[32,16,128]{2,1,0:T(8,128)(2,1)S(1)}, u32[]{:S(2)}, u32[]{:S(2)}) collective-permute-start(bf16[32,16,128]{2,1,0:T(8,128)(2,1)} %get-tuple-element.64), channel_id=1, source_target_pairs={{0,20},{4,16},{8,28},{12,24},{16,4},{20,0},{24,12},{28,8},{1,21},{... | collective-permute-start | bytes 393224 | tf_op jit(solution)/shard_map/ppermute | solution.py:664
  130.8 18.1 %copy-start.8 = (bf16[32,16,128]{2,1,0:T(8,128)(2,1)}, bf16[32,16,128]{2,1,0:T(8,128)(2,1)S(1)}, u32[]{:S(2)}) copy-start(bf16[32,16,128]{2,1,0:T(8,128)(2,1)S(1)} %collective-permute-done.14.refs_1_) | copy-start | bytes 393220
  130.8 18.1 %collective-permute-start.19 = (bf16[32,16,128]{2,1,0:T(8,128)(2,1)}, bf16[32,16,128]{2,1,0:T(8,128)(2,1)S(1)}, u32[]{:S(2)}, u32[]{:S(2)}) collective-permute-start(bf16[32,16,128]{2,1,0:T(8,128)(2,1)} %get-tuple-element.65), channel_id=1, source_target_pairs={{0,24},{4,28},{8,16},{12,20},{16,8},{20,12},{24,0},{28,4},{1,25},{... | collective-permute-start | bytes 393224 | tf_op jit(solution)/shard_map/ppermute | solution.py:664
  134.5 14.5 %copy-start.9 = (bf16[32,16,128]{2,1,0:T(8,128)(2,1)}, bf16[32,16,128]{2,1,0:T(8,128)(2,1)S(1)}, u32[]{:S(2)}) copy-start(bf16[32,16,128]{2,1,0:T(8,128)(2,1)S(1)} %collective-permute-done.15.refs_2_) | copy-start | bytes 393220
  134.5 14.4 %collective-permute-start.20 = (bf16[32,16,128]{2,1,0:T(8,128)(2,1)}, bf16[32,16,128]{2,1,0:T(8,128)(2,1)S(1)}, u32[]{:S(2)}, u32[]{:S(2)}) collective-permute-start(bf16[32,16,128]{2,1,0:T(8,128)(2,1)} %get-tuple-element.66), channel_id=1, source_target_pairs={{0,28},{4,24},{8,20},{12,16},{16,12},{20,8},{24,4},{28,0},{1,29},{... | collective-permute-start | bytes 393224 | tf_op jit(solution)/shard_map/ppermute | solution.py:664
  140.2 8.8 %copy-start.10 = (bf16[32,16,128]{2,1,0:T(8,128)(2,1)}, bf16[32,16,128]{2,1,0:T(8,128)(2,1)S(1)}, u32[]{:S(2)}) copy-start(bf16[32,16,128]{2,1,0:T(8,128)(2,1)S(1)} %collective-permute-done.16.refs_3_) | copy-start | bytes 393220
  140.2 8.8 %copy-start.11 = (bf16[32,16,128]{2,1,0:T(8,128)(2,1)}, bf16[32,16,128]{2,1,0:T(8,128)(2,1)S(1)}, u32[]{:S(2)}) copy-start(bf16[32,16,128]{2,1,0:T(8,128)(2,1)S(1)} %collective-permute-done.17.refs_4_) | copy-start | bytes 393220
  148.9 0.7 copy-start.12
  148.9 0.7 copy-start.13
  148.9 0.7 copy-start.14
  149.0 11.7 %copy-start = (bf16[8,32,16,128]{3,2,1,0:T(8,128)(2,1)}, bf16[8,32,16,128]{3,2,1,0:T(8,128)(2,1)S(1)}, u32[]{:S(2)}) copy-start(bf16[8,32,16,128]{3,2,1,0:T(8,128)(2,1)S(1)} %all-to-all-done.1.part_ref) | copy-start | bytes 3145732
  160.7 10.2 %collective-permute-start.21 = (bf16[32,16,128]{2,1,0:T(8,128)(2,1)}, bf16[32,16,128]{2,1,0:T(8,128)(2,1)S(1)}, u32[]{:S(2)}, u32[]{:S(2)}) collective-permute-start(bf16[32,16,128]{2,1,0:T(8,128)(2,1)} %get-tuple-element.79), channel_id=1, source_target_pairs={{0,4},{4,0},{8,12},{12,8},{16,20},{20,16},{24,28},{28,24},{1,5},{5... | collective-permute-start | bytes 393224 | tf_op jit(solution)/shard_map/ppermute | solution.py:664
  161.1 12.1 %collective-permute-start.22 = (bf16[32,16,128]{2,1,0:T(8,128)(2,1)}, bf16[32,16,128]{2,1,0:T(8,128)(2,1)S(1)}, u32[]{:S(2)}, u32[]{:S(2)}) collective-permute-start(bf16[32,16,128]{2,1,0:T(8,128)(2,1)} %get-tuple-element.80), channel_id=1, source_target_pairs={{0,8},{4,12},{8,0},{12,4},{16,24},{20,28},{24,16},{28,20},{1,9},{5... | collective-permute-start | bytes 393224 | tf_op jit(solution)/shard_map/ppermute | solution.py:664
  167.6 27.3 %collective-permute-start.23 = (bf16[32,16,128]{2,1,0:T(8,128)(2,1)}, bf16[32,16,128]{2,1,0:T(8,128)(2,1)S(1)}, u32[]{:S(2)}, u32[]{:S(2)}) collective-permute-start(bf16[32,16,128]{2,1,0:T(8,128)(2,1)} %get-tuple-element.81), channel_id=1, source_target_pairs={{0,12},{4,8},{8,4},{12,0},{16,28},{20,24},{24,20},{28,16},{1,13},{... | collective-permute-start | bytes 393224 | tf_op jit(solution)/shard_map/ppermute | solution.py:664
  167.6 27.2 %collective-permute-start.24 = (bf16[32,16,128]{2,1,0:T(8,128)(2,1)}, bf16[32,16,128]{2,1,0:T(8,128)(2,1)S(1)}, u32[]{:S(2)}, u32[]{:S(2)}) collective-permute-start(bf16[32,16,128]{2,1,0:T(8,128)(2,1)} %get-tuple-element.82), channel_id=1, source_target_pairs={{0,16},{4,20},{8,24},{12,28},{16,0},{20,4},{24,8},{28,12},{1,17},{... | collective-permute-start | bytes 393224 | tf_op jit(solution)/shard_map/ppermute | solution.py:664
  170.9 24.1 %collective-permute-start.25 = (bf16[32,16,128]{2,1,0:T(8,128)(2,1)}, bf16[32,16,128]{2,1,0:T(8,128)(2,1)S(1)}, u32[]{:S(2)}, u32[]{:S(2)}) collective-permute-start(bf16[32,16,128]{2,1,0:T(8,128)(2,1)} %get-tuple-element.83), channel_id=1, source_target_pairs={{0,20},{4,16},{8,28},{12,24},{16,4},{20,0},{24,12},{28,8},{1,21},{... | collective-permute-start | bytes 393224 | tf_op jit(solution)/shard_map/ppermute | solution.py:664
  170.9 24.0 %copy-start.15 = (bf16[32,16,128]{2,1,0:T(8,128)(2,1)}, bf16[32,16,128]{2,1,0:T(8,128)(2,1)S(1)}, u32[]{:S(2)}) copy-start(bf16[32,16,128]{2,1,0:T(8,128)(2,1)S(1)} %collective-permute-done.21.refs_1_) | copy-start | bytes 393220
  170.9 24.1 %collective-permute-start.26 = (bf16[32,16,128]{2,1,0:T(8,128)(2,1)}, bf16[32,16,128]{2,1,0:T(8,128)(2,1)S(1)}, u32[]{:S(2)}, u32[]{:S(2)}) collective-permute-start(bf16[32,16,128]{2,1,0:T(8,128)(2,1)} %get-tuple-element.84), channel_id=1, source_target_pairs={{0,24},{4,28},{8,16},{12,20},{16,8},{20,12},{24,0},{28,4},{1,25},{... | collective-permute-start | bytes 393224 | tf_op jit(solution)/shard_map/ppermute | solution.py:664
  173.2 21.6 %copy-start.16 = (bf16[32,16,128]{2,1,0:T(8,128)(2,1)}, bf16[32,16,128]{2,1,0:T(8,128)(2,1)S(1)}, u32[]{:S(2)}) copy-start(bf16[32,16,128]{2,1,0:T(8,128)(2,1)S(1)} %collective-permute-done.22.refs_2_) | copy-start | bytes 393220
  173.2 21.7 %collective-permute-start.27 = (bf16[32,16,128]{2,1,0:T(8,128)(2,1)}, bf16[32,16,128]{2,1,0:T(8,128)(2,1)S(1)}, u32[]{:S(2)}, u32[]{:S(2)}) collective-permute-start(bf16[32,16,128]{2,1,0:T(8,128)(2,1)} %get-tuple-element.85), channel_id=1, source_target_pairs={{0,28},{4,24},{8,20},{12,16},{16,12},{20,8},{24,4},{28,0},{1,29},{... | collective-permute-start | bytes 393224 | tf_op jit(solution)/shard_map/ppermute | solution.py:664
  194.9 0.7 copy-start.17
  194.9 0.7 copy-start.18
  194.9 0.7 copy-start.19
  194.9 0.7 copy-start.20
  195.0 0.8 copy-start.21

commit v4 on v3

--- a/solution.py
+++ b/solution.py
@@ -130,13 +130,17 @@
 FAST = 32
 SLOT = 2 * FAST
 PAIR = 2 * SLOT
+STEP = SLOT + 8
+GAP = FAST + 8
 LANES = 128
 CHIPS = 4
+OUTWARD = (4, 5, 6, 7, 2, 3, 1, 0)
+HOMEWARD = (2, 3, 6, 7, 4, 5, 1, 0)
 F32, BF16 = jnp.float32, jnp.bfloat16
 PARAMS = pltpu.CompilerParams(vmem_limit_bytes=60 * 2**20)
 VM = pl.BlockSpec(memory_space=pltpu.VMEM)
 ANY = pl.BlockSpec(memory_space=pl.ANY)
-U1, U2 = 16, 16
+U1, U2 = 16, 32
 
 
 def sds(shape, dtype):
@@ -168,22 +172,32 @@
     inv[0, FAST:] = 0.0
 
     def paired(blocks):
-        out = np.zeros((half // 2 + 1, PAIR, PAIR))
-        out[:-1, :SLOT, :SLOT] = blocks[0:half:2]
-        out[:-1, SLOT:, SLOT:] = blocks[1:half:2]
+        out = np.zeros((half // 2 + 1, SLOT, PAIR))
+        out[:-1, :, :SLOT] = blocks[0:half:2]
+        out[:-1, :, SLOT:] = blocks[1:half:2]
         return out
 
     fwd, inv, edge_fwd, edge_inv = paired(fwd), paired(inv), fwd[half], inv[half]
-    fwd[-1, :SLOT, FAST:SLOT] = edge_fwd[:, :FAST]
-    inv[-1, FAST:SLOT, :SLOT] = edge_inv[:FAST]
+    fwd[-1, :, FAST:SLOT] = edge_fwd[:, :FAST]
+    inv[-1, FAST:, :SLOT] = edge_inv[:FAST]
     blocks = np.arange(half).reshape(2 * CHIPS, -1)
-    order = [np.concatenate([blocks[c ^ d] for d in range(2 * CHIPS)]) for c in range(2 * CHIPS)]
-    firsts, lasts = np.stack([first[:, o] for o in order]), np.stack([last[o] for o in order])
+
+    def orders(reach):
+        return [np.concatenate([blocks[c ^ d] for d in reach]) for c in range(2 * CHIPS)] + [np.arange(half)]
+
+    firsts = np.stack([first[:, o] for o in orders(OUTWARD)])
+    lasts = np.stack([last[o] for o in orders(HOMEWARD)])
     return [jnp.asarray(t.astype(ml_dtypes.bfloat16)) for t in (firsts, fwd, inv, lasts)]
 
 
 def dot(left, right):
     return jnp.dot(left, right, preferred_element_type=F32)
+
+
+def pair_dot(pair, rows):
+    low = lax.broadcasted_iota(jnp.int32, pair.shape, 1) < SLOT
+    zero = jnp.zeros_like(pair)
+    return dot(jnp.concatenate([jnp.where(low, pair, zero), jnp.where(low, zero, pair)], 0), rows)
 
 
 def loop(count, unroll, step):
@@ -199,13 +213,39 @@
     return pl.ds(pl.multiple_of(start * size, size), size)
 
 
+def slots(ref, p):
+    return [ref.at[pl.ds(pl.multiple_of(p * 2 * STEP + i * STEP, 8), SLOT), :] for i in range(2)]
+
+
+def read_slots(ref, p):
+    return jnp.concatenate([rows[...] for rows in slots(ref, p)], 0).astype(BF16)
+
+
+def write_slots(ref, p, value):
+    for i, rows in enumerate(slots(ref, p)):
+        rows[...] = value[i * SLOT : (i + 1) * SLOT]
+
+
+def gapped(ref, index, count):
+    return [ref.at[pl.ds(pl.multiple_of((index * count + i) * GAP, 8), FAST), :] for i in range(count)]
+
+
+def read_gapped(ref, index, count):
+    return jnp.concatenate([rows[...] for rows in gapped(ref, index, count)], 0)
+
+
+def write_gapped(ref, index, value):
+    for i, rows in enumerate(gapped(ref, index, value.shape[0] // FAST)):
+        rows[...] = value[i * FAST : (i + 1) * FAST]
+
+
 def spread(signal, first_ref, mid_ref):
     half = first_ref.shape[1]
 
     def step(a):
         out = dot(first_ref[...], signal(a))
-        mid_ref[pl.ds(a, half, stride=SLOT), :] = out[:half]
-        mid_ref[pl.ds(FAST + a, half, stride=SLOT), :] = out[half:]
+        mid_ref[pl.ds(a, half, stride=STEP), :] = out[:half]
+        mid_ref[pl.ds(FAST + a, half, stride=STEP), :] = out[half:]
 
     loop(FAST, U1, step)
 
@@ -214,14 +254,15 @@
     half = last_ref.shape[0]
 
     def step(a):
-        re = back_ref[pl.ds(a, half, stride=SLOT), :]
-        im = back_ref[pl.ds(FAST + a, half, stride=SLOT), :]
+        re = back_ref[pl.ds(a, half, stride=STEP), :]
+        im = back_ref[pl.ds(FAST + a, half, stride=STEP), :]
         emit(a, dot(last_ref[...], jnp.concatenate([re, im], 0).astype(BF16)))
 
     loop(FAST, U1, step)
 
 
 def times(x, y, conjugate):
+    x, y = x.astype(F32), y.astype(F32)
     parts = []
     for i in range(0, x.shape[0], SLOT):
         xr, xi, yr, yi = (v[i + j : i + j + FAST] for v in (x, y) for j in (0, FAST))
@@ -237,16 +278,16 @@
     seq = h_ref.shape[1]
 
     def turn(i):
-        time_ref[span(i, LANES), :] = h_ref[:, span(i, LANES)].T
+        write_gapped(time_ref, i, h_ref[:, span(i, LANES)].T)
 
     loop(seq // LANES, 8, turn)
-    spread(lambda a: time_ref[pl.ds(a, half, stride=FAST), :].astype(BF16), first_ref, mid_ref)
+    spread(lambda a: time_ref[pl.ds(a, half, stride=GAP), :].astype(BF16), first_ref, mid_ref)
 
     def step(p):
-        spec_ref[span(p, PAIR), :] = dot(fwd_ref[p], mid_ref[span(p, PAIR), :].astype(BF16))
+        spec_ref[span(p, PAIR), :] = pair_dot(fwd_ref[p], read_slots(mid_ref, p)).astype(BF16)
 
     loop(half // 2, U2, step)
-    spec_ref[span(half // 2, PAIR), :] = dot(fwd_ref[half // 2], mid_ref[:PAIR, :].astype(BF16))
+    spec_ref[span(half // 2, PAIR), :] = pair_dot(fwd_ref[half // 2], read_slots(mid_ref, 0)).astype(BF16)
 
 
 def convolve_kernel(conjugate, count, place_ref, *refs):
@@ -268,17 +309,17 @@
         load.wait()
 
     def step(p):
-        x = dot(fwd_ref[p], mid_ref[span(p, PAIR), :].astype(BF16))
-        spec_ref[span(p, PAIR), :] = x
-        back_ref[span(p, PAIR), :] = dot(inv_ref[p], times(x, h_ref[span(p, PAIR), :], conjugate))
+        x = pair_dot(fwd_ref[p], read_slots(mid_ref, p))
+        spec_ref[span(p, PAIR), :] = x.astype(BF16)
+        write_slots(back_ref, p, pair_dot(inv_ref[p], times(x, h_ref[span(p, PAIR), :], conjugate)))
 
     loop(half // 2, U2, step)
     tail = span(half // 2, PAIR)
-    x = dot(fwd_ref[half // 2], mid_ref[:PAIR, :].astype(BF16))
-    spec_ref[tail, :] = x
+    x = pair_dot(fwd_ref[half // 2], read_slots(mid_ref, 0))
+    spec_ref[tail, :] = x.astype(BF16)
     store = pltpu.make_async_copy(spec_ref, spec_any, sem.at[3])
     store.start()
-    back_ref[:PAIR, :] += dot(inv_ref[half // 2], times(x, h_ref[tail, :], conjugate))
+    back_ref[:SLOT, :] += pair_dot(inv_ref[half // 2], times(x, h_ref[tail, :], conjugate))[:SLOT]
     if len(outs) == 1:
 
         def emit(a, rows):
@@ -302,19 +343,19 @@
 
     def step(p):
         rows = span(p, PAIR)
-        back_ref[rows, :] = dot(inv_ref[p], times(s_ref[rows, :], g_ref[rows, :], True))
+        write_slots(back_ref, p, pair_dot(inv_ref[p], times(s_ref[rows, :], g_ref[rows, :], True)))
 
     loop(half // 2, U2, step)
     tail = span(half // 2, PAIR)
-    back_ref[:PAIR, :] += dot(inv_ref[half // 2], times(s_ref[tail, :], g_ref[tail, :], True))
+    back_ref[:SLOT, :] += pair_dot(inv_ref[half // 2], times(s_ref[tail, :], g_ref[tail, :], True))[:SLOT]
 
     def emit(a, rows):
-        time_ref[pl.ds(a, half, stride=FAST), :] = rows * scale
+        time_ref[pl.ds(a, half, stride=GAP), :] = rows * scale
 
     collect(last_ref, back_ref, emit)
 
     def turn(i):
-        out_ref[:, span(i, LANES)] = time_ref[span(i, LANES), :].T
+        out_ref[:, span(i, LANES)] = read_gapped(time_ref, i, LANES // FAST).T
 
     loop(seq // LANES, 8, turn)
 
@@ -324,10 +365,10 @@
     seq = h.shape[1]
     return pl.pallas_call(
         filter_kernel,
-        out_shape=sds((2 * seq + PAIR, LANES), F32),
+        out_shape=sds((2 * seq + PAIR, LANES), BF16),
         in_specs=[VM] * 3,
         out_specs=VM,
-        scratch_shapes=[pltpu.VMEM((seq, LANES), F32), pltpu.VMEM((2 * seq, LANES), F32)],
+        scratch_shapes=[pltpu.VMEM((seq // FAST * GAP, LANES), F32), pltpu.VMEM((seq // FAST * STEP, LANES), F32)],
         compiler_params=PARAMS,
         cost_estimate=cost(10**9, 8 * 2**20),
         name="filter_spectrum",
@@ -346,20 +387,20 @@
     outs = (sds((FAST, half // groups, LANES), BF16),) * groups
     if whole:
         outs = (sds((groups, FAST, half // groups, LANES), BF16),)
-    big = pltpu.VMEM((spec.shape[0] - PAIR, LANES), F32)
+    big = pltpu.VMEM((half * STEP, LANES), F32)
     *out, spec = pl.pallas_call(
         functools.partial(convolve_kernel, conjugate, count),
-        out_shape=outs + (sds(spec.shape, F32),),
+        out_shape=outs + (sds(spec.shape, BF16),),
         grid_spec=pltpu.PrefetchScalarGridSpec(
             num_scalar_prefetch=1,
             grid=(1,),
             in_specs=[VM] * count + [ANY, own(first), ANY, ANY, own(last)],
             out_specs=(VM,) * len(outs) + (ANY,),
             scratch_shapes=[
-                pltpu.VMEM(spec.shape, F32),
+                pltpu.VMEM(spec.shape, BF16),
                 pltpu.VMEM(fwd.shape, BF16),
                 pltpu.VMEM(fwd.shape, BF16),
-                pltpu.VMEM(spec.shape, F32),
+                pltpu.VMEM(spec.shape, BF16),
                 big,
                 big,
                 pltpu.SemaphoreType.DMA((4,)),
@@ -380,7 +421,7 @@
         out_shape=sds((LANES, seq), F32),
         in_specs=[VM] * 4,
         out_specs=VM,
-        scratch_shapes=[pltpu.VMEM((seq, LANES), F32), pltpu.VMEM((2 * seq, LANES), F32)],
+        scratch_shapes=[pltpu.VMEM((seq // FAST * GAP, LANES), F32), pltpu.VMEM((seq // FAST * STEP, LANES), F32)],
         compiler_params=PARAMS,
         cost_estimate=cost(10**9, 12 * 2**20),
         name="filter_gradient",
@@ -388,10 +429,10 @@
 
 
 def permuted(value, hold_ref, emit):
-    hold_ref[...] = value
+    write_gapped(hold_ref, 0, value)
     per = value.shape[0] // FAST
     for a in range(FAST):
-        emit(a, hold_ref[pl.ds(a, per, stride=FAST), :].astype(BF16))
+        emit(a, hold_ref[pl.ds(a, per, stride=GAP), :].astype(BF16))
 
 
 def gate_kernel(key_ref, value_ref, out_ref, hold_ref):
@@ -413,7 +454,7 @@
         out_shape=sds((groups, FAST, rows // FAST, LANES), BF16),
         in_specs=[block, block],
         out_specs=pl.BlockSpec((WIDE // LANES, FAST, rows // FAST, LANES), lambda j: (j, 0, 0, 0)),
-        scratch_shapes=[pltpu.VMEM((rows, LANES), F32)],
+        scratch_shapes=[pltpu.VMEM((rows // FAST * GAP, LANES), F32)],
         compiler_params=PARAMS,
         cost_estimate=cost(10**6, 3 * 2**20),
         name="gate",
@@ -421,6 +462,7 @@
 
 
 WIDE = 256
+BATCH = 4
 
 
 def pieces_of(x_ref, piece, lane, depth):
@@ -434,17 +476,18 @@
 def terms_kernel(dists, place_ref, *refs):
     count = 2 * sum(1 if d == 0 else 2 for d in dists)
     xs, ws, sum_ref, x_ref, sem = refs[:4], refs[4 : 4 + count], refs[4 + count], refs[-2], refs[-1]
-    mine = place_ref[2]
+    here, core, mine = place_ref[0], place_ref[1], place_ref[2]
 
     @pl.when(pl.program_id(0) == 0)
     def _():
-        copies = [pltpu.make_async_copy(xs[i], x_ref.at[mine ^ i], sem.at[i]) for i in range(4)]
-        for copy in copies:
-            copy.start()
-        for copy in copies:
-            copy.wait()
-
-    here, core = place_ref[0], place_ref[1]
+        for start in (True, False):
+            for i in range(4):
+
+                @pl.when(jnp.abs((mine ^ i) - here) <= dists[-1])
+                def _():
+                    copy = pltpu.make_async_copy(xs[i], x_ref.at[mine ^ i], sem.at[i])
+                    copy.start() if start else copy.wait()
+
     depth = ws[0].shape[1]
 
     def part(piece, near_ref, swap_ref):
@@ -528,8 +571,8 @@
         mix = total.astype(BF16)
         mix_ref[...] = mix
         scaled = mix.astype(F32) * query_ref[...].astype(F32)
-        for g in range(2):
-            hold_ref[g] = scaled[:, g * LANES : (g + 1) * LANES]
+        for g in range(BATCH):
+            write_gapped(hold_ref.at[g], 0, scaled[:, g * LANES : (g + 1) * LANES])
 
     for place, two, last in ((0, 2, True), (1, 2, False), (2, 0, False), (3, 0, True)):
 
@@ -538,13 +581,13 @@
             total = sum_ref[...] + part(two_ref, ws[two], ws[two + 1])
             give(total + part(three_ref, ws[4], ws[5]) if last else total)
 
-    for k in range(CHIPS):
+    for k in range(2 * CHIPS // BATCH):
 
         @pl.when(pl.program_id(0) == k)
         def _():
-            for e in range(2):
+            for e in range(BATCH):
                 for a in range(FAST):
-                    outs[2 * k + e][a] = hold_ref[e ^ core, pl.ds(a, per, stride=FAST), :].astype(BF16)
+                    outs[OUTWARD.index(BATCH * k + e)][a] = hold_ref[e ^ (place_ref[3] % BATCH), pl.ds(a, per, stride=GAP), :].astype(BF16)
 
 
 def mix_late(place, xs, ws, total, query):
@@ -552,7 +595,7 @@
     depth = ws[0].shape[1]
 
     def block(j, place):
-        return j ^ place[0]
+        return j ^ (place[3] // BATCH)
 
     def above(j, place):
         return (jnp.where(place[0] >= 2, block(j, place), 0), 0)
@@ -563,20 +606,20 @@
     def last(j, place):
         return (jnp.where((place[0] == 0) | (place[0] == CHIPS - 1), block(j, place), 0), 0)
 
-    wide = pl.BlockSpec((rows, WIDE), lambda j, place: (0, block(j, place)))
+    wide = pl.BlockSpec((rows, BATCH * LANES), lambda j, place: (0, block(j, place)))
     part = pl.BlockSpec((FAST, rows // FAST, LANES), lambda j, place: (0, 0, 0))
     grad_mix, *scaled = pl.pallas_call(
         late_kernel,
         out_shape=(sds((rows, cols), BF16),) + (sds((FAST, rows // FAST, LANES), BF16),) * (2 * CHIPS),
         grid_spec=pltpu.PrefetchScalarGridSpec(
             num_scalar_prefetch=1,
-            grid=(CHIPS,),
+            grid=(2 * CHIPS // BATCH,),
             in_specs=[ANY] * 4
-            + [pl.BlockSpec((WIDE, depth), m) for m in (above, above, below, below, last, last)]
+            + [pl.BlockSpec((BATCH * LANES, depth), m) for m in (above, above, below, below, last, last)]
             + [wide, wide],
             out_specs=(wide,) + (part,) * (2 * CHIPS),
             scratch_shapes=[
-                pltpu.VMEM((2, rows, LANES), F32),
+                pltpu.VMEM((BATCH, rows // FAST * GAP, LANES), F32),
                 pltpu.VMEM((2,) + xs[0].shape, BF16),
                 pltpu.SemaphoreType.DMA((2,)),
             ],
@@ -591,19 +634,19 @@
 def finish_kernel(count, place_ref, *refs):
     parts, factors, outs = refs[: 2 * CHIPS], refs[2 * CHIPS : 2 * CHIPS + count], refs[2 * CHIPS + count : -1]
     hold_ref = refs[-1]
-    core = place_ref[1]
+    here = place_ref[3] % BATCH
     per = parts[0].shape[1]
-    for k in range(CHIPS):
+    for k in range(2 * CHIPS // BATCH):
 
         @pl.when(pl.program_id(0) == k)
         def _():
-            for e in range(2):
+            for e in range(BATCH):
                 for a in range(FAST):
-                    hold_ref[e ^ core, pl.ds(a, per, stride=FAST), :] = parts[2 * k + e][a].astype(F32)
-
-    for g in range(2):
+                    hold_ref[e ^ here, pl.ds(a, per, stride=GAP), :] = parts[HOMEWARD.index(BATCH * k + e)][a].astype(F32)
+
+    for g in range(BATCH):
         lanes = pl.ds(g * LANES, LANES)
-        value = hold_ref[g]
+        value = read_gapped(hold_ref.at[g], 0, per)
         for factor_ref, out_ref in zip(factors, outs):
             out_ref[:, lanes] = (value * factor_ref[:, lanes].astype(F32)).astype(BF16)
 
@@ -611,17 +654,17 @@
 def finish(place, parts, *factors):
     rows, cols = factors[0].shape
     count = len(factors)
-    wide = pl.BlockSpec((rows, WIDE), lambda j, place: (0, j ^ place[0]))
+    block = pl.BlockSpec((rows, BATCH * LANES), lambda j, place: (0, j ^ (place[3] // BATCH)))
     part = pl.BlockSpec(parts[0].shape, lambda j, place: (0, 0, 0))
     return pl.pallas_call(
         functools.partial(finish_kernel, count),
         out_shape=(sds((rows, cols), BF16),) * count,
         grid_spec=pltpu.PrefetchScalarGridSpec(
             num_scalar_prefetch=1,
-            grid=(CHIPS,),
-            in_specs=[part] * (2 * CHIPS) + [wide] * count,
-            out_specs=(wide,) * count,
-            scratch_shapes=[pltpu.VMEM((2, rows, LANES), F32)],
+            grid=(2 * CHIPS // BATCH,),
+            in_specs=[part] * (2 * CHIPS) + [block] * count,
+            out_specs=(block,) * count,
+            scratch_shapes=[pltpu.VMEM((BATCH, rows // FAST * GAP, LANES), F32)],
         ),
         compiler_params=PARAMS,
         cost_estimate=cost(10**6, (1 + 2 * count) * 2**20),
@@ -633,9 +676,9 @@
     per = part_ref.shape[2]
     for g in range(2):
         for a in range(FAST):
-            hold_ref[pl.ds(a, per, stride=FAST), :] = part_ref[g, a].astype(F32)
+            hold_ref[pl.ds(a, per, stride=GAP), :] = part_ref[g, a].astype(F32)
         lanes = pl.ds(g * LANES, LANES)
-        out_ref[:, lanes] = (hold_ref[...] * factor_ref[:, lanes].astype(F32)).astype(BF16)
+        out_ref[:, lanes] = (read_gapped(hold_ref, 0, per) * factor_ref[:, lanes].astype(F32)).astype(BF16)
 
 
 def finish_whole(parts, factor):
@@ -648,7 +691,7 @@
         grid=(CHIPS,),
         in_specs=[part, wide],
         out_specs=wide,
-        scratch_shapes=[pltpu.VMEM((rows, LANES), F32)],
+        scratch_shapes=[pltpu.VMEM((rows // FAST * GAP, LANES), F32)],
         compiler_params=PARAMS,
         cost_estimate=cost(10**6, 3 * 2**20),
         name="finish_whole",
@@ -659,9 +702,9 @@
     return lax.all_to_all(parts, "ctx", split_axis=0, concat_axis=0, tiled=True)
 
 
-def scatter(parts, first=0):
+def scatter(parts, reach):
     ids = range(2 * CHIPS)
-    return [lax.ppermute(p, "ctx", [(i, i ^ (first + d)) for i in ids]) if first + d else p for d, p in enumerate(parts)]
+    return [lax.ppermute(part, "ctx", [(i, i ^ d) for i in ids]) if d else part for part, d in zip(parts, reach)]
 
 
 SWAP = [(i, i ^ 1) for i in range(2 * CHIPS)]
@@ -685,7 +728,7 @@
     firsts, fwd, inv, lasts = tables(seq)
     tie = lax.optimization_barrier
     ctx = lax.axis_index("ctx")
-    place = jnp.stack([ctx // 2, ctx % 2, lax.axis_index("mp")]).astype(jnp.int32)
+    place = jnp.stack([ctx // 2, ctx % 2, lax.axis_index("mp"), ctx]).astype(jnp.int32)
     index = ctx.astype(jnp.int32)[None]
 
     def across(x, d):
@@ -694,13 +737,13 @@
     low1, high1 = hop(proj_out, proj_out, 1)
     x1, x2 = across(grad_out, 1), across(grad_out, 2)
     gated = exchange(gate(key_in, value_in, groups))
-    spec = filter_spectrum(filters, (firsts[0], fwd))
+    spec = filter_spectrum(filters, (firsts[-1], fwd))
     low1, high1, spec, own = tie((low1, high1, spec, proj_out))
 
     low2, high2 = hop(low1, high1, 2)
     x3, _, _ = tie((grad_out, x1, x2))
     xs = [grad_out, x1, x2, across(x3, 3)]
-    (conv,), gated_spec = convolve(index * 0, [gated], spec, (firsts, fwd, inv, lasts), False, True)
+    (conv,), gated_spec = convolve(jnp.full_like(index, 2 * CHIPS), [gated], spec, (firsts, fwd, inv, lasts), False, True)
     own, low1, high1, _ = tie((own, low1, high1, conv))
     ws = [own, lax.ppermute(own, "ctx", SWAP)] + with_swaps(low1, high1, 1)
     low2, high2, _ = tie((low2, high2, conv))
@@ -715,11 +758,11 @@
     last, _ = tie((last, total))
     ws += [last, lax.ppermute(last, "ctx", end_swap)]
     grad_mix, scaled = mix_late(place, xs, ws, total, query)
-    scaled = scatter(scaled)
+    scaled = scatter(scaled, OUTWARD)
     *scaled, conv = tie((*scaled, conv))
     back, scaled_spec = convolve(index, scaled, spec, (firsts, fwd, inv, lasts), True, False)
-    back = scatter(back)
-    filter_grad = filter_gradient(scaled_spec, gated_spec, (None, fwd, inv, lasts[0]), 1.0 / math.sqrt(seq))
+    back = scatter(back, HOMEWARD)
+    filter_grad = filter_gradient(scaled_spec, gated_spec, (None, fwd, inv, lasts[-1]), 1.0 / math.sqrt(seq))
     grad_query = finish_whole(conv, grad_mix)
     grad_key, grad_value = finish(place, back, value_in, key_in)
     return (grad_query, grad_key, grad_value, filter_grad)

time: 202 us -> 192 us (0.950)
  waiting for transfers between devices: 34.8 us -> 56.6 us
  Pallas kernels: 78.1 us -> 58.7 us
  starting transfers between devices: 81.8 us -> 68.6 us
    ppermute x14, waiting for transfers between devices: 11.1 us -> 26.2 us  [scatter(): lax.ppermute(part, 'ctx', [(i, i ^ d) for i in ids])]
    ppermute x14, starting transfers between devices: 30 us -> 15.5 us  [scatter(): lax.ppermute(part, 'ctx', [(i, i ^ d) for i in ids])]
    pallas_call x2, Pallas kernels: 21.9 us -> 15.2 us  [convolve(): pl.pallas_call(functools.partial(convolve_kernel, conjugate, count), out_...]
    ppermute x4, waiting for transfers between devices: 0.47 us -> 6.48 us  [hop(): return (lax.ppermute(low, 'ctx', up), lax.ppermute(high, 'ctx', down))]
    pallas_call x1, Pallas kernels: 10.5 us -> 6.2 us  [filter_spectrum(): pl.pallas_call(filter_kernel, out_shape=sds((2 * seq + PAIR, LANES), BF16...]
    pallas_call x1, Pallas kernels: 11.5 us -> 7.35 us  [filter_gradient(): pl.pallas_call(functools.partial(gradient_kernel, scale), out_shape=sds((...]
  transfers between devices with their start and end apart: 30 -> 30, of which waited for: 8 -> 13; matrix products, arithmetic and copies ran while one was open for 1% -> 2% of each run, Pallas kernels for 30% -> 25%
where the time goes in v4:
time: 192 us; the launch traced here: 191 us
  starting transfers between devices  68.6 us (36%)
  Pallas kernels  58.7 us (31%)
  waiting for transfers between devices  56.6 us (29%)
  local copies, waits for them, and re-layouts  3.33 us (2%)
  other arithmetic  2.93 us (2%)
    ppermute x14, waiting for transfers between devices, scatter(): lax.ppermute(part, 'ctx', [(i, i ^ d) for i in ids])  26.2 us
    all_to_all x2, starting transfers between devices, exchange(): return lax.all_to_all(parts, 'ctx', split_axis=0, concat_axis=0, tiled=True)  19.2 us
    ppermute x14, starting transfers between devices, scatter(): lax.ppermute(part, 'ctx', [(i, i ^ d) for i in ids])  15.5 us
    pallas_call x2, Pallas kernels, convolve(): pl.pallas_call(functools.partial(convolve_kernel, conjugate, count), out_...  15.2 us
    ppermute x1, starting transfers between devices, lane_body(): ws += [last, lax.ppermute(last, 'ctx', end_swap)]  10.1 us
    all_to_all x2, waiting for transfers between devices, exchange(): return lax.all_to_all(parts, 'ctx', split_axis=0, concat_axis=0, tiled=True)  9.59 us
    ppermute x4, starting transfers between devices, hop(): return (lax.ppermute(low, 'ctx', up), lax.ppermute(high, 'ctx', down))  9.44 us
    pallas_call x1, Pallas kernels, mix_late(): pl.pallas_call(late_kernel, out_shape=(sds((rows, cols), BF16),) + (sds((...  9.41 us
  transfers between devices with their start and end apart: 30, of which 13 were waited for; matrix products, arithmetic and copies ran while one was open for 2% of the time, Pallas kernels for 25%

profile of v4, /device:TPU:1, one launch (start us, length us, event | category | flops | bytes accessed | tf_op | source)
XLA Modules:
  0.0 191.2 jit_solution(14451108912788695399)
XLA Ops:
  0.6 0.0 copy-start.2
  0.6 5.2 %collective-permute-start.3 = (bf16[1024,512]{1,0:T(8,128)(2,1)}, bf16[1024,512]{1,0:T(8,128)(2,1)}, u32[]{:S(2)}, u32[]{:S(2)}) collective-permute-start(bf16[1024,512]{1,0:T(8,128)(2,1)} %refs_4_.1), channel_id=1, source_target_pairs={{0,8},{4,12},{8,16},{12,20},{16,24},{20,28},{1,9},{5,13},{9,17},{1... | collective-permute-start | bytes 3145736 | tf_op jit(solution)/shard_map/ppermute | solution.py:716
  5.8 1.3 collective-permute-start.4
  7.1 3.8 %gate.1 = bf16[8,32,16,128]{3,2,1,0:T(8,128)(2,1)} custom-call(bf16[512,1024]{1,0:T(8,128)(2,1)} %refs_9_.2, bf16[512,1024]{1,0:T(8,128)(2,1)} %refs_8_.1), custom_call_target="tpu_custom_call" | custom-call | flops 1 | bytes 3145 | tf_op jit(solution)/shard_map/gate/pallas_call | solution.py:451
  10.9 6.9 %all-to-all-start = ((bf16[8,32,16,128]{3,2,1,0:T(8,128)(2,1)}), bf16[8,32,16,128]{3,2,1,0:T(8,128)(2,1)S(1)}, u32[]{:S(2)}, u32[]{:S(2)}) async-start(bf16[8,32,16,128]{3,2,1,0:T(8,128)(2,1)} %gate.1), calls=%async_computation | async-start | bytes 2097152 | tf_op jit(solution)/shard_map/all_to_all | solution.py:702
  17.8 1.2 collective-permute-start
  19.0 1.2 collective-permute-start.1
  20.3 6.2 %filter_spectrum.1.refs_1_.refs_8_ = bf16[8320,128]{1,0:T(8,128)(2,1)} custom-call(f32[128,4096]{1,0:T(8,128)} %h_ref.1, bf16[256,128]{1,0:T(8,128)(2,1)} %constant.50.first_ref, bf16[65,64,128]{2,1,0:T(8,128)(2,1)} %constant.46.clone.fwd_ref.refs_3_.refs_10_), custom_call_target="tpu_custom_call" | custom-call | flops 1000 | bytes 8388 | tf_op jit(solution)/shard_map/filter_spectrum/pallas_call | solution.py:366
  26.5 0.5 collective-permute-done.3.refs_6_
  26.9 4.8 %collective-permute-done.4.refs_8_ = bf16[1024,512]{1,0:T(8,128)(2,1)} collective-permute-done((bf16[1024,512]{1,0:T(8,128)(2,1)}, bf16[1024,512]{1,0:T(8,128)(2,1)}, u32[]{:S(2)}, u32[]{:S(2)}) %collective-permute-start.4) | collective-permute-done | bytes 1048608 | tf_op jit(solution)/shard_map/ppermute | solution.py:716
  31.7 1.7 collective-permute-start.5
  33.4 1.3 collective-permute-start.6
  34.7 7.9 %collective-permute-done.refs_1_ = bf16[512,1024]{1,0:T(8,128)(2,1)S(1)} collective-permute-done((bf16[512,1024]{1,0:T(8,128)(2,1)S(1)}, bf16[512,1024]{1,0:T(8,128)(2,1)S(1)}, u32[]{:S(2)}, u32[]{:S(2)}) %collective-permute-start) | collective-permute-done | bytes 1048608 | tf_op jit(solution)/shard_map/ppermute | solution.py:735
  42.6 0.9 collective-permute-done.1.refs_2_
  43.5 1.3 collective-permute-start.2
  44.8 9.6 %all-to-all-done.refs_0_ = bf16[8,32,16,128]{3,2,1,0:T(8,128)(2,1)S(1)} async-done(((bf16[8,32,16,128]{3,2,1,0:T(8,128)(2,1)}), bf16[8,32,16,128]{3,2,1,0:T(8,128)(2,1)S(1)}, u32[]{:S(2)}, u32[]{:S(2)}) %all-to-all-start) | async-done | bytes 1048608 | tf_op jit(solution)/shard_map/all_to_all | solution.py:702
  54.4 1.0 copy-done.1
  55.4 7.6 %convolve.2 = (bf16[8,32,16,128]{3,2,1,0:T(8,128)(2,1)}, bf16[8320,128]{1,0:T(8,128)(2,1)}) custom-call(s32[1]{0:T(128)} %constant.43.clone.1.place_ref, bf16[8,32,16,128]{3,2,1,0:T(8,128)(2,1)} %copy-done.1, bf16[8320,128]{1,0:T(8,128)(2,1)} %filter_spectrum.1.refs_1_.refs_8_, bf16[9,256,128]{2,1,0:T(8,128)(2,1)} %constant.45.clone.refs_2_.refs_9_, ...), custom_call_target="tpu_custom_call" | custom-call | flops 2000 | bytes 14680 | tf_op jit(solution)/shard_map/convolve/pallas_call | solution.py:391
  62.9 3.2 %collective-permute-start.10 = (bf16[1024,512]{1,0:T(8,128)(2,1)}, bf16[1024,512]{1,0:T(8,128)(2,1)S(1)}, u32[]{:S(2)}, u32[]{:S(2)}) collective-permute-start(bf16[1024,512]{1,0:T(8,128)(2,1)} %refs_4_.1), channel_id=1, source_target_pairs={{0,4},{4,0},{8,12},{12,8},{16,20},{20,16},{24,28},{28,24},{1,5},{5... | collective-permute-start | bytes 3145736 | tf_op jit(solution)/shard_map/ppermute | solution.py:748
  66.1 1.7 collective-permute-start.11
  67.8 0.0 collective-permute-done.5.refs_4_
  67.8 1.9 %collective-permute-start.12 = (bf16[1024,512]{1,0:T(8,128)(2,1)}, bf16[1024,512]{1,0:T(8,128)(2,1)}, u32[]{:S(2)}, u32[]{:S(2)}) collective-permute-start(bf16[1024,512]{1,0:T(8,128)(2,1)} %collective-permute-done.4.refs_8_), channel_id=1, source_target_pairs={{0,4},{4,0},{8,12},{12,8},{16,20},{20,16},{1,5},{5,1},{9,13},{13,9... | collective-permute-start | bytes 3145736 | tf_op jit(solution)/shard_map/ppermute | solution.py:721
  69.8 1.3 collective-permute-done.6.refs_6_
  71.0 2.3 %broadcast_select_fusion = bf16[1024,512]{1,0:T(8,128)(2,1)} fusion(bf16[1024,512]{1,0:T(8,128)(2,1)} %collective-permute-done.5.refs_4_, bf16[1024,512]{1,0:T(8,128)(2,1)} %collective-permute-done.6.refs_6_, pred[]{:T(512)S(6)} %ge.3), kind=kLoop, calls=%fused_computation | loop fusion | flops 524288 | bytes 3145729 | tf_op jit(solution)/shard_map/jit(_where)/select_n | solution.py:753
  73.3 1.3 collective-permute-start.9
  74.6 0.6 pad_add_fusion.place_ref
  75.3 0.0 collective-permute-done.11.refs_7_
  75.3 0.9 copy-done.4
  76.3 8.9 %terms.1.refs_10_ = f32[512,1024]{1,0:T(8,128)} custom-call(s32[4]{0:T(128)} %pad_add_fusion.place_ref, bf16[512,1024]{1,0:T(8,128)(2,1)} %refs_0_.3, bf16[512,1024]{1,0:T(8,128)(2,1)} %copy-done.3, bf16[512,1024]{1,0:T(8,128)(2,1)} %collective-permute-done.1.refs_2_, bf16[512,1024]{1,0:T(8,128)(2,1)} %collective-permute-done.2.refs_3_, ...), custom_call_target="tpu_custom_call" | custom-call | flops 2000 | bytes 14680 | tf_op jit(solution)/shard_map/terms/pallas_call | solution.py:529
  85.2 12.3 %all-to-all-start.1 = ((bf16[8,32,16,128]{3,2,1,0:T(8,128)(2,1)}), bf16[8,32,16,128]{3,2,1,0:T(8,128)(2,1)S(1)}, u32[]{:S(2)}, u32[]{:S(2)}) async-start(bf16[8,32,16,128]{3,2,1,0:T(8,128)(2,1)} %get-tuple-element.67), calls=%async_computation.1 | async-start | bytes 2097152 | tf_op jit(solution)/shard_map/all_to_all | solution.py:702
  97.5 0.7 collective-permute-start.7
  98.2 1.9 %collective-permute-start.8 = (bf16[1024,512]{1,0:T(8,128)(2,1)}, bf16[1024,512]{1,0:T(8,128)(2,1)S(1)}, u32[]{:S(2)}, u32[]{:S(2)}) collective-permute-start(bf16[1024,512]{1,0:T(8,128)(2,1)} %collective-permute-done.6.refs_6_), channel_id=1, source_target_pairs={{0,4},{4,0},{8,12},{12,8},{1,5},{5,1},{9,13},{13,9},{2,6},{6,2},{1... | collective-permute-start | bytes 3145736 | tf_op jit(solution)/shard_map/ppermute | solution.py:721
  100.2 3.2 %collective-permute-done.9.refs_8_ = bf16[1024,512]{1,0:T(8,128)(2,1)} collective-permute-done((bf16[1024,512]{1,0:T(8,128)(2,1)}, bf16[1024,512]{1,0:T(8,128)(2,1)}, u32[]{:S(2)}, u32[]{:S(2)}) %collective-permute-start.9) | collective-permute-done | bytes 1048608 | tf_op jit(solution)/shard_map/ppermute | solution.py:753
  103.4 10.1 %collective-permute-start.13 = (bf16[1024,512]{1,0:T(8,128)(2,1)}, bf16[1024,512]{1,0:T(8,128)(2,1)}, u32[]{:S(2)}, u32[]{:S(2)}) collective-permute-start(bf16[1024,512]{1,0:T(8,128)(2,1)} %collective-permute-done.9.refs_8_), channel_id=1, source_target_pairs={{0,4},{4,0},{24,28},{28,24},{1,5},{5,1},{25,29},{29,25},{2,6},{6,2... | collective-permute-start | bytes 3145736 | tf_op jit(solution)/shard_map/ppermute | solution.py:759
  113.4 0.0 copy-start.5
  113.5 0.0 collective-permute-done.8.refs_7_
  113.5 2.4 %collective-permute-done.13.refs_9_ = bf16[1024,512]{1,0:T(8,128)(2,1)} collective-permute-done((bf16[1024,512]{1,0:T(8,128)(2,1)}, bf16[1024,512]{1,0:T(8,128)(2,1)}, u32[]{:S(2)}, u32[]{:S(2)}) %collective-permute-start.13) | collective-permute-done | bytes 1048608 | tf_op jit(solution)/shard_map/ppermute | solution.py:759
  115.9 9.4 %mix_late.1 = (bf16[512,1024]{1,0:T(8,128)(2,1)}, bf16[32,16,128]{2,1,0:T(8,128)(2,1)}, bf16[32,16,128]{2,1,0:T(8,128)(2,1)}, bf16[32,16,128]{2,1,0:T(8,128)(2,1...) custom-call(s32[4]{0:T(128)} %pad_add_fusion.place_ref, ...), custom_call_target="tpu_custom_call" | custom-call | flops 1000 | bytes 8388 | tf_op jit(solution)/shard_map/mix_late/pallas_call | solution.py:611
  125.3 0.1 collective-permute-start.14
  125.4 2.9 %collective-permute-start.15 = (bf16[32,16,128]{2,1,0:T(8,128)(2,1)}, bf16[32,16,128]{2,1,0:T(8,128)(2,1)S(1)}, u32[]{:S(2)}, u32[]{:S(2)}) collective-permute-start(bf16[32,16,128]{2,1,0:T(8,128)(2,1)} %get-tuple-element.60), channel_id=1, source_target_pairs={{0,20},{4,16},{8,28},{12,24},{16,4},{20,0},{24,12},{28,8},{1,21},{... | collective-permute-start | bytes 393224 | tf_op jit(solution)/shard_map/ppermute | solution.py:707
  128.2 3.7 %collective-permute-start.16 = (bf16[32,16,128]{2,1,0:T(8,128)(2,1)}, bf16[32,16,128]{2,1,0:T(8,128)(2,1)S(1)}, u32[]{:S(2)}, u32[]{:S(2)}) collective-permute-start(bf16[32,16,128]{2,1,0:T(8,128)(2,1)} %get-tuple-element.61), channel_id=1, source_target_pairs={{0,24},{4,28},{8,16},{12,20},{16,8},{20,12},{24,0},{28,4},{1,25},{... | collective-permute-start | bytes 393224 | tf_op jit(solution)/shard_map/ppermute | solution.py:707
  131.9 0.0 collective-permute-start.17
  131.9 0.0 collective-permute-start.18
  131.9 10.5 %collective-permute-done.14.refs_0_ = bf16[32,16,128]{2,1,0:T(8,128)(2,1)S(1)} collective-permute-done((bf16[32,16,128]{2,1,0:T(8,128)(2,1)}, bf16[32,16,128]{2,1,0:T(8,128)(2,1)S(1)}, u32[]{:S(2)}, u32[]{:S(2)}) %collective-permute-start.14) | collective-permute-done | bytes 131104 | tf_op jit(solution)/shard_map/ppermute | solution.py:707
  142.4 4.1 %collective-permute-done.15.refs_1_ = bf16[32,16,128]{2,1,0:T(8,128)(2,1)S(1)} collective-permute-done((bf16[32,16,128]{2,1,0:T(8,128)(2,1)}, bf16[32,16,128]{2,1,0:T(8,128)(2,1)S(1)}, u32[]{:S(2)}, u32[]{:S(2)}) %collective-permute-start.15) | collective-permute-done | bytes 131104 | tf_op jit(solution)/shard_map/ppermute | solution.py:707
  146.6 3.6 %collective-permute-done.19.refs_5_ = bf16[32,16,128]{2,1,0:T(8,128)(2,1)S(1)} collective-permute-done((bf16[32,16,128]{2,1,0:T(8,128)(2,1)}, bf16[32,16,128]{2,1,0:T(8,128)(2,1)S(1)}, u32[]{:S(2)}, u32[]{:S(2)}) %collective-permute-start.19) | collective-permute-done | bytes 131104 | tf_op jit(solution)/shard_map/ppermute | solution.py:707
  150.2 0.0 copy-start
  150.3 0.6 copy-done.12
  150.8 0.1 copy-done.13
  150.9 7.6 %convolve.3 = (bf16[32,16,128]{2,1,0:T(8,128)(2,1)}, bf16[32,16,128]{2,1,0:T(8,128)(2,1)}, bf16[32,16,128]{2,1,0:T(8,128)(2,1)}, bf16[32,16,128]{2,1,0:T(8,128)(...) custom-call(s32[1]{0:T(128)} %bitcast.3.place_ref, ...), custom_call_target="tpu_custom_call" | custom-call | flops 2000 | bytes 14680 | tf_op jit(solution)/shard_map/convolve/pallas_call | solution.py:391
  158.5 1.7 collective-permute-start.21
  160.2 0.4 collective-permute-start.22
  160.6 2.3 %collective-permute-start.23 = (bf16[32,16,128]{2,1,0:T(8,128)(2,1)}, bf16[32,16,128]{2,1,0:T(8,128)(2,1)S(1)}, u32[]{:S(2)}, u32[]{:S(2)}) collective-permute-start(bf16[32,16,128]{2,1,0:T(8,128)(2,1)} %get-tuple-element.80), channel_id=1, source_target_pairs={{0,24},{4,28},{8,16},{12,20},{16,8},{20,12},{24,0},{28,4},{1,25},{... | collective-permute-start | bytes 393224 | tf_op jit(solution)/shard_map/ppermute | solution.py:707
  162.9 1.2 collective-permute-start.24
  164.1 2.8 %collective-permute-start.26 = (bf16[32,16,128]{2,1,0:T(8,128)(2,1)}, bf16[32,16,128]{2,1,0:T(8,128)(2,1)S(1)}, u32[]{:S(2)}, u32[]{:S(2)}) collective-permute-start(bf16[32,16,128]{2,1,0:T(8,128)(2,1)} %get-tuple-element.83), channel_id=1, source_target_pairs={{0,20},{4,16},{8,28},{12,24},{16,4},{20,0},{24,12},{28,8},{1,21},{... | collective-permute-start | bytes 393224 | tf_op jit(solution)/shard_map/ppermute | solution.py:707
  167.0 0.0 collective-permute-done.22.refs_1_
  167.0 0.4 collective-permute-start.27
  167.4 3.8 %finish_whole.1 = bf16[512,1024]{1,0:T(8,128)(2,1)} custom-call(bf16[8,32,16,128]{3,2,1,0:T(8,128)(2,1)} %copy-done, bf16[512,1024]{1,0:T(8,128)(2,1)} %get-tuple-element.69.factor_ref), custom_call_target="tpu_custom_call" | custom-call | flops 1 | bytes 3145 | tf_op jit(solution)/shard_map/finish_whole/pallas_call | solution.py:688
  171.2 7.4 %filter_gradient.1 = f32[128,4096]{1,0:T(8,128)} custom-call(bf16[8320,128]{1,0:T(8,128)(2,1)} %get-tuple-element.88.s_ref, bf16[8320,128]{1,0:T(8,128)(2,1)} %get-tuple-element.89.g_ref, bf16[65,64,128]{2,1,0:T(8,128)(2,1)} %constant.47.clone.refs_4_.refs_11_.inv_ref, bf16[128,256]{1,0:T(8,128)(2,1)} %constant.52.last_ref), custom_call_target="tpu_custom_call" | custom-call | flops 1000 | bytes 12582 | tf_op jit(solution)/shard_map/filter_gradient/pallas_call | solution.py:419
  178.6 4.7 %collective-permute-done.25.refs_4_ = bf16[32,16,128]{2,1,0:T(8,128)(2,1)S(1)} collective-permute-done((bf16[32,16,128]{2,1,0:T(8,128)(2,1)}, bf16[32,16,128]{2,1,0:T(8,128)(2,1)S(1)}, u32[]{:S(2)}, u32[]{:S(2)}) %collective-permute-start.25) | collective-permute-done | bytes 131104 | tf_op jit(solution)/shard_map/ppermute | solution.py:707
  183.2 3.3 %collective-permute-done.26.refs_5_ = bf16[32,16,128]{2,1,0:T(8,128)(2,1)S(1)} collective-permute-done((bf16[32,16,128]{2,1,0:T(8,128)(2,1)}, bf16[32,16,128]{2,1,0:T(8,128)(2,1)S(1)}, u32[]{:S(2)}, u32[]{:S(2)}) %collective-permute-start.26) | collective-permute-done | bytes 131104 | tf_op jit(solution)/shard_map/ppermute | solution.py:707
  186.6 0.6 copy-done.19
  187.2 0.1 copy-done.20
  187.3 4.0 %finish.1 = (bf16[512,1024]{1,0:T(8,128)(2,1)}, bf16[512,1024]{1,0:T(8,128)(2,1)}) custom-call(s32[4]{0:T(128)} %pad_add_fusion.place_ref, bf16[32,16,128]{2,1,0:T(8,128)(2,1)} %copy-done.14, bf16[32,16,128]{2,1,0:T(8,128)(2,1)} %copy-done.15, bf16[32,16,128]{2,1,0:T(8,128)(2,1)} %copy-done.16, bf16[32,16,128]{2,1,0:T(8,128)(2,1)} %copy-done.17, ...), custom_call_target="tpu_custom_call" | custom-call | flops 1 | bytes 5242 | tf_op jit(solution)/shard_map/finish/pallas_call | solution.py:659
  (49 shorter events, 0.1 us)
Async XLA Ops:
  0.6 17.2 %copy-start.2 = (bf16[512,1024]{1,0:T(8,128)(2,1)S(1)}, bf16[512,1024]{1,0:T(8,128)(2,1)}, u32[]{:S(2)}) copy-start(bf16[512,1024]{1,0:T(8,128)(2,1)} %refs_0_.3) | copy-start | bytes 3145732
  0.6 26.3 %collective-permute-start.3 = (bf16[1024,512]{1,0:T(8,128)(2,1)}, bf16[1024,512]{1,0:T(8,128)(2,1)}, u32[]{:S(2)}, u32[]{:S(2)}) collective-permute-start(bf16[1024,512]{1,0:T(8,128)(2,1)} %refs_4_.1), channel_id=1, source_target_pairs={{0,8},{4,12},{8,16},{12,20},{16,24},{20,28},{1,9},{5,13},{9,17},{1... | collective-permute-start | bytes 3145736 | tf_op jit(solution)/shard_map/ppermute | solution.py:716
  5.8 25.9 %collective-permute-start.4 = (bf16[1024,512]{1,0:T(8,128)(2,1)}, bf16[1024,512]{1,0:T(8,128)(2,1)}, u32[]{:S(2)}, u32[]{:S(2)}) collective-permute-start(bf16[1024,512]{1,0:T(8,128)(2,1)} %refs_4_.1), channel_id=1, source_target_pairs={{8,0},{12,4},{16,8},{20,12},{24,16},{28,20},{9,1},{13,5},{17,9},{2... | collective-permute-start | bytes 3145736 | tf_op jit(solution)/shard_map/ppermute | solution.py:716
  10.9 43.5 %all-to-all-start = ((bf16[8,32,16,128]{3,2,1,0:T(8,128)(2,1)}), bf16[8,32,16,128]{3,2,1,0:T(8,128)(2,1)S(1)}, u32[]{:S(2)}, u32[]{:S(2)}) async-start(bf16[8,32,16,128]{3,2,1,0:T(8,128)(2,1)} %gate.1), calls=%async_computation | async-start | bytes 2097152 | tf_op jit(solution)/shard_map/all_to_all | solution.py:702
  17.8 24.8 %collective-permute-start = (bf16[512,1024]{1,0:T(8,128)(2,1)S(1)}, bf16[512,1024]{1,0:T(8,128)(2,1)S(1)}, u32[]{:S(2)}, u32[]{:S(2)}) collective-permute-start(bf16[512,1024]{1,0:T(8,128)(2,1)S(1)} %copy-done.2), channel_id=1, source_target_pairs={{0,1},{1,0},{2,3},{3,2},{4,5},{5,4},{6,7},{7,6},{8,9},{9,8},{10,11... | collective-permute-start | bytes 3145736 | tf_op jit(solution)/shard_map/ppermute | solution.py:735
  19.0 24.5 %collective-permute-start.1 = (bf16[512,1024]{1,0:T(8,128)(2,1)S(1)}, bf16[512,1024]{1,0:T(8,128)(2,1)}, u32[]{:S(2)}, u32[]{:S(2)}) collective-permute-start(bf16[512,1024]{1,0:T(8,128)(2,1)S(1)} %copy-done.2), channel_id=1, source_target_pairs={{0,2},{1,3},{2,0},{3,1},{4,6},{5,7},{6,4},{7,5},{8,10},{9,11},{10,... | collective-permute-start | bytes 3145736 | tf_op jit(solution)/shard_map/ppermute | solution.py:735
  31.7 36.1 %collective-permute-start.5 = (bf16[1024,512]{1,0:T(8,128)(2,1)}, bf16[1024,512]{1,0:T(8,128)(2,1)}, u32[]{:S(2)}, u32[]{:S(2)}) collective-permute-start(bf16[1024,512]{1,0:T(8,128)(2,1)} %collective-permute-done.3.refs_6_), channel_id=1, source_target_pairs={{8,16},{12,20},{16,24},{20,28},{9,17},{13,21},{17,25},{21,29},{10,... | collective-permute-start | bytes 3145736 | tf_op jit(solution)/shard_map/ppermute | solution.py:716
  33.4 37.6 %collective-permute-start.6 = (bf16[1024,512]{1,0:T(8,128)(2,1)}, bf16[1024,512]{1,0:T(8,128)(2,1)}, u32[]{:S(2)}, u32[]{:S(2)}) collective-permute-start(bf16[1024,512]{1,0:T(8,128)(2,1)} %collective-permute-done.4.refs_8_), channel_id=1, source_target_pairs={{8,0},{12,4},{16,8},{20,12},{9,1},{13,5},{17,9},{21,13},{10,2},{14... | collective-permute-start | bytes 3145736 | tf_op jit(solution)/shard_map/ppermute | solution.py:716
  42.6 32.7 %copy-start.3 = (bf16[512,1024]{1,0:T(8,128)(2,1)}, bf16[512,1024]{1,0:T(8,128)(2,1)S(1)}, u32[]{:S(2)}) copy-start(bf16[512,1024]{1,0:T(8,128)(2,1)S(1)} %collective-permute-done.refs_1_) | copy-start | bytes 3145732
  43.5 31.7 %collective-permute-start.2 = (bf16[512,1024]{1,0:T(8,128)(2,1)S(1)}, bf16[512,1024]{1,0:T(8,128)(2,1)}, u32[]{:S(2)}, u32[]{:S(2)}) collective-permute-start(bf16[512,1024]{1,0:T(8,128)(2,1)S(1)} %copy-done.2), channel_id=1, source_target_pairs={{0,3},{1,2},{2,1},{3,0},{4,7},{5,6},{6,5},{7,4},{8,11},{9,10},{10,... | collective-permute-start | bytes 3145736 | tf_op jit(solution)/shard_map/ppermute | solution.py:735
  54.4 1.0 copy-start.1
  62.9 12.3 %collective-permute-start.10 = (bf16[1024,512]{1,0:T(8,128)(2,1)}, bf16[1024,512]{1,0:T(8,128)(2,1)S(1)}, u32[]{:S(2)}, u32[]{:S(2)}) collective-permute-start(bf16[1024,512]{1,0:T(8,128)(2,1)} %refs_4_.1), channel_id=1, source_target_pairs={{0,4},{4,0},{8,12},{12,8},{16,20},{20,16},{24,28},{28,24},{1,5},{5... | collective-permute-start | bytes 3145736 | tf_op jit(solution)/shard_map/ppermute | solution.py:748
  66.1 9.2 %collective-permute-start.11 = (bf16[1024,512]{1,0:T(8,128)(2,1)}, bf16[1024,512]{1,0:T(8,128)(2,1)}, u32[]{:S(2)}, u32[]{:S(2)}) collective-permute-start(bf16[1024,512]{1,0:T(8,128)(2,1)} %collective-permute-done.3.refs_6_), channel_id=1, source_target_pairs={{8,12},{12,8},{16,20},{20,16},{24,28},{28,24},{9,13},{13,9},{17,21... | collective-permute-start | bytes 3145736 | tf_op jit(solution)/shard_map/ppermute | solution.py:720
  67.8 7.5 %collective-permute-start.12 = (bf16[1024,512]{1,0:T(8,128)(2,1)}, bf16[1024,512]{1,0:T(8,128)(2,1)}, u32[]{:S(2)}, u32[]{:S(2)}) collective-permute-start(bf16[1024,512]{1,0:T(8,128)(2,1)} %collective-permute-done.4.refs_8_), channel_id=1, source_target_pairs={{0,4},{4,0},{8,12},{12,8},{16,20},{20,16},{1,5},{5,1},{9,13},{13,9... | collective-permute-start | bytes 3145736 | tf_op jit(solution)/shard_map/ppermute | solution.py:721
  73.3 30.0 %collective-permute-start.9 = (bf16[1024,512]{1,0:T(8,128)(2,1)}, bf16[1024,512]{1,0:T(8,128)(2,1)}, u32[]{:S(2)}, u32[]{:S(2)}) collective-permute-start(bf16[1024,512]{1,0:T(8,128)(2,1)} %broadcast_select_fusion), channel_id=1, source_target_pairs={{16,24},{20,28},{8,0},{12,4},{17,25},{21,29},{9,1},{13,5},{18,26},... | collective-permute-start | bytes 3145736 | tf_op jit(solution)/shard_map/ppermute | solution.py:753
  75.3 1.0 copy-start.4
  85.2 65.0 %all-to-all-start.1 = ((bf16[8,32,16,128]{3,2,1,0:T(8,128)(2,1)}), bf16[8,32,16,128]{3,2,1,0:T(8,128)(2,1)S(1)}, u32[]{:S(2)}, u32[]{:S(2)}) async-start(bf16[8,32,16,128]{3,2,1,0:T(8,128)(2,1)} %get-tuple-element.67), calls=%async_computation.1 | async-start | bytes 2097152 | tf_op jit(solution)/shard_map/all_to_all | solution.py:702
  97.5 15.9 %collective-permute-start.7 = (bf16[1024,512]{1,0:T(8,128)(2,1)}, bf16[1024,512]{1,0:T(8,128)(2,1)S(1)}, u32[]{:S(2)}, u32[]{:S(2)}) collective-permute-start(bf16[1024,512]{1,0:T(8,128)(2,1)} %collective-permute-done.5.refs_4_), channel_id=1, source_target_pairs={{16,20},{20,16},{24,28},{28,24},{17,21},{21,17},{25,29},{29,25},{1... | collective-permute-start | bytes 3145736 | tf_op jit(solution)/shard_map/ppermute | solution.py:720
  98.2 15.2 %collective-permute-start.8 = (bf16[1024,512]{1,0:T(8,128)(2,1)}, bf16[1024,512]{1,0:T(8,128)(2,1)S(1)}, u32[]{:S(2)}, u32[]{:S(2)}) collective-permute-start(bf16[1024,512]{1,0:T(8,128)(2,1)} %collective-permute-done.6.refs_6_), channel_id=1, source_target_pairs={{0,4},{4,0},{8,12},{12,8},{1,5},{5,1},{9,13},{13,9},{2,6},{6,2},{1... | collective-permute-start | bytes 3145736 | tf_op jit(solution)/shard_map/ppermute | solution.py:721
  103.4 12.5 %collective-permute-start.13 = (bf16[1024,512]{1,0:T(8,128)(2,1)}, bf16[1024,512]{1,0:T(8,128)(2,1)}, u32[]{:S(2)}, u32[]{:S(2)}) collective-permute-start(bf16[1024,512]{1,0:T(8,128)(2,1)} %collective-permute-done.9.refs_8_), channel_id=1, source_target_pairs={{0,4},{4,0},{24,28},{28,24},{1,5},{5,1},{25,29},{29,25},{2,6},{6,2... | collective-permute-start | bytes 3145736 | tf_op jit(solution)/shard_map/ppermute | solution.py:759
  113.4 2.4 %copy-start.5 = (bf16[1024,512]{1,0:T(8,128)(2,1)}, bf16[1024,512]{1,0:T(8,128)(2,1)S(1)}, u32[]{:S(2)}) copy-start(bf16[1024,512]{1,0:T(8,128)(2,1)S(1)} %collective-permute-done.7.refs_5_) | copy-start | bytes 3145732
  113.5 2.4 %copy-start.6 = (bf16[1024,512]{1,0:T(8,128)(2,1)}, bf16[1024,512]{1,0:T(8,128)(2,1)S(1)}, u32[]{:S(2)}) copy-start(bf16[1024,512]{1,0:T(8,128)(2,1)S(1)} %collective-permute-done.8.refs_7_) | copy-start | bytes 3145732
  125.3 17.2 %collective-permute-start.14 = (bf16[32,16,128]{2,1,0:T(8,128)(2,1)}, bf16[32,16,128]{2,1,0:T(8,128)(2,1)S(1)}, u32[]{:S(2)}, u32[]{:S(2)}) collective-permute-start(bf16[32,16,128]{2,1,0:T(8,128)(2,1)} %get-tuple-element.59), channel_id=1, source_target_pairs={{0,16},{4,20},{8,24},{12,28},{16,0},{20,4},{24,8},{28,12},{1,17},{... | collective-permute-start | bytes 393224 | tf_op jit(solution)/shard_map/ppermute | solution.py:707
  125.4 21.2 %collective-permute-start.15 = (bf16[32,16,128]{2,1,0:T(8,128)(2,1)}, bf16[32,16,128]{2,1,0:T(8,128)(2,1)S(1)}, u32[]{:S(2)}, u32[]{:S(2)}) collective-permute-start(bf16[32,16,128]{2,1,0:T(8,128)(2,1)} %get-tuple-element.60), channel_id=1, source_target_pairs={{0,20},{4,16},{8,28},{12,24},{16,4},{20,0},{24,12},{28,8},{1,21},{... | collective-permute-start | bytes 393224 | tf_op jit(solution)/shard_map/ppermute | solution.py:707
  128.2 18.3 %collective-permute-start.16 = (bf16[32,16,128]{2,1,0:T(8,128)(2,1)}, bf16[32,16,128]{2,1,0:T(8,128)(2,1)S(1)}, u32[]{:S(2)}, u32[]{:S(2)}) collective-permute-start(bf16[32,16,128]{2,1,0:T(8,128)(2,1)} %get-tuple-element.61), channel_id=1, source_target_pairs={{0,24},{4,28},{8,16},{12,20},{16,8},{20,12},{24,0},{28,4},{1,25},{... | collective-permute-start | bytes 393224 | tf_op jit(solution)/shard_map/ppermute | solution.py:707
  131.9 14.6 %collective-permute-start.17 = (bf16[32,16,128]{2,1,0:T(8,128)(2,1)}, bf16[32,16,128]{2,1,0:T(8,128)(2,1)S(1)}, u32[]{:S(2)}, u32[]{:S(2)}) collective-permute-start(bf16[32,16,128]{2,1,0:T(8,128)(2,1)} %get-tuple-element.62), channel_id=1, source_target_pairs={{0,28},{4,24},{8,20},{12,16},{16,12},{20,8},{24,4},{28,0},{1,29},{... | collective-permute-start | bytes 393224 | tf_op jit(solution)/shard_map/ppermute | solution.py:707
  131.9 14.7 %collective-permute-start.18 = (bf16[32,16,128]{2,1,0:T(8,128)(2,1)}, bf16[32,16,128]{2,1,0:T(8,128)(2,1)S(1)}, u32[]{:S(2)}, u32[]{:S(2)}) collective-permute-start(bf16[32,16,128]{2,1,0:T(8,128)(2,1)} %get-tuple-element.63), channel_id=1, source_target_pairs={{0,8},{4,12},{8,0},{12,4},{16,24},{20,28},{24,16},{28,20},{1,9},{5... | collective-permute-start | bytes 393224 | tf_op jit(solution)/shard_map/ppermute | solution.py:707
  142.4 7.8 %copy-start.7 = (bf16[32,16,128]{2,1,0:T(8,128)(2,1)}, bf16[32,16,128]{2,1,0:T(8,128)(2,1)S(1)}, u32[]{:S(2)}) copy-start(bf16[32,16,128]{2,1,0:T(8,128)(2,1)S(1)} %collective-permute-done.14.refs_0_) | copy-start | bytes 393220
  142.4 7.7 %collective-permute-start.19 = (bf16[32,16,128]{2,1,0:T(8,128)(2,1)}, bf16[32,16,128]{2,1,0:T(8,128)(2,1)S(1)}, u32[]{:S(2)}, u32[]{:S(2)}) collective-permute-start(bf16[32,16,128]{2,1,0:T(8,128)(2,1)} %get-tuple-element.64), channel_id=1, source_target_pairs={{0,12},{4,8},{8,4},{12,0},{16,28},{20,24},{24,20},{28,16},{1,13},{... | collective-permute-start | bytes 393224 | tf_op jit(solution)/shard_map/ppermute | solution.py:707
  146.6 3.7 %copy-start.8 = (bf16[32,16,128]{2,1,0:T(8,128)(2,1)}, bf16[32,16,128]{2,1,0:T(8,128)(2,1)S(1)}, u32[]{:S(2)}) copy-start(bf16[32,16,128]{2,1,0:T(8,128)(2,1)S(1)} %collective-permute-done.15.refs_1_) | copy-start | bytes 393220
  146.6 3.6 %collective-permute-start.20 = (bf16[32,16,128]{2,1,0:T(8,128)(2,1)}, bf16[32,16,128]{2,1,0:T(8,128)(2,1)S(1)}, u32[]{:S(2)}, u32[]{:S(2)}) collective-permute-start(bf16[32,16,128]{2,1,0:T(8,128)(2,1)} %get-tuple-element.65), channel_id=1, source_target_pairs={{0,4},{4,0},{8,12},{12,8},{16,20},{20,16},{24,28},{28,24},{1,5},{5... | collective-permute-start | bytes 393224 | tf_op jit(solution)/shard_map/ppermute | solution.py:707
  146.6 3.7 %copy-start.9 = (bf16[32,16,128]{2,1,0:T(8,128)(2,1)}, bf16[32,16,128]{2,1,0:T(8,128)(2,1)S(1)}, u32[]{:S(2)}) copy-start(bf16[32,16,128]{2,1,0:T(8,128)(2,1)S(1)} %collective-permute-done.16.refs_2_) | copy-start | bytes 393220
  146.6 3.6 %copy-start.10 = (bf16[32,16,128]{2,1,0:T(8,128)(2,1)}, bf16[32,16,128]{2,1,0:T(8,128)(2,1)S(1)}, u32[]{:S(2)}) copy-start(bf16[32,16,128]{2,1,0:T(8,128)(2,1)S(1)} %collective-permute-done.17.refs_3_) | copy-start | bytes 393220
  146.6 3.6 %copy-start.11 = (bf16[32,16,128]{2,1,0:T(8,128)(2,1)}, bf16[32,16,128]{2,1,0:T(8,128)(2,1)S(1)}, u32[]{:S(2)}) copy-start(bf16[32,16,128]{2,1,0:T(8,128)(2,1)S(1)} %collective-permute-done.18.refs_4_) | copy-start | bytes 393220
  150.2 0.7 copy-start.12
  150.2 0.7 copy-start.13
  150.2 8.3 %copy-start = (bf16[8,32,16,128]{3,2,1,0:T(8,128)(2,1)}, bf16[8,32,16,128]{3,2,1,0:T(8,128)(2,1)S(1)}, u32[]{:S(2)}) copy-start(bf16[8,32,16,128]{3,2,1,0:T(8,128)(2,1)S(1)} %all-to-all-done.1.part_ref) | copy-start | bytes 3145732
  158.5 5.6 %collective-permute-start.21 = (bf16[32,16,128]{2,1,0:T(8,128)(2,1)}, bf16[32,16,128]{2,1,0:T(8,128)(2,1)S(1)}, u32[]{:S(2)}, u32[]{:S(2)}) collective-permute-start(bf16[32,16,128]{2,1,0:T(8,128)(2,1)} %get-tuple-element.78), channel_id=1, source_target_pairs={{0,8},{4,12},{8,0},{12,4},{16,24},{20,28},{24,16},{28,20},{1,9},{5... | collective-permute-start | bytes 393224 | tf_op jit(solution)/shard_map/ppermute | solution.py:707
  160.2 6.8 %collective-permute-start.22 = (bf16[32,16,128]{2,1,0:T(8,128)(2,1)}, bf16[32,16,128]{2,1,0:T(8,128)(2,1)S(1)}, u32[]{:S(2)}, u32[]{:S(2)}) collective-permute-start(bf16[32,16,128]{2,1,0:T(8,128)(2,1)} %get-tuple-element.79), channel_id=1, source_target_pairs={{0,12},{4,8},{8,4},{12,0},{16,28},{20,24},{24,20},{28,16},{1,13},{... | collective-permute-start | bytes 393224 | tf_op jit(solution)/shard_map/ppermute | solution.py:707
  160.6 17.9 %collective-permute-start.23 = (bf16[32,16,128]{2,1,0:T(8,128)(2,1)}, bf16[32,16,128]{2,1,0:T(8,128)(2,1)S(1)}, u32[]{:S(2)}, u32[]{:S(2)}) collective-permute-start(bf16[32,16,128]{2,1,0:T(8,128)(2,1)} %get-tuple-element.80), channel_id=1, source_target_pairs={{0,24},{4,28},{8,16},{12,20},{16,8},{20,12},{24,0},{28,4},{1,25},{... | collective-permute-start | bytes 393224 | tf_op jit(solution)/shard_map/ppermute | solution.py:707
  162.9 15.6 %collective-permute-start.24 = (bf16[32,16,128]{2,1,0:T(8,128)(2,1)}, bf16[32,16,128]{2,1,0:T(8,128)(2,1)S(1)}, u32[]{:S(2)}, u32[]{:S(2)}) collective-permute-start(bf16[32,16,128]{2,1,0:T(8,128)(2,1)} %get-tuple-element.81), channel_id=1, source_target_pairs={{0,28},{4,24},{8,20},{12,16},{16,12},{20,8},{24,4},{28,0},{1,29},{... | collective-permute-start | bytes 393224 | tf_op jit(solution)/shard_map/ppermute | solution.py:707
  164.1 19.1 %collective-permute-start.25 = (bf16[32,16,128]{2,1,0:T(8,128)(2,1)}, bf16[32,16,128]{2,1,0:T(8,128)(2,1)S(1)}, u32[]{:S(2)}, u32[]{:S(2)}) collective-permute-start(bf16[32,16,128]{2,1,0:T(8,128)(2,1)} %get-tuple-element.82), channel_id=1, source_target_pairs={{0,16},{4,20},{8,24},{12,28},{16,0},{20,4},{24,8},{28,12},{1,17},{... | collective-permute-start | bytes 393224 | tf_op jit(solution)/shard_map/ppermute | solution.py:707
  164.1 14.4 %copy-start.14 = (bf16[32,16,128]{2,1,0:T(8,128)(2,1)}, bf16[32,16,128]{2,1,0:T(8,128)(2,1)S(1)}, u32[]{:S(2)}) copy-start(bf16[32,16,128]{2,1,0:T(8,128)(2,1)S(1)} %collective-permute-done.21.refs_0_) | copy-start | bytes 393220
  164.1 22.4 %collective-permute-start.26 = (bf16[32,16,128]{2,1,0:T(8,128)(2,1)}, bf16[32,16,128]{2,1,0:T(8,128)(2,1)S(1)}, u32[]{:S(2)}, u32[]{:S(2)}) collective-permute-start(bf16[32,16,128]{2,1,0:T(8,128)(2,1)} %get-tuple-element.83), channel_id=1, source_target_pairs={{0,20},{4,16},{8,28},{12,24},{16,4},{20,0},{24,12},{28,8},{1,21},{... | collective-permute-start | bytes 393224 | tf_op jit(solution)/shard_map/ppermute | solution.py:707
  167.0 11.6 %copy-start.15 = (bf16[32,16,128]{2,1,0:T(8,128)(2,1)}, bf16[32,16,128]{2,1,0:T(8,128)(2,1)S(1)}, u32[]{:S(2)}) copy-start(bf16[32,16,128]{2,1,0:T(8,128)(2,1)S(1)} %collective-permute-done.22.refs_1_) | copy-start | bytes 393220
  167.0 19.5 %collective-permute-start.27 = (bf16[32,16,128]{2,1,0:T(8,128)(2,1)}, bf16[32,16,128]{2,1,0:T(8,128)(2,1)S(1)}, u32[]{:S(2)}, u32[]{:S(2)}) collective-permute-start(bf16[32,16,128]{2,1,0:T(8,128)(2,1)} %get-tuple-element.84), channel_id=1, source_target_pairs={{0,4},{4,0},{8,12},{12,8},{16,20},{20,16},{24,28},{28,24},{1,5},{5... | collective-permute-start | bytes 393224 | tf_op jit(solution)/shard_map/ppermute | solution.py:707
  178.5 8.0 %copy-start.16 = (bf16[32,16,128]{2,1,0:T(8,128)(2,1)}, bf16[32,16,128]{2,1,0:T(8,128)(2,1)S(1)}, u32[]{:S(2)}) copy-start(bf16[32,16,128]{2,1,0:T(8,128)(2,1)S(1)} %collective-permute-done.23.refs_2_) | copy-start | bytes 393220
  178.6 8.0 %copy-start.17 = (bf16[32,16,128]{2,1,0:T(8,128)(2,1)}, bf16[32,16,128]{2,1,0:T(8,128)(2,1)S(1)}, u32[]{:S(2)}) copy-start(bf16[32,16,128]{2,1,0:T(8,128)(2,1)S(1)} %collective-permute-done.24.refs_3_) | copy-start | bytes 393220
  183.2 3.3 %copy-start.18 = (bf16[32,16,128]{2,1,0:T(8,128)(2,1)}, bf16[32,16,128]{2,1,0:T(8,128)(2,1)S(1)}, u32[]{:S(2)}) copy-start(bf16[32,16,128]{2,1,0:T(8,128)(2,1)S(1)} %collective-permute-done.25.refs_4_) | copy-start | bytes 393220
  186.5 0.7 copy-start.19
  186.5 0.7 copy-start.20

commit v5 on v4

--- a/solution.py
+++ b/solution.py
@@ -134,10 +134,10 @@
 GAP = FAST + 8
 LANES = 128
 CHIPS = 4
-OUTWARD = (4, 5, 6, 7, 2, 3, 1, 0)
-HOMEWARD = (2, 3, 6, 7, 4, 5, 1, 0)
+OUTWARD = (6, 4, 2, 7, 5, 3, 1, 0)
+HOMEWARD = (6, 2, 3, 7, 4, 5, 1, 0)
 F32, BF16 = jnp.float32, jnp.bfloat16
-PARAMS = pltpu.CompilerParams(vmem_limit_bytes=60 * 2**20)
+PARAMS = pltpu.CompilerParams(vmem_limit_bytes=63 * 2**20)
 VM = pl.BlockSpec(memory_space=pltpu.VMEM)
 ANY = pl.BlockSpec(memory_space=pl.ANY)
 U1, U2 = 16, 32
@@ -473,67 +473,62 @@
     return lax.dot_general(left, w_ref[...], (((1,), (1,)), ((), ())), preferred_element_type=F32)
 
 
-def terms_kernel(dists, place_ref, *refs):
-    count = 2 * sum(1 if d == 0 else 2 for d in dists)
-    xs, ws, sum_ref, x_ref, sem = refs[:4], refs[4 : 4 + count], refs[4 + count], refs[-2], refs[-1]
+def is_end(place):
+    return (place[0] == 0) | (place[0] == CHIPS - 1)
+
+
+def terms_kernel(place_ref, *refs):
+    xs, ws, (sum_ref, x_ref, sem) = refs[:4], refs[4:10], refs[-3:]
     here, core, mine = place_ref[0], place_ref[1], place_ref[2]
+    depth = ws[0].shape[1]
+    inside = jnp.logical_not(is_end(place_ref))
 
     @pl.when(pl.program_id(0) == 0)
     def _():
         for start in (True, False):
             for i in range(4):
-
-                @pl.when(jnp.abs((mine ^ i) - here) <= dists[-1])
+                apart = mine ^ i ^ here
+
+                @pl.when((apart < 2) | (inside & (apart == CHIPS - 1)))
                 def _():
                     copy = pltpu.make_async_copy(xs[i], x_ref.at[mine ^ i], sem.at[i])
                     copy.start() if start else copy.wait()
 
-    depth = ws[0].shape[1]
-
     def part(piece, near_ref, swap_ref):
         one = against(pieces_of(x_ref, piece, core, depth), near_ref)
         return one + against(pieces_of(x_ref, piece, 1 - core, depth), swap_ref)
 
-    for d in dists:
-        if d == 0:
-            sum_ref[...] = part(here, ws[0], ws[1])
-            ws = ws[2:]
-            continue
-        up, up_swap, down, down_swap = ws[:4]
-        ws = ws[4:]
-
-        @pl.when(here >= d)
-        def _():
-            sum_ref[...] += part(here - d, up, up_swap)
-
-        @pl.when(here + d < CHIPS)
-        def _():
-            sum_ref[...] += part(here + d, down, down_swap)
-
-
-def above(d):
-    return lambda j, place: (jnp.where(place[0] >= d, j, 0), 0)
-
-
-def below(d):
-    return lambda j, place: (jnp.where(place[0] + d < CHIPS, j, 0), 0)
-
-
-def terms(dists, place, xs, ws):
+    total = part(here, ws[0], ws[1]) + part(here ^ 1, ws[2], ws[3])
+
+    @pl.when(inside)
+    def _():
+        sum_ref[...] = total + part(CHIPS - 1 - here, ws[4], ws[5])
+
+    @pl.when(is_end(place_ref))
+    def _():
+        sum_ref[...] = total
+
+
+def always(j, place):
+    return (j, 0)
+
+
+def inside_only(j, place):
+    return (jnp.where(is_end(place), 0, j), 0)
+
+
+def terms(place, xs, ws):
     rows, piece = xs[0].shape
     cols, depth = ws[0].shape
-    maps = []
-    for d in dists:
-        maps += [above(d), above(d)] + ([below(d), below(d)] if d else [])
-    wide = pl.BlockSpec((rows, WIDE), lambda j, place: (0, j))
+    maps = [always] * 4 + [inside_only] * 2
     return pl.pallas_call(
-        functools.partial(terms_kernel, dists),
+        terms_kernel,
         out_shape=sds((rows, cols), F32),
         grid_spec=pltpu.PrefetchScalarGridSpec(
             num_scalar_prefetch=1,
             grid=(cols // WIDE,),
             in_specs=[ANY] * 4 + [pl.BlockSpec((WIDE, depth), m) for m in maps],
-            out_specs=wide,
+            out_specs=pl.BlockSpec((rows, WIDE), lambda j, place: (0, j)),
             scratch_shapes=[pltpu.VMEM((4, rows, piece), BF16), pltpu.SemaphoreType.DMA((4,))],
         ),
         compiler_params=PARAMS,
@@ -548,20 +543,21 @@
     here, core, mine = place_ref[0], place_ref[1], place_ref[2]
     two_ref, three_ref = x_ref.at[pl.ds(0, 1)], x_ref.at[pl.ds(1, 1)]
 
+    ends = is_end(place_ref)
+
     @pl.when(pl.program_id(0) == 0)
     def _():
         for start in (True, False):
-            for slot, piece in enumerate((here ^ 2, CHIPS - 1 - here)):
+            for slot, piece, needed in ((0, here ^ 2, True), (1, CHIPS - 1 - here, ends)):
                 for i in range(4):
 
-                    @pl.when(mine ^ piece == i)
+                    @pl.when((mine ^ piece == i) & needed)
                     def _():
                         copy = pltpu.make_async_copy(xs[i], x_ref.at[slot], sem.at[slot])
                         copy.start() if start else copy.wait()
 
-    rows = sum_ref.shape[0]
     depth = ws[0].shape[1]
-    per = rows // FAST
+    per = sum_ref.shape[0] // FAST
 
     def part(piece_ref, near_ref, swap_ref):
         one = against(pieces_of(piece_ref, 0, core, depth), near_ref)
@@ -574,12 +570,13 @@
         for g in range(BATCH):
             write_gapped(hold_ref.at[g], 0, scaled[:, g * LANES : (g + 1) * LANES])
 
-    for place, two, last in ((0, 2, True), (1, 2, False), (2, 0, False), (3, 0, True)):
-
-        @pl.when(here == place)
-        def _():
-            total = sum_ref[...] + part(two_ref, ws[two], ws[two + 1])
-            give(total + part(three_ref, ws[4], ws[5]) if last else total)
+    @pl.when(ends)
+    def _():
+        give(sum_ref[...] + part(two_ref, ws[2], ws[3]) + part(three_ref, ws[4], ws[5]))
+
+    @pl.when(jnp.logical_not(ends))
+    def _():
+        give(sum_ref[...] + part(two_ref, ws[0], ws[1]))
 
     for k in range(2 * CHIPS // BATCH):
 
@@ -597,14 +594,11 @@
     def block(j, place):
         return j ^ (place[3] // BATCH)
 
-    def above(j, place):
-        return (jnp.where(place[0] >= 2, block(j, place), 0), 0)
-
-    def below(j, place):
-        return (jnp.where(place[0] < 2, block(j, place), 0), 0)
-
-    def last(j, place):
-        return (jnp.where((place[0] == 0) | (place[0] == CHIPS - 1), block(j, place), 0), 0)
+    def inner(j, place):
+        return (jnp.where(is_end(place), 0, block(j, place)), 0)
+
+    def outer(j, place):
+        return (jnp.where(is_end(place), block(j, place), 0), 0)
 
     wide = pl.BlockSpec((rows, BATCH * LANES), lambda j, place: (0, block(j, place)))
     part = pl.BlockSpec((FAST, rows // FAST, LANES), lambda j, place: (0, 0, 0))
@@ -615,7 +609,7 @@
             num_scalar_prefetch=1,
             grid=(2 * CHIPS // BATCH,),
             in_specs=[ANY] * 4
-            + [pl.BlockSpec((BATCH * LANES, depth), m) for m in (above, above, below, below, last, last)]
+            + [pl.BlockSpec((BATCH * LANES, depth), m) for m in (inner, inner, outer, outer, outer, outer)]
             + [wide, wide],
             out_specs=(wide,) + (part,) * (2 * CHIPS),
             scratch_shapes=[
@@ -707,19 +701,15 @@
     return [lax.ppermute(part, "ctx", [(i, i ^ d) for i in ids]) if d else part for part, d in zip(parts, reach)]
 
 
-SWAP = [(i, i ^ 1) for i in range(2 * CHIPS)]
-
-
-def hop(low, high, d):
-    up = [(i, i + 2) for i in range(2 * (d - 1), 2 * CHIPS - 2)]
-    down = [(i, i - 2) for i in range(2, 2 * (CHIPS - d + 1))]
-    return lax.ppermute(low, "ctx", up), lax.ppermute(high, "ctx", down)
-
-
-def with_swaps(low, high, d):
-    low_swap = lax.ppermute(low, "ctx", [p for p in SWAP if p[0] >= 2 * d])
-    high_swap = lax.ppermute(high, "ctx", [p for p in SWAP if p[0] < 2 * (CHIPS - d)])
-    return [low, low_swap, high, high_swap]
+SWAP = [(i, i ^ 1) for i in range(8)]
+SIDE = [(i, i ^ 2) for i in range(8)]
+MIDDLE = [(2, 4), (3, 5), (4, 2), (5, 3)]
+OUT = [(2, 0), (3, 1), (4, 6), (5, 7)]
+INNER_SWAP, END_SWAP = SWAP[2:6], SWAP[:2] + SWAP[6:]
+
+
+def to(x, pairs):
+    return lax.ppermute(x, "ctx", pairs)
 
 
 def lane_body(grad_out, proj_out, query, key_in, value_in, filters):
@@ -734,29 +724,27 @@
     def across(x, d):
         return lax.ppermute(x, "mp", [(i, i ^ d) for i in range(4)])
 
-    low1, high1 = hop(proj_out, proj_out, 1)
+    side, middle = to(proj_out, SIDE), to(proj_out, MIDDLE)
     x1, x2 = across(grad_out, 1), across(grad_out, 2)
     gated = exchange(gate(key_in, value_in, groups))
     spec = filter_spectrum(filters, (firsts[-1], fwd))
-    low1, high1, spec, own = tie((low1, high1, spec, proj_out))
-
-    low2, high2 = hop(low1, high1, 2)
-    x3, _, _ = tie((grad_out, x1, x2))
+    side, middle, spec = tie((side, middle, spec))
+
+    crossed, sent_out = to(side, MIDDLE), to(middle, OUT)
+    ws = [side, to(side, SWAP), middle, to(middle, INNER_SWAP)]
+    x3, own, *_ = tie((grad_out, proj_out, x1, x2, ws[1], ws[3]))
+    ws = [own, to(own, SWAP)] + ws
     xs = [grad_out, x1, x2, across(x3, 3)]
     (conv,), gated_spec = convolve(jnp.full_like(index, 2 * CHIPS), [gated], spec, (firsts, fwd, inv, lasts), False, True)
-    own, low1, high1, _ = tie((own, low1, high1, conv))
-    ws = [own, lax.ppermute(own, "ctx", SWAP)] + with_swaps(low1, high1, 1)
-    low2, high2, _ = tie((low2, high2, conv))
-
-    end = [(i, i + 2) for i in (4, 5)] + [(i, i - 2) for i in (2, 3)]
-    end_swap = [p for p in SWAP if p[0] in (0, 1, 6, 7)]
-    last = lax.ppermute(jnp.where(ctx >= CHIPS, low2, high2), "ctx", end)
-    total = terms((0, 1), place, xs, ws)
+    crossed, _ = tie((crossed, conv))
+
+    last = to(crossed, OUT)
+    total = terms(place, xs, ws)
     conv, _ = tie((conv, total))
     conv = exchange(conv)
-    ws = with_swaps(low2, high2, 2)
+    ws = [crossed, to(crossed, INNER_SWAP), sent_out, to(sent_out, END_SWAP)]
     last, _ = tie((last, total))
-    ws += [last, lax.ppermute(last, "ctx", end_swap)]
+    ws += [last, to(last, END_SWAP)]
     grad_mix, scaled = mix_late(place, xs, ws, total, query)
     scaled = scatter(scaled, OUTWARD)
     *scaled, conv = tie((*scaled, conv))

time: 192 us -> 185 us (0.964)
  waiting for transfers between devices: 56.6 us -> 45.8 us
  starting transfers between devices: 68.6 us -> 77.6 us
  other arithmetic: 2.93 us -> 0.66 us
  local copies, waits for them, and re-layouts: 3.33 us -> 1.4 us
    ppermute x14, waiting for transfers between devices: 26.2 us -> 16 us  [scatter(): lax.ppermute(part, 'ctx', [(i, i ^ d) for i in ids])]
    ppermute x14, starting transfers between devices: 15.5 us -> 23.1 us  [scatter(): lax.ppermute(part, 'ctx', [(i, i ^ d) for i in ids])]
    all_to_all x2, starting transfers between devices: 19.2 us -> 25 us  [exchange(): return lax.all_to_all(parts, 'ctx', split_axis=0, concat_axis=0, tiled=True)]
    ppermute x11, starting transfers between devices: 30.2 us -> 25.7 us  [to(): return lax.ppermute(x, 'ctx', pairs)]
    ppermute x3, waiting for transfers between devices: 8.8 us -> 11.5 us  [across(): return lax.ppermute(x, 'mp', [(i, i ^ d) for i in range(4)])]
    ppermute x11, waiting for transfers between devices: 12.1 us -> 9.75 us  [to(): return lax.ppermute(x, 'ctx', pairs)]
    select_n x1 -> x0, other arithmetic: 2.31 us -> none  [lane_body(): last = lax.ppermute(jnp.where(ctx >= CHIPS, low2, high2), 'ctx', end)]
    unnamed x42 -> x28, local copies, waits for them, and re-layouts: 3.33 us -> 1.4 us
  transfers between devices with their start and end apart: 30 -> 30, of which waited for: 13 -> 12; matrix products, arithmetic and copies ran while one was open for 2% -> 0% of each run, Pallas kernels for 25% -> 25%
where the time goes in v5:
time: 185 us; the launch traced here: 184 us
  starting transfers between devices  77.6 us (42%)
  Pallas kernels  58 us (31%)
  waiting for transfers between devices  45.8 us (25%)
    ppermute x11, starting transfers between devices, to(): return lax.ppermute(x, 'ctx', pairs)  25.7 us
    all_to_all x2, starting transfers between devices, exchange(): return lax.all_to_all(parts, 'ctx', split_axis=0, concat_axis=0, tiled=True)  25 us
    ppermute x14, starting transfers between devices, scatter(): lax.ppermute(part, 'ctx', [(i, i ^ d) for i in ids])  23.1 us
    ppermute x14, waiting for transfers between devices, scatter(): lax.ppermute(part, 'ctx', [(i, i ^ d) for i in ids])  16 us
    pallas_call x2, Pallas kernels, convolve(): pl.pallas_call(functools.partial(convolve_kernel, conjugate, count), out_...  15.2 us
    ppermute x3, waiting for transfers between devices, across(): return lax.ppermute(x, 'mp', [(i, i ^ d) for i in range(4)])  11.5 us
    ppermute x11, waiting for transfers between devices, to(): return lax.ppermute(x, 'ctx', pairs)  9.75 us
    pallas_call x1, Pallas kernels, mix_late(): pl.pallas_call(late_kernel, out_shape=(sds((rows, cols), BF16),) + (sds((...  9.32 us
  transfers between devices with their start and end apart: 30, of which 12 were waited for; matrix products, arithmetic and copies ran while one was open for 0% of the time, Pallas kernels for 25%

profile of v5, /device:TPU:1, one launch (start us, length us, event | category | flops | bytes accessed | tf_op | source)
XLA Modules:
  0.0 184.4 jit_solution(13871444403442711053)
XLA Ops:
  0.6 2.2 %collective-permute-start.2 = (bf16[1024,512]{1,0:T(8,128)(2,1)}, bf16[1024,512]{1,0:T(8,128)(2,1)}, u32[]{:S(2)}, u32[]{:S(2)}) collective-permute-start(bf16[1024,512]{1,0:T(8,128)(2,1)} %refs_4_.1), channel_id=1, source_target_pairs={{0,8},{4,12},{8,0},{12,4},{16,24},{20,28},{24,16},{28,20},{1,9},{5... | collective-permute-start | bytes 3145736 | tf_op jit(solution)/shard_map/ppermute | solution.py:712
  2.8 1.7 collective-permute-start.3
  4.5 3.8 %gate.1 = bf16[8,32,16,128]{3,2,1,0:T(8,128)(2,1)} custom-call(bf16[512,1024]{1,0:T(8,128)(2,1)} %refs_9_.2, bf16[512,1024]{1,0:T(8,128)(2,1)} %refs_8_.1), custom_call_target="tpu_custom_call" | custom-call | flops 1 | bytes 3145 | tf_op jit(solution)/shard_map/gate/pallas_call | solution.py:451
  8.4 5.6 %all-to-all-start = ((bf16[8,32,16,128]{3,2,1,0:T(8,128)(2,1)}), bf16[8,32,16,128]{3,2,1,0:T(8,128)(2,1)}, u32[]{:S(2)}, u32[]{:S(2)}) async-start(bf16[8,32,16,128]{3,2,1,0:T(8,128)(2,1)} %gate.1), calls=%async_computation | async-start | bytes 2097152 | tf_op jit(solution)/shard_map/all_to_all | solution.py:696
  13.9 1.2 collective-permute-start.1
  15.2 1.2 collective-permute-start
  16.4 6.2 %filter_spectrum.1.refs_1_.refs_8_ = bf16[8320,128]{1,0:T(8,128)(2,1)} custom-call(f32[128,4096]{1,0:T(8,128)} %h_ref.1, bf16[256,128]{1,0:T(8,128)(2,1)} %constant.48.first_ref, bf16[65,64,128]{2,1,0:T(8,128)(2,1)} %constant.44.clone.fwd_ref.refs_3_.refs_10_), custom_call_target="tpu_custom_call" | custom-call | flops 1000 | bytes 8388 | tf_op jit(solution)/shard_map/filter_spectrum/pallas_call | solution.py:366
  22.6 3.4 %collective-permute-done.2.refs_6_ = bf16[1024,512]{1,0:T(8,128)(2,1)} collective-permute-done((bf16[1024,512]{1,0:T(8,128)(2,1)}, bf16[1024,512]{1,0:T(8,128)(2,1)}, u32[]{:S(2)}, u32[]{:S(2)}) %collective-permute-start.2) | collective-permute-done | bytes 1048608 | tf_op jit(solution)/shard_map/ppermute | solution.py:712
  26.0 0.0 collective-permute-done.3.refs_8_
  26.0 2.1 %collective-permute-start.4 = (bf16[1024,512]{1,0:T(8,128)(2,1)}, bf16[1024,512]{1,0:T(8,128)(2,1)}, u32[]{:S(2)}, u32[]{:S(2)}) collective-permute-start(bf16[1024,512]{1,0:T(8,128)(2,1)} %collective-permute-done.2.refs_6_), channel_id=1, source_target_pairs={{0,4},{4,0},{8,12},{12,8},{16,20},{20,16},{24,28},{28,24},{1,5},{5... | collective-permute-start | bytes 3145736 | tf_op jit(solution)/shard_map/ppermute | solution.py:712
  28.1 1.6 collective-permute-start.5
  29.7 1.6 collective-permute-start.7
  31.3 7.7 %collective-permute-done.1.refs_2_ = bf16[512,1024]{1,0:T(8,128)(2,1)} collective-permute-done((bf16[512,1024]{1,0:T(8,128)(2,1)}, bf16[512,1024]{1,0:T(8,128)(2,1)}, u32[]{:S(2)}, u32[]{:S(2)}) %collective-permute-start.1) | collective-permute-done | bytes 1048608 | tf_op jit(solution)/shard_map/ppermute | solution.py:725
  39.1 0.9 collective-permute-done.refs_1_
  40.0 1.3 collective-permute-start.6
  41.3 1.2 collective-permute-start.12
  42.5 1.3 collective-permute-start.9
  43.8 8.6 %all-to-all-done.refs_0_ = bf16[8,32,16,128]{3,2,1,0:T(8,128)(2,1)} async-done(((bf16[8,32,16,128]{3,2,1,0:T(8,128)(2,1)}), bf16[8,32,16,128]{3,2,1,0:T(8,128)(2,1)}, u32[]{:S(2)}, u32[]{:S(2)}) %all-to-all-start) | async-done | bytes 1048608 | tf_op jit(solution)/shard_map/all_to_all | solution.py:696
  52.4 7.6 %convolve.2 = (bf16[8,32,16,128]{3,2,1,0:T(8,128)(2,1)}, bf16[8320,128]{1,0:T(8,128)(2,1)}) custom-call(s32[1]{0:T(128)} %constant.42.clone.1.place_ref, bf16[8,32,16,128]{3,2,1,0:T(8,128)(2,1)} %all-to-all-done.refs_0_, bf16[8320,128]{1,0:T(8,128)(2,1)} %filter_spectrum.1.refs_1_.refs_8_, bf16[9,256,128]{2,1,0:T(8,128)(2,1)} %constant.43.clone.refs_2_.refs_9_, ...), custom_call_target="tpu_custom_call" | custom-call | flops 2000 | bytes 14680 | tf_op jit(solution)/shard_map/convolve/pallas_call | solution.py:391
  60.0 0.0 collective-permute-done.7.refs_4_
  60.0 1.3 collective-permute-start.11
  61.3 0.7 pad_add_fusion.place_ref
  62.0 2.8 %collective-permute-done.6.refs_3_ = bf16[512,1024]{1,0:T(8,128)(2,1)} collective-permute-done((bf16[512,1024]{1,0:T(8,128)(2,1)}, bf16[512,1024]{1,0:T(8,128)(2,1)}, u32[]{:S(2)}, u32[]{:S(2)}) %collective-permute-start.6) | collective-permute-done | bytes 1048608 | tf_op jit(solution)/shard_map/ppermute | solution.py:725
  64.8 8.4 %terms.1.refs_10_ = f32[512,1024]{1,0:T(8,128)} custom-call(s32[4]{0:T(128)} %pad_add_fusion.place_ref, bf16[512,1024]{1,0:T(8,128)(2,1)} %refs_0_.3, bf16[512,1024]{1,0:T(8,128)(2,1)} %collective-permute-done.refs_1_, bf16[512,1024]{1,0:T(8,128)(2,1)} %collective-permute-done.1.refs_2_, bf16[512,1024]{1,0:T(8,128)(2,1)} %collective-permute-done.6.refs_3_, ...), custom_call_target="tpu_custom_call" | custom-call | flops 2000 | bytes 14680 | tf_op jit(solution)/shard_map/terms/pallas_call | solution.py:524
  73.1 19.4 %all-to-all-start.1 = ((bf16[8,32,16,128]{3,2,1,0:T(8,128)(2,1)}), bf16[8,32,16,128]{3,2,1,0:T(8,128)(2,1)}, u32[]{:S(2)}, u32[]{:S(2)}) async-start(bf16[8,32,16,128]{3,2,1,0:T(8,128)(2,1)} %get-tuple-element.59), calls=%async_computation.1 | async-start | bytes 2097152 | tf_op jit(solution)/shard_map/all_to_all | solution.py:696
  92.5 1.6 collective-permute-start.8
  94.2 1.9 %collective-permute-start.10 = (bf16[1024,512]{1,0:T(8,128)(2,1)}, bf16[1024,512]{1,0:T(8,128)(2,1)}, u32[]{:S(2)}, u32[]{:S(2)}) collective-permute-start(bf16[1024,512]{1,0:T(8,128)(2,1)} %collective-permute-done.9.refs_6_), channel_id=1, source_target_pairs={{0,4},{4,0},{24,28},{28,24},{1,5},{5,1},{25,29},{29,25},{2,6},{6,2... | collective-permute-start | bytes 3145736 | tf_op jit(solution)/shard_map/ppermute | solution.py:712
  96.1 3.9 %collective-permute-done.11.refs_8_ = bf16[1024,512]{1,0:T(8,128)(2,1)} collective-permute-done((bf16[1024,512]{1,0:T(8,128)(2,1)}, bf16[1024,512]{1,0:T(8,128)(2,1)}, u32[]{:S(2)}, u32[]{:S(2)}) %collective-permute-start.11) | collective-permute-done | bytes 1048608 | tf_op jit(solution)/shard_map/ppermute | solution.py:712
  100.0 9.2 %collective-permute-start.13 = (bf16[1024,512]{1,0:T(8,128)(2,1)}, bf16[1024,512]{1,0:T(8,128)(2,1)}, u32[]{:S(2)}, u32[]{:S(2)}) collective-permute-start(bf16[1024,512]{1,0:T(8,128)(2,1)} %collective-permute-done.11.refs_8_), channel_id=1, source_target_pairs={{0,4},{4,0},{24,28},{28,24},{1,5},{5,1},{25,29},{29,25},{2,6},{6,2... | collective-permute-start | bytes 3145736 | tf_op jit(solution)/shard_map/ppermute | solution.py:712
  109.1 0.0 collective-permute-done.10.refs_7_
  109.1 0.0 collective-permute-done.8.refs_5_
  109.2 2.4 %collective-permute-done.13.refs_9_ = bf16[1024,512]{1,0:T(8,128)(2,1)} collective-permute-done((bf16[1024,512]{1,0:T(8,128)(2,1)}, bf16[1024,512]{1,0:T(8,128)(2,1)}, u32[]{:S(2)}, u32[]{:S(2)}) %collective-permute-start.13) | collective-permute-done | bytes 1048608 | tf_op jit(solution)/shard_map/ppermute | solution.py:712
  111.6 9.3 %mix_late.1 = (bf16[512,1024]{1,0:T(8,128)(2,1)}, bf16[32,16,128]{2,1,0:T(8,128)(2,1)}, bf16[32,16,128]{2,1,0:T(8,128)(2,1)}, bf16[32,16,128]{2,1,0:T(8,128)(2,1...) custom-call(s32[4]{0:T(128)} %pad_add_fusion.place_ref, ...), custom_call_target="tpu_custom_call" | custom-call | flops 1000 | bytes 8388 | tf_op jit(solution)/shard_map/mix_late/pallas_call | solution.py:605
  120.9 5.0 %collective-permute-start.14 = (bf16[32,16,128]{2,1,0:T(8,128)(2,1)}, bf16[32,16,128]{2,1,0:T(8,128)(2,1)S(1)}, u32[]{:S(2)}, u32[]{:S(2)}) collective-permute-start(bf16[32,16,128]{2,1,0:T(8,128)(2,1)} %get-tuple-element.51), channel_id=1, source_target_pairs={{0,24},{4,28},{8,16},{12,20},{16,8},{20,12},{24,0},{28,4},{1,25},{... | collective-permute-start | bytes 393224 | tf_op jit(solution)/shard_map/ppermute | solution.py:701
  125.9 0.0 collective-permute-start.15
  125.9 0.4 collective-permute-start.16
  126.3 4.3 %collective-permute-start.17 = (bf16[32,16,128]{2,1,0:T(8,128)(2,1)}, bf16[32,16,128]{2,1,0:T(8,128)(2,1)S(1)}, u32[]{:S(2)}, u32[]{:S(2)}) collective-permute-start(bf16[32,16,128]{2,1,0:T(8,128)(2,1)} %get-tuple-element.54), channel_id=1, source_target_pairs={{0,28},{4,24},{8,20},{12,16},{16,12},{20,8},{24,4},{28,0},{1,29},{... | collective-permute-start | bytes 393224 | tf_op jit(solution)/shard_map/ppermute | solution.py:701
  130.5 0.0 collective-permute-start.18
  130.6 0.0 collective-permute-done.14.refs_0_
  130.6 0.4 collective-permute-start.19
  130.9 5.2 %collective-permute-done.15.refs_1_ = bf16[32,16,128]{2,1,0:T(8,128)(2,1)S(1)} collective-permute-done((bf16[32,16,128]{2,1,0:T(8,128)(2,1)}, bf16[32,16,128]{2,1,0:T(8,128)(2,1)S(1)}, u32[]{:S(2)}, u32[]{:S(2)}) %collective-permute-start.15) | collective-permute-done | bytes 131104 | tf_op jit(solution)/shard_map/ppermute | solution.py:701
  136.1 5.4 %collective-permute-start.20 = (bf16[32,16,128]{2,1,0:T(8,128)(2,1)}, bf16[32,16,128]{2,1,0:T(8,128)(2,1)S(1)}, u32[]{:S(2)}, u32[]{:S(2)}) collective-permute-start(bf16[32,16,128]{2,1,0:T(8,128)(2,1)} %get-tuple-element.57), channel_id=1, source_target_pairs={{0,4},{4,0},{8,12},{12,8},{16,20},{20,16},{24,28},{28,24},{1,5},{5... | collective-permute-start | bytes 393224 | tf_op jit(solution)/shard_map/ppermute | solution.py:701
  141.5 0.0 collective-permute-done.16.refs_2_
  141.5 0.0 collective-permute-done.17.refs_3_
  141.6 5.4 %collective-permute-done.18.refs_4_ = bf16[32,16,128]{2,1,0:T(8,128)(2,1)S(1)} collective-permute-done((bf16[32,16,128]{2,1,0:T(8,128)(2,1)}, bf16[32,16,128]{2,1,0:T(8,128)(2,1)S(1)}, u32[]{:S(2)}, u32[]{:S(2)}) %collective-permute-start.18) | collective-permute-done | bytes 131104 | tf_op jit(solution)/shard_map/ppermute | solution.py:701
  147.0 0.0 collective-permute-done.19.refs_5_
  147.0 0.6 copy-done.4
  147.6 0.1 copy-done.5
  147.7 0.0 copy-done.6
  147.7 7.6 %convolve.3 = (bf16[32,16,128]{2,1,0:T(8,128)(2,1)}, bf16[32,16,128]{2,1,0:T(8,128)(2,1)}, bf16[32,16,128]{2,1,0:T(8,128)(2,1)}, bf16[32,16,128]{2,1,0:T(8,128)(...) custom-call(s32[1]{0:T(128)} %bitcast.3.place_ref, ...), custom_call_target="tpu_custom_call" | custom-call | flops 2000 | bytes 14680 | tf_op jit(solution)/shard_map/convolve/pallas_call | solution.py:391
  155.4 2.3 %collective-permute-start.21 = (bf16[32,16,128]{2,1,0:T(8,128)(2,1)}, bf16[32,16,128]{2,1,0:T(8,128)(2,1)S(1)}, u32[]{:S(2)}, u32[]{:S(2)}) collective-permute-start(bf16[32,16,128]{2,1,0:T(8,128)(2,1)} %get-tuple-element.70), channel_id=1, source_target_pairs={{0,24},{4,28},{8,16},{12,20},{16,8},{20,12},{24,0},{28,4},{1,25},{... | collective-permute-start | bytes 393224 | tf_op jit(solution)/shard_map/ppermute | solution.py:701
  157.7 1.8 collective-permute-start.23
  159.5 1.0 collective-permute-start.24
  160.4 0.2 collective-permute-start.25
  160.7 1.5 collective-permute-done.21.refs_0_
  162.1 1.8 collective-permute-start.26
  163.9 1.9 %collective-permute-done.22.refs_1_ = bf16[32,16,128]{2,1,0:T(8,128)(2,1)S(1)} collective-permute-done((bf16[32,16,128]{2,1,0:T(8,128)(2,1)}, bf16[32,16,128]{2,1,0:T(8,128)(2,1)S(1)}, u32[]{:S(2)}, u32[]{:S(2)}) %collective-permute-start.22) | collective-permute-done | bytes 131104 | tf_op jit(solution)/shard_map/ppermute | solution.py:701
  165.8 0.6 collective-permute-start.27
  166.4 3.8 %finish_whole.1 = bf16[512,1024]{1,0:T(8,128)(2,1)} custom-call(bf16[8,32,16,128]{3,2,1,0:T(8,128)(2,1)} %all-to-all-done.1.part_ref, bf16[512,1024]{1,0:T(8,128)(2,1)} %get-tuple-element.61.factor_ref), custom_call_target="tpu_custom_call" | custom-call | flops 1 | bytes 3145 | tf_op jit(solution)/shard_map/finish_whole/pallas_call | solution.py:682
  170.2 7.3 %filter_gradient.1 = f32[128,4096]{1,0:T(8,128)} custom-call(bf16[8320,128]{1,0:T(8,128)(2,1)} %get-tuple-element.80.s_ref, bf16[8320,128]{1,0:T(8,128)(2,1)} %get-tuple-element.81.g_ref, bf16[65,64,128]{2,1,0:T(8,128)(2,1)} %constant.45.clone.refs_4_.refs_11_.inv_ref, bf16[128,256]{1,0:T(8,128)(2,1)} %constant.50.last_ref), custom_call_target="tpu_custom_call" | custom-call | flops 1000 | bytes 12582 | tf_op jit(solution)/shard_map/filter_gradient/pallas_call | solution.py:419
  177.6 2.1 %collective-permute-done.26.refs_5_ = bf16[32,16,128]{2,1,0:T(8,128)(2,1)S(1)} collective-permute-done((bf16[32,16,128]{2,1,0:T(8,128)(2,1)}, bf16[32,16,128]{2,1,0:T(8,128)(2,1)S(1)}, u32[]{:S(2)}, u32[]{:S(2)}) %collective-permute-start.26) | collective-permute-done | bytes 131104 | tf_op jit(solution)/shard_map/ppermute | solution.py:701
  179.7 0.6 copy-done.12
  180.3 0.1 copy-done.13
  180.4 4.0 %finish.1 = (bf16[512,1024]{1,0:T(8,128)(2,1)}, bf16[512,1024]{1,0:T(8,128)(2,1)}) custom-call(s32[4]{0:T(128)} %pad_add_fusion.place_ref, bf16[32,16,128]{2,1,0:T(8,128)(2,1)} %copy-done.7, bf16[32,16,128]{2,1,0:T(8,128)(2,1)} %copy-done.8, bf16[32,16,128]{2,1,0:T(8,128)(2,1)} %copy-done.9, bf16[32,16,128]{2,1,0:T(8,128)(2,1)} %copy-done.10, ...), custom_call_target="tpu_custom_call" | custom-call | flops 1 | bytes 5242 | tf_op jit(solution)/shard_map/finish/pallas_call | solution.py:653
  (34 shorter events, 0.1 us)
Async XLA Ops:
  0.6 25.4 %collective-permute-start.2 = (bf16[1024,512]{1,0:T(8,128)(2,1)}, bf16[1024,512]{1,0:T(8,128)(2,1)}, u32[]{:S(2)}, u32[]{:S(2)}) collective-permute-start(bf16[1024,512]{1,0:T(8,128)(2,1)} %refs_4_.1), channel_id=1, source_target_pairs={{0,8},{4,12},{8,0},{12,4},{16,24},{20,28},{24,16},{28,20},{1,9},{5... | collective-permute-start | bytes 3145736 | tf_op jit(solution)/shard_map/ppermute | solution.py:712
  2.8 23.2 %collective-permute-start.3 = (bf16[1024,512]{1,0:T(8,128)(2,1)}, bf16[1024,512]{1,0:T(8,128)(2,1)}, u32[]{:S(2)}, u32[]{:S(2)}) collective-permute-start(bf16[1024,512]{1,0:T(8,128)(2,1)} %refs_4_.1), channel_id=1, source_target_pairs={{8,16},{12,20},{16,8},{20,12},{9,17},{13,21},{17,9},{21,13},{10,18... | collective-permute-start | bytes 3145736 | tf_op jit(solution)/shard_map/ppermute | solution.py:712
  8.4 44.0 %all-to-all-start = ((bf16[8,32,16,128]{3,2,1,0:T(8,128)(2,1)}), bf16[8,32,16,128]{3,2,1,0:T(8,128)(2,1)}, u32[]{:S(2)}, u32[]{:S(2)}) async-start(bf16[8,32,16,128]{3,2,1,0:T(8,128)(2,1)} %gate.1), calls=%async_computation | async-start | bytes 2097152 | tf_op jit(solution)/shard_map/all_to_all | solution.py:696
  13.9 25.1 %collective-permute-start.1 = (bf16[512,1024]{1,0:T(8,128)(2,1)}, bf16[512,1024]{1,0:T(8,128)(2,1)}, u32[]{:S(2)}, u32[]{:S(2)}) collective-permute-start(bf16[512,1024]{1,0:T(8,128)(2,1)} %refs_0_.3), channel_id=1, source_target_pairs={{0,2},{1,3},{2,0},{3,1},{4,6},{5,7},{6,4},{7,5},{8,10},{9,11},{10,... | collective-permute-start | bytes 3145736 | tf_op jit(solution)/shard_map/ppermute | solution.py:725
  15.2 24.8 %collective-permute-start = (bf16[512,1024]{1,0:T(8,128)(2,1)}, bf16[512,1024]{1,0:T(8,128)(2,1)}, u32[]{:S(2)}, u32[]{:S(2)}) collective-permute-start(bf16[512,1024]{1,0:T(8,128)(2,1)} %refs_0_.3), channel_id=1, source_target_pairs={{0,1},{1,0},{2,3},{3,2},{4,5},{5,4},{6,7},{7,6},{8,9},{9,8},{10,11... | collective-permute-start | bytes 3145736 | tf_op jit(solution)/shard_map/ppermute | solution.py:725
  26.0 14.0 %collective-permute-start.4 = (bf16[1024,512]{1,0:T(8,128)(2,1)}, bf16[1024,512]{1,0:T(8,128)(2,1)}, u32[]{:S(2)}, u32[]{:S(2)}) collective-permute-start(bf16[1024,512]{1,0:T(8,128)(2,1)} %collective-permute-done.2.refs_6_), channel_id=1, source_target_pairs={{0,4},{4,0},{8,12},{12,8},{16,20},{20,16},{24,28},{28,24},{1,5},{5... | collective-permute-start | bytes 3145736 | tf_op jit(solution)/shard_map/ppermute | solution.py:712
  28.1 11.9 %collective-permute-start.5 = (bf16[1024,512]{1,0:T(8,128)(2,1)}, bf16[1024,512]{1,0:T(8,128)(2,1)}, u32[]{:S(2)}, u32[]{:S(2)}) collective-permute-start(bf16[1024,512]{1,0:T(8,128)(2,1)} %collective-permute-done.3.refs_8_), channel_id=1, source_target_pairs={{8,12},{12,8},{16,20},{20,16},{9,13},{13,9},{17,21},{21,17},{10,14... | collective-permute-start | bytes 3145736 | tf_op jit(solution)/shard_map/ppermute | solution.py:712
  29.7 30.3 %collective-permute-start.7 = (bf16[1024,512]{1,0:T(8,128)(2,1)}, bf16[1024,512]{1,0:T(8,128)(2,1)}, u32[]{:S(2)}, u32[]{:S(2)}) collective-permute-start(bf16[1024,512]{1,0:T(8,128)(2,1)} %collective-permute-done.2.refs_6_), channel_id=1, source_target_pairs={{8,16},{12,20},{16,8},{20,12},{9,17},{13,21},{17,9},{21,13},{10,18... | collective-permute-start | bytes 3145736 | tf_op jit(solution)/shard_map/ppermute | solution.py:712
  40.0 24.8 %collective-permute-start.6 = (bf16[512,1024]{1,0:T(8,128)(2,1)}, bf16[512,1024]{1,0:T(8,128)(2,1)}, u32[]{:S(2)}, u32[]{:S(2)}) collective-permute-start(bf16[512,1024]{1,0:T(8,128)(2,1)} %refs_0_.3), channel_id=1, source_target_pairs={{0,3},{1,2},{2,1},{3,0},{4,7},{5,6},{6,5},{7,4},{8,11},{9,10},{10,... | collective-permute-start | bytes 3145736 | tf_op jit(solution)/shard_map/ppermute | solution.py:725
  41.3 23.5 %collective-permute-start.12 = (bf16[1024,512]{1,0:T(8,128)(2,1)}, bf16[1024,512]{1,0:T(8,128)(2,1)}, u32[]{:S(2)}, u32[]{:S(2)}) collective-permute-start(bf16[1024,512]{1,0:T(8,128)(2,1)} %refs_4_.1), channel_id=1, source_target_pairs={{0,4},{4,0},{8,12},{12,8},{16,20},{20,16},{24,28},{28,24},{1,5},{5... | collective-permute-start | bytes 3145736 | tf_op jit(solution)/shard_map/ppermute | solution.py:712
  42.5 51.6 %collective-permute-start.9 = (bf16[1024,512]{1,0:T(8,128)(2,1)}, bf16[1024,512]{1,0:T(8,128)(2,1)}, u32[]{:S(2)}, u32[]{:S(2)}) collective-permute-start(bf16[1024,512]{1,0:T(8,128)(2,1)} %collective-permute-done.3.refs_8_), channel_id=1, source_target_pairs={{8,0},{12,4},{16,24},{20,28},{9,1},{13,5},{17,25},{21,29},{10,2},{... | collective-permute-start | bytes 3145736 | tf_op jit(solution)/shard_map/ppermute | solution.py:712
  60.0 40.0 %collective-permute-start.11 = (bf16[1024,512]{1,0:T(8,128)(2,1)}, bf16[1024,512]{1,0:T(8,128)(2,1)}, u32[]{:S(2)}, u32[]{:S(2)}) collective-permute-start(bf16[1024,512]{1,0:T(8,128)(2,1)} %collective-permute-done.7.refs_4_), channel_id=1, source_target_pairs={{8,0},{12,4},{16,24},{20,28},{9,1},{13,5},{17,25},{21,29},{10,2},{... | collective-permute-start | bytes 3145736 | tf_op jit(solution)/shard_map/ppermute | solution.py:712
  73.1 73.8 %all-to-all-start.1 = ((bf16[8,32,16,128]{3,2,1,0:T(8,128)(2,1)}), bf16[8,32,16,128]{3,2,1,0:T(8,128)(2,1)}, u32[]{:S(2)}, u32[]{:S(2)}) async-start(bf16[8,32,16,128]{3,2,1,0:T(8,128)(2,1)} %get-tuple-element.59), calls=%async_computation.1 | async-start | bytes 2097152 | tf_op jit(solution)/shard_map/all_to_all | solution.py:696
  92.5 16.6 %collective-permute-start.8 = (bf16[1024,512]{1,0:T(8,128)(2,1)}, bf16[1024,512]{1,0:T(8,128)(2,1)}, u32[]{:S(2)}, u32[]{:S(2)}) collective-permute-start(bf16[1024,512]{1,0:T(8,128)(2,1)} %collective-permute-done.7.refs_4_), channel_id=1, source_target_pairs={{8,12},{12,8},{16,20},{20,16},{9,13},{13,9},{17,21},{21,17},{10,14... | collective-permute-start | bytes 3145736 | tf_op jit(solution)/shard_map/ppermute | solution.py:712
  94.2 15.0 %collective-permute-start.10 = (bf16[1024,512]{1,0:T(8,128)(2,1)}, bf16[1024,512]{1,0:T(8,128)(2,1)}, u32[]{:S(2)}, u32[]{:S(2)}) collective-permute-start(bf16[1024,512]{1,0:T(8,128)(2,1)} %collective-permute-done.9.refs_6_), channel_id=1, source_target_pairs={{0,4},{4,0},{24,28},{28,24},{1,5},{5,1},{25,29},{29,25},{2,6},{6,2... | collective-permute-start | bytes 3145736 | tf_op jit(solution)/shard_map/ppermute | solution.py:712
  100.0 11.6 %collective-permute-start.13 = (bf16[1024,512]{1,0:T(8,128)(2,1)}, bf16[1024,512]{1,0:T(8,128)(2,1)}, u32[]{:S(2)}, u32[]{:S(2)}) collective-permute-start(bf16[1024,512]{1,0:T(8,128)(2,1)} %collective-permute-done.11.refs_8_), channel_id=1, source_target_pairs={{0,4},{4,0},{24,28},{28,24},{1,5},{5,1},{25,29},{29,25},{2,6},{6,2... | collective-permute-start | bytes 3145736 | tf_op jit(solution)/shard_map/ppermute | solution.py:712
  120.9 9.7 %collective-permute-start.14 = (bf16[32,16,128]{2,1,0:T(8,128)(2,1)}, bf16[32,16,128]{2,1,0:T(8,128)(2,1)S(1)}, u32[]{:S(2)}, u32[]{:S(2)}) collective-permute-start(bf16[32,16,128]{2,1,0:T(8,128)(2,1)} %get-tuple-element.51), channel_id=1, source_target_pairs={{0,24},{4,28},{8,16},{12,20},{16,8},{20,12},{24,0},{28,4},{1,25},{... | collective-permute-start | bytes 393224 | tf_op jit(solution)/shard_map/ppermute | solution.py:701
  125.9 10.2 %collective-permute-start.15 = (bf16[32,16,128]{2,1,0:T(8,128)(2,1)}, bf16[32,16,128]{2,1,0:T(8,128)(2,1)S(1)}, u32[]{:S(2)}, u32[]{:S(2)}) collective-permute-start(bf16[32,16,128]{2,1,0:T(8,128)(2,1)} %get-tuple-element.52), channel_id=1, source_target_pairs={{0,16},{4,20},{8,24},{12,28},{16,0},{20,4},{24,8},{28,12},{1,17},{... | collective-permute-start | bytes 393224 | tf_op jit(solution)/shard_map/ppermute | solution.py:701
  125.9 15.6 %collective-permute-start.16 = (bf16[32,16,128]{2,1,0:T(8,128)(2,1)}, bf16[32,16,128]{2,1,0:T(8,128)(2,1)S(1)}, u32[]{:S(2)}, u32[]{:S(2)}) collective-permute-start(bf16[32,16,128]{2,1,0:T(8,128)(2,1)} %get-tuple-element.53), channel_id=1, source_target_pairs={{0,8},{4,12},{8,0},{12,4},{16,24},{20,28},{24,16},{28,20},{1,9},{5... | collective-permute-start | bytes 393224 | tf_op jit(solution)/shard_map/ppermute | solution.py:701
  126.3 15.3 %collective-permute-start.17 = (bf16[32,16,128]{2,1,0:T(8,128)(2,1)}, bf16[32,16,128]{2,1,0:T(8,128)(2,1)S(1)}, u32[]{:S(2)}, u32[]{:S(2)}) collective-permute-start(bf16[32,16,128]{2,1,0:T(8,128)(2,1)} %get-tuple-element.54), channel_id=1, source_target_pairs={{0,28},{4,24},{8,20},{12,16},{16,12},{20,8},{24,4},{28,0},{1,29},{... | collective-permute-start | bytes 393224 | tf_op jit(solution)/shard_map/ppermute | solution.py:701
  130.5 16.4 %collective-permute-start.18 = (bf16[32,16,128]{2,1,0:T(8,128)(2,1)}, bf16[32,16,128]{2,1,0:T(8,128)(2,1)S(1)}, u32[]{:S(2)}, u32[]{:S(2)}) collective-permute-start(bf16[32,16,128]{2,1,0:T(8,128)(2,1)} %get-tuple-element.55), channel_id=1, source_target_pairs={{0,20},{4,16},{8,28},{12,24},{16,4},{20,0},{24,12},{28,8},{1,21},{... | collective-permute-start | bytes 393224 | tf_op jit(solution)/shard_map/ppermute | solution.py:701
  130.6 16.4 %copy-start = (bf16[32,16,128]{2,1,0:T(8,128)(2,1)}, bf16[32,16,128]{2,1,0:T(8,128)(2,1)S(1)}, u32[]{:S(2)}) copy-start(bf16[32,16,128]{2,1,0:T(8,128)(2,1)S(1)} %collective-permute-done.14.refs_0_) | copy-start | bytes 393220
  130.6 16.4 %collective-permute-start.19 = (bf16[32,16,128]{2,1,0:T(8,128)(2,1)}, bf16[32,16,128]{2,1,0:T(8,128)(2,1)S(1)}, u32[]{:S(2)}, u32[]{:S(2)}) collective-permute-start(bf16[32,16,128]{2,1,0:T(8,128)(2,1)} %get-tuple-element.56), channel_id=1, source_target_pairs={{0,12},{4,8},{8,4},{12,0},{16,28},{20,24},{24,20},{28,16},{1,13},{... | collective-permute-start | bytes 393224 | tf_op jit(solution)/shard_map/ppermute | solution.py:701
  136.1 10.9 %copy-start.1 = (bf16[32,16,128]{2,1,0:T(8,128)(2,1)}, bf16[32,16,128]{2,1,0:T(8,128)(2,1)S(1)}, u32[]{:S(2)}) copy-start(bf16[32,16,128]{2,1,0:T(8,128)(2,1)S(1)} %collective-permute-done.15.refs_1_) | copy-start | bytes 393220
  136.1 10.9 %collective-permute-start.20 = (bf16[32,16,128]{2,1,0:T(8,128)(2,1)}, bf16[32,16,128]{2,1,0:T(8,128)(2,1)S(1)}, u32[]{:S(2)}, u32[]{:S(2)}) collective-permute-start(bf16[32,16,128]{2,1,0:T(8,128)(2,1)} %get-tuple-element.57), channel_id=1, source_target_pairs={{0,4},{4,0},{8,12},{12,8},{16,20},{20,16},{24,28},{28,24},{1,5},{5... | collective-permute-start | bytes 393224 | tf_op jit(solution)/shard_map/ppermute | solution.py:701
  141.5 5.5 %copy-start.2 = (bf16[32,16,128]{2,1,0:T(8,128)(2,1)}, bf16[32,16,128]{2,1,0:T(8,128)(2,1)S(1)}, u32[]{:S(2)}) copy-start(bf16[32,16,128]{2,1,0:T(8,128)(2,1)S(1)} %collective-permute-done.16.refs_2_) | copy-start | bytes 393220
  141.5 5.5 %copy-start.3 = (bf16[32,16,128]{2,1,0:T(8,128)(2,1)}, bf16[32,16,128]{2,1,0:T(8,128)(2,1)S(1)}, u32[]{:S(2)}) copy-start(bf16[32,16,128]{2,1,0:T(8,128)(2,1)S(1)} %collective-permute-done.17.refs_3_) | copy-start | bytes 393220
  147.0 0.7 copy-start.4
  147.0 0.7 copy-start.5
  147.0 0.7 copy-start.6
  155.4 6.8 %collective-permute-start.21 = (bf16[32,16,128]{2,1,0:T(8,128)(2,1)}, bf16[32,16,128]{2,1,0:T(8,128)(2,1)S(1)}, u32[]{:S(2)}, u32[]{:S(2)}) collective-permute-start(bf16[32,16,128]{2,1,0:T(8,128)(2,1)} %get-tuple-element.70), channel_id=1, source_target_pairs={{0,24},{4,28},{8,16},{12,20},{16,8},{20,12},{24,0},{28,4},{1,25},{... | collective-permute-start | bytes 393224 | tf_op jit(solution)/shard_map/ppermute | solution.py:701
  157.7 8.1 %collective-permute-start.22 = (bf16[32,16,128]{2,1,0:T(8,128)(2,1)}, bf16[32,16,128]{2,1,0:T(8,128)(2,1)S(1)}, u32[]{:S(2)}, u32[]{:S(2)}) collective-permute-start(bf16[32,16,128]{2,1,0:T(8,128)(2,1)} %get-tuple-element.71), channel_id=1, source_target_pairs={{0,8},{4,12},{8,0},{12,4},{16,24},{20,28},{24,16},{28,20},{1,9},{5... | collective-permute-start | bytes 393224 | tf_op jit(solution)/shard_map/ppermute | solution.py:701
  157.7 19.9 %collective-permute-start.23 = (bf16[32,16,128]{2,1,0:T(8,128)(2,1)}, bf16[32,16,128]{2,1,0:T(8,128)(2,1)S(1)}, u32[]{:S(2)}, u32[]{:S(2)}) collective-permute-start(bf16[32,16,128]{2,1,0:T(8,128)(2,1)} %get-tuple-element.72), channel_id=1, source_target_pairs={{0,12},{4,8},{8,4},{12,0},{16,28},{20,24},{24,20},{28,16},{1,13},{... | collective-permute-start | bytes 393224 | tf_op jit(solution)/shard_map/ppermute | solution.py:701
  159.5 18.1 %collective-permute-start.24 = (bf16[32,16,128]{2,1,0:T(8,128)(2,1)}, bf16[32,16,128]{2,1,0:T(8,128)(2,1)S(1)}, u32[]{:S(2)}, u32[]{:S(2)}) collective-permute-start(bf16[32,16,128]{2,1,0:T(8,128)(2,1)} %get-tuple-element.73), channel_id=1, source_target_pairs={{0,28},{4,24},{8,20},{12,16},{16,12},{20,8},{24,4},{28,0},{1,29},{... | collective-permute-start | bytes 393224 | tf_op jit(solution)/shard_map/ppermute | solution.py:701
  160.4 17.1 %collective-permute-start.25 = (bf16[32,16,128]{2,1,0:T(8,128)(2,1)}, bf16[32,16,128]{2,1,0:T(8,128)(2,1)S(1)}, u32[]{:S(2)}, u32[]{:S(2)}) collective-permute-start(bf16[32,16,128]{2,1,0:T(8,128)(2,1)} %get-tuple-element.74), channel_id=1, source_target_pairs={{0,16},{4,20},{8,24},{12,28},{16,0},{20,4},{24,8},{28,12},{1,17},{... | collective-permute-start | bytes 393224 | tf_op jit(solution)/shard_map/ppermute | solution.py:701
  162.1 15.4 %copy-start.7 = (bf16[32,16,128]{2,1,0:T(8,128)(2,1)}, bf16[32,16,128]{2,1,0:T(8,128)(2,1)S(1)}, u32[]{:S(2)}) copy-start(bf16[32,16,128]{2,1,0:T(8,128)(2,1)S(1)} %collective-permute-done.21.refs_0_) | copy-start | bytes 393220
  162.1 17.6 %collective-permute-start.26 = (bf16[32,16,128]{2,1,0:T(8,128)(2,1)}, bf16[32,16,128]{2,1,0:T(8,128)(2,1)S(1)}, u32[]{:S(2)}, u32[]{:S(2)}) collective-permute-start(bf16[32,16,128]{2,1,0:T(8,128)(2,1)} %get-tuple-element.75), channel_id=1, source_target_pairs={{0,20},{4,16},{8,28},{12,24},{16,4},{20,0},{24,12},{28,8},{1,21},{... | collective-permute-start | bytes 393224 | tf_op jit(solution)/shard_map/ppermute | solution.py:701
  165.8 11.7 %copy-start.8 = (bf16[32,16,128]{2,1,0:T(8,128)(2,1)}, bf16[32,16,128]{2,1,0:T(8,128)(2,1)S(1)}, u32[]{:S(2)}) copy-start(bf16[32,16,128]{2,1,0:T(8,128)(2,1)S(1)} %collective-permute-done.22.refs_1_) | copy-start | bytes 393220
  165.8 13.9 %collective-permute-start.27 = (bf16[32,16,128]{2,1,0:T(8,128)(2,1)}, bf16[32,16,128]{2,1,0:T(8,128)(2,1)S(1)}, u32[]{:S(2)}, u32[]{:S(2)}) collective-permute-start(bf16[32,16,128]{2,1,0:T(8,128)(2,1)} %get-tuple-element.76), channel_id=1, source_target_pairs={{0,4},{4,0},{8,12},{12,8},{16,20},{20,16},{24,28},{28,24},{1,5},{5... | collective-permute-start | bytes 393224 | tf_op jit(solution)/shard_map/ppermute | solution.py:701
  177.5 2.2 %copy-start.9 = (bf16[32,16,128]{2,1,0:T(8,128)(2,1)}, bf16[32,16,128]{2,1,0:T(8,128)(2,1)S(1)}, u32[]{:S(2)}) copy-start(bf16[32,16,128]{2,1,0:T(8,128)(2,1)S(1)} %collective-permute-done.23.refs_2_) | copy-start | bytes 393220
  177.6 2.2 %copy-start.10 = (bf16[32,16,128]{2,1,0:T(8,128)(2,1)}, bf16[32,16,128]{2,1,0:T(8,128)(2,1)S(1)}, u32[]{:S(2)}) copy-start(bf16[32,16,128]{2,1,0:T(8,128)(2,1)S(1)} %collective-permute-done.24.refs_3_) | copy-start | bytes 393220
  177.6 2.1 %copy-start.11 = (bf16[32,16,128]{2,1,0:T(8,128)(2,1)}, bf16[32,16,128]{2,1,0:T(8,128)(2,1)S(1)}, u32[]{:S(2)}) copy-start(bf16[32,16,128]{2,1,0:T(8,128)(2,1)S(1)} %collective-permute-done.25.refs_4_) | copy-start | bytes 393220
  179.7 0.6 copy-start.12
  179.7 0.7 copy-start.13

commit v6 on v5

--- a/solution.py
+++ b/solution.py
@@ -138,9 +138,11 @@
 HOMEWARD = (6, 2, 3, 7, 4, 5, 1, 0)
 F32, BF16 = jnp.float32, jnp.bfloat16
 PARAMS = pltpu.CompilerParams(vmem_limit_bytes=63 * 2**20)
+SMALL = pltpu.CompilerParams(vmem_limit_bytes=52 * 2**20)
 VM = pl.BlockSpec(memory_space=pltpu.VMEM)
 ANY = pl.BlockSpec(memory_space=pl.ANY)
-U1, U2 = 16, 32
+HBM = pl.BlockSpec(memory_space=pltpu.HBM)
+U1, U2 = 32, 64
 
 
 def sds(shape, dtype):
@@ -394,8 +396,8 @@
         grid_spec=pltpu.PrefetchScalarGridSpec(
             num_scalar_prefetch=1,
             grid=(1,),
-            in_specs=[VM] * count + [ANY, own(first), ANY, ANY, own(last)],
-            out_specs=(VM,) * len(outs) + (ANY,),
+            in_specs=[VM] * count + [HBM, own(first), HBM, HBM, own(last)],
+            out_specs=(VM,) * len(outs) + (HBM,),
             scratch_shapes=[
                 pltpu.VMEM(spec.shape, BF16),
                 pltpu.VMEM(fwd.shape, BF16),
@@ -406,7 +408,7 @@
                 pltpu.SemaphoreType.DMA((4,)),
             ],
         ),
-        compiler_params=PARAMS,
+        compiler_params=SMALL,
         cost_estimate=cost(2 * 10**9, 14 * 2**20),
         name="convolve",
     )(index, *parts, spec, *tabs)
@@ -545,17 +547,17 @@
 
     ends = is_end(place_ref)
 
-    @pl.when(pl.program_id(0) == 0)
-    def _():
-        for start in (True, False):
-            for slot, piece, needed in ((0, here ^ 2, True), (1, CHIPS - 1 - here, ends)):
-                for i in range(4):
-
-                    @pl.when((mine ^ piece == i) & needed)
-                    def _():
-                        copy = pltpu.make_async_copy(xs[i], x_ref.at[slot], sem.at[slot])
-                        copy.start() if start else copy.wait()
-
+    def fetch(start, slot, piece, needed):
+        for i in range(4):
+
+            @pl.when((pl.program_id(0) == 0) & (mine ^ piece == i) & needed)
+            def _():
+                copy = pltpu.make_async_copy(xs[i], x_ref.at[slot], sem.at[slot])
+                copy.start() if start else copy.wait()
+
+    fetch(True, 0, here ^ 2, True)
+    fetch(True, 1, CHIPS - 1 - here, ends)
+    fetch(False, 0, here ^ 2, True)
     depth = ws[0].shape[1]
     per = sum_ref.shape[0] // FAST
 
@@ -572,7 +574,9 @@
 
     @pl.when(ends)
     def _():
-        give(sum_ref[...] + part(two_ref, ws[2], ws[3]) + part(three_ref, ws[4], ws[5]))
+        total = sum_ref[...] + part(two_ref, ws[2], ws[3])
+        fetch(False, 1, CHIPS - 1 - here, ends)
+        give(total + part(three_ref, ws[4], ws[5]))
 
     @pl.when(jnp.logical_not(ends))
     def _():

time: 185 us -> 183 us (0.989)
  Pallas kernels: 58 us -> 55.7 us
where the time goes in v6:
time: 183 us; the launch traced here: 182 us
  starting transfers between devices  77.9 us (43%)
  Pallas kernels  55.7 us (30%)
  waiting for transfers between devices  45.4 us (25%)
    ppermute x11, starting transfers between devices, to(): return lax.ppermute(x, 'ctx', pairs)  25.8 us
    all_to_all x2, starting transfers between devices, exchange(): return lax.all_to_all(parts, 'ctx', split_axis=0, concat_axis=0, tiled=True)  25.1 us
    ppermute x14, starting transfers between devices, scatter(): lax.ppermute(part, 'ctx', [(i, i ^ d) for i in ids])  23.2 us
    ppermute x14, waiting for transfers between devices, scatter(): lax.ppermute(part, 'ctx', [(i, i ^ d) for i in ids])  15.9 us
    pallas_call x2, Pallas kernels, convolve(): pl.pallas_call(functools.partial(convolve_kernel, conjugate, count), out_...  13.4 us
    ppermute x3, waiting for transfers between devices, across(): return lax.ppermute(x, 'mp', [(i, i ^ d) for i in range(4)])  10.7 us
    ppermute x11, waiting for transfers between devices, to(): return lax.ppermute(x, 'ctx', pairs)  10.2 us
    pallas_call x1, Pallas kernels, mix_late(): pl.pallas_call(late_kernel, out_shape=(sds((rows, cols), BF16),) + (sds((...  9.31 us
  transfers between devices with their start and end apart: 30, of which 12 were waited for; matrix products, arithmetic and copies ran while one was open for 0% of the time, Pallas kernels for 25%

profile of v6, /device:TPU:1, one launch (start us, length us, event | category | flops | bytes accessed | tf_op | source)
XLA Modules:
  0.0 182.1 jit_solution(3851808510437707505)
XLA Ops:
  0.6 2.2 %collective-permute-start.2 = (bf16[1024,512]{1,0:T(8,128)(2,1)}, bf16[1024,512]{1,0:T(8,128)(2,1)}, u32[]{:S(2)}, u32[]{:S(2)}) collective-permute-start(bf16[1024,512]{1,0:T(8,128)(2,1)} %refs_4_.1), channel_id=1, source_target_pairs={{0,8},{4,12},{8,0},{12,4},{16,24},{20,28},{24,16},{28,20},{1,9},{5... | collective-permute-start | bytes 3145736 | tf_op jit(solution)/shard_map/ppermute | solution.py:716
  2.8 1.7 collective-permute-start.3
  4.5 3.8 %gate.1 = bf16[8,32,16,128]{3,2,1,0:T(8,128)(2,1)} custom-call(bf16[512,1024]{1,0:T(8,128)(2,1)} %refs_9_.2, bf16[512,1024]{1,0:T(8,128)(2,1)} %refs_8_.1), custom_call_target="tpu_custom_call" | custom-call | flops 1 | bytes 3145 | tf_op jit(solution)/shard_map/gate/pallas_call | solution.py:453
  8.3 5.6 %all-to-all-start = ((bf16[8,32,16,128]{3,2,1,0:T(8,128)(2,1)}), bf16[8,32,16,128]{3,2,1,0:T(8,128)(2,1)}, u32[]{:S(2)}, u32[]{:S(2)}) async-start(bf16[8,32,16,128]{3,2,1,0:T(8,128)(2,1)} %gate.1), calls=%async_computation | async-start | bytes 2097152 | tf_op jit(solution)/shard_map/all_to_all | solution.py:700
  14.0 1.2 collective-permute-start.1
  15.2 1.2 collective-permute-start
  16.4 5.8 %filter_spectrum.1.refs_1_.refs_8_ = bf16[8320,128]{1,0:T(8,128)(2,1)} custom-call(f32[128,4096]{1,0:T(8,128)} %h_ref.1, bf16[256,128]{1,0:T(8,128)(2,1)} %constant.48.first_ref, bf16[65,64,128]{2,1,0:T(8,128)(2,1)} %constant.44.clone.fwd_ref.refs_3_.refs_10_), custom_call_target="tpu_custom_call" | custom-call | flops 1000 | bytes 8388 | tf_op jit(solution)/shard_map/filter_spectrum/pallas_call | solution.py:368
  22.3 3.8 %collective-permute-done.2.refs_6_ = bf16[1024,512]{1,0:T(8,128)(2,1)} collective-permute-done((bf16[1024,512]{1,0:T(8,128)(2,1)}, bf16[1024,512]{1,0:T(8,128)(2,1)}, u32[]{:S(2)}, u32[]{:S(2)}) %collective-permute-start.2) | collective-permute-done | bytes 1048608 | tf_op jit(solution)/shard_map/ppermute | solution.py:716
  26.0 0.0 collective-permute-done.3.refs_8_
  26.0 2.1 %collective-permute-start.4 = (bf16[1024,512]{1,0:T(8,128)(2,1)}, bf16[1024,512]{1,0:T(8,128)(2,1)}, u32[]{:S(2)}, u32[]{:S(2)}) collective-permute-start(bf16[1024,512]{1,0:T(8,128)(2,1)} %collective-permute-done.2.refs_6_), channel_id=1, source_target_pairs={{0,4},{4,0},{8,12},{12,8},{16,20},{20,16},{24,28},{28,24},{1,5},{5... | collective-permute-start | bytes 3145736 | tf_op jit(solution)/shard_map/ppermute | solution.py:716
  28.1 1.6 collective-permute-start.5
  29.7 1.6 collective-permute-start.7
  31.3 7.6 %collective-permute-done.1.refs_2_ = bf16[512,1024]{1,0:T(8,128)(2,1)} collective-permute-done((bf16[512,1024]{1,0:T(8,128)(2,1)}, bf16[512,1024]{1,0:T(8,128)(2,1)}, u32[]{:S(2)}, u32[]{:S(2)}) %collective-permute-start.1) | collective-permute-done | bytes 1048608 | tf_op jit(solution)/shard_map/ppermute | solution.py:729
  39.0 0.9 collective-permute-done.refs_1_
  39.9 0.0 collective-permute-done.4.refs_7_
  39.9 0.0 collective-permute-done.5.refs_9_
  39.9 1.3 collective-permute-start.6
  41.2 1.3 collective-permute-start.12
  42.5 1.3 collective-permute-start.9
  43.8 8.6 %all-to-all-done.refs_0_ = bf16[8,32,16,128]{3,2,1,0:T(8,128)(2,1)} async-done(((bf16[8,32,16,128]{3,2,1,0:T(8,128)(2,1)}), bf16[8,32,16,128]{3,2,1,0:T(8,128)(2,1)}, u32[]{:S(2)}, u32[]{:S(2)}) %all-to-all-start) | async-done | bytes 1048608 | tf_op jit(solution)/shard_map/all_to_all | solution.py:700
  52.4 1.1 copy-done.1
  53.4 7.1 %convolve.2 = (bf16[8,32,16,128]{3,2,1,0:T(8,128)(2,1)}, bf16[8320,128]{1,0:T(8,128)(2,1)}) custom-call(s32[1]{0:T(128)} %constant.42.clone.1.place_ref, bf16[8,32,16,128]{3,2,1,0:T(8,128)(2,1)} %all-to-all-done.refs_0_, bf16[8320,128]{1,0:T(8,128)(2,1)} %filter_spectrum.1.refs_1_.refs_8_, bf16[9,256,128]{2,1,0:T(8,128)(2,1)S(1)} %copy-done.1, ...), custom_call_target="tpu_custom_call" | custom-call | flops 2000 | bytes 14680 | tf_op jit(solution)/shard_map/convolve/pallas_call | solution.py:393
  60.5 0.0 collective-permute-done.7.refs_4_
  60.5 1.3 collective-permute-start.11
  61.8 0.6 pad_add_fusion.place_ref
  62.4 2.2 %collective-permute-done.6.refs_3_ = bf16[512,1024]{1,0:T(8,128)(2,1)} collective-permute-done((bf16[512,1024]{1,0:T(8,128)(2,1)}, bf16[512,1024]{1,0:T(8,128)(2,1)}, u32[]{:S(2)}, u32[]{:S(2)}) %collective-permute-start.6) | collective-permute-done | bytes 1048608 | tf_op jit(solution)/shard_map/ppermute | solution.py:729
  64.6 0.0 collective-permute-done.12.refs_5_
  64.6 8.4 %terms.1.refs_10_ = f32[512,1024]{1,0:T(8,128)} custom-call(s32[4]{0:T(128)} %pad_add_fusion.place_ref, bf16[512,1024]{1,0:T(8,128)(2,1)} %refs_0_.3, bf16[512,1024]{1,0:T(8,128)(2,1)} %collective-permute-done.refs_1_, bf16[512,1024]{1,0:T(8,128)(2,1)} %collective-permute-done.1.refs_2_, bf16[512,1024]{1,0:T(8,128)(2,1)} %collective-permute-done.6.refs_3_, ...), custom_call_target="tpu_custom_call" | custom-call | flops 2000 | bytes 14680 | tf_op jit(solution)/shard_map/terms/pallas_call | solution.py:526
  73.0 19.5 %all-to-all-start.1 = ((bf16[8,32,16,128]{3,2,1,0:T(8,128)(2,1)}), bf16[8,32,16,128]{3,2,1,0:T(8,128)(2,1)}, u32[]{:S(2)}, u32[]{:S(2)}) async-start(bf16[8,32,16,128]{3,2,1,0:T(8,128)(2,1)} %get-tuple-element.59), calls=%async_computation.1 | async-start | bytes 2097152 | tf_op jit(solution)/shard_map/all_to_all | solution.py:700
  92.5 1.6 collective-permute-start.8
  94.1 1.9 %collective-permute-start.10 = (bf16[1024,512]{1,0:T(8,128)(2,1)}, bf16[1024,512]{1,0:T(8,128)(2,1)}, u32[]{:S(2)}, u32[]{:S(2)}) collective-permute-start(bf16[1024,512]{1,0:T(8,128)(2,1)} %collective-permute-done.9.refs_6_), channel_id=1, source_target_pairs={{0,4},{4,0},{24,28},{28,24},{1,5},{5,1},{25,29},{29,25},{2,6},{6,2... | collective-permute-start | bytes 3145736 | tf_op jit(solution)/shard_map/ppermute | solution.py:716
  96.0 4.0 %collective-permute-done.11.refs_8_ = bf16[1024,512]{1,0:T(8,128)(2,1)} collective-permute-done((bf16[1024,512]{1,0:T(8,128)(2,1)}, bf16[1024,512]{1,0:T(8,128)(2,1)}, u32[]{:S(2)}, u32[]{:S(2)}) %collective-permute-start.11) | collective-permute-done | bytes 1048608 | tf_op jit(solution)/shard_map/ppermute | solution.py:716
  100.0 9.2 %collective-permute-start.13 = (bf16[1024,512]{1,0:T(8,128)(2,1)}, bf16[1024,512]{1,0:T(8,128)(2,1)}, u32[]{:S(2)}, u32[]{:S(2)}) collective-permute-start(bf16[1024,512]{1,0:T(8,128)(2,1)} %collective-permute-done.11.refs_8_), channel_id=1, source_target_pairs={{0,4},{4,0},{24,28},{28,24},{1,5},{5,1},{25,29},{29,25},{2,6},{6,2... | collective-permute-start | bytes 3145736 | tf_op jit(solution)/shard_map/ppermute | solution.py:716
  109.2 0.0 collective-permute-done.10.refs_7_
  109.2 0.0 collective-permute-done.8.refs_5_
  109.2 2.4 %collective-permute-done.13.refs_9_ = bf16[1024,512]{1,0:T(8,128)(2,1)} collective-permute-done((bf16[1024,512]{1,0:T(8,128)(2,1)}, bf16[1024,512]{1,0:T(8,128)(2,1)}, u32[]{:S(2)}, u32[]{:S(2)}) %collective-permute-start.13) | collective-permute-done | bytes 1048608 | tf_op jit(solution)/shard_map/ppermute | solution.py:716
  111.6 9.3 %mix_late.1 = (bf16[512,1024]{1,0:T(8,128)(2,1)}, bf16[32,16,128]{2,1,0:T(8,128)(2,1)}, bf16[32,16,128]{2,1,0:T(8,128)(2,1)}, bf16[32,16,128]{2,1,0:T(8,128)(2,1...) custom-call(s32[4]{0:T(128)} %pad_add_fusion.place_ref, ...), custom_call_target="tpu_custom_call" | custom-call | flops 1000 | bytes 8388 | tf_op jit(solution)/shard_map/mix_late/pallas_call | solution.py:609
  120.9 5.0 %collective-permute-start.14 = (bf16[32,16,128]{2,1,0:T(8,128)(2,1)}, bf16[32,16,128]{2,1,0:T(8,128)(2,1)S(1)}, u32[]{:S(2)}, u32[]{:S(2)}) collective-permute-start(bf16[32,16,128]{2,1,0:T(8,128)(2,1)} %get-tuple-element.51), channel_id=1, source_target_pairs={{0,24},{4,28},{8,16},{12,20},{16,8},{20,12},{24,0},{28,4},{1,25},{... | collective-permute-start | bytes 393224 | tf_op jit(solution)/shard_map/ppermute | solution.py:705
  125.9 0.0 collective-permute-start.15
  125.9 0.4 collective-permute-start.16
  126.2 4.3 %collective-permute-start.17 = (bf16[32,16,128]{2,1,0:T(8,128)(2,1)}, bf16[32,16,128]{2,1,0:T(8,128)(2,1)S(1)}, u32[]{:S(2)}, u32[]{:S(2)}) collective-permute-start(bf16[32,16,128]{2,1,0:T(8,128)(2,1)} %get-tuple-element.54), channel_id=1, source_target_pairs={{0,28},{4,24},{8,20},{12,16},{16,12},{20,8},{24,4},{28,0},{1,29},{... | collective-permute-start | bytes 393224 | tf_op jit(solution)/shard_map/ppermute | solution.py:705
  130.5 0.4 collective-permute-start.19
  130.9 5.2 %collective-permute-done.15.refs_1_ = bf16[32,16,128]{2,1,0:T(8,128)(2,1)S(1)} collective-permute-done((bf16[32,16,128]{2,1,0:T(8,128)(2,1)}, bf16[32,16,128]{2,1,0:T(8,128)(2,1)S(1)}, u32[]{:S(2)}, u32[]{:S(2)}) %collective-permute-start.15) | collective-permute-done | bytes 131104 | tf_op jit(solution)/shard_map/ppermute | solution.py:705
  136.1 5.4 %collective-permute-start.20 = (bf16[32,16,128]{2,1,0:T(8,128)(2,1)}, bf16[32,16,128]{2,1,0:T(8,128)(2,1)S(1)}, u32[]{:S(2)}, u32[]{:S(2)}) collective-permute-start(bf16[32,16,128]{2,1,0:T(8,128)(2,1)} %get-tuple-element.57), channel_id=1, source_target_pairs={{0,4},{4,0},{8,12},{12,8},{16,20},{20,16},{24,28},{28,24},{1,5},{5... | collective-permute-start | bytes 393224 | tf_op jit(solution)/shard_map/ppermute | solution.py:705
  141.5 5.4 %collective-permute-done.18.refs_4_ = bf16[32,16,128]{2,1,0:T(8,128)(2,1)S(1)} collective-permute-done((bf16[32,16,128]{2,1,0:T(8,128)(2,1)}, bf16[32,16,128]{2,1,0:T(8,128)(2,1)S(1)}, u32[]{:S(2)}, u32[]{:S(2)}) %collective-permute-start.18) | collective-permute-done | bytes 131104 | tf_op jit(solution)/shard_map/ppermute | solution.py:705
  146.9 0.0 collective-permute-done.19.refs_5_
  147.0 0.0 collective-permute-done.20.refs_6_
  147.0 0.0 all-to-all-done.1.part_ref
  147.0 6.4 %convolve.3 = (bf16[32,16,128]{2,1,0:T(8,128)(2,1)S(1)}, bf16[32,16,128]{2,1,0:T(8,128)(2,1)S(1)}, bf16[32,16,128]{2,1,0:T(8,128)(2,1)S(1)}, bf16[32,16,128]{2,1...) custom-call(s32[1]{0:T(128)} %bitcast.3.place_ref, ...), custom_call_target="tpu_custom_call" | custom-call | flops 2000 | bytes 14680 | tf_op jit(solution)/shard_map/convolve/pallas_call | solution.py:393
  153.3 0.7 copy-done.2
  154.0 2.2 %collective-permute-start.21 = (bf16[32,16,128]{2,1,0:T(8,128)(2,1)S(1)}, bf16[32,16,128]{2,1,0:T(8,128)(2,1)S(1)}, u32[]{:S(2)}, u32[]{:S(2)}) collective-permute-start(bf16[32,16,128]{2,1,0:T(8,128)(2,1)S(1)} %get-tuple-element.70), channel_id=1, source_target_pairs={{0,24},{4,28},{8,16},{12,20},{16,8},{20,12},{24,0},{28,4},{1,25},{... | collective-permute-start | bytes 393224 | tf_op jit(solution)/shard_map/ppermute | solution.py:705
  156.2 1.8 collective-permute-start.23
  158.1 1.0 collective-permute-start.24
  159.0 0.2 collective-permute-start.25
  159.2 1.2 collective-permute-done.21.refs_0_
  160.5 2.0 %collective-permute-start.26 = (bf16[32,16,128]{2,1,0:T(8,128)(2,1)S(1)}, bf16[32,16,128]{2,1,0:T(8,128)(2,1)}, u32[]{:S(2)}, u32[]{:S(2)}) collective-permute-start(bf16[32,16,128]{2,1,0:T(8,128)(2,1)S(1)} %get-tuple-element.75), channel_id=1, source_target_pairs={{0,20},{4,16},{8,28},{12,24},{16,4},{20,0},{24,12},{28,8},{1,21},{... | collective-permute-start | bytes 393224 | tf_op jit(solution)/shard_map/ppermute | solution.py:705
  162.5 1.6 collective-permute-done.22.refs_1_
  164.2 0.6 collective-permute-start.27
  164.7 3.8 %finish_whole.1 = bf16[512,1024]{1,0:T(8,128)(2,1)} custom-call(bf16[8,32,16,128]{3,2,1,0:T(8,128)(2,1)} %all-to-all-done.1.part_ref, bf16[512,1024]{1,0:T(8,128)(2,1)} %get-tuple-element.61.factor_ref), custom_call_target="tpu_custom_call" | custom-call | flops 1 | bytes 3145 | tf_op jit(solution)/shard_map/finish_whole/pallas_call | solution.py:686
  168.5 7.2 %filter_gradient.1 = f32[128,4096]{1,0:T(8,128)} custom-call(bf16[8320,128]{1,0:T(8,128)(2,1)} %get-tuple-element.80.s_ref, bf16[8320,128]{1,0:T(8,128)(2,1)} %get-tuple-element.81.g_ref, bf16[65,64,128]{2,1,0:T(8,128)(2,1)} %constant.45.clone.refs_4_.refs_11_.inv_ref, bf16[128,256]{1,0:T(8,128)(2,1)} %constant.50.last_ref), custom_call_target="tpu_custom_call" | custom-call | flops 1000 | bytes 12582 | tf_op jit(solution)/shard_map/filter_gradient/pallas_call | solution.py:421
  175.7 0.0 collective-permute-done.24.refs_3_
  175.7 0.0 collective-permute-done.25.refs_4_
  175.8 2.4 %collective-permute-done.26.refs_5_ = bf16[32,16,128]{2,1,0:T(8,128)(2,1)} collective-permute-done((bf16[32,16,128]{2,1,0:T(8,128)(2,1)S(1)}, bf16[32,16,128]{2,1,0:T(8,128)(2,1)}, u32[]{:S(2)}, u32[]{:S(2)}) %collective-permute-start.26) | collective-permute-done | bytes 131104 | tf_op jit(solution)/shard_map/ppermute | solution.py:705
  178.2 4.0 %finish.1 = (bf16[512,1024]{1,0:T(8,128)(2,1)}, bf16[512,1024]{1,0:T(8,128)(2,1)}) custom-call(s32[4]{0:T(128)} %pad_add_fusion.place_ref, bf16[32,16,128]{2,1,0:T(8,128)(2,1)} %copy-done.3, bf16[32,16,128]{2,1,0:T(8,128)(2,1)} %copy-done.4, bf16[32,16,128]{2,1,0:T(8,128)(2,1)} %collective-permute-done.23.refs_2_, ...), custom_call_target="tpu_custom_call" | custom-call | flops 1 | bytes 5242 | tf_op jit(solution)/shard_map/finish/pallas_call | solution.py:657
  (16 shorter events, 0.0 us)
Async XLA Ops:
  0.6 25.4 %collective-permute-start.2 = (bf16[1024,512]{1,0:T(8,128)(2,1)}, bf16[1024,512]{1,0:T(8,128)(2,1)}, u32[]{:S(2)}, u32[]{:S(2)}) collective-permute-start(bf16[1024,512]{1,0:T(8,128)(2,1)} %refs_4_.1), channel_id=1, source_target_pairs={{0,8},{4,12},{8,0},{12,4},{16,24},{20,28},{24,16},{28,20},{1,9},{5... | collective-permute-start | bytes 3145736 | tf_op jit(solution)/shard_map/ppermute | solution.py:716
  2.8 23.2 %collective-permute-start.3 = (bf16[1024,512]{1,0:T(8,128)(2,1)}, bf16[1024,512]{1,0:T(8,128)(2,1)}, u32[]{:S(2)}, u32[]{:S(2)}) collective-permute-start(bf16[1024,512]{1,0:T(8,128)(2,1)} %refs_4_.1), channel_id=1, source_target_pairs={{8,16},{12,20},{16,8},{20,12},{9,17},{13,21},{17,9},{21,13},{10,18... | collective-permute-start | bytes 3145736 | tf_op jit(solution)/shard_map/ppermute | solution.py:716
  8.3 44.0 %all-to-all-start = ((bf16[8,32,16,128]{3,2,1,0:T(8,128)(2,1)}), bf16[8,32,16,128]{3,2,1,0:T(8,128)(2,1)}, u32[]{:S(2)}, u32[]{:S(2)}) async-start(bf16[8,32,16,128]{3,2,1,0:T(8,128)(2,1)} %gate.1), calls=%async_computation | async-start | bytes 2097152 | tf_op jit(solution)/shard_map/all_to_all | solution.py:700
  13.9 38.4 %copy-start = (bf16[9,128,256]{2,1,0:T(8,128)(2,1)S(1)}, bf16[9,128,256]{2,1,0:T(8,128)(2,1)}, u32[]{:S(2)}) copy-start(bf16[9,128,256]{2,1,0:T(8,128)(2,1)} %constant.46.clone.refs_5_.refs_12_) | copy-start | bytes 1769476
  14.0 25.0 %collective-permute-start.1 = (bf16[512,1024]{1,0:T(8,128)(2,1)}, bf16[512,1024]{1,0:T(8,128)(2,1)}, u32[]{:S(2)}, u32[]{:S(2)}) collective-permute-start(bf16[512,1024]{1,0:T(8,128)(2,1)} %refs_0_.3), channel_id=1, source_target_pairs={{0,2},{1,3},{2,0},{3,1},{4,6},{5,7},{6,4},{7,5},{8,10},{9,11},{10,... | collective-permute-start | bytes 3145736 | tf_op jit(solution)/shard_map/ppermute | solution.py:729
  15.2 24.7 %collective-permute-start = (bf16[512,1024]{1,0:T(8,128)(2,1)}, bf16[512,1024]{1,0:T(8,128)(2,1)}, u32[]{:S(2)}, u32[]{:S(2)}) collective-permute-start(bf16[512,1024]{1,0:T(8,128)(2,1)} %refs_0_.3), channel_id=1, source_target_pairs={{0,1},{1,0},{2,3},{3,2},{4,5},{5,4},{6,7},{7,6},{8,9},{9,8},{10,11... | collective-permute-start | bytes 3145736 | tf_op jit(solution)/shard_map/ppermute | solution.py:729
  26.0 13.9 %collective-permute-start.4 = (bf16[1024,512]{1,0:T(8,128)(2,1)}, bf16[1024,512]{1,0:T(8,128)(2,1)}, u32[]{:S(2)}, u32[]{:S(2)}) collective-permute-start(bf16[1024,512]{1,0:T(8,128)(2,1)} %collective-permute-done.2.refs_6_), channel_id=1, source_target_pairs={{0,4},{4,0},{8,12},{12,8},{16,20},{20,16},{24,28},{28,24},{1,5},{5... | collective-permute-start | bytes 3145736 | tf_op jit(solution)/shard_map/ppermute | solution.py:716
  28.1 11.8 %collective-permute-start.5 = (bf16[1024,512]{1,0:T(8,128)(2,1)}, bf16[1024,512]{1,0:T(8,128)(2,1)}, u32[]{:S(2)}, u32[]{:S(2)}) collective-permute-start(bf16[1024,512]{1,0:T(8,128)(2,1)} %collective-permute-done.3.refs_8_), channel_id=1, source_target_pairs={{8,12},{12,8},{16,20},{20,16},{9,13},{13,9},{17,21},{21,17},{10,14... | collective-permute-start | bytes 3145736 | tf_op jit(solution)/shard_map/ppermute | solution.py:716
  29.7 30.8 %collective-permute-start.7 = (bf16[1024,512]{1,0:T(8,128)(2,1)}, bf16[1024,512]{1,0:T(8,128)(2,1)}, u32[]{:S(2)}, u32[]{:S(2)}) collective-permute-start(bf16[1024,512]{1,0:T(8,128)(2,1)} %collective-permute-done.2.refs_6_), channel_id=1, source_target_pairs={{8,16},{12,20},{16,8},{20,12},{9,17},{13,21},{17,9},{21,13},{10,18... | collective-permute-start | bytes 3145736 | tf_op jit(solution)/shard_map/ppermute | solution.py:716
  39.9 24.7 %collective-permute-start.6 = (bf16[512,1024]{1,0:T(8,128)(2,1)}, bf16[512,1024]{1,0:T(8,128)(2,1)}, u32[]{:S(2)}, u32[]{:S(2)}) collective-permute-start(bf16[512,1024]{1,0:T(8,128)(2,1)} %refs_0_.3), channel_id=1, source_target_pairs={{0,3},{1,2},{2,1},{3,0},{4,7},{5,6},{6,5},{7,4},{8,11},{9,10},{10,... | collective-permute-start | bytes 3145736 | tf_op jit(solution)/shard_map/ppermute | solution.py:729
  41.2 23.4 %collective-permute-start.12 = (bf16[1024,512]{1,0:T(8,128)(2,1)}, bf16[1024,512]{1,0:T(8,128)(2,1)}, u32[]{:S(2)}, u32[]{:S(2)}) collective-permute-start(bf16[1024,512]{1,0:T(8,128)(2,1)} %refs_4_.1), channel_id=1, source_target_pairs={{0,4},{4,0},{8,12},{12,8},{16,20},{20,16},{24,28},{28,24},{1,5},{5... | collective-permute-start | bytes 3145736 | tf_op jit(solution)/shard_map/ppermute | solution.py:716
  42.5 51.6 %collective-permute-start.9 = (bf16[1024,512]{1,0:T(8,128)(2,1)}, bf16[1024,512]{1,0:T(8,128)(2,1)}, u32[]{:S(2)}, u32[]{:S(2)}) collective-permute-start(bf16[1024,512]{1,0:T(8,128)(2,1)} %collective-permute-done.3.refs_8_), channel_id=1, source_target_pairs={{8,0},{12,4},{16,24},{20,28},{9,1},{13,5},{17,25},{21,29},{10,2},{... | collective-permute-start | bytes 3145736 | tf_op jit(solution)/shard_map/ppermute | solution.py:716
  52.4 1.1 copy-start.1
  60.5 39.5 %collective-permute-start.11 = (bf16[1024,512]{1,0:T(8,128)(2,1)}, bf16[1024,512]{1,0:T(8,128)(2,1)}, u32[]{:S(2)}, u32[]{:S(2)}) collective-permute-start(bf16[1024,512]{1,0:T(8,128)(2,1)} %collective-permute-done.7.refs_4_), channel_id=1, source_target_pairs={{8,0},{12,4},{16,24},{20,28},{9,1},{13,5},{17,25},{21,29},{10,2},{... | collective-permute-start | bytes 3145736 | tf_op jit(solution)/shard_map/ppermute | solution.py:716
  73.0 74.0 %all-to-all-start.1 = ((bf16[8,32,16,128]{3,2,1,0:T(8,128)(2,1)}), bf16[8,32,16,128]{3,2,1,0:T(8,128)(2,1)}, u32[]{:S(2)}, u32[]{:S(2)}) async-start(bf16[8,32,16,128]{3,2,1,0:T(8,128)(2,1)} %get-tuple-element.59), calls=%async_computation.1 | async-start | bytes 2097152 | tf_op jit(solution)/shard_map/all_to_all | solution.py:700
  92.5 16.7 %collective-permute-start.8 = (bf16[1024,512]{1,0:T(8,128)(2,1)}, bf16[1024,512]{1,0:T(8,128)(2,1)}, u32[]{:S(2)}, u32[]{:S(2)}) collective-permute-start(bf16[1024,512]{1,0:T(8,128)(2,1)} %collective-permute-done.7.refs_4_), channel_id=1, source_target_pairs={{8,12},{12,8},{16,20},{20,16},{9,13},{13,9},{17,21},{21,17},{10,14... | collective-permute-start | bytes 3145736 | tf_op jit(solution)/shard_map/ppermute | solution.py:716
  94.1 15.1 %collective-permute-start.10 = (bf16[1024,512]{1,0:T(8,128)(2,1)}, bf16[1024,512]{1,0:T(8,128)(2,1)}, u32[]{:S(2)}, u32[]{:S(2)}) collective-permute-start(bf16[1024,512]{1,0:T(8,128)(2,1)} %collective-permute-done.9.refs_6_), channel_id=1, source_target_pairs={{0,4},{4,0},{24,28},{28,24},{1,5},{5,1},{25,29},{29,25},{2,6},{6,2... | collective-permute-start | bytes 3145736 | tf_op jit(solution)/shard_map/ppermute | solution.py:716
  100.0 11.6 %collective-permute-start.13 = (bf16[1024,512]{1,0:T(8,128)(2,1)}, bf16[1024,512]{1,0:T(8,128)(2,1)}, u32[]{:S(2)}, u32[]{:S(2)}) collective-permute-start(bf16[1024,512]{1,0:T(8,128)(2,1)} %collective-permute-done.11.refs_8_), channel_id=1, source_target_pairs={{0,4},{4,0},{24,28},{28,24},{1,5},{5,1},{25,29},{29,25},{2,6},{6,2... | collective-permute-start | bytes 3145736 | tf_op jit(solution)/shard_map/ppermute | solution.py:716
  120.9 9.6 %collective-permute-start.14 = (bf16[32,16,128]{2,1,0:T(8,128)(2,1)}, bf16[32,16,128]{2,1,0:T(8,128)(2,1)S(1)}, u32[]{:S(2)}, u32[]{:S(2)}) collective-permute-start(bf16[32,16,128]{2,1,0:T(8,128)(2,1)} %get-tuple-element.51), channel_id=1, source_target_pairs={{0,24},{4,28},{8,16},{12,20},{16,8},{20,12},{24,0},{28,4},{1,25},{... | collective-permute-start | bytes 393224 | tf_op jit(solution)/shard_map/ppermute | solution.py:705
  125.9 10.2 %collective-permute-start.15 = (bf16[32,16,128]{2,1,0:T(8,128)(2,1)}, bf16[32,16,128]{2,1,0:T(8,128)(2,1)S(1)}, u32[]{:S(2)}, u32[]{:S(2)}) collective-permute-start(bf16[32,16,128]{2,1,0:T(8,128)(2,1)} %get-tuple-element.52), channel_id=1, source_target_pairs={{0,16},{4,20},{8,24},{12,28},{16,0},{20,4},{24,8},{28,12},{1,17},{... | collective-permute-start | bytes 393224 | tf_op jit(solution)/shard_map/ppermute | solution.py:705
  125.9 15.6 %collective-permute-start.16 = (bf16[32,16,128]{2,1,0:T(8,128)(2,1)}, bf16[32,16,128]{2,1,0:T(8,128)(2,1)S(1)}, u32[]{:S(2)}, u32[]{:S(2)}) collective-permute-start(bf16[32,16,128]{2,1,0:T(8,128)(2,1)} %get-tuple-element.53), channel_id=1, source_target_pairs={{0,8},{4,12},{8,0},{12,4},{16,24},{20,28},{24,16},{28,20},{1,9},{5... | collective-permute-start | bytes 393224 | tf_op jit(solution)/shard_map/ppermute | solution.py:705
  126.2 15.3 %collective-permute-start.17 = (bf16[32,16,128]{2,1,0:T(8,128)(2,1)}, bf16[32,16,128]{2,1,0:T(8,128)(2,1)S(1)}, u32[]{:S(2)}, u32[]{:S(2)}) collective-permute-start(bf16[32,16,128]{2,1,0:T(8,128)(2,1)} %get-tuple-element.54), channel_id=1, source_target_pairs={{0,28},{4,24},{8,20},{12,16},{16,12},{20,8},{24,4},{28,0},{1,29},{... | collective-permute-start | bytes 393224 | tf_op jit(solution)/shard_map/ppermute | solution.py:705
  130.5 16.4 %collective-permute-start.18 = (bf16[32,16,128]{2,1,0:T(8,128)(2,1)}, bf16[32,16,128]{2,1,0:T(8,128)(2,1)S(1)}, u32[]{:S(2)}, u32[]{:S(2)}) collective-permute-start(bf16[32,16,128]{2,1,0:T(8,128)(2,1)} %get-tuple-element.55), channel_id=1, source_target_pairs={{0,20},{4,16},{8,28},{12,24},{16,4},{20,0},{24,12},{28,8},{1,21},{... | collective-permute-start | bytes 393224 | tf_op jit(solution)/shard_map/ppermute | solution.py:705
  130.5 16.4 %collective-permute-start.19 = (bf16[32,16,128]{2,1,0:T(8,128)(2,1)}, bf16[32,16,128]{2,1,0:T(8,128)(2,1)S(1)}, u32[]{:S(2)}, u32[]{:S(2)}) collective-permute-start(bf16[32,16,128]{2,1,0:T(8,128)(2,1)} %get-tuple-element.56), channel_id=1, source_target_pairs={{0,12},{4,8},{8,4},{12,0},{16,28},{20,24},{24,20},{28,16},{1,13},{... | collective-permute-start | bytes 393224 | tf_op jit(solution)/shard_map/ppermute | solution.py:705
  136.1 10.9 %collective-permute-start.20 = (bf16[32,16,128]{2,1,0:T(8,128)(2,1)}, bf16[32,16,128]{2,1,0:T(8,128)(2,1)S(1)}, u32[]{:S(2)}, u32[]{:S(2)}) collective-permute-start(bf16[32,16,128]{2,1,0:T(8,128)(2,1)} %get-tuple-element.57), channel_id=1, source_target_pairs={{0,4},{4,0},{8,12},{12,8},{16,20},{20,16},{24,28},{28,24},{1,5},{5... | collective-permute-start | bytes 393224 | tf_op jit(solution)/shard_map/ppermute | solution.py:705
  153.3 0.7 copy-start.2
  154.0 6.5 %collective-permute-start.21 = (bf16[32,16,128]{2,1,0:T(8,128)(2,1)S(1)}, bf16[32,16,128]{2,1,0:T(8,128)(2,1)S(1)}, u32[]{:S(2)}, u32[]{:S(2)}) collective-permute-start(bf16[32,16,128]{2,1,0:T(8,128)(2,1)S(1)} %get-tuple-element.70), channel_id=1, source_target_pairs={{0,24},{4,28},{8,16},{12,20},{16,8},{20,12},{24,0},{28,4},{1,25},{... | collective-permute-start | bytes 393224 | tf_op jit(solution)/shard_map/ppermute | solution.py:705
  156.2 7.9 %collective-permute-start.22 = (bf16[32,16,128]{2,1,0:T(8,128)(2,1)S(1)}, bf16[32,16,128]{2,1,0:T(8,128)(2,1)S(1)}, u32[]{:S(2)}, u32[]{:S(2)}) collective-permute-start(bf16[32,16,128]{2,1,0:T(8,128)(2,1)S(1)} %get-tuple-element.71), channel_id=1, source_target_pairs={{0,8},{4,12},{8,0},{12,4},{16,24},{20,28},{24,16},{28,20},{1,9},{5... | collective-permute-start | bytes 393224 | tf_op jit(solution)/shard_map/ppermute | solution.py:705
  156.2 19.5 %collective-permute-start.23 = (bf16[32,16,128]{2,1,0:T(8,128)(2,1)S(1)}, bf16[32,16,128]{2,1,0:T(8,128)(2,1)}, u32[]{:S(2)}, u32[]{:S(2)}) collective-permute-start(bf16[32,16,128]{2,1,0:T(8,128)(2,1)S(1)} %get-tuple-element.72), channel_id=1, source_target_pairs={{0,12},{4,8},{8,4},{12,0},{16,28},{20,24},{24,20},{28,16},{1,13},{... | collective-permute-start | bytes 393224 | tf_op jit(solution)/shard_map/ppermute | solution.py:705
  158.1 17.7 %collective-permute-start.24 = (bf16[32,16,128]{2,1,0:T(8,128)(2,1)S(1)}, bf16[32,16,128]{2,1,0:T(8,128)(2,1)}, u32[]{:S(2)}, u32[]{:S(2)}) collective-permute-start(bf16[32,16,128]{2,1,0:T(8,128)(2,1)S(1)} %get-tuple-element.73), channel_id=1, source_target_pairs={{0,28},{4,24},{8,20},{12,16},{16,12},{20,8},{24,4},{28,0},{1,29},{... | collective-permute-start | bytes 393224 | tf_op jit(solution)/shard_map/ppermute | solution.py:705
  159.0 16.7 %collective-permute-start.25 = (bf16[32,16,128]{2,1,0:T(8,128)(2,1)S(1)}, bf16[32,16,128]{2,1,0:T(8,128)(2,1)}, u32[]{:S(2)}, u32[]{:S(2)}) collective-permute-start(bf16[32,16,128]{2,1,0:T(8,128)(2,1)S(1)} %get-tuple-element.74), channel_id=1, source_target_pairs={{0,16},{4,20},{8,24},{12,28},{16,0},{20,4},{24,8},{28,12},{1,17},{... | collective-permute-start | bytes 393224 | tf_op jit(solution)/shard_map/ppermute | solution.py:705
  160.5 15.2 %copy-start.3 = (bf16[32,16,128]{2,1,0:T(8,128)(2,1)}, bf16[32,16,128]{2,1,0:T(8,128)(2,1)S(1)}, u32[]{:S(2)}) copy-start(bf16[32,16,128]{2,1,0:T(8,128)(2,1)S(1)} %collective-permute-done.21.refs_0_) | copy-start | bytes 393220
  160.5 17.7 %collective-permute-start.26 = (bf16[32,16,128]{2,1,0:T(8,128)(2,1)S(1)}, bf16[32,16,128]{2,1,0:T(8,128)(2,1)}, u32[]{:S(2)}, u32[]{:S(2)}) collective-permute-start(bf16[32,16,128]{2,1,0:T(8,128)(2,1)S(1)} %get-tuple-element.75), channel_id=1, source_target_pairs={{0,20},{4,16},{8,28},{12,24},{16,4},{20,0},{24,12},{28,8},{1,21},{... | collective-permute-start | bytes 393224 | tf_op jit(solution)/shard_map/ppermute | solution.py:705
  164.2 11.6 %copy-start.4 = (bf16[32,16,128]{2,1,0:T(8,128)(2,1)}, bf16[32,16,128]{2,1,0:T(8,128)(2,1)S(1)}, u32[]{:S(2)}) copy-start(bf16[32,16,128]{2,1,0:T(8,128)(2,1)S(1)} %collective-permute-done.22.refs_1_) | copy-start | bytes 393220
  164.2 14.0 %collective-permute-start.27 = (bf16[32,16,128]{2,1,0:T(8,128)(2,1)S(1)}, bf16[32,16,128]{2,1,0:T(8,128)(2,1)}, u32[]{:S(2)}, u32[]{:S(2)}) collective-permute-start(bf16[32,16,128]{2,1,0:T(8,128)(2,1)S(1)} %get-tuple-element.76), channel_id=1, source_target_pairs={{0,4},{4,0},{8,12},{12,8},{16,20},{20,16},{24,28},{28,24},{1,5},{5... | collective-permute-start | bytes 393224 | tf_op jit(solution)/shard_map/ppermute | solution.py:705

commit v7 on v6

--- a/solution.py
+++ b/solution.py
@@ -664,7 +664,7 @@
             out_specs=(block,) * count,
             scratch_shapes=[pltpu.VMEM((BATCH, rows // FAST * GAP, LANES), F32)],
         ),
-        compiler_params=PARAMS,
+        compiler_params=SMALL,
         cost_estimate=cost(10**6, (1 + 2 * count) * 2**20),
         name="finish",
     )(place, *parts, *factors)

time: 183 us -> 183 us (level)
  no operation moved by 1% of the time
where the time goes in v7:
time: 183 us; the launch traced here: 182 us
  starting transfers between devices  78 us (43%)
  Pallas kernels  56.1 us (31%)
  waiting for transfers between devices  45.4 us (25%)
    ppermute x11, starting transfers between devices, to(): return lax.ppermute(x, 'ctx', pairs)  25.8 us
    all_to_all x2, starting transfers between devices, exchange(): return lax.all_to_all(parts, 'ctx', split_axis=0, concat_axis=0, tiled=True)  25.1 us
    ppermute x14, starting transfers between devices, scatter(): lax.ppermute(part, 'ctx', [(i, i ^ d) for i in ids])  23.3 us
    ppermute x14, waiting for transfers between devices, scatter(): lax.ppermute(part, 'ctx', [(i, i ^ d) for i in ids])  15.9 us
    pallas_call x2, Pallas kernels, convolve(): pl.pallas_call(functools.partial(convolve_kernel, conjugate, count), out_...  14.2 us
    ppermute x3, waiting for transfers between devices, across(): return lax.ppermute(x, 'mp', [(i, i ^ d) for i in range(4)])  10.7 us
    ppermute x11, waiting for transfers between devices, to(): return lax.ppermute(x, 'ctx', pairs)  10.2 us
    pallas_call x1, Pallas kernels, mix_late(): pl.pallas_call(late_kernel, out_shape=(sds((rows, cols), BF16),) + (sds((...  9.31 us
  transfers between devices with their start and end apart: 30, of which 12 were waited for; matrix products, arithmetic and copies ran while one was open for 0% of the time, Pallas kernels for 25%

profile of v7, /device:TPU:1, one launch (start us, length us, event | category | flops | bytes accessed | tf_op | source)
XLA Modules:
  0.0 181.9 jit_solution(8523409878885267566)
XLA Ops:
  0.6 2.2 %collective-permute-start.2 = (bf16[1024,512]{1,0:T(8,128)(2,1)}, bf16[1024,512]{1,0:T(8,128)(2,1)}, u32[]{:S(2)}, u32[]{:S(2)}) collective-permute-start(bf16[1024,512]{1,0:T(8,128)(2,1)} %refs_4_.1), channel_id=1, source_target_pairs={{0,8},{4,12},{8,0},{12,4},{16,24},{20,28},{24,16},{28,20},{1,9},{5... | collective-permute-start | bytes 3145736 | tf_op jit(solution)/shard_map/ppermute | solution.py:716
  2.8 1.7 collective-permute-start.3
  4.5 3.8 %gate.1 = bf16[8,32,16,128]{3,2,1,0:T(8,128)(2,1)} custom-call(bf16[512,1024]{1,0:T(8,128)(2,1)} %refs_9_.2, bf16[512,1024]{1,0:T(8,128)(2,1)} %refs_8_.1), custom_call_target="tpu_custom_call" | custom-call | flops 1 | bytes 3145 | tf_op jit(solution)/shard_map/gate/pallas_call | solution.py:453
  8.3 5.6 %all-to-all-start = ((bf16[8,32,16,128]{3,2,1,0:T(8,128)(2,1)}), bf16[8,32,16,128]{3,2,1,0:T(8,128)(2,1)}, u32[]{:S(2)}, u32[]{:S(2)}) async-start(bf16[8,32,16,128]{3,2,1,0:T(8,128)(2,1)} %gate.1), calls=%async_computation | async-start | bytes 2097152 | tf_op jit(solution)/shard_map/all_to_all | solution.py:700
  14.0 1.2 collective-permute-start.1
  15.2 1.2 collective-permute-start
  16.4 5.9 %filter_spectrum.1.refs_1_.refs_8_ = bf16[8320,128]{1,0:T(8,128)(2,1)} custom-call(f32[128,4096]{1,0:T(8,128)} %h_ref.1, bf16[256,128]{1,0:T(8,128)(2,1)} %constant.48.first_ref, bf16[65,64,128]{2,1,0:T(8,128)(2,1)} %constant.44.clone.fwd_ref.refs_3_.refs_10_), custom_call_target="tpu_custom_call" | custom-call | flops 1000 | bytes 8388 | tf_op jit(solution)/shard_map/filter_spectrum/pallas_call | solution.py:368
  22.3 3.8 %collective-permute-done.2.refs_6_ = bf16[1024,512]{1,0:T(8,128)(2,1)} collective-permute-done((bf16[1024,512]{1,0:T(8,128)(2,1)}, bf16[1024,512]{1,0:T(8,128)(2,1)}, u32[]{:S(2)}, u32[]{:S(2)}) %collective-permute-start.2) | collective-permute-done | bytes 1048608 | tf_op jit(solution)/shard_map/ppermute | solution.py:716
  26.0 0.0 collective-permute-done.3.refs_8_
  26.0 2.1 %collective-permute-start.4 = (bf16[1024,512]{1,0:T(8,128)(2,1)}, bf16[1024,512]{1,0:T(8,128)(2,1)}, u32[]{:S(2)}, u32[]{:S(2)}) collective-permute-start(bf16[1024,512]{1,0:T(8,128)(2,1)} %collective-permute-done.2.refs_6_), channel_id=1, source_target_pairs={{0,4},{4,0},{8,12},{12,8},{16,20},{20,16},{24,28},{28,24},{1,5},{5... | collective-permute-start | bytes 3145736 | tf_op jit(solution)/shard_map/ppermute | solution.py:716
  28.1 1.6 collective-permute-start.5
  29.7 1.6 collective-permute-start.7
  31.3 7.6 %collective-permute-done.1.refs_2_ = bf16[512,1024]{1,0:T(8,128)(2,1)} collective-permute-done((bf16[512,1024]{1,0:T(8,128)(2,1)}, bf16[512,1024]{1,0:T(8,128)(2,1)}, u32[]{:S(2)}, u32[]{:S(2)}) %collective-permute-start.1) | collective-permute-done | bytes 1048608 | tf_op jit(solution)/shard_map/ppermute | solution.py:729
  39.0 0.9 collective-permute-done.refs_1_
  39.9 0.0 collective-permute-done.4.refs_7_
  39.9 1.3 collective-permute-start.6
  41.2 1.3 collective-permute-start.12
  42.5 1.3 collective-permute-start.9
  43.8 8.6 %all-to-all-done.refs_0_ = bf16[8,32,16,128]{3,2,1,0:T(8,128)(2,1)} async-done(((bf16[8,32,16,128]{3,2,1,0:T(8,128)(2,1)}), bf16[8,32,16,128]{3,2,1,0:T(8,128)(2,1)}, u32[]{:S(2)}, u32[]{:S(2)}) %all-to-all-start) | async-done | bytes 1048608 | tf_op jit(solution)/shard_map/all_to_all | solution.py:700
  52.4 1.1 copy-done.1
  53.4 7.0 %convolve.2 = (bf16[8,32,16,128]{3,2,1,0:T(8,128)(2,1)}, bf16[8320,128]{1,0:T(8,128)(2,1)}) custom-call(s32[1]{0:T(128)} %constant.42.clone.1.place_ref, bf16[8,32,16,128]{3,2,1,0:T(8,128)(2,1)} %all-to-all-done.refs_0_, bf16[8320,128]{1,0:T(8,128)(2,1)} %filter_spectrum.1.refs_1_.refs_8_, bf16[9,256,128]{2,1,0:T(8,128)(2,1)S(1)} %copy-done.1, ...), custom_call_target="tpu_custom_call" | custom-call | flops 2000 | bytes 14680 | tf_op jit(solution)/shard_map/convolve/pallas_call | solution.py:393
  60.5 0.0 collective-permute-done.7.refs_4_
  60.5 1.3 collective-permute-start.11
  61.8 0.6 pad_add_fusion.place_ref
  62.4 2.2 %collective-permute-done.6.refs_3_ = bf16[512,1024]{1,0:T(8,128)(2,1)} collective-permute-done((bf16[512,1024]{1,0:T(8,128)(2,1)}, bf16[512,1024]{1,0:T(8,128)(2,1)}, u32[]{:S(2)}, u32[]{:S(2)}) %collective-permute-start.6) | collective-permute-done | bytes 1048608 | tf_op jit(solution)/shard_map/ppermute | solution.py:729
  64.6 8.4 %terms.1.refs_10_ = f32[512,1024]{1,0:T(8,128)} custom-call(s32[4]{0:T(128)} %pad_add_fusion.place_ref, bf16[512,1024]{1,0:T(8,128)(2,1)} %refs_0_.3, bf16[512,1024]{1,0:T(8,128)(2,1)} %collective-permute-done.refs_1_, bf16[512,1024]{1,0:T(8,128)(2,1)} %collective-permute-done.1.refs_2_, bf16[512,1024]{1,0:T(8,128)(2,1)} %collective-permute-done.6.refs_3_, ...), custom_call_target="tpu_custom_call" | custom-call | flops 2000 | bytes 14680 | tf_op jit(solution)/shard_map/terms/pallas_call | solution.py:526
  73.0 19.5 %all-to-all-start.1 = ((bf16[8,32,16,128]{3,2,1,0:T(8,128)(2,1)}), bf16[8,32,16,128]{3,2,1,0:T(8,128)(2,1)}, u32[]{:S(2)}, u32[]{:S(2)}) async-start(bf16[8,32,16,128]{3,2,1,0:T(8,128)(2,1)} %get-tuple-element.59), calls=%async_computation.1 | async-start | bytes 2097152 | tf_op jit(solution)/shard_map/all_to_all | solution.py:700
  92.5 1.6 collective-permute-start.8
  94.1 0.0 collective-permute-done.9.refs_6_
  94.1 1.9 %collective-permute-start.10 = (bf16[1024,512]{1,0:T(8,128)(2,1)}, bf16[1024,512]{1,0:T(8,128)(2,1)}, u32[]{:S(2)}, u32[]{:S(2)}) collective-permute-start(bf16[1024,512]{1,0:T(8,128)(2,1)} %collective-permute-done.9.refs_6_), channel_id=1, source_target_pairs={{0,4},{4,0},{24,28},{28,24},{1,5},{5,1},{25,29},{29,25},{2,6},{6,2... | collective-permute-start | bytes 3145736 | tf_op jit(solution)/shard_map/ppermute | solution.py:716
  96.0 4.0 %collective-permute-done.11.refs_8_ = bf16[1024,512]{1,0:T(8,128)(2,1)} collective-permute-done((bf16[1024,512]{1,0:T(8,128)(2,1)}, bf16[1024,512]{1,0:T(8,128)(2,1)}, u32[]{:S(2)}, u32[]{:S(2)}) %collective-permute-start.11) | collective-permute-done | bytes 1048608 | tf_op jit(solution)/shard_map/ppermute | solution.py:716
  100.0 9.2 %collective-permute-start.13 = (bf16[1024,512]{1,0:T(8,128)(2,1)}, bf16[1024,512]{1,0:T(8,128)(2,1)}, u32[]{:S(2)}, u32[]{:S(2)}) collective-permute-start(bf16[1024,512]{1,0:T(8,128)(2,1)} %collective-permute-done.11.refs_8_), channel_id=1, source_target_pairs={{0,4},{4,0},{24,28},{28,24},{1,5},{5,1},{25,29},{29,25},{2,6},{6,2... | collective-permute-start | bytes 3145736 | tf_op jit(solution)/shard_map/ppermute | solution.py:716
  109.2 0.0 collective-permute-done.10.refs_7_
  109.2 2.4 %collective-permute-done.13.refs_9_ = bf16[1024,512]{1,0:T(8,128)(2,1)} collective-permute-done((bf16[1024,512]{1,0:T(8,128)(2,1)}, bf16[1024,512]{1,0:T(8,128)(2,1)}, u32[]{:S(2)}, u32[]{:S(2)}) %collective-permute-start.13) | collective-permute-done | bytes 1048608 | tf_op jit(solution)/shard_map/ppermute | solution.py:716
  111.6 9.3 %mix_late.1 = (bf16[512,1024]{1,0:T(8,128)(2,1)}, bf16[32,16,128]{2,1,0:T(8,128)(2,1)}, bf16[32,16,128]{2,1,0:T(8,128)(2,1)}, bf16[32,16,128]{2,1,0:T(8,128)(2,1...) custom-call(s32[4]{0:T(128)} %pad_add_fusion.place_ref, ...), custom_call_target="tpu_custom_call" | custom-call | flops 1000 | bytes 8388 | tf_op jit(solution)/shard_map/mix_late/pallas_call | solution.py:609
  120.9 5.0 %collective-permute-start.14 = (bf16[32,16,128]{2,1,0:T(8,128)(2,1)}, bf16[32,16,128]{2,1,0:T(8,128)(2,1)S(1)}, u32[]{:S(2)}, u32[]{:S(2)}) collective-permute-start(bf16[32,16,128]{2,1,0:T(8,128)(2,1)} %get-tuple-element.51), channel_id=1, source_target_pairs={{0,24},{4,28},{8,16},{12,20},{16,8},{20,12},{24,0},{28,4},{1,25},{... | collective-permute-start | bytes 393224 | tf_op jit(solution)/shard_map/ppermute | solution.py:705
  125.9 0.0 collective-permute-start.15
  125.9 0.4 collective-permute-start.16
  126.2 4.3 %collective-permute-start.17 = (bf16[32,16,128]{2,1,0:T(8,128)(2,1)}, bf16[32,16,128]{2,1,0:T(8,128)(2,1)S(1)}, u32[]{:S(2)}, u32[]{:S(2)}) collective-permute-start(bf16[32,16,128]{2,1,0:T(8,128)(2,1)} %get-tuple-element.54), channel_id=1, source_target_pairs={{0,28},{4,24},{8,20},{12,16},{16,12},{20,8},{24,4},{28,0},{1,29},{... | collective-permute-start | bytes 393224 | tf_op jit(solution)/shard_map/ppermute | solution.py:705
  130.5 0.0 collective-permute-done.14.refs_0_
  130.5 0.4 collective-permute-start.19
  130.9 5.2 %collective-permute-done.15.refs_1_ = bf16[32,16,128]{2,1,0:T(8,128)(2,1)S(1)} collective-permute-done((bf16[32,16,128]{2,1,0:T(8,128)(2,1)}, bf16[32,16,128]{2,1,0:T(8,128)(2,1)S(1)}, u32[]{:S(2)}, u32[]{:S(2)}) %collective-permute-start.15) | collective-permute-done | bytes 131104 | tf_op jit(solution)/shard_map/ppermute | solution.py:705
  136.1 5.4 %collective-permute-start.20 = (bf16[32,16,128]{2,1,0:T(8,128)(2,1)}, bf16[32,16,128]{2,1,0:T(8,128)(2,1)S(1)}, u32[]{:S(2)}, u32[]{:S(2)}) collective-permute-start(bf16[32,16,128]{2,1,0:T(8,128)(2,1)} %get-tuple-element.57), channel_id=1, source_target_pairs={{0,4},{4,0},{8,12},{12,8},{16,20},{20,16},{24,28},{28,24},{1,5},{5... | collective-permute-start | bytes 393224 | tf_op jit(solution)/shard_map/ppermute | solution.py:705
  141.5 5.4 %collective-permute-done.18.refs_4_ = bf16[32,16,128]{2,1,0:T(8,128)(2,1)S(1)} collective-permute-done((bf16[32,16,128]{2,1,0:T(8,128)(2,1)}, bf16[32,16,128]{2,1,0:T(8,128)(2,1)S(1)}, u32[]{:S(2)}, u32[]{:S(2)}) %collective-permute-start.18) | collective-permute-done | bytes 131104 | tf_op jit(solution)/shard_map/ppermute | solution.py:705
  147.0 0.0 collective-permute-done.19.refs_5_
  147.0 0.0 collective-permute-done.20.refs_6_
  147.0 0.0 all-to-all-done.1.part_ref
  147.0 7.2 %convolve.3 = (bf16[32,16,128]{2,1,0:T(8,128)(2,1)S(1)}, bf16[32,16,128]{2,1,0:T(8,128)(2,1)S(1)}, bf16[32,16,128]{2,1,0:T(8,128)(2,1)}, bf16[32,16,128]{2,1,0:T...) custom-call(s32[1]{0:T(128)} %bitcast.3.place_ref, ...), custom_call_target="tpu_custom_call" | custom-call | flops 2000 | bytes 14680 | tf_op jit(solution)/shard_map/convolve/pallas_call | solution.py:393
  154.2 2.3 %collective-permute-start.21 = (bf16[32,16,128]{2,1,0:T(8,128)(2,1)S(1)}, bf16[32,16,128]{2,1,0:T(8,128)(2,1)S(1)}, u32[]{:S(2)}, u32[]{:S(2)}) collective-permute-start(bf16[32,16,128]{2,1,0:T(8,128)(2,1)S(1)} %get-tuple-element.70), channel_id=1, source_target_pairs={{0,24},{4,28},{8,16},{12,20},{16,8},{20,12},{24,0},{28,4},{1,25},{... | collective-permute-start | bytes 393224 | tf_op jit(solution)/shard_map/ppermute | solution.py:705
  156.5 0.0 collective-permute-start.22
  156.5 1.8 collective-permute-start.23
  158.3 1.0 collective-permute-start.24
  159.3 0.2 collective-permute-start.25
  159.5 1.2 collective-permute-done.21.refs_0_
  160.7 2.0 %collective-permute-start.26 = (bf16[32,16,128]{2,1,0:T(8,128)(2,1)}, bf16[32,16,128]{2,1,0:T(8,128)(2,1)S(1)}, u32[]{:S(2)}, u32[]{:S(2)}) collective-permute-start(bf16[32,16,128]{2,1,0:T(8,128)(2,1)} %get-tuple-element.75), channel_id=1, source_target_pairs={{0,20},{4,16},{8,28},{12,24},{16,4},{20,0},{24,12},{28,8},{1,21},{... | collective-permute-start | bytes 393224 | tf_op jit(solution)/shard_map/ppermute | solution.py:705
  162.7 1.6 collective-permute-done.22.refs_1_
  164.3 0.6 collective-permute-start.27
  164.9 3.8 %finish_whole.1 = bf16[512,1024]{1,0:T(8,128)(2,1)} custom-call(bf16[8,32,16,128]{3,2,1,0:T(8,128)(2,1)} %all-to-all-done.1.part_ref, bf16[512,1024]{1,0:T(8,128)(2,1)} %get-tuple-element.61.factor_ref), custom_call_target="tpu_custom_call" | custom-call | flops 1 | bytes 3145 | tf_op jit(solution)/shard_map/finish_whole/pallas_call | solution.py:686
  168.7 7.2 %filter_gradient.1 = f32[128,4096]{1,0:T(8,128)} custom-call(bf16[8320,128]{1,0:T(8,128)(2,1)} %get-tuple-element.80.s_ref, bf16[8320,128]{1,0:T(8,128)(2,1)} %get-tuple-element.81.g_ref, bf16[65,64,128]{2,1,0:T(8,128)(2,1)} %constant.45.clone.refs_4_.refs_11_.inv_ref, bf16[128,256]{1,0:T(8,128)(2,1)} %constant.50.last_ref), custom_call_target="tpu_custom_call" | custom-call | flops 1000 | bytes 12582 | tf_op jit(solution)/shard_map/filter_gradient/pallas_call | solution.py:421
  175.9 0.0 collective-permute-done.23.refs_2_
  175.9 0.0 collective-permute-done.24.refs_3_
  175.9 2.5 %collective-permute-done.26.refs_5_ = bf16[32,16,128]{2,1,0:T(8,128)(2,1)S(1)} collective-permute-done((bf16[32,16,128]{2,1,0:T(8,128)(2,1)}, bf16[32,16,128]{2,1,0:T(8,128)(2,1)S(1)}, u32[]{:S(2)}, u32[]{:S(2)}) %collective-permute-start.26) | collective-permute-done | bytes 131104 | tf_op jit(solution)/shard_map/ppermute | solution.py:705
  178.4 0.0 collective-permute-done.27.refs_6_
  178.4 3.5 %finish.1 = (bf16[512,1024]{1,0:T(8,128)(2,1)}, bf16[512,1024]{1,0:T(8,128)(2,1)}) custom-call(s32[4]{0:T(128)S(1)} %copy-done.2, bf16[32,16,128]{2,1,0:T(8,128)(2,1)S(1)} %collective-permute-done.21.refs_0_, bf16[32,16,128]{2,1,0:T(8,128)(2,1)S(1)} %collective-permute-done.22.refs_1_, bf16[32,16,128]{2,1,0:T(8,128)(2,1)S(1)} %collective-permute-done.23.refs_2_, ...), custom_call_target="tpu_custom_call" | custom-call | flops 1 | bytes 5242 | tf_op jit(solution)/shard_map/finish/pallas_call | solution.py:657
  (12 shorter events, 0.0 us)
Async XLA Ops:
  0.6 25.4 %collective-permute-start.2 = (bf16[1024,512]{1,0:T(8,128)(2,1)}, bf16[1024,512]{1,0:T(8,128)(2,1)}, u32[]{:S(2)}, u32[]{:S(2)}) collective-permute-start(bf16[1024,512]{1,0:T(8,128)(2,1)} %refs_4_.1), channel_id=1, source_target_pairs={{0,8},{4,12},{8,0},{12,4},{16,24},{20,28},{24,16},{28,20},{1,9},{5... | collective-permute-start | bytes 3145736 | tf_op jit(solution)/shard_map/ppermute | solution.py:716
  2.8 23.2 %collective-permute-start.3 = (bf16[1024,512]{1,0:T(8,128)(2,1)}, bf16[1024,512]{1,0:T(8,128)(2,1)}, u32[]{:S(2)}, u32[]{:S(2)}) collective-permute-start(bf16[1024,512]{1,0:T(8,128)(2,1)} %refs_4_.1), channel_id=1, source_target_pairs={{8,16},{12,20},{16,8},{20,12},{9,17},{13,21},{17,9},{21,13},{10,18... | collective-permute-start | bytes 3145736 | tf_op jit(solution)/shard_map/ppermute | solution.py:716
  8.3 44.0 %all-to-all-start = ((bf16[8,32,16,128]{3,2,1,0:T(8,128)(2,1)}), bf16[8,32,16,128]{3,2,1,0:T(8,128)(2,1)}, u32[]{:S(2)}, u32[]{:S(2)}) async-start(bf16[8,32,16,128]{3,2,1,0:T(8,128)(2,1)} %gate.1), calls=%async_computation | async-start | bytes 2097152 | tf_op jit(solution)/shard_map/all_to_all | solution.py:700
  13.9 38.4 %copy-start = (bf16[9,128,256]{2,1,0:T(8,128)(2,1)S(1)}, bf16[9,128,256]{2,1,0:T(8,128)(2,1)}, u32[]{:S(2)}) copy-start(bf16[9,128,256]{2,1,0:T(8,128)(2,1)} %constant.46.clone.refs_5_.refs_12_) | copy-start | bytes 1769476
  14.0 25.0 %collective-permute-start.1 = (bf16[512,1024]{1,0:T(8,128)(2,1)}, bf16[512,1024]{1,0:T(8,128)(2,1)}, u32[]{:S(2)}, u32[]{:S(2)}) collective-permute-start(bf16[512,1024]{1,0:T(8,128)(2,1)} %refs_0_.3), channel_id=1, source_target_pairs={{0,2},{1,3},{2,0},{3,1},{4,6},{5,7},{6,4},{7,5},{8,10},{9,11},{10,... | collective-permute-start | bytes 3145736 | tf_op jit(solution)/shard_map/ppermute | solution.py:729
  15.2 24.7 %collective-permute-start = (bf16[512,1024]{1,0:T(8,128)(2,1)}, bf16[512,1024]{1,0:T(8,128)(2,1)}, u32[]{:S(2)}, u32[]{:S(2)}) collective-permute-start(bf16[512,1024]{1,0:T(8,128)(2,1)} %refs_0_.3), channel_id=1, source_target_pairs={{0,1},{1,0},{2,3},{3,2},{4,5},{5,4},{6,7},{7,6},{8,9},{9,8},{10,11... | collective-permute-start | bytes 3145736 | tf_op jit(solution)/shard_map/ppermute | solution.py:729
  26.0 13.9 %collective-permute-start.4 = (bf16[1024,512]{1,0:T(8,128)(2,1)}, bf16[1024,512]{1,0:T(8,128)(2,1)}, u32[]{:S(2)}, u32[]{:S(2)}) collective-permute-start(bf16[1024,512]{1,0:T(8,128)(2,1)} %collective-permute-done.2.refs_6_), channel_id=1, source_target_pairs={{0,4},{4,0},{8,12},{12,8},{16,20},{20,16},{24,28},{28,24},{1,5},{5... | collective-permute-start | bytes 3145736 | tf_op jit(solution)/shard_map/ppermute | solution.py:716
  28.1 11.8 %collective-permute-start.5 = (bf16[1024,512]{1,0:T(8,128)(2,1)}, bf16[1024,512]{1,0:T(8,128)(2,1)}, u32[]{:S(2)}, u32[]{:S(2)}) collective-permute-start(bf16[1024,512]{1,0:T(8,128)(2,1)} %collective-permute-done.3.refs_8_), channel_id=1, source_target_pairs={{8,12},{12,8},{16,20},{20,16},{9,13},{13,9},{17,21},{21,17},{10,14... | collective-permute-start | bytes 3145736 | tf_op jit(solution)/shard_map/ppermute | solution.py:716
  29.7 30.8 %collective-permute-start.7 = (bf16[1024,512]{1,0:T(8,128)(2,1)}, bf16[1024,512]{1,0:T(8,128)(2,1)}, u32[]{:S(2)}, u32[]{:S(2)}) collective-permute-start(bf16[1024,512]{1,0:T(8,128)(2,1)} %collective-permute-done.2.refs_6_), channel_id=1, source_target_pairs={{8,16},{12,20},{16,8},{20,12},{9,17},{13,21},{17,9},{21,13},{10,18... | collective-permute-start | bytes 3145736 | tf_op jit(solution)/shard_map/ppermute | solution.py:716
  39.9 24.7 %collective-permute-start.6 = (bf16[512,1024]{1,0:T(8,128)(2,1)}, bf16[512,1024]{1,0:T(8,128)(2,1)}, u32[]{:S(2)}, u32[]{:S(2)}) collective-permute-start(bf16[512,1024]{1,0:T(8,128)(2,1)} %refs_0_.3), channel_id=1, source_target_pairs={{0,3},{1,2},{2,1},{3,0},{4,7},{5,6},{6,5},{7,4},{8,11},{9,10},{10,... | collective-permute-start | bytes 3145736 | tf_op jit(solution)/shard_map/ppermute | solution.py:729
  41.2 23.4 %collective-permute-start.12 = (bf16[1024,512]{1,0:T(8,128)(2,1)}, bf16[1024,512]{1,0:T(8,128)(2,1)}, u32[]{:S(2)}, u32[]{:S(2)}) collective-permute-start(bf16[1024,512]{1,0:T(8,128)(2,1)} %refs_4_.1), channel_id=1, source_target_pairs={{0,4},{4,0},{8,12},{12,8},{16,20},{20,16},{24,28},{28,24},{1,5},{5... | collective-permute-start | bytes 3145736 | tf_op jit(solution)/shard_map/ppermute | solution.py:716
  42.5 51.6 %collective-permute-start.9 = (bf16[1024,512]{1,0:T(8,128)(2,1)}, bf16[1024,512]{1,0:T(8,128)(2,1)}, u32[]{:S(2)}, u32[]{:S(2)}) collective-permute-start(bf16[1024,512]{1,0:T(8,128)(2,1)} %collective-permute-done.3.refs_8_), channel_id=1, source_target_pairs={{8,0},{12,4},{16,24},{20,28},{9,1},{13,5},{17,25},{21,29},{10,2},{... | collective-permute-start | bytes 3145736 | tf_op jit(solution)/shard_map/ppermute | solution.py:716
  52.4 1.1 copy-start.1
  60.5 39.5 %collective-permute-start.11 = (bf16[1024,512]{1,0:T(8,128)(2,1)}, bf16[1024,512]{1,0:T(8,128)(2,1)}, u32[]{:S(2)}, u32[]{:S(2)}) collective-permute-start(bf16[1024,512]{1,0:T(8,128)(2,1)} %collective-permute-done.7.refs_4_), channel_id=1, source_target_pairs={{8,0},{12,4},{16,24},{20,28},{9,1},{13,5},{17,25},{21,29},{10,2},{... | collective-permute-start | bytes 3145736 | tf_op jit(solution)/shard_map/ppermute | solution.py:716
  73.0 74.0 %all-to-all-start.1 = ((bf16[8,32,16,128]{3,2,1,0:T(8,128)(2,1)}), bf16[8,32,16,128]{3,2,1,0:T(8,128)(2,1)}, u32[]{:S(2)}, u32[]{:S(2)}) async-start(bf16[8,32,16,128]{3,2,1,0:T(8,128)(2,1)} %get-tuple-element.59), calls=%async_computation.1 | async-start | bytes 2097152 | tf_op jit(solution)/shard_map/all_to_all | solution.py:700
  92.5 16.7 %collective-permute-start.8 = (bf16[1024,512]{1,0:T(8,128)(2,1)}, bf16[1024,512]{1,0:T(8,128)(2,1)}, u32[]{:S(2)}, u32[]{:S(2)}) collective-permute-start(bf16[1024,512]{1,0:T(8,128)(2,1)} %collective-permute-done.7.refs_4_), channel_id=1, source_target_pairs={{8,12},{12,8},{16,20},{20,16},{9,13},{13,9},{17,21},{21,17},{10,14... | collective-permute-start | bytes 3145736 | tf_op jit(solution)/shard_map/ppermute | solution.py:716
  94.1 15.1 %collective-permute-start.10 = (bf16[1024,512]{1,0:T(8,128)(2,1)}, bf16[1024,512]{1,0:T(8,128)(2,1)}, u32[]{:S(2)}, u32[]{:S(2)}) collective-permute-start(bf16[1024,512]{1,0:T(8,128)(2,1)} %collective-permute-done.9.refs_6_), channel_id=1, source_target_pairs={{0,4},{4,0},{24,28},{28,24},{1,5},{5,1},{25,29},{29,25},{2,6},{6,2... | collective-permute-start | bytes 3145736 | tf_op jit(solution)/shard_map/ppermute | solution.py:716
  100.0 11.6 %collective-permute-start.13 = (bf16[1024,512]{1,0:T(8,128)(2,1)}, bf16[1024,512]{1,0:T(8,128)(2,1)}, u32[]{:S(2)}, u32[]{:S(2)}) collective-permute-start(bf16[1024,512]{1,0:T(8,128)(2,1)} %collective-permute-done.11.refs_8_), channel_id=1, source_target_pairs={{0,4},{4,0},{24,28},{28,24},{1,5},{5,1},{25,29},{29,25},{2,6},{6,2... | collective-permute-start | bytes 3145736 | tf_op jit(solution)/shard_map/ppermute | solution.py:716
  120.9 9.6 %collective-permute-start.14 = (bf16[32,16,128]{2,1,0:T(8,128)(2,1)}, bf16[32,16,128]{2,1,0:T(8,128)(2,1)S(1)}, u32[]{:S(2)}, u32[]{:S(2)}) collective-permute-start(bf16[32,16,128]{2,1,0:T(8,128)(2,1)} %get-tuple-element.51), channel_id=1, source_target_pairs={{0,24},{4,28},{8,16},{12,20},{16,8},{20,12},{24,0},{28,4},{1,25},{... | collective-permute-start | bytes 393224 | tf_op jit(solution)/shard_map/ppermute | solution.py:705
  125.9 10.2 %collective-permute-start.15 = (bf16[32,16,128]{2,1,0:T(8,128)(2,1)}, bf16[32,16,128]{2,1,0:T(8,128)(2,1)S(1)}, u32[]{:S(2)}, u32[]{:S(2)}) collective-permute-start(bf16[32,16,128]{2,1,0:T(8,128)(2,1)} %get-tuple-element.52), channel_id=1, source_target_pairs={{0,16},{4,20},{8,24},{12,28},{16,0},{20,4},{24,8},{28,12},{1,17},{... | collective-permute-start | bytes 393224 | tf_op jit(solution)/shard_map/ppermute | solution.py:705
  125.9 15.6 %collective-permute-start.16 = (bf16[32,16,128]{2,1,0:T(8,128)(2,1)}, bf16[32,16,128]{2,1,0:T(8,128)(2,1)S(1)}, u32[]{:S(2)}, u32[]{:S(2)}) collective-permute-start(bf16[32,16,128]{2,1,0:T(8,128)(2,1)} %get-tuple-element.53), channel_id=1, source_target_pairs={{0,8},{4,12},{8,0},{12,4},{16,24},{20,28},{24,16},{28,20},{1,9},{5... | collective-permute-start | bytes 393224 | tf_op jit(solution)/shard_map/ppermute | solution.py:705
  126.2 15.3 %collective-permute-start.17 = (bf16[32,16,128]{2,1,0:T(8,128)(2,1)}, bf16[32,16,128]{2,1,0:T(8,128)(2,1)S(1)}, u32[]{:S(2)}, u32[]{:S(2)}) collective-permute-start(bf16[32,16,128]{2,1,0:T(8,128)(2,1)} %get-tuple-element.54), channel_id=1, source_target_pairs={{0,28},{4,24},{8,20},{12,16},{16,12},{20,8},{24,4},{28,0},{1,29},{... | collective-permute-start | bytes 393224 | tf_op jit(solution)/shard_map/ppermute | solution.py:705
  130.5 16.4 %collective-permute-start.18 = (bf16[32,16,128]{2,1,0:T(8,128)(2,1)}, bf16[32,16,128]{2,1,0:T(8,128)(2,1)S(1)}, u32[]{:S(2)}, u32[]{:S(2)}) collective-permute-start(bf16[32,16,128]{2,1,0:T(8,128)(2,1)} %get-tuple-element.55), channel_id=1, source_target_pairs={{0,20},{4,16},{8,28},{12,24},{16,4},{20,0},{24,12},{28,8},{1,21},{... | collective-permute-start | bytes 393224 | tf_op jit(solution)/shard_map/ppermute | solution.py:705
  130.5 16.4 %collective-permute-start.19 = (bf16[32,16,128]{2,1,0:T(8,128)(2,1)}, bf16[32,16,128]{2,1,0:T(8,128)(2,1)S(1)}, u32[]{:S(2)}, u32[]{:S(2)}) collective-permute-start(bf16[32,16,128]{2,1,0:T(8,128)(2,1)} %get-tuple-element.56), channel_id=1, source_target_pairs={{0,12},{4,8},{8,4},{12,0},{16,28},{20,24},{24,20},{28,16},{1,13},{... | collective-permute-start | bytes 393224 | tf_op jit(solution)/shard_map/ppermute | solution.py:705
  136.1 10.9 %collective-permute-start.20 = (bf16[32,16,128]{2,1,0:T(8,128)(2,1)}, bf16[32,16,128]{2,1,0:T(8,128)(2,1)S(1)}, u32[]{:S(2)}, u32[]{:S(2)}) collective-permute-start(bf16[32,16,128]{2,1,0:T(8,128)(2,1)} %get-tuple-element.57), channel_id=1, source_target_pairs={{0,4},{4,0},{8,12},{12,8},{16,20},{20,16},{24,28},{28,24},{1,5},{5... | collective-permute-start | bytes 393224 | tf_op jit(solution)/shard_map/ppermute | solution.py:705
  154.2 6.5 %collective-permute-start.21 = (bf16[32,16,128]{2,1,0:T(8,128)(2,1)S(1)}, bf16[32,16,128]{2,1,0:T(8,128)(2,1)S(1)}, u32[]{:S(2)}, u32[]{:S(2)}) collective-permute-start(bf16[32,16,128]{2,1,0:T(8,128)(2,1)S(1)} %get-tuple-element.70), channel_id=1, source_target_pairs={{0,24},{4,28},{8,16},{12,20},{16,8},{20,12},{24,0},{28,4},{1,25},{... | collective-permute-start | bytes 393224 | tf_op jit(solution)/shard_map/ppermute | solution.py:705
  156.5 7.8 %collective-permute-start.22 = (bf16[32,16,128]{2,1,0:T(8,128)(2,1)S(1)}, bf16[32,16,128]{2,1,0:T(8,128)(2,1)S(1)}, u32[]{:S(2)}, u32[]{:S(2)}) collective-permute-start(bf16[32,16,128]{2,1,0:T(8,128)(2,1)S(1)} %get-tuple-element.71), channel_id=1, source_target_pairs={{0,8},{4,12},{8,0},{12,4},{16,24},{20,28},{24,16},{28,20},{1,9},{5... | collective-permute-start | bytes 393224 | tf_op jit(solution)/shard_map/ppermute | solution.py:705
  156.5 19.4 %collective-permute-start.23 = (bf16[32,16,128]{2,1,0:T(8,128)(2,1)}, bf16[32,16,128]{2,1,0:T(8,128)(2,1)S(1)}, u32[]{:S(2)}, u32[]{:S(2)}) collective-permute-start(bf16[32,16,128]{2,1,0:T(8,128)(2,1)} %get-tuple-element.72), channel_id=1, source_target_pairs={{0,12},{4,8},{8,4},{12,0},{16,28},{20,24},{24,20},{28,16},{1,13},{... | collective-permute-start | bytes 393224 | tf_op jit(solution)/shard_map/ppermute | solution.py:705
  158.3 17.6 %collective-permute-start.24 = (bf16[32,16,128]{2,1,0:T(8,128)(2,1)}, bf16[32,16,128]{2,1,0:T(8,128)(2,1)S(1)}, u32[]{:S(2)}, u32[]{:S(2)}) collective-permute-start(bf16[32,16,128]{2,1,0:T(8,128)(2,1)} %get-tuple-element.73), channel_id=1, source_target_pairs={{0,28},{4,24},{8,20},{12,16},{16,12},{20,8},{24,4},{28,0},{1,29},{... | collective-permute-start | bytes 393224 | tf_op jit(solution)/shard_map/ppermute | solution.py:705
  159.3 16.6 %collective-permute-start.25 = (bf16[32,16,128]{2,1,0:T(8,128)(2,1)}, bf16[32,16,128]{2,1,0:T(8,128)(2,1)S(1)}, u32[]{:S(2)}, u32[]{:S(2)}) collective-permute-start(bf16[32,16,128]{2,1,0:T(8,128)(2,1)} %get-tuple-element.74), channel_id=1, source_target_pairs={{0,16},{4,20},{8,24},{12,28},{16,0},{20,4},{24,8},{28,12},{1,17},{... | collective-permute-start | bytes 393224 | tf_op jit(solution)/shard_map/ppermute | solution.py:705
  160.7 17.7 %collective-permute-start.26 = (bf16[32,16,128]{2,1,0:T(8,128)(2,1)}, bf16[32,16,128]{2,1,0:T(8,128)(2,1)S(1)}, u32[]{:S(2)}, u32[]{:S(2)}) collective-permute-start(bf16[32,16,128]{2,1,0:T(8,128)(2,1)} %get-tuple-element.75), channel_id=1, source_target_pairs={{0,20},{4,16},{8,28},{12,24},{16,4},{20,0},{24,12},{28,8},{1,21},{... | collective-permute-start | bytes 393224 | tf_op jit(solution)/shard_map/ppermute | solution.py:705
  164.3 14.1 %collective-permute-start.27 = (bf16[32,16,128]{2,1,0:T(8,128)(2,1)}, bf16[32,16,128]{2,1,0:T(8,128)(2,1)}, u32[]{:S(2)}, u32[]{:S(2)}) collective-permute-start(bf16[32,16,128]{2,1,0:T(8,128)(2,1)} %get-tuple-element.76), channel_id=1, source_target_pairs={{0,4},{4,0},{8,12},{12,8},{16,20},{20,16},{24,28},{28,24},{1,5},{5... | collective-permute-start | bytes 393224 | tf_op jit(solution)/shard_map/ppermute | solution.py:705
  168.7 9.7 %copy-start.2 = (s32[4]{0:T(128)S(1)}, s32[4]{0:T(128)}, u32[]{:S(2)}) copy-start(s32[4]{0:T(128)} %pad_add_fusion.place_ref) | copy-start | bytes 52

commit v8 on v6

--- a/solution.py
+++ b/solution.py
@@ -439,7 +439,7 @@
 
 def gate_kernel(key_ref, value_ref, out_ref, hold_ref):
     product = key_ref[...].astype(F32) * value_ref[...].astype(F32)
-    for g in range(WIDE // LANES):
+    for g in range(BATCH):
 
         def emit(a, rows):
             out_ref[g, a] = rows
@@ -449,13 +449,13 @@
 
 def gate(key_in, value_in, groups):
     rows, cols = key_in.shape
-    block = pl.BlockSpec((rows, WIDE), lambda j: (0, j))
+    block = pl.BlockSpec((rows, BATCH * LANES), lambda j: (0, j))
     return pl.pallas_call(
         gate_kernel,
-        grid=(cols // WIDE,),
+        grid=(cols // (BATCH * LANES),),
         out_shape=sds((groups, FAST, rows // FAST, LANES), BF16),
         in_specs=[block, block],
-        out_specs=pl.BlockSpec((WIDE // LANES, FAST, rows // FAST, LANES), lambda j: (j, 0, 0, 0)),
+        out_specs=pl.BlockSpec((BATCH, FAST, rows // FAST, LANES), lambda j: (j, 0, 0, 0)),
         scratch_shapes=[pltpu.VMEM((rows // FAST * GAP, LANES), F32)],
         compiler_params=PARAMS,
         cost_estimate=cost(10**6, 3 * 2**20),

time: 183 us -> 183 us (level)
    ppermute x3, waiting for transfers between devices: 10.7 us -> 8.61 us  [across(): return lax.ppermute(x, 'mp', [(i, i ^ d) for i in range(4)])]
  transfers between devices with their start and end apart: 30 -> 30, of which waited for: 12 -> 12; matrix products, arithmetic and copies ran while one was open for 0% -> 0% of each run, Pallas kernels for 25% -> 24%
where the time goes in v8:
time: 183 us; the launch traced here: 182 us
  starting transfers between devices  78.9 us (43%)
  Pallas kernels  54.7 us (30%)
  waiting for transfers between devices  45.4 us (25%)
    all_to_all x2, starting transfers between devices, exchange(): return lax.all_to_all(parts, 'ctx', split_axis=0, concat_axis=0, tiled=True)  26.2 us
    ppermute x11, starting transfers between devices, to(): return lax.ppermute(x, 'ctx', pairs)  25.8 us
    ppermute x14, starting transfers between devices, scatter(): lax.ppermute(part, 'ctx', [(i, i ^ d) for i in ids])  23.2 us
    ppermute x14, waiting for transfers between devices, scatter(): lax.ppermute(part, 'ctx', [(i, i ^ d) for i in ids])  15.9 us
    pallas_call x2, Pallas kernels, convolve(): pl.pallas_call(functools.partial(convolve_kernel, conjugate, count), out_...  13.4 us
    ppermute x11, waiting for transfers between devices, to(): return lax.ppermute(x, 'ctx', pairs)  11.2 us
    all_to_all x2, waiting for transfers between devices, exchange(): return lax.all_to_all(parts, 'ctx', split_axis=0, concat_axis=0, tiled=True)  9.62 us
    pallas_call x1, Pallas kernels, mix_late(): pl.pallas_call(late_kernel, out_shape=(sds((rows, cols), BF16),) + (sds((...  9.31 us
  transfers between devices with their start and end apart: 30, of which 12 were waited for; matrix products, arithmetic and copies ran while one was open for 0% of the time, Pallas kernels for 24%

profile of v8, /device:TPU:1, one launch (start us, length us, event | category | flops | bytes accessed | tf_op | source)
XLA Modules:
  0.0 182.1 jit_solution(17108075429500284624)
XLA Ops:
  0.6 2.2 %collective-permute-start.2 = (bf16[1024,512]{1,0:T(8,128)(2,1)}, bf16[1024,512]{1,0:T(8,128)(2,1)}, u32[]{:S(2)}, u32[]{:S(2)}) collective-permute-start(bf16[1024,512]{1,0:T(8,128)(2,1)} %refs_4_.1), channel_id=1, source_target_pairs={{0,8},{4,12},{8,0},{12,4},{16,24},{20,28},{24,16},{28,20},{1,9},{5... | collective-permute-start | bytes 3145736 | tf_op jit(solution)/shard_map/ppermute | solution.py:716
  2.8 1.7 collective-permute-start.3
  4.5 2.8 %gate.1 = bf16[8,32,16,128]{3,2,1,0:T(8,128)(2,1)} custom-call(bf16[512,1024]{1,0:T(8,128)(2,1)} %refs_9_.2, bf16[512,1024]{1,0:T(8,128)(2,1)} %refs_8_.1), custom_call_target="tpu_custom_call" | custom-call | flops 1 | bytes 3145 | tf_op jit(solution)/shard_map/gate/pallas_call | solution.py:453
  7.3 5.6 %all-to-all-start = ((bf16[8,32,16,128]{3,2,1,0:T(8,128)(2,1)}), bf16[8,32,16,128]{3,2,1,0:T(8,128)(2,1)}, u32[]{:S(2)}, u32[]{:S(2)}) async-start(bf16[8,32,16,128]{3,2,1,0:T(8,128)(2,1)} %gate.1), calls=%async_computation | async-start | bytes 2097152 | tf_op jit(solution)/shard_map/all_to_all | solution.py:700
  12.9 1.2 collective-permute-start.1
  14.1 1.2 collective-permute-start
  15.4 5.8 %filter_spectrum.1.refs_1_.refs_8_ = bf16[8320,128]{1,0:T(8,128)(2,1)} custom-call(f32[128,4096]{1,0:T(8,128)} %h_ref.1, bf16[256,128]{1,0:T(8,128)(2,1)} %constant.48.first_ref, bf16[65,64,128]{2,1,0:T(8,128)(2,1)} %constant.44.clone.fwd_ref.refs_3_.refs_10_), custom_call_target="tpu_custom_call" | custom-call | flops 1000 | bytes 8388 | tf_op jit(solution)/shard_map/filter_spectrum/pallas_call | solution.py:368
  21.2 4.8 %collective-permute-done.2.refs_6_ = bf16[1024,512]{1,0:T(8,128)(2,1)} collective-permute-done((bf16[1024,512]{1,0:T(8,128)(2,1)}, bf16[1024,512]{1,0:T(8,128)(2,1)}, u32[]{:S(2)}, u32[]{:S(2)}) %collective-permute-start.2) | collective-permute-done | bytes 1048608 | tf_op jit(solution)/shard_map/ppermute | solution.py:716
  26.0 0.0 collective-permute-done.3.refs_8_
  26.0 2.1 %collective-permute-start.4 = (bf16[1024,512]{1,0:T(8,128)(2,1)}, bf16[1024,512]{1,0:T(8,128)(2,1)}, u32[]{:S(2)}, u32[]{:S(2)}) collective-permute-start(bf16[1024,512]{1,0:T(8,128)(2,1)} %collective-permute-done.2.refs_6_), channel_id=1, source_target_pairs={{0,4},{4,0},{8,12},{12,8},{16,20},{20,16},{24,28},{28,24},{1,5},{5... | collective-permute-start | bytes 3145736 | tf_op jit(solution)/shard_map/ppermute | solution.py:716
  28.1 1.6 collective-permute-start.5
  29.7 1.6 collective-permute-start.7
  31.3 6.6 %collective-permute-done.1.refs_2_ = bf16[512,1024]{1,0:T(8,128)(2,1)} collective-permute-done((bf16[512,1024]{1,0:T(8,128)(2,1)}, bf16[512,1024]{1,0:T(8,128)(2,1)}, u32[]{:S(2)}, u32[]{:S(2)}) %collective-permute-start.1) | collective-permute-done | bytes 1048608 | tf_op jit(solution)/shard_map/ppermute | solution.py:729
  37.9 0.9 collective-permute-done.refs_1_
  38.8 0.0 collective-permute-done.4.refs_7_
  38.8 0.0 collective-permute-done.5.refs_9_
  38.9 1.3 collective-permute-start.6
  40.2 1.3 collective-permute-start.12
  41.5 1.3 collective-permute-start.9
  42.8 9.6 %all-to-all-done.refs_0_ = bf16[8,32,16,128]{3,2,1,0:T(8,128)(2,1)} async-done(((bf16[8,32,16,128]{3,2,1,0:T(8,128)(2,1)}), bf16[8,32,16,128]{3,2,1,0:T(8,128)(2,1)}, u32[]{:S(2)}, u32[]{:S(2)}) %all-to-all-start) | async-done | bytes 1048608 | tf_op jit(solution)/shard_map/all_to_all | solution.py:700
  52.4 1.1 copy-done.1
  53.4 7.1 %convolve.2 = (bf16[8,32,16,128]{3,2,1,0:T(8,128)(2,1)}, bf16[8320,128]{1,0:T(8,128)(2,1)}) custom-call(s32[1]{0:T(128)} %constant.42.clone.1.place_ref, bf16[8,32,16,128]{3,2,1,0:T(8,128)(2,1)} %all-to-all-done.refs_0_, bf16[8320,128]{1,0:T(8,128)(2,1)} %filter_spectrum.1.refs_1_.refs_8_, bf16[9,256,128]{2,1,0:T(8,128)(2,1)S(1)} %copy-done.1, ...), custom_call_target="tpu_custom_call" | custom-call | flops 2000 | bytes 14680 | tf_op jit(solution)/shard_map/convolve/pallas_call | solution.py:393
  60.5 0.0 collective-permute-done.7.refs_4_
  60.5 1.3 collective-permute-start.11
  61.8 0.6 pad_add_fusion.place_ref
  62.4 1.1 collective-permute-done.6.refs_3_
  63.5 8.4 %terms.1.refs_10_ = f32[512,1024]{1,0:T(8,128)} custom-call(s32[4]{0:T(128)} %pad_add_fusion.place_ref, bf16[512,1024]{1,0:T(8,128)(2,1)} %refs_0_.3, bf16[512,1024]{1,0:T(8,128)(2,1)} %collective-permute-done.refs_1_, bf16[512,1024]{1,0:T(8,128)(2,1)} %collective-permute-done.1.refs_2_, bf16[512,1024]{1,0:T(8,128)(2,1)} %collective-permute-done.6.refs_3_, ...), custom_call_target="tpu_custom_call" | custom-call | flops 2000 | bytes 14680 | tf_op jit(solution)/shard_map/terms/pallas_call | solution.py:526
  71.9 20.5 %all-to-all-start.1 = ((bf16[8,32,16,128]{3,2,1,0:T(8,128)(2,1)}), bf16[8,32,16,128]{3,2,1,0:T(8,128)(2,1)}, u32[]{:S(2)}, u32[]{:S(2)}) async-start(bf16[8,32,16,128]{3,2,1,0:T(8,128)(2,1)} %get-tuple-element.59), calls=%async_computation.1 | async-start | bytes 2097152 | tf_op jit(solution)/shard_map/all_to_all | solution.py:700
  92.5 1.6 collective-permute-start.8
  94.1 1.9 %collective-permute-start.10 = (bf16[1024,512]{1,0:T(8,128)(2,1)}, bf16[1024,512]{1,0:T(8,128)(2,1)}, u32[]{:S(2)}, u32[]{:S(2)}) collective-permute-start(bf16[1024,512]{1,0:T(8,128)(2,1)} %collective-permute-done.9.refs_6_), channel_id=1, source_target_pairs={{0,4},{4,0},{24,28},{28,24},{1,5},{5,1},{25,29},{29,25},{2,6},{6,2... | collective-permute-start | bytes 3145736 | tf_op jit(solution)/shard_map/ppermute | solution.py:716
  96.0 4.0 %collective-permute-done.11.refs_8_ = bf16[1024,512]{1,0:T(8,128)(2,1)} collective-permute-done((bf16[1024,512]{1,0:T(8,128)(2,1)}, bf16[1024,512]{1,0:T(8,128)(2,1)}, u32[]{:S(2)}, u32[]{:S(2)}) %collective-permute-start.11) | collective-permute-done | bytes 1048608 | tf_op jit(solution)/shard_map/ppermute | solution.py:716
  100.0 9.2 %collective-permute-start.13 = (bf16[1024,512]{1,0:T(8,128)(2,1)}, bf16[1024,512]{1,0:T(8,128)(2,1)}, u32[]{:S(2)}, u32[]{:S(2)}) collective-permute-start(bf16[1024,512]{1,0:T(8,128)(2,1)} %collective-permute-done.11.refs_8_), channel_id=1, source_target_pairs={{0,4},{4,0},{24,28},{28,24},{1,5},{5,1},{25,29},{29,25},{2,6},{6,2... | collective-permute-start | bytes 3145736 | tf_op jit(solution)/shard_map/ppermute | solution.py:716
  109.2 0.0 collective-permute-done.10.refs_7_
  109.2 0.0 collective-permute-done.8.refs_5_
  109.2 2.4 %collective-permute-done.13.refs_9_ = bf16[1024,512]{1,0:T(8,128)(2,1)} collective-permute-done((bf16[1024,512]{1,0:T(8,128)(2,1)}, bf16[1024,512]{1,0:T(8,128)(2,1)}, u32[]{:S(2)}, u32[]{:S(2)}) %collective-permute-start.13) | collective-permute-done | bytes 1048608 | tf_op jit(solution)/shard_map/ppermute | solution.py:716
  111.6 9.3 %mix_late.1 = (bf16[512,1024]{1,0:T(8,128)(2,1)}, bf16[32,16,128]{2,1,0:T(8,128)(2,1)}, bf16[32,16,128]{2,1,0:T(8,128)(2,1)}, bf16[32,16,128]{2,1,0:T(8,128)(2,1...) custom-call(s32[4]{0:T(128)} %pad_add_fusion.place_ref, ...), custom_call_target="tpu_custom_call" | custom-call | flops 1000 | bytes 8388 | tf_op jit(solution)/shard_map/mix_late/pallas_call | solution.py:609
  120.9 5.0 %collective-permute-start.14 = (bf16[32,16,128]{2,1,0:T(8,128)(2,1)}, bf16[32,16,128]{2,1,0:T(8,128)(2,1)S(1)}, u32[]{:S(2)}, u32[]{:S(2)}) collective-permute-start(bf16[32,16,128]{2,1,0:T(8,128)(2,1)} %get-tuple-element.51), channel_id=1, source_target_pairs={{0,24},{4,28},{8,16},{12,20},{16,8},{20,12},{24,0},{28,4},{1,25},{... | collective-permute-start | bytes 393224 | tf_op jit(solution)/shard_map/ppermute | solution.py:705
  125.9 0.0 collective-permute-start.15
  125.9 0.4 collective-permute-start.16
  126.2 4.3 %collective-permute-start.17 = (bf16[32,16,128]{2,1,0:T(8,128)(2,1)}, bf16[32,16,128]{2,1,0:T(8,128)(2,1)S(1)}, u32[]{:S(2)}, u32[]{:S(2)}) collective-permute-start(bf16[32,16,128]{2,1,0:T(8,128)(2,1)} %get-tuple-element.54), channel_id=1, source_target_pairs={{0,28},{4,24},{8,20},{12,16},{16,12},{20,8},{24,4},{28,0},{1,29},{... | collective-permute-start | bytes 393224 | tf_op jit(solution)/shard_map/ppermute | solution.py:705
  130.5 0.4 collective-permute-start.19
  130.9 5.2 %collective-permute-done.15.refs_1_ = bf16[32,16,128]{2,1,0:T(8,128)(2,1)S(1)} collective-permute-done((bf16[32,16,128]{2,1,0:T(8,128)(2,1)}, bf16[32,16,128]{2,1,0:T(8,128)(2,1)S(1)}, u32[]{:S(2)}, u32[]{:S(2)}) %collective-permute-start.15) | collective-permute-done | bytes 131104 | tf_op jit(solution)/shard_map/ppermute | solution.py:705
  136.1 5.4 %collective-permute-start.20 = (bf16[32,16,128]{2,1,0:T(8,128)(2,1)}, bf16[32,16,128]{2,1,0:T(8,128)(2,1)S(1)}, u32[]{:S(2)}, u32[]{:S(2)}) collective-permute-start(bf16[32,16,128]{2,1,0:T(8,128)(2,1)} %get-tuple-element.57), channel_id=1, source_target_pairs={{0,4},{4,0},{8,12},{12,8},{16,20},{20,16},{24,28},{28,24},{1,5},{5... | collective-permute-start | bytes 393224 | tf_op jit(solution)/shard_map/ppermute | solution.py:705
  141.5 5.4 %collective-permute-done.18.refs_4_ = bf16[32,16,128]{2,1,0:T(8,128)(2,1)S(1)} collective-permute-done((bf16[32,16,128]{2,1,0:T(8,128)(2,1)}, bf16[32,16,128]{2,1,0:T(8,128)(2,1)S(1)}, u32[]{:S(2)}, u32[]{:S(2)}) %collective-permute-start.18) | collective-permute-done | bytes 131104 | tf_op jit(solution)/shard_map/ppermute | solution.py:705
  146.9 0.0 collective-permute-done.19.refs_5_
  147.0 0.0 collective-permute-done.20.refs_6_
  147.0 0.0 all-to-all-done.1.part_ref
  147.0 6.4 %convolve.3 = (bf16[32,16,128]{2,1,0:T(8,128)(2,1)S(1)}, bf16[32,16,128]{2,1,0:T(8,128)(2,1)S(1)}, bf16[32,16,128]{2,1,0:T(8,128)(2,1)S(1)}, bf16[32,16,128]{2,1...) custom-call(s32[1]{0:T(128)} %bitcast.3.place_ref, ...), custom_call_target="tpu_custom_call" | custom-call | flops 2000 | bytes 14680 | tf_op jit(solution)/shard_map/convolve/pallas_call | solution.py:393
  153.3 0.7 copy-done.2
  154.0 2.2 %collective-permute-start.21 = (bf16[32,16,128]{2,1,0:T(8,128)(2,1)S(1)}, bf16[32,16,128]{2,1,0:T(8,128)(2,1)S(1)}, u32[]{:S(2)}, u32[]{:S(2)}) collective-permute-start(bf16[32,16,128]{2,1,0:T(8,128)(2,1)S(1)} %get-tuple-element.70), channel_id=1, source_target_pairs={{0,24},{4,28},{8,16},{12,20},{16,8},{20,12},{24,0},{28,4},{1,25},{... | collective-permute-start | bytes 393224 | tf_op jit(solution)/shard_map/ppermute | solution.py:705
  156.2 1.8 collective-permute-start.23
  158.1 1.0 collective-permute-start.24
  159.0 0.2 collective-permute-start.25
  159.2 1.2 collective-permute-done.21.refs_0_
  160.5 2.0 %collective-permute-start.26 = (bf16[32,16,128]{2,1,0:T(8,128)(2,1)S(1)}, bf16[32,16,128]{2,1,0:T(8,128)(2,1)}, u32[]{:S(2)}, u32[]{:S(2)}) collective-permute-start(bf16[32,16,128]{2,1,0:T(8,128)(2,1)S(1)} %get-tuple-element.75), channel_id=1, source_target_pairs={{0,20},{4,16},{8,28},{12,24},{16,4},{20,0},{24,12},{28,8},{1,21},{... | collective-permute-start | bytes 393224 | tf_op jit(solution)/shard_map/ppermute | solution.py:705
  162.5 1.6 collective-permute-done.22.refs_1_
  164.2 0.6 collective-permute-start.27
  164.7 3.8 %finish_whole.1 = bf16[512,1024]{1,0:T(8,128)(2,1)} custom-call(bf16[8,32,16,128]{3,2,1,0:T(8,128)(2,1)} %all-to-all-done.1.part_ref, bf16[512,1024]{1,0:T(8,128)(2,1)} %get-tuple-element.61.factor_ref), custom_call_target="tpu_custom_call" | custom-call | flops 1 | bytes 3145 | tf_op jit(solution)/shard_map/finish_whole/pallas_call | solution.py:686
  168.5 7.2 %filter_gradient.1 = f32[128,4096]{1,0:T(8,128)} custom-call(bf16[8320,128]{1,0:T(8,128)(2,1)} %get-tuple-element.80.s_ref, bf16[8320,128]{1,0:T(8,128)(2,1)} %get-tuple-element.81.g_ref, bf16[65,64,128]{2,1,0:T(8,128)(2,1)} %constant.45.clone.refs_4_.refs_11_.inv_ref, bf16[128,256]{1,0:T(8,128)(2,1)} %constant.50.last_ref), custom_call_target="tpu_custom_call" | custom-call | flops 1000 | bytes 12582 | tf_op jit(solution)/shard_map/filter_gradient/pallas_call | solution.py:421
  175.7 0.0 collective-permute-done.24.refs_3_
  175.7 0.0 collective-permute-done.25.refs_4_
  175.8 2.4 %collective-permute-done.26.refs_5_ = bf16[32,16,128]{2,1,0:T(8,128)(2,1)} collective-permute-done((bf16[32,16,128]{2,1,0:T(8,128)(2,1)S(1)}, bf16[32,16,128]{2,1,0:T(8,128)(2,1)}, u32[]{:S(2)}, u32[]{:S(2)}) %collective-permute-start.26) | collective-permute-done | bytes 131104 | tf_op jit(solution)/shard_map/ppermute | solution.py:705
  178.2 0.0 collective-permute-done.27.refs_6_
  178.2 4.0 %finish.1 = (bf16[512,1024]{1,0:T(8,128)(2,1)}, bf16[512,1024]{1,0:T(8,128)(2,1)}) custom-call(s32[4]{0:T(128)} %pad_add_fusion.place_ref, bf16[32,16,128]{2,1,0:T(8,128)(2,1)} %copy-done.3, bf16[32,16,128]{2,1,0:T(8,128)(2,1)} %copy-done.4, bf16[32,16,128]{2,1,0:T(8,128)(2,1)} %collective-permute-done.23.refs_2_, ...), custom_call_target="tpu_custom_call" | custom-call | flops 1 | bytes 5242 | tf_op jit(solution)/shard_map/finish/pallas_call | solution.py:657
  (16 shorter events, 0.0 us)
Async XLA Ops:
  0.6 25.4 %collective-permute-start.2 = (bf16[1024,512]{1,0:T(8,128)(2,1)}, bf16[1024,512]{1,0:T(8,128)(2,1)}, u32[]{:S(2)}, u32[]{:S(2)}) collective-permute-start(bf16[1024,512]{1,0:T(8,128)(2,1)} %refs_4_.1), channel_id=1, source_target_pairs={{0,8},{4,12},{8,0},{12,4},{16,24},{20,28},{24,16},{28,20},{1,9},{5... | collective-permute-start | bytes 3145736 | tf_op jit(solution)/shard_map/ppermute | solution.py:716
  2.8 23.2 %collective-permute-start.3 = (bf16[1024,512]{1,0:T(8,128)(2,1)}, bf16[1024,512]{1,0:T(8,128)(2,1)}, u32[]{:S(2)}, u32[]{:S(2)}) collective-permute-start(bf16[1024,512]{1,0:T(8,128)(2,1)} %refs_4_.1), channel_id=1, source_target_pairs={{8,16},{12,20},{16,8},{20,12},{9,17},{13,21},{17,9},{21,13},{10,18... | collective-permute-start | bytes 3145736 | tf_op jit(solution)/shard_map/ppermute | solution.py:716
  7.3 45.1 %all-to-all-start = ((bf16[8,32,16,128]{3,2,1,0:T(8,128)(2,1)}), bf16[8,32,16,128]{3,2,1,0:T(8,128)(2,1)}, u32[]{:S(2)}, u32[]{:S(2)}) async-start(bf16[8,32,16,128]{3,2,1,0:T(8,128)(2,1)} %gate.1), calls=%async_computation | async-start | bytes 2097152 | tf_op jit(solution)/shard_map/all_to_all | solution.py:700
  12.9 39.5 %copy-start = (bf16[9,128,256]{2,1,0:T(8,128)(2,1)S(1)}, bf16[9,128,256]{2,1,0:T(8,128)(2,1)}, u32[]{:S(2)}) copy-start(bf16[9,128,256]{2,1,0:T(8,128)(2,1)} %constant.46.clone.refs_5_.refs_12_) | copy-start | bytes 1769476
  12.9 25.0 %collective-permute-start.1 = (bf16[512,1024]{1,0:T(8,128)(2,1)}, bf16[512,1024]{1,0:T(8,128)(2,1)}, u32[]{:S(2)}, u32[]{:S(2)}) collective-permute-start(bf16[512,1024]{1,0:T(8,128)(2,1)} %refs_0_.3), channel_id=1, source_target_pairs={{0,2},{1,3},{2,0},{3,1},{4,6},{5,7},{6,4},{7,5},{8,10},{9,11},{10,... | collective-permute-start | bytes 3145736 | tf_op jit(solution)/shard_map/ppermute | solution.py:729
  14.1 24.7 %collective-permute-start = (bf16[512,1024]{1,0:T(8,128)(2,1)}, bf16[512,1024]{1,0:T(8,128)(2,1)}, u32[]{:S(2)}, u32[]{:S(2)}) collective-permute-start(bf16[512,1024]{1,0:T(8,128)(2,1)} %refs_0_.3), channel_id=1, source_target_pairs={{0,1},{1,0},{2,3},{3,2},{4,5},{5,4},{6,7},{7,6},{8,9},{9,8},{10,11... | collective-permute-start | bytes 3145736 | tf_op jit(solution)/shard_map/ppermute | solution.py:729
  26.0 12.8 %collective-permute-start.4 = (bf16[1024,512]{1,0:T(8,128)(2,1)}, bf16[1024,512]{1,0:T(8,128)(2,1)}, u32[]{:S(2)}, u32[]{:S(2)}) collective-permute-start(bf16[1024,512]{1,0:T(8,128)(2,1)} %collective-permute-done.2.refs_6_), channel_id=1, source_target_pairs={{0,4},{4,0},{8,12},{12,8},{16,20},{20,16},{24,28},{28,24},{1,5},{5... | collective-permute-start | bytes 3145736 | tf_op jit(solution)/shard_map/ppermute | solution.py:716
  28.1 10.8 %collective-permute-start.5 = (bf16[1024,512]{1,0:T(8,128)(2,1)}, bf16[1024,512]{1,0:T(8,128)(2,1)}, u32[]{:S(2)}, u32[]{:S(2)}) collective-permute-start(bf16[1024,512]{1,0:T(8,128)(2,1)} %collective-permute-done.3.refs_8_), channel_id=1, source_target_pairs={{8,12},{12,8},{16,20},{20,16},{9,13},{13,9},{17,21},{21,17},{10,14... | collective-permute-start | bytes 3145736 | tf_op jit(solution)/shard_map/ppermute | solution.py:716
  29.7 30.8 %collective-permute-start.7 = (bf16[1024,512]{1,0:T(8,128)(2,1)}, bf16[1024,512]{1,0:T(8,128)(2,1)}, u32[]{:S(2)}, u32[]{:S(2)}) collective-permute-start(bf16[1024,512]{1,0:T(8,128)(2,1)} %collective-permute-done.2.refs_6_), channel_id=1, source_target_pairs={{8,16},{12,20},{16,8},{20,12},{9,17},{13,21},{17,9},{21,13},{10,18... | collective-permute-start | bytes 3145736 | tf_op jit(solution)/shard_map/ppermute | solution.py:716
  38.9 24.7 %collective-permute-start.6 = (bf16[512,1024]{1,0:T(8,128)(2,1)}, bf16[512,1024]{1,0:T(8,128)(2,1)}, u32[]{:S(2)}, u32[]{:S(2)}) collective-permute-start(bf16[512,1024]{1,0:T(8,128)(2,1)} %refs_0_.3), channel_id=1, source_target_pairs={{0,3},{1,2},{2,1},{3,0},{4,7},{5,6},{6,5},{7,4},{8,11},{9,10},{10,... | collective-permute-start | bytes 3145736 | tf_op jit(solution)/shard_map/ppermute | solution.py:729
  40.2 23.4 %collective-permute-start.12 = (bf16[1024,512]{1,0:T(8,128)(2,1)}, bf16[1024,512]{1,0:T(8,128)(2,1)}, u32[]{:S(2)}, u32[]{:S(2)}) collective-permute-start(bf16[1024,512]{1,0:T(8,128)(2,1)} %refs_4_.1), channel_id=1, source_target_pairs={{0,4},{4,0},{8,12},{12,8},{16,20},{20,16},{24,28},{28,24},{1,5},{5... | collective-permute-start | bytes 3145736 | tf_op jit(solution)/shard_map/ppermute | solution.py:716
  41.5 52.6 %collective-permute-start.9 = (bf16[1024,512]{1,0:T(8,128)(2,1)}, bf16[1024,512]{1,0:T(8,128)(2,1)}, u32[]{:S(2)}, u32[]{:S(2)}) collective-permute-start(bf16[1024,512]{1,0:T(8,128)(2,1)} %collective-permute-done.3.refs_8_), channel_id=1, source_target_pairs={{8,0},{12,4},{16,24},{20,28},{9,1},{13,5},{17,25},{21,29},{10,2},{... | collective-permute-start | bytes 3145736 | tf_op jit(solution)/shard_map/ppermute | solution.py:716
  52.4 1.1 copy-start.1
  60.5 39.5 %collective-permute-start.11 = (bf16[1024,512]{1,0:T(8,128)(2,1)}, bf16[1024,512]{1,0:T(8,128)(2,1)}, u32[]{:S(2)}, u32[]{:S(2)}) collective-permute-start(bf16[1024,512]{1,0:T(8,128)(2,1)} %collective-permute-done.7.refs_4_), channel_id=1, source_target_pairs={{8,0},{12,4},{16,24},{20,28},{9,1},{13,5},{17,25},{21,29},{10,2},{... | collective-permute-start | bytes 3145736 | tf_op jit(solution)/shard_map/ppermute | solution.py:716
  71.9 75.0 %all-to-all-start.1 = ((bf16[8,32,16,128]{3,2,1,0:T(8,128)(2,1)}), bf16[8,32,16,128]{3,2,1,0:T(8,128)(2,1)}, u32[]{:S(2)}, u32[]{:S(2)}) async-start(bf16[8,32,16,128]{3,2,1,0:T(8,128)(2,1)} %get-tuple-element.59), calls=%async_computation.1 | async-start | bytes 2097152 | tf_op jit(solution)/shard_map/all_to_all | solution.py:700
  92.5 16.7 %collective-permute-start.8 = (bf16[1024,512]{1,0:T(8,128)(2,1)}, bf16[1024,512]{1,0:T(8,128)(2,1)}, u32[]{:S(2)}, u32[]{:S(2)}) collective-permute-start(bf16[1024,512]{1,0:T(8,128)(2,1)} %collective-permute-done.7.refs_4_), channel_id=1, source_target_pairs={{8,12},{12,8},{16,20},{20,16},{9,13},{13,9},{17,21},{21,17},{10,14... | collective-permute-start | bytes 3145736 | tf_op jit(solution)/shard_map/ppermute | solution.py:716
  94.1 15.1 %collective-permute-start.10 = (bf16[1024,512]{1,0:T(8,128)(2,1)}, bf16[1024,512]{1,0:T(8,128)(2,1)}, u32[]{:S(2)}, u32[]{:S(2)}) collective-permute-start(bf16[1024,512]{1,0:T(8,128)(2,1)} %collective-permute-done.9.refs_6_), channel_id=1, source_target_pairs={{0,4},{4,0},{24,28},{28,24},{1,5},{5,1},{25,29},{29,25},{2,6},{6,2... | collective-permute-start | bytes 3145736 | tf_op jit(solution)/shard_map/ppermute | solution.py:716
  100.0 11.6 %collective-permute-start.13 = (bf16[1024,512]{1,0:T(8,128)(2,1)}, bf16[1024,512]{1,0:T(8,128)(2,1)}, u32[]{:S(2)}, u32[]{:S(2)}) collective-permute-start(bf16[1024,512]{1,0:T(8,128)(2,1)} %collective-permute-done.11.refs_8_), channel_id=1, source_target_pairs={{0,4},{4,0},{24,28},{28,24},{1,5},{5,1},{25,29},{29,25},{2,6},{6,2... | collective-permute-start | bytes 3145736 | tf_op jit(solution)/shard_map/ppermute | solution.py:716
  120.9 9.6 %collective-permute-start.14 = (bf16[32,16,128]{2,1,0:T(8,128)(2,1)}, bf16[32,16,128]{2,1,0:T(8,128)(2,1)S(1)}, u32[]{:S(2)}, u32[]{:S(2)}) collective-permute-start(bf16[32,16,128]{2,1,0:T(8,128)(2,1)} %get-tuple-element.51), channel_id=1, source_target_pairs={{0,24},{4,28},{8,16},{12,20},{16,8},{20,12},{24,0},{28,4},{1,25},{... | collective-permute-start | bytes 393224 | tf_op jit(solution)/shard_map/ppermute | solution.py:705
  125.9 10.2 %collective-permute-start.15 = (bf16[32,16,128]{2,1,0:T(8,128)(2,1)}, bf16[32,16,128]{2,1,0:T(8,128)(2,1)S(1)}, u32[]{:S(2)}, u32[]{:S(2)}) collective-permute-start(bf16[32,16,128]{2,1,0:T(8,128)(2,1)} %get-tuple-element.52), channel_id=1, source_target_pairs={{0,16},{4,20},{8,24},{12,28},{16,0},{20,4},{24,8},{28,12},{1,17},{... | collective-permute-start | bytes 393224 | tf_op jit(solution)/shard_map/ppermute | solution.py:705
  125.9 15.6 %collective-permute-start.16 = (bf16[32,16,128]{2,1,0:T(8,128)(2,1)}, bf16[32,16,128]{2,1,0:T(8,128)(2,1)S(1)}, u32[]{:S(2)}, u32[]{:S(2)}) collective-permute-start(bf16[32,16,128]{2,1,0:T(8,128)(2,1)} %get-tuple-element.53), channel_id=1, source_target_pairs={{0,8},{4,12},{8,0},{12,4},{16,24},{20,28},{24,16},{28,20},{1,9},{5... | collective-permute-start | bytes 393224 | tf_op jit(solution)/shard_map/ppermute | solution.py:705
  126.2 15.3 %collective-permute-start.17 = (bf16[32,16,128]{2,1,0:T(8,128)(2,1)}, bf16[32,16,128]{2,1,0:T(8,128)(2,1)S(1)}, u32[]{:S(2)}, u32[]{:S(2)}) collective-permute-start(bf16[32,16,128]{2,1,0:T(8,128)(2,1)} %get-tuple-element.54), channel_id=1, source_target_pairs={{0,28},{4,24},{8,20},{12,16},{16,12},{20,8},{24,4},{28,0},{1,29},{... | collective-permute-start | bytes 393224 | tf_op jit(solution)/shard_map/ppermute | solution.py:705
  130.5 16.4 %collective-permute-start.18 = (bf16[32,16,128]{2,1,0:T(8,128)(2,1)}, bf16[32,16,128]{2,1,0:T(8,128)(2,1)S(1)}, u32[]{:S(2)}, u32[]{:S(2)}) collective-permute-start(bf16[32,16,128]{2,1,0:T(8,128)(2,1)} %get-tuple-element.55), channel_id=1, source_target_pairs={{0,20},{4,16},{8,28},{12,24},{16,4},{20,0},{24,12},{28,8},{1,21},{... | collective-permute-start | bytes 393224 | tf_op jit(solution)/shard_map/ppermute | solution.py:705
  130.5 16.4 %collective-permute-start.19 = (bf16[32,16,128]{2,1,0:T(8,128)(2,1)}, bf16[32,16,128]{2,1,0:T(8,128)(2,1)S(1)}, u32[]{:S(2)}, u32[]{:S(2)}) collective-permute-start(bf16[32,16,128]{2,1,0:T(8,128)(2,1)} %get-tuple-element.56), channel_id=1, source_target_pairs={{0,12},{4,8},{8,4},{12,0},{16,28},{20,24},{24,20},{28,16},{1,13},{... | collective-permute-start | bytes 393224 | tf_op jit(solution)/shard_map/ppermute | solution.py:705
  136.1 10.9 %collective-permute-start.20 = (bf16[32,16,128]{2,1,0:T(8,128)(2,1)}, bf16[32,16,128]{2,1,0:T(8,128)(2,1)S(1)}, u32[]{:S(2)}, u32[]{:S(2)}) collective-permute-start(bf16[32,16,128]{2,1,0:T(8,128)(2,1)} %get-tuple-element.57), channel_id=1, source_target_pairs={{0,4},{4,0},{8,12},{12,8},{16,20},{20,16},{24,28},{28,24},{1,5},{5... | collective-permute-start | bytes 393224 | tf_op jit(solution)/shard_map/ppermute | solution.py:705
  153.3 0.7 copy-start.2
  154.0 6.5 %collective-permute-start.21 = (bf16[32,16,128]{2,1,0:T(8,128)(2,1)S(1)}, bf16[32,16,128]{2,1,0:T(8,128)(2,1)S(1)}, u32[]{:S(2)}, u32[]{:S(2)}) collective-permute-start(bf16[32,16,128]{2,1,0:T(8,128)(2,1)S(1)} %get-tuple-element.70), channel_id=1, source_target_pairs={{0,24},{4,28},{8,16},{12,20},{16,8},{20,12},{24,0},{28,4},{1,25},{... | collective-permute-start | bytes 393224 | tf_op jit(solution)/shard_map/ppermute | solution.py:705
  156.2 7.9 %collective-permute-start.22 = (bf16[32,16,128]{2,1,0:T(8,128)(2,1)S(1)}, bf16[32,16,128]{2,1,0:T(8,128)(2,1)S(1)}, u32[]{:S(2)}, u32[]{:S(2)}) collective-permute-start(bf16[32,16,128]{2,1,0:T(8,128)(2,1)S(1)} %get-tuple-element.71), channel_id=1, source_target_pairs={{0,8},{4,12},{8,0},{12,4},{16,24},{20,28},{24,16},{28,20},{1,9},{5... | collective-permute-start | bytes 393224 | tf_op jit(solution)/shard_map/ppermute | solution.py:705
  156.2 19.5 %collective-permute-start.23 = (bf16[32,16,128]{2,1,0:T(8,128)(2,1)S(1)}, bf16[32,16,128]{2,1,0:T(8,128)(2,1)}, u32[]{:S(2)}, u32[]{:S(2)}) collective-permute-start(bf16[32,16,128]{2,1,0:T(8,128)(2,1)S(1)} %get-tuple-element.72), channel_id=1, source_target_pairs={{0,12},{4,8},{8,4},{12,0},{16,28},{20,24},{24,20},{28,16},{1,13},{... | collective-permute-start | bytes 393224 | tf_op jit(solution)/shard_map/ppermute | solution.py:705
  158.1 17.7 %collective-permute-start.24 = (bf16[32,16,128]{2,1,0:T(8,128)(2,1)S(1)}, bf16[32,16,128]{2,1,0:T(8,128)(2,1)}, u32[]{:S(2)}, u32[]{:S(2)}) collective-permute-start(bf16[32,16,128]{2,1,0:T(8,128)(2,1)S(1)} %get-tuple-element.73), channel_id=1, source_target_pairs={{0,28},{4,24},{8,20},{12,16},{16,12},{20,8},{24,4},{28,0},{1,29},{... | collective-permute-start | bytes 393224 | tf_op jit(solution)/shard_map/ppermute | solution.py:705
  159.0 16.7 %collective-permute-start.25 = (bf16[32,16,128]{2,1,0:T(8,128)(2,1)S(1)}, bf16[32,16,128]{2,1,0:T(8,128)(2,1)}, u32[]{:S(2)}, u32[]{:S(2)}) collective-permute-start(bf16[32,16,128]{2,1,0:T(8,128)(2,1)S(1)} %get-tuple-element.74), channel_id=1, source_target_pairs={{0,16},{4,20},{8,24},{12,28},{16,0},{20,4},{24,8},{28,12},{1,17},{... | collective-permute-start | bytes 393224 | tf_op jit(solution)/shard_map/ppermute | solution.py:705
  160.5 15.2 %copy-start.3 = (bf16[32,16,128]{2,1,0:T(8,128)(2,1)}, bf16[32,16,128]{2,1,0:T(8,128)(2,1)S(1)}, u32[]{:S(2)}) copy-start(bf16[32,16,128]{2,1,0:T(8,128)(2,1)S(1)} %collective-permute-done.21.refs_0_) | copy-start | bytes 393220
  160.5 17.7 %collective-permute-start.26 = (bf16[32,16,128]{2,1,0:T(8,128)(2,1)S(1)}, bf16[32,16,128]{2,1,0:T(8,128)(2,1)}, u32[]{:S(2)}, u32[]{:S(2)}) collective-permute-start(bf16[32,16,128]{2,1,0:T(8,128)(2,1)S(1)} %get-tuple-element.75), channel_id=1, source_target_pairs={{0,20},{4,16},{8,28},{12,24},{16,4},{20,0},{24,12},{28,8},{1,21},{... | collective-permute-start | bytes 393224 | tf_op jit(solution)/shard_map/ppermute | solution.py:705
  164.2 11.6 %copy-start.4 = (bf16[32,16,128]{2,1,0:T(8,128)(2,1)}, bf16[32,16,128]{2,1,0:T(8,128)(2,1)S(1)}, u32[]{:S(2)}) copy-start(bf16[32,16,128]{2,1,0:T(8,128)(2,1)S(1)} %collective-permute-done.22.refs_1_) | copy-start | bytes 393220
  164.2 14.0 %collective-permute-start.27 = (bf16[32,16,128]{2,1,0:T(8,128)(2,1)S(1)}, bf16[32,16,128]{2,1,0:T(8,128)(2,1)}, u32[]{:S(2)}, u32[]{:S(2)}) collective-permute-start(bf16[32,16,128]{2,1,0:T(8,128)(2,1)S(1)} %get-tuple-element.76), channel_id=1, source_target_pairs={{0,4},{4,0},{8,12},{12,8},{16,20},{20,16},{24,28},{28,24},{1,5},{5... | collective-permute-start | bytes 393224 | tf_op jit(solution)/shard_map/ppermute | solution.py:705
